TPU v7x, 32 devices: a whole 2x2x4 slice. The times are simulated.
32 devices in a mesh: dp: 8 (over y, x, core), expert: 4 (over z).
Axes of the slice: x: 2, y: 2, z: 4, core: 2. Of those that a mesh axis runs over, the one named last changes fastest.
Arguments:
- attended: bfloat16 [2560, 1536], P(('dp', 'expert')), may hold values from -6 to 6
- residual: bfloat16 [2560, 1536], P(('dp', 'expert')), may hold values from -16 to 16
- out_weight: bfloat16 [1536, 1536], replicated, may hold values from -0.15625 to 0.15625
- norm_gain: float32 [1536], replicated, may hold values from 0.1 to 1.9
- final_gain: float32 [1536], replicated, may hold values from 0.5 to 1.5
- routes: int32 [2560, 8], P(('dp', 'expert')), may hold values from 0 to 19, as said below
- gate_logits: int32 [2560, 8], P(('dp', 'expert')), may hold values from -1 to 1
- placement: int32 [20], replicated, may hold values from 0 to 19, each once
- gate_up: bfloat16 [20, 1536, 1024], P('expert', 'dp'), may hold values from -0.15625 to 0.15625
- down_weight: bfloat16 [20, 1536, 512], P('expert', 'dp'), may hold values from -0.5 to 0.5
Outputs:
- stream: bfloat16 [2560, 1536], P(('dp', 'expert'))
- normed: bfloat16 [2560, 1536], P(('dp', 'expert'))
Inputs may be any that keep to these rules, and one draw needn't show every extreme that they name: `routes`: each row names 8 different experts. Within the rows of one device no expert is named by more than 64 rows, and some expert is named by exactly 64 rows on every device. `placement`: slot s lies on index s // 5 of the expert axis; every expert is held by exactly one slot.
All inputs are finite; a program needn't handle non-finite values.
Results may differ from a plain program's by a relative error of at most 0.006.
Values may be sent and summed in bfloat16 or wider, within the bound.
No kernel may reach another device: no remote copies, remote signals or barrier semaphores. Data moves between devices by JAX's collectives and lax.ppermute only.
A program may use at most 128 MiB of HBM per device.

v0:
```python
import jax
import jax.numpy as jnp
from jax import lax
from jax.sharding import PartitionSpec as P

TOP = 8


EPS = 1e-06
LOGIT_SCALE = 0.5


def normalize(values, gain):
    return values * lax.rsqrt(jnp.mean(values * values, axis=-1, keepdims=True) + EPS) * gain


def combine_weights(logits):
    scores = jnp.exp(logits.astype(jnp.float32) * LOGIT_SCALE)
    return scores / jnp.sum(scores, axis=-1, keepdims=True)


def slot_numbers(routes, placement):
    count = placement.shape[0]
    ident = jnp.arange(count, dtype=jnp.int32)
    slot_of = jnp.sum(jnp.where(placement[None, :] == ident[:, None], ident[None, :], 0), axis=1)
    return jnp.sum(jnp.where(routes[..., None] == ident, slot_of, 0), axis=-1)


def ranks_within(slots, count):
    onehot = (slots[..., None] == jnp.arange(count, dtype=jnp.int32)).astype(jnp.int32)
    before = jnp.cumsum(onehot, axis=-2) - onehot
    return jnp.sum(before * onehot, axis=-1)


def expert_apply(buffer, gate_up, down_weight):
    whole_gate_up = lax.all_gather(gate_up, "dp", axis=1, tiled=True)
    gate_vals = jnp.einsum(
        "erd,edf->erf", buffer, whole_gate_up, preferred_element_type=jnp.float32
    )
    half = gate_vals.shape[-1] // 2
    hidden = (jax.nn.silu(gate_vals[..., :half]) * gate_vals[..., half:]).astype(jnp.bfloat16)
    whole_down = lax.all_gather(down_weight, "dp", axis=1, tiled=True)
    return jnp.einsum(
        "erf,edf->erd", hidden, whole_down, preferred_element_type=jnp.float32
    ).astype(jnp.bfloat16)


def body(
    attended,
    residual,
    out_weight,
    norm_gain,
    final_gain,
    routes,
    gate_logits,
    placement,
    gate_up,
    down_weight,
):
    mixed = residual.astype(jnp.float32) + jnp.dot(
        attended, out_weight, preferred_element_type=jnp.float32
    )
    stored = lax.optimization_barrier(mixed.astype(jnp.bfloat16))
    stream_in = stored.astype(jnp.float32)
    normed_in = normalize(stream_in, norm_gain).astype(jnp.bfloat16)
    tok_rows = attended.shape[0]
    width = attended.shape[1]
    groups = lax.axis_size("expert")
    local = gate_up.shape[0]
    capacity = 2 * tok_rows * TOP // (local * groups)
    per_expert = groups * capacity
    slots_total = local * per_expert
    count = placement.shape[0]
    weights = combine_weights(gate_logits)
    slots = slot_numbers(routes, placement).reshape(-1)
    ranks = ranks_within(slots, count)
    position = slots % local * per_expert + slots // local * capacity + ranks
    row_index = jnp.arange(tok_rows * TOP, dtype=jnp.int32) // TOP
    source_row = jnp.zeros((slots_total,), jnp.int32).at[position].set(row_index)
    filled = jnp.zeros((slots_total,), jnp.bool_).at[position].set(True)
    outgoing = jnp.where(filled[:, None], normed_in[source_row], jnp.zeros((), jnp.bfloat16))
    outgoing = outgoing.reshape(local, groups, capacity, width)
    incoming = lax.all_to_all(outgoing, "expert", split_axis=1, concat_axis=1, tiled=True).reshape(
        local, per_expert, width
    )
    produced = expert_apply(incoming, gate_up, down_weight)
    returned = lax.all_to_all(
        produced.reshape(local, groups, capacity, width),
        "expert",
        split_axis=1,
        concat_axis=1,
        tiled=True,
    )
    picked = returned.reshape(slots_total, width)[position].reshape(tok_rows, TOP, width)
    branch = jnp.sum(weights[..., None] * picked.astype(jnp.float32), axis=1)
    total = stream_in + branch
    return (total.astype(jnp.bfloat16), normalize(total, final_gain).astype(jnp.bfloat16))


def solution(mesh):
    placed = (
        P(("dp", "expert"), None),
        P(("dp", "expert"), None),
        P(),
        P(),
        P(),
        P(("dp", "expert"), None),
        P(("dp", "expert"), None),
        P(),
        P("expert", "dp", None),
        P("expert", "dp", None),
    )
    return jax.shard_map(
        body,
        mesh=mesh,
        in_specs=placed,
        out_specs=(P(("dp", "expert"), None), P(("dp", "expert"), None)),
        check_vma=False,
    )
```

profile of v0, /device:TPU:0, one launch (start us, length us, event | category | flops | bytes accessed | tf_op | source)
XLA Modules:
  0.0 276.5 jit_solution(17365143490671645590)
XLA Ops:
  7.2 0.7 all-gather.3.cloned.1.call-update
  8.0 0.7 all-gather.5.cloned.1.call-update
  8.7 0.8 select_reduce_fusion.1
  9.5 0.8 select_reduce_fusion
  10.5 1.5 reduce-window.6
  12.0 0.3 slice_reduce_fusion
  13.1 3.3 %fusion.2 = bf16[80,1536]{1,0:T(8,128)(2,1)S(1)} fusion(bf16[80,1536]{1,0:T(8,128)(2,1)S(1)} %copy-done, bf16[1536,1536]{1,0:T(8,128)(2,1)} %param.12, bf16[80,1536]{1,0:T(8,128)(2,1)S(1)} %copy-done.2), kind=kOutput, calls=%fused_computation.11 | convolution fusion | flops 377856000 | bytes 5455872 | tf_op jit(solution)/shard_map/dot_general | solution.py:60
  16.4 4.1 %scatter_custom_fusion.1 = s32[1280]{0:T(1024)S(1)} fusion(s32[640]{0:T(1024)S(1)} %fusion.21, s32[640]{0:T(1024)S(1)} %add_select_fusion, s32[]{:T(128)} %constant.52.clone.1), kind=kCustom, calls=%fused_computation.46 | custom fusion | bytes 5124 | tf_op jit(solution)/shard_map/scatter | solution.py:79
  20.5 2.9 %scatter_custom_fusion = pred[1280]{0:T(1024)(128)(4,1)S(1)} fusion(s32[640]{0:T(1024)S(1)} %fusion.21, pred[640]{0:T(1024)(128)(4,1)S(1)} %broadcast.160, pred[]{:T(512)} %constant.51.clone.1), kind=kCustom, calls=%fused_computation.51 | custom fusion | bytes 1281 | tf_op jit(solution)/shard_map/scatter | solution.py:80
  23.9 5.5 %gather_fusion = bf16[1280,1536]{1,0:T(8,128)(2,1)} fusion(bf16[80,1536]{1,0:T(8,128)(2,1)S(1)} %fusion.7, s32[2048]{0:T(1024)S(1)} %pad_clamp_fusion), kind=kCustom, calls=%fused_computation | custom fusion | bytes 7869440 | tf_op jit(solution)/shard_map/gather | solution.py:81
  29.4 2.4 copy_select_fusion
  31.7 93.6 %all_to_all.10 = bf16[5,4,64,1536]{3,2,0,1:T(8,128)(2,1)S(1)} all-to-all(bf16[5,4,64,1536]{3,2,0,1:T(8,128)(2,1)S(1)} %copy_select_fusion), channel_id=1, replica_groups=mesh['dp'=8,'expert'=4] {'expert'}, dimensions={1} | all-to-all | bytes 7864320 | tf_op jit(solution)/shard_map/all_to_all | solution.py:83
  125.4 2.5 copy.41
  127.8 13.8 %fusion.26 = f32[5,256,1024]{2,1,0:T(8,128)} fusion(bf16[5,256,1536]{2,1,0:T(8,128)(2,1)} %bitcast.24, bf16[5,1536,1024]{2,1,0:T(8,128)(2,1)} %all-gather.3.cloned.1.call-done), kind=kOutput, calls=%fused_computation.64 | convolution fusion | flops 4026531840 | bytes 24903680 | tf_op jit(solution)/shard_map/erd,edf->erf/dot_general | solution.py:37
  141.6 10.6 %all-gather.5.cloned.1.call-done = bf16[5,1536,512]{2,1,0:T(8,128)(2,1)} async-done(((bf16[5,192,512]{2,1,0:T(8,128)(2,1)}), bf16[5,1536,512]{2,1,0:T(8,128)(2,1)}) %all-gather.5.cloned.1.call-update) | async-done | bytes 7864336 | tf_op jit(solution)/shard_map/all_gather | solution.py:42
  152.2 7.1 %convolution_convert_fusion = bf16[5,256,1536]{2,1,0:T(8,128)(2,1)S(1)} fusion(bf16[5,1536,512]{2,1,0:T(8,128)(2,1)} %all-gather.5.cloned.1.call-done, f32[5,256,1024]{2,1,0:T(8,128)} %fusion.26), kind=kOutput, calls=%fused_computation.4 | convolution fusion | flops 2019164160 | bytes 17039360 | tf_op jit(solution)/shard_map/erf,edf->erd/dot_general | solution.py:43
  159.3 2.2 copy.42
  161.4 4.9 %all-to-all-start.1 = ((bf16[5,4,64,1536]{3,2,0,1:T(8,128)(2,1)}), bf16[5,4,64,1536]{3,2,0,1:T(8,128)(2,1)}, u32[]{:S(2)}, u32[]{:S(2)}) async-start(bf16[5,4,64,1536]{3,2,0,1:T(8,128)(2,1)} %copy.42), calls=%async_computation.1 | async-start | bytes 7864320 | tf_op jit(solution)/shard_map/all_to_all | solution.py:87
  166.5 88.1 %all-to-all-done.1 = bf16[5,4,64,1536]{3,2,0,1:T(8,128)(2,1)} async-done(((bf16[5,4,64,1536]{3,2,0,1:T(8,128)(2,1)}), bf16[5,4,64,1536]{3,2,0,1:T(8,128)(2,1)}, u32[]{:S(2)}, u32[]{:S(2)}) %all-to-all-start.1) | async-done | bytes 3932192 | tf_op jit(solution)/shard_map/all_to_all | solution.py:87
  254.6 4.4 %copy.43 = bf16[5,4,64,1536]{3,2,1,0:T(8,128)(2,1)} copy(bf16[5,4,64,1536]{3,2,0,1:T(8,128)(2,1)} %all-to-all-done.1) | data formatting | bytes 7864320 | tf_op jit(solution)/shard_map/all_to_all | solution.py:87
  259.0 7.9 %gather_fusion.1 = bf16[640,1536]{1,0:T(8,128)(2,1)S(1)} fusion(bf16[1280,1536]{1,0:T(8,128)(2,1)} %bitcast.22, s32[1024]{0:T(1024)S(1)} %pad_clamp_fusion.1), kind=kCustom, calls=%fused_computation.1 | custom fusion | bytes 3934720 | tf_op jit(solution)/shard_map/gather | solution.py:94
  267.0 1.7 fusion
  268.6 0.2 multiply_reduce_fusion
  268.8 0.8 multiply_convert_fusion
  (48 shorter events, 1.7 us)
Async XLA Ops:
  7.2 5.9 %copy-start = (bf16[80,1536]{1,0:T(8,128)(2,1)S(1)}, bf16[80,1536]{1,0:T(8,128)(2,1)}, u32[]{:S(2)}) copy-start(bf16[80,1536]{1,0:T(8,128)(2,1)} %param.10) | copy-start | bytes 737284
  7.2 5.9 %copy-start.2 = (bf16[80,1536]{1,0:T(8,128)(2,1)S(1)}, bf16[80,1536]{1,0:T(8,128)(2,1)}, u32[]{:S(2)}) copy-start(bf16[80,1536]{1,0:T(8,128)(2,1)} %param.11) | copy-start | bytes 737284
  7.2 120.7 %all-gather.3.cloned.1.call-start = ((), (), s32[]{:S(2)}) async-start(), calls=%async_computation.2 | async-start | bytes 17694720 | tf_op jit(solution)/shard_map/all_gather | solution.py:36
  7.9 15.8 %copy-start.4 = (f32[1536]{0:T(1024)S(1)}, f32[1536]{0:T(1024)}, u32[]{:S(2)}) copy-start(f32[1536]{0:T(1024)} %param.13) | copy-start | bytes 18436
  7.9 144.3 %all-gather.5.cloned.1.call-start = ((), (), s32[]{:S(2)}) async-start(), calls=%async_computation.3 | async-start | bytes 8847360 | tf_op jit(solution)/shard_map/all_gather | solution.py:42
  161.4 4.9 %copy-start.3 = (s32[80,8]{0,1:T(8,128)S(1)}, s32[80,8]{0,1:T(8,128)}, u32[]{:S(2)}) copy-start(s32[80,8]{0,1:T(8,128)} %param.16) | copy-start | bytes 7684
  161.4 93.2 %all-to-all-start.1 = ((bf16[5,4,64,1536]{3,2,0,1:T(8,128)(2,1)}), bf16[5,4,64,1536]{3,2,0,1:T(8,128)(2,1)}, u32[]{:S(2)}, u32[]{:S(2)}) async-start(bf16[5,4,64,1536]{3,2,0,1:T(8,128)(2,1)} %copy.42), calls=%async_computation.1 | async-start | bytes 7864320 | tf_op jit(solution)/shard_map/all_to_all | solution.py:87
  259.0 9.8 %copy-start.5 = (f32[1536]{0:T(1024)S(1)}, f32[1536]{0:T(1024)}, u32[]{:S(2)}) copy-start(f32[1536]{0:T(1024)} %param.14) | copy-start | bytes 18436
  259.0 10.7 %copy-start.1 = (bf16[80,1536]{1,0:T(8,128)(2,1)S(1)}, bf16[80,1536]{1,0:T(8,128)(2,1)}, u32[]{:S(2)}) copy-start(bf16[80,1536]{1,0:T(8,128)(2,1)} %param.10) | copy-start | bytes 737284
Sparse Core Ops, SparseCore 0:
  9.9 88.1 all-gather.2
  100.0 52.1 all-gather.4
where the time goes:
time: 277 us
  waiting for transfers between devices  100 us (36%)
  blocking collectives  93.6 us (34%)
  local copies, waits for them, and re-layouts  30.8 us (11%)
  matrix products  24.1 us (9%)
  between operations  14.3 us (5%)
  other arithmetic  8.59 us (3%)
  starting transfers between devices  5 us (2%)
    all_to_all x1, blocking collectives, body(): lax.all_to_all(outgoing, 'expert', split_axis=1, concat_axis=1, tiled=True)  93.6 us
    all_to_all x1, waiting for transfers between devices, body(): lax.all_to_all(produced.reshape(local, groups, capacity, width), 'expert'...  88.1 us
    dot_general x1, matrix products, expert_apply(): jnp.einsum('erd,edf->erf', buffer, whole_gate_up, preferred_element_type=...  13.8 us
    all_gather x1, waiting for transfers between devices, expert_apply(): whole_down = lax.all_gather(down_weight, 'dp', axis=1, tiled=True)  10.6 us
    gather x1, local copies, waits for them, and re-layouts, body(): returned.reshape(slots_total, width)[position].reshape(tok_rows, TOP, width)  7.94 us
    dot_general x1, matrix products, expert_apply(): jnp.einsum('erf,edf->erd', hidden, whole_down, preferred_element_type=jnp...  7.06 us
  transfers between devices with their start and end apart: 3, of which 2 were waited for; matrix products, arithmetic and copies ran while one was open for 14% of the time, Pallas kernels for 0%

commit v1 on v0

v1 whole, which is shorter than its diff:
```python
import functools

import jax
import jax.numpy as jnp
from jax import lax
from jax.experimental import pallas as pl
from jax.experimental.pallas import tpu as pltpu
from jax.sharding import PartitionSpec as P

EPS = 1e-06
LOGIT_SCALE = 0.5
LANES = 128
LOW = 64
QUAD = 4


def normalize(values, gain):
    return values * lax.rsqrt(jnp.mean(values * values, axis=-1, keepdims=True) + EPS) * gain


def combine_weights(logits):
    scores = jnp.exp(logits.astype(jnp.float32) * LOGIT_SCALE)
    return scores / jnp.sum(scores, axis=-1, keepdims=True)


def slot_gates(routes, logits, placement):
    gates = combine_weights(logits)
    hit = routes[:, :, None] == placement[None, None, :]
    return jnp.sum(jnp.where(hit, gates[:, :, None], 0.0), axis=1)


def gate_lanes(gates):
    high = gates.astype(jnp.bfloat16)
    low = (gates - high.astype(jnp.float32)).astype(jnp.bfloat16)
    pad = ((0, 0), (0, LOW - gates.shape[1]))
    return jnp.concatenate([jnp.pad(high, pad), jnp.pad(low, pad)], axis=1)


def swap_blocks(values, index, blocks):
    lead = values.shape[:-1]
    out = values.reshape(*lead, blocks, -1)
    bit = 1
    while bit < blocks:
        order = [m ^ bit for m in range(blocks)]
        swapped = jnp.concatenate([out[..., m : m + 1, :] for m in order], axis=-2)
        out = jnp.where((index & bit) != 0, swapped, out)
        bit *= 2
    return out.reshape(values.shape)


def up_kernel(rows, place_ref, x_ref, *refs):
    own, nbr, out_ref = refs[:rows], refs[rows : 2 * rows], refs[2 * rows]
    first = place_ref[0] == 0
    zone = place_ref[1]
    local = place_ref[2]
    expert = pl.program_id(0)
    width = out_ref.shape[1]
    acc = None
    for m in range(rows):
        a, b = own[m][0], nbr[m][0]
        w = jnp.concatenate([jnp.where(first, a, b), jnp.where(first, b, a)], axis=0)
        depth = w.shape[0]
        part = jnp.dot(
            x_ref[:, m * depth : (m + 1) * depth], w, preferred_element_type=jnp.float32
        )
        acc = part if acc is None else acc + part
    feats = x_ref.shape[1] - LANES
    lane = lax.broadcasted_iota(jnp.int32, (LANES, width), 0)
    slot = zone * local + expert
    pick = jnp.where((lane == slot) | (lane == slot + LOW), 1.0, 0.0).astype(jnp.bfloat16)
    gate = jnp.dot(x_ref[:, feats:], pick, preferred_element_type=jnp.float32)
    g, u = acc[:, :width], acc[:, width:]
    out_ref[...] = (g / (1.0 + jnp.exp(-g)) * u * gate).astype(jnp.bfloat16)


def up_call(place, x, own, nbr):
    rows = len(own)
    local, depth, cols = own[0].shape
    tokens, lanes = x.shape
    piece = pl.BlockSpec((1, depth, cols), lambda e, p: (e, 0, 0))
    return pl.pallas_call(
        functools.partial(up_kernel, rows),
        grid_spec=pltpu.PrefetchScalarGridSpec(
            num_scalar_prefetch=1,
            grid=(local,),
            in_specs=[pl.BlockSpec((tokens, lanes), lambda e, p: (0, 0))] + [piece] * (2 * rows),
            out_specs=pl.BlockSpec((tokens, cols // 2), lambda e, p: (0, e)),
        ),
        out_shape=jax.ShapeDtypeStruct((tokens, local * cols // 2), jnp.bfloat16),
        compiler_params=pltpu.CompilerParams(vmem_limit_bytes=40 * 1024 * 1024),
        cost_estimate=pl.CostEstimate(
            flops=2 * tokens * lanes * local * cols,
            bytes_accessed=2 * (tokens * lanes + local * lanes * cols),
            transcendentals=tokens * local * cols // 2,
        ),
        name="up",
    )(place, x, *own, *nbr)


def down_kernel(h_ref, w_ref, out_ref):
    w = jnp.concatenate([w_ref[e] for e in range(w_ref.shape[0])], axis=1)
    out_ref[...] = lax.dot_general(
        h_ref[...], w, (((1,), (1,)), ((), ())), preferred_element_type=jnp.float32
    ).astype(out_ref.dtype)


def down_call(hidden, weight):
    tokens, depth = hidden.shape
    local, feats, part = weight.shape
    steps = 2
    return pl.pallas_call(
        down_kernel,
        grid=(steps,),
        in_specs=[
            pl.BlockSpec((tokens // steps, depth), lambda i: (i, 0)),
            pl.BlockSpec((local, feats, part), lambda i: (0, 0, 0)),
        ],
        out_specs=pl.BlockSpec((tokens // steps, feats), lambda i: (i, 0)),
        out_shape=jax.ShapeDtypeStruct((tokens, feats), jnp.bfloat16),
        compiler_params=pltpu.CompilerParams(vmem_limit_bytes=40 * 1024 * 1024),
        cost_estimate=pl.CostEstimate(
            flops=2 * tokens * depth * feats,
            bytes_accessed=2 * (tokens * depth + depth * feats + tokens * feats),
            transcendentals=0,
        ),
        name="down",
    )(hidden, weight)


def body(
    attended,
    residual,
    out_weight,
    norm_gain,
    final_gain,
    routes,
    gate_logits,
    placement,
    gate_up,
    down_weight,
):
    ranks = lax.axis_size("dp")
    zones = lax.axis_size("expert")
    rows = ranks // QUAD
    me = lax.axis_index("dp")
    zone = lax.axis_index("expert")
    core, side, row = me % 2, (me // 2) % 2, me // QUAD
    tok, width = attended.shape
    local, depth, _ = gate_up.shape
    hid = down_weight.shape[2]
    part = hid // QUAD

    def flip(values, bit):
        return lax.ppermute(values, "dp", [(i, i ^ bit) for i in range(ranks)])

    def shift(values, step):
        return lax.ppermute(values, "expert", [(i, (i + step) % zones) for i in range(zones)])

    def columns(values, offset):
        return lax.dynamic_slice_in_dim(values, offset, part, axis=2)

    def quarter(values, c, s):
        blocks = values.shape[2] // hid
        cuts = [columns(values, b * hid + (2 * c + s) * part) for b in range(blocks)]
        return jnp.concatenate(cuts, axis=2) if blocks > 1 else cuts[0]

    def spread(values):
        away = jnp.concatenate([quarter(values, 1 - core, s) for s in range(2)], axis=2)
        got = flip(away, 1)
        size = got.shape[2] // 2
        both = []
        for s in (side, 1 - side):
            mine = quarter(values, core, s)
            theirs = lax.dynamic_slice_in_dim(got, s * size, size, axis=2)
            both.append(
                jnp.where(
                    core == 0,
                    jnp.concatenate([mine, theirs], axis=1),
                    jnp.concatenate([theirs, mine], axis=1),
                )
            )
        return both[0], flip(both[1], 2)

    def widen(pieces):
        bit = 1
        while bit < rows:
            pieces = pieces + [flip(p, bit * QUAD) for p in pieces]
            bit *= 2
        return pieces

    gu_own, gu_nbr = spread(gate_up)
    own, nbr = widen([gu_own]), widen([gu_nbr])
    dn_own, dn_nbr = spread(down_weight)
    halves = [
        widen([jnp.where(side == j, dn_own, dn_nbr)]) for j in range(2)
    ]

    mixed = residual.astype(jnp.float32) + jnp.dot(
        attended, out_weight, preferred_element_type=jnp.float32
    )
    stored = lax.optimization_barrier(mixed.astype(jnp.bfloat16))
    stream_in = stored.astype(jnp.float32)
    normed_in = normalize(stream_in, norm_gain).astype(jnp.bfloat16)
    gates = gate_lanes(slot_gates(routes, gate_logits, placement))
    sent = jnp.concatenate([swap_blocks(normed_in, row, rows), gates], axis=1)

    column = [sent] + [shift(sent, k) for k in range(1, zones)]
    beside = [flip(v, 2) for v in column]
    chip = column + beside
    mate = [flip(v, 1) for v in chip]
    x = jnp.concatenate(chip + mate, axis=0)

    place = jnp.stack([side, zone, jnp.int32(local)]).astype(jnp.int32)
    hidden = up_call(place, x, own, nbr)

    count = zones * tok
    chunks = []
    for m in range(rows):
        for j in range(2):
            partial = down_call(hidden, halves[j][m])
            back = flip(partial[2 * count :], 1)
            summed = (
                partial[: 2 * count].astype(jnp.float32) + back.astype(jnp.float32)
            )
            back = flip(summed[count:].astype(jnp.bfloat16), 2)
            summed = summed[:count] + back.astype(jnp.float32)
            total = summed[:tok]
            for k in range(1, zones):
                piece = summed[k * tok : (k + 1) * tok].astype(jnp.bfloat16)
                total = total + shift(piece, -k).astype(jnp.float32)
            chunks.append(total)
    branch = swap_blocks(jnp.concatenate(chunks, axis=1), row, rows)
    total = stream_in + branch
    return (total.astype(jnp.bfloat16), normalize(total, final_gain).astype(jnp.bfloat16))


def solution(mesh):
    tokens = P(("dp", "expert"), None)
    weights = P("expert", "dp", None)
    return jax.shard_map(
        body,
        mesh=mesh,
        in_specs=(tokens, tokens, P(), P(), P(), tokens, tokens, P(), weights, weights),
        out_specs=(tokens, tokens),
        check_vma=False,
    )
```

time: 277 us -> 178 us (0.64)
  blocking collectives: 93.6 us -> 0 us
  starting transfers between devices: 5 us -> 56.1 us
  waiting for transfers between devices: 100 us -> 70.6 us
  matrix products: 24.1 us -> 3.3 us
  between operations: 14.3 us -> 1.19 us
  Pallas kernels: 0 us -> 12.5 us
  local copies, waits for them, and re-layouts: 30.8 us -> 24.2 us
    all_to_all x1 -> x0, blocking collectives: 93.6 us -> none  [body(): lax.all_to_all(outgoing, 'expert', split_axis=1, concat_axis=1, tiled=True)]
    all_to_all x1 -> x0, waiting for transfers between devices: 88.1 us -> none  [body(): lax.all_to_all(produced.reshape(local, groups, capacity, width), 'expert'...]
    ppermute x0 -> x43, waiting for transfers between devices: none -> 70.6 us  [the longest x28 58.9 us: flip(): return lax.ppermute(values, 'dp', [(i, i ^ bit) for i in range(ranks)])]
    ppermute x0 -> x43, starting transfers between devices: none -> 56.1 us  [the longest x15 37 us: shift(): lax.ppermute(values, 'expert', [(i, (i + step) % zones) for i in range(zo...]
    dot_general x2 -> x0, matrix products: 20.8 us -> none  [the longest x1 13.8 us: expert_apply(): jnp.einsum('erd,edf->erf', buffer, whole_gate_up, preferred_element_type=...]
    unnamed x14 -> x31, local copies, waits for them, and re-layouts: 0.05 us -> 17.9 us
    gather x2 -> x0, local copies, waits for them, and re-layouts: 13.4 us -> none  [the longest x1 7.94 us: body(): returned.reshape(slots_total, width)[position].reshape(tok_rows, TOP, width)]
    pallas_call x0 -> x5, Pallas kernels: none -> 12.5 us  [the longest x1 7.34 us: up_call(): pl.pallas_call(functools.partial(up_kernel, rows), grid_spec=pltpu.Prefet...]
  transfers between devices with their start and end apart: 3 -> 43, of which waited for: 2 -> 14; matrix products, arithmetic and copies ran while one was open for 14% -> 14% of each run, Pallas kernels for 0% -> 7%
where the time goes in v1:
time: 178 us
  waiting for transfers between devices  70.6 us (40%)
  starting transfers between devices  56.1 us (32%)
  local copies, waits for them, and re-layouts  24.2 us (14%)
  Pallas kernels  12.5 us (7%)
  other arithmetic  9.9 us (6%)
  matrix products  3.3 us (2%)
    ppermute x28, waiting for transfers between devices, flip(): return lax.ppermute(values, 'dp', [(i, i ^ bit) for i in range(ranks)])  58.9 us
    ppermute x15, starting transfers between devices, shift(): lax.ppermute(values, 'expert', [(i, (i + step) % zones) for i in range(zo...  37 us
    ppermute x28, starting transfers between devices, flip(): return lax.ppermute(values, 'dp', [(i, i ^ bit) for i in range(ranks)])  19 us
    unnamed x31, local copies, waits for them, and re-layouts  17.9 us
    ppermute x15, waiting for transfers between devices, shift(): lax.ppermute(values, 'expert', [(i, (i + step) % zones) for i in range(zo...  11.7 us
    pallas_call x1, Pallas kernels, up_call(): pl.pallas_call(functools.partial(up_kernel, rows), grid_spec=pltpu.Prefet...  7.34 us
    pallas_call x4, Pallas kernels, down_call(): pl.pallas_call(down_kernel, grid=(steps,), in_specs=[pl.BlockSpec((tokens...  5.21 us
  transfers between devices with their start and end apart: 43, of which 14 were waited for; matrix products, arithmetic and copies ran while one was open for 14% of the time, Pallas kernels for 7%

profile of v1, /device:TPU:0, one launch (start us, length us, event | category | flops | bytes accessed | tf_op | source)
XLA Modules:
  0.0 177.8 jit_solution(5692984695504355690)
XLA Ops:
  3.0 3.3 %fusion = bf16[80,1536]{1,0:T(8,128)(2,1)S(1)} fusion(bf16[80,1536]{1,0:T(8,128)(2,1)S(1)} %copy-done, bf16[1536,1536]{1,0:T(8,128)(2,1)} %param.12, bf16[80,1536]{1,0:T(8,128)(2,1)} %param.11), kind=kOutput, calls=%fused_computation.1 | convolution fusion | flops 377856000 | bytes 5455872 | tf_op jit(solution)/shard_map/dot_general | solution.py:198
  8.1 3.1 %collective-permute-start = (bf16[80,1664]{1,0:T(8,128)(2,1)S(1)}, bf16[80,1664]{1,0:T(8,128)(2,1)}, u32[]{:S(2)}, u32[]{:S(2)}) collective-permute-start(bf16[80,1664]{1,0:T(8,128)(2,1)S(1)} %concatenate.57), channel_id=1, source_target_pairs={{0,1},{1,2},{2,3},{3,0},{4,5},{5,6},{6,7},{7,4},{8,9},{9,10},{10,1... | collective-permute-start | bytes 798728 | tf_op jit(solution)/shard_map/ppermute | solution.py:157
  11.2 2.6 %collective-permute-start.1 = (bf16[80,1664]{1,0:T(8,128)(2,1)S(1)}, bf16[80,1664]{1,0:T(8,128)(2,1)}, u32[]{:S(2)}, u32[]{:S(2)}) collective-permute-start(bf16[80,1664]{1,0:T(8,128)(2,1)S(1)} %concatenate.57), channel_id=1, source_target_pairs={{0,2},{1,3},{2,0},{3,1},{4,6},{5,7},{6,4},{7,5},{8,10},{9,11},{10,... | collective-permute-start | bytes 798728 | tf_op jit(solution)/shard_map/ppermute | solution.py:157
  17.3 2.1 %constant_dynamic-slice_fusion.5 = (bf16[5,192,128]{2,1,0:T(8,128)(2,1)S(1)}, bf16[5,192,128]{2,1,0:T(8,128)(2,1)S(1)}, bf16[5,192,128]{2,1,0:T(8,128)(2,1)}, bf16[5,192,128]{2,1,0:T(8,128)(2,1)S(1)}) fusion(bf16[5,192,512]{2,1,0:T(8,128)(2,1)} %param.19, s32[]{:T(128)S(6)} %select_n.144, s32[]{:T(128)S(6)} %select_n.145, s32[]{:T(128)S(6)} %select_n.149, ...), kind=kLoop, calls=%fused_computation.70 | loop fusion | bytes 1966096 | tf_op jit(solution)/shard_map/dynamic_slice | solution.py:160
  25.5 5.7 %collective-permute-done.1 = bf16[80,1664]{1,0:T(8,128)(2,1)} collective-permute-done((bf16[80,1664]{1,0:T(8,128)(2,1)S(1)}, bf16[80,1664]{1,0:T(8,128)(2,1)}, u32[]{:S(2)}, u32[]{:S(2)}) %collective-permute-start.1) | collective-permute-done | bytes 266272 | tf_op jit(solution)/shard_map/ppermute | solution.py:157
  43.1 5.0 %collective-permute-done.5 = bf16[80,1664]{1,0:T(8,128)(2,1)S(1)} collective-permute-done((bf16[80,1664]{1,0:T(8,128)(2,1)}, bf16[80,1664]{1,0:T(8,128)(2,1)S(1)}, u32[]{:S(2)}, u32[]{:S(2)}) %collective-permute-start.5) | collective-permute-done | bytes 266272 | tf_op jit(solution)/shard_map/ppermute | solution.py:154
  48.8 4.6 %collective-permute-done.6 = bf16[80,1664]{1,0:T(8,128)(2,1)S(1)} collective-permute-done((bf16[80,1664]{1,0:T(8,128)(2,1)}, bf16[80,1664]{1,0:T(8,128)(2,1)S(1)}, u32[]{:S(2)}, u32[]{:S(2)}) %collective-permute-start.6) | collective-permute-done | bytes 266272 | tf_op jit(solution)/shard_map/ppermute | solution.py:154
  56.5 1.7 constant_dynamic-update-slice_fusion.7
  63.3 16.4 %collective-permute-done.17.refs_2_ = bf16[5,384,256]{2,1,0:T(8,128)(2,1)S(1)} collective-permute-done((bf16[5,384,256]{2,1,0:T(8,128)(2,1)S(1)}, bf16[5,384,256]{2,1,0:T(8,128)(2,1)S(1)}, u32[]{:S(2)}, u32[]{:S(2)}) %collective-permute-start.17) | collective-permute-done | bytes 983072 | tf_op jit(solution)/shard_map/ppermute | solution.py:154
  84.2 5.1 %collective-permute-done.20 = bf16[5,384,128]{2,1,0:T(8,128)(2,1)S(1)} collective-permute-done((bf16[5,384,128]{2,1,0:T(8,128)(2,1)S(1)}, bf16[5,384,128]{2,1,0:T(8,128)(2,1)S(1)}, u32[]{:S(2)}, u32[]{:S(2)}) %collective-permute-start.20) | collective-permute-done | bytes 491552 | tf_op jit(solution)/shard_map/ppermute | solution.py:154
  91.6 15.9 %collective-permute-done.18.refs_3_ = bf16[5,384,256]{2,1,0:T(8,128)(2,1)S(1)} collective-permute-done((bf16[5,384,256]{2,1,0:T(8,128)(2,1)S(1)}, bf16[5,384,256]{2,1,0:T(8,128)(2,1)S(1)}, u32[]{:S(2)}, u32[]{:S(2)}) %collective-permute-start.18) | collective-permute-done | bytes 983072 | tf_op jit(solution)/shard_map/ppermute | solution.py:154
  107.5 2.2 %copy-done.1 = bf16[1280,1664]{1,0:T(8,128)(2,1)S(1)} copy-done((bf16[1280,1664]{1,0:T(8,128)(2,1)S(1)}, bf16[1280,1664]{1,0:T(8,128)(2,1)}, u32[]{:S(2)}) %copy-start.1) | copy-done | bytes 4259864
  109.7 7.3 %up.1.h_ref = bf16[1280,640]{1,0:T(8,128)(2,1)S(1)} custom-call(s32[3]{0:T(128)S(1)} %pad_add_fusion.place_ref, bf16[1280,1664]{1,0:T(8,128)(2,1)S(1)} %copy-done.1, bf16[5,384,256]{2,1,0:T(8,128)(2,1)S(1)} %maximum_select_fusion.refs_0_, bf16[5,384,256]{2,1,0:T(8,128)(2,1)S(1)} %collective-permute-done.16.refs_1_, ...), custom_call_target="tpu_custom_call" | custom-call | flops 5452595200 | bytes 8519680 | tf_op jit(solution)/shard_map/up/pallas_call | solution.py:81
  121.9 5.7 %collective-permute-done.37.w_ref = bf16[5,384,128]{2,1,0:T(8,128)(2,1)S(1)} collective-permute-done((bf16[5,384,128]{2,1,0:T(8,128)(2,1)S(1)}, bf16[5,384,128]{2,1,0:T(8,128)(2,1)S(1)}, u32[]{:S(2)}, u32[]{:S(2)}) %collective-permute-start.37) | collective-permute-done | bytes 491552 | tf_op jit(solution)/shard_map/ppermute | solution.py:154
  133.9 4.1 %collective-permute-done.22 = bf16[320,384]{1,0:T(8,128)(2,1)S(1)} collective-permute-done((bf16[320,384]{1,0:T(8,128)(2,1)S(1)}, bf16[320,384]{1,0:T(8,128)(2,1)S(1)}, u32[]{:S(2)}, u32[]{:S(2)}) %collective-permute-start.22) | collective-permute-done | bytes 245792 | tf_op jit(solution)/shard_map/ppermute | solution.py:154
  138.1 7.2 %collective-permute-start.23 = (bf16[80,384]{1,0:T(8,128)(2,1)S(1)}, bf16[80,384]{1,0:T(8,128)(2,1)S(1)}, u32[]{:S(2)}, u32[]{:S(2)}) collective-permute-start(bf16[80,384]{1,0:T(8,128)(2,1)S(1)} %get-tuple-element.34), channel_id=1, source_target_pairs={{0,3},{1,0},{2,1},{3,2},{4,7},{5,4},{6,5},{7,6},{8,11},{9,8},{10,9... | collective-permute-start | bytes 184328 | tf_op jit(solution)/shard_map/ppermute | solution.py:157
  145.3 2.2 %collective-permute-start.25 = (bf16[80,384]{1,0:T(8,128)(2,1)S(1)}, bf16[80,384]{1,0:T(8,128)(2,1)S(1)}, u32[]{:S(2)}, u32[]{:S(2)}) collective-permute-start(bf16[80,384]{1,0:T(8,128)(2,1)S(1)} %get-tuple-element.35), channel_id=1, source_target_pairs={{0,1},{1,2},{2,3},{3,0},{4,5},{5,6},{6,7},{7,4},{8,9},{9,10},{10,1... | collective-permute-start | bytes 184328 | tf_op jit(solution)/shard_map/ppermute | solution.py:157
  148.5 7.2 %collective-permute-start.28 = (bf16[80,384]{1,0:T(8,128)(2,1)S(1)}, bf16[80,384]{1,0:T(8,128)(2,1)S(1)}, u32[]{:S(2)}, u32[]{:S(2)}) collective-permute-start(bf16[80,384]{1,0:T(8,128)(2,1)S(1)} %get-tuple-element.37), channel_id=1, source_target_pairs={{0,3},{1,0},{2,1},{3,2},{4,7},{5,4},{6,5},{7,6},{8,11},{9,8},{10,9... | collective-permute-start | bytes 184328 | tf_op jit(solution)/shard_map/ppermute | solution.py:157
  156.9 4.4 %collective-permute-start.30 = (bf16[80,384]{1,0:T(8,128)(2,1)S(1)}, bf16[80,384]{1,0:T(8,128)(2,1)S(1)}, u32[]{:S(2)}, u32[]{:S(2)}) collective-permute-start(bf16[80,384]{1,0:T(8,128)(2,1)S(1)} %get-tuple-element.38), channel_id=1, source_target_pairs={{0,1},{1,2},{2,3},{3,0},{4,5},{5,6},{6,7},{7,4},{8,9},{9,10},{10,1... | collective-permute-start | bytes 184328 | tf_op jit(solution)/shard_map/ppermute | solution.py:157
  163.5 3.8 %collective-permute-start.40 = (bf16[80,384]{1,0:T(8,128)(2,1)S(1)}, bf16[80,384]{1,0:T(8,128)(2,1)S(1)}, u32[]{:S(2)}, u32[]{:S(2)}) collective-permute-start(bf16[80,384]{1,0:T(8,128)(2,1)S(1)} %get-tuple-element.43), channel_id=1, source_target_pairs={{0,3},{1,0},{2,1},{3,2},{4,7},{5,4},{6,5},{7,6},{8,11},{9,8},{10,9... | collective-permute-start | bytes 184328 | tf_op jit(solution)/shard_map/ppermute | solution.py:157
  167.3 2.0 %collective-permute-start.41 = (bf16[80,384]{1,0:T(8,128)(2,1)S(1)}, bf16[80,384]{1,0:T(8,128)(2,1)S(1)}, u32[]{:S(2)}, u32[]{:S(2)}) collective-permute-start(bf16[80,384]{1,0:T(8,128)(2,1)S(1)} %get-tuple-element.45), channel_id=1, source_target_pairs={{0,2},{1,3},{2,0},{3,1},{4,6},{5,7},{6,4},{7,5},{8,10},{9,11},{10,... | collective-permute-start | bytes 184328 | tf_op jit(solution)/shard_map/ppermute | solution.py:157
  169.4 2.4 %collective-permute-done.35 = bf16[80,384]{1,0:T(8,128)(2,1)S(1)} collective-permute-done((bf16[80,384]{1,0:T(8,128)(2,1)S(1)}, bf16[80,384]{1,0:T(8,128)(2,1)S(1)}, u32[]{:S(2)}, u32[]{:S(2)}) %collective-permute-start.35) | collective-permute-done | bytes 61472 | tf_op jit(solution)/shard_map/ppermute | solution.py:157
  171.9 1.8 %collective-permute-done.41 = bf16[80,384]{1,0:T(8,128)(2,1)S(1)} collective-permute-done((bf16[80,384]{1,0:T(8,128)(2,1)S(1)}, bf16[80,384]{1,0:T(8,128)(2,1)S(1)}, u32[]{:S(2)}, u32[]{:S(2)}) %collective-permute-start.41) | collective-permute-done | bytes 61472 | tf_op jit(solution)/shard_map/ppermute | solution.py:157
  173.7 1.8 collective-permute-done.42
  (159 shorter events, 59.1 us)
Async XLA Ops:
  8.1 15.2 %collective-permute-start = (bf16[80,1664]{1,0:T(8,128)(2,1)S(1)}, bf16[80,1664]{1,0:T(8,128)(2,1)}, u32[]{:S(2)}, u32[]{:S(2)}) collective-permute-start(bf16[80,1664]{1,0:T(8,128)(2,1)S(1)} %concatenate.57), channel_id=1, source_target_pairs={{0,1},{1,2},{2,3},{3,0},{4,5},{5,6},{6,7},{7,4},{8,9},{9,10},{10,1... | collective-permute-start | bytes 798728 | tf_op jit(solution)/shard_map/ppermute | solution.py:157
  11.2 20.1 %collective-permute-start.1 = (bf16[80,1664]{1,0:T(8,128)(2,1)S(1)}, bf16[80,1664]{1,0:T(8,128)(2,1)}, u32[]{:S(2)}, u32[]{:S(2)}) collective-permute-start(bf16[80,1664]{1,0:T(8,128)(2,1)S(1)} %concatenate.57), channel_id=1, source_target_pairs={{0,2},{1,3},{2,0},{3,1},{4,6},{5,7},{6,4},{7,5},{8,10},{9,11},{10,... | collective-permute-start | bytes 798728 | tf_op jit(solution)/shard_map/ppermute | solution.py:157
  13.8 19.2 %collective-permute-start.2 = (bf16[80,1664]{1,0:T(8,128)(2,1)S(1)}, bf16[80,1664]{1,0:T(8,128)(2,1)}, u32[]{:S(2)}, u32[]{:S(2)}) collective-permute-start(bf16[80,1664]{1,0:T(8,128)(2,1)S(1)} %concatenate.57), channel_id=1, source_target_pairs={{0,3},{1,0},{2,1},{3,2},{4,7},{5,4},{6,5},{7,6},{8,11},{9,8},{10,9... | collective-permute-start | bytes 798728 | tf_op jit(solution)/shard_map/ppermute | solution.py:157
  15.1 21.0 %collective-permute-start.3 = (bf16[80,1664]{1,0:T(8,128)(2,1)S(1)}, bf16[80,1664]{1,0:T(8,128)(2,1)}, u32[]{:S(2)}, u32[]{:S(2)}) collective-permute-start(bf16[80,1664]{1,0:T(8,128)(2,1)S(1)} %concatenate.57), channel_id=1, source_target_pairs={{0,8},{4,12},{8,0},{12,4},{16,24},{20,28},{24,16},{28,20},{1,9},{5... | collective-permute-start | bytes 798728 | tf_op jit(solution)/shard_map/ppermute | solution.py:154
  16.6 38.4 %collective-permute-start.7 = (bf16[80,1664]{1,0:T(8,128)(2,1)S(1)}, bf16[80,1664]{1,0:T(8,128)(2,1)}, u32[]{:S(2)}, u32[]{:S(2)}) collective-permute-start(bf16[80,1664]{1,0:T(8,128)(2,1)S(1)} %concatenate.57), channel_id=1, source_target_pairs={{0,4},{4,0},{8,12},{12,8},{16,20},{20,16},{24,28},{28,24},{1,5},{5... | collective-permute-start | bytes 798728 | tf_op jit(solution)/shard_map/ppermute | solution.py:154
  23.3 30.8 %collective-permute-start.15 = (bf16[5,192,512]{2,1,0:T(8,128)(2,1)S(1)}, bf16[5,192,512]{2,1,0:T(8,128)(2,1)S(1)}, u32[]{:S(2)}, u32[]{:S(2)}) collective-permute-start(bf16[5,192,512]{2,1,0:T(8,128)(2,1)S(1)} %pad_maximum_fusion), channel_id=1, source_target_pairs={{0,4},{4,0},{8,12},{12,8},{16,20},{20,16},{24,28},{28,24},{1,5},{5... | collective-permute-start | bytes 2949128 | tf_op jit(solution)/shard_map/ppermute | solution.py:154
  36.1 11.9 %collective-permute-start.5 = (bf16[80,1664]{1,0:T(8,128)(2,1)}, bf16[80,1664]{1,0:T(8,128)(2,1)S(1)}, u32[]{:S(2)}, u32[]{:S(2)}) collective-permute-start(bf16[80,1664]{1,0:T(8,128)(2,1)} %collective-permute-done.1), channel_id=1, source_target_pairs={{0,8},{4,12},{8,0},{12,4},{16,24},{20,28},{24,16},{28,20},{1,9},{5... | collective-permute-start | bytes 798728 | tf_op jit(solution)/shard_map/ppermute | solution.py:154
  38.3 15.0 %collective-permute-start.6 = (bf16[80,1664]{1,0:T(8,128)(2,1)}, bf16[80,1664]{1,0:T(8,128)(2,1)S(1)}, u32[]{:S(2)}, u32[]{:S(2)}) collective-permute-start(bf16[80,1664]{1,0:T(8,128)(2,1)} %collective-permute-done.2), channel_id=1, source_target_pairs={{0,8},{4,12},{8,0},{12,4},{16,24},{20,28},{24,16},{28,20},{1,9},{5... | collective-permute-start | bytes 798728 | tf_op jit(solution)/shard_map/ppermute | solution.py:154
  42.3 15.9 %collective-permute-start.8 = (bf16[80,1664]{1,0:T(8,128)(2,1)}, bf16[80,1664]{1,0:T(8,128)(2,1)S(1)}, u32[]{:S(2)}, u32[]{:S(2)}) collective-permute-start(bf16[80,1664]{1,0:T(8,128)(2,1)} %collective-permute-done), channel_id=1, source_target_pairs={{0,4},{4,0},{8,12},{12,8},{16,20},{20,16},{24,28},{28,24},{1,5},{5... | collective-permute-start | bytes 798728 | tf_op jit(solution)/shard_map/ppermute | solution.py:154
  55.0 24.7 %collective-permute-start.17 = (bf16[5,384,256]{2,1,0:T(8,128)(2,1)S(1)}, bf16[5,384,256]{2,1,0:T(8,128)(2,1)S(1)}, u32[]{:S(2)}, u32[]{:S(2)}) collective-permute-start(bf16[5,384,256]{2,1,0:T(8,128)(2,1)S(1)} %maximum_select_fusion.1), channel_id=1, source_target_pairs={{0,8},{4,12},{8,0},{12,4},{16,24},{20,28},{24,16},{28,20},{1,9},{5... | collective-permute-start | bytes 2949128 | tf_op jit(solution)/shard_map/ppermute | solution.py:154
  58.2 31.0 %collective-permute-start.20 = (bf16[5,384,128]{2,1,0:T(8,128)(2,1)S(1)}, bf16[5,384,128]{2,1,0:T(8,128)(2,1)S(1)}, u32[]{:S(2)}, u32[]{:S(2)}) collective-permute-start(bf16[5,384,128]{2,1,0:T(8,128)(2,1)S(1)} %maximum_select_fusion.3), channel_id=1, source_target_pairs={{0,8},{4,12},{8,0},{12,4},{16,24},{20,28},{24,16},{28,20},{1,9},{5... | collective-permute-start | bytes 1474568 | tf_op jit(solution)/shard_map/ppermute | solution.py:154
  59.5 22.4 %collective-permute-start.12 = (bf16[80,1664]{1,0:T(8,128)(2,1)S(1)}, bf16[80,1664]{1,0:T(8,128)(2,1)S(1)}, u32[]{:S(2)}, u32[]{:S(2)}) collective-permute-start(bf16[80,1664]{1,0:T(8,128)(2,1)S(1)} %collective-permute-done.4), channel_id=1, source_target_pairs={{0,4},{4,0},{8,12},{12,8},{16,20},{20,16},{24,28},{28,24},{1,5},{5... | collective-permute-start | bytes 798728 | tf_op jit(solution)/shard_map/ppermute | solution.py:154
  60.2 22.4 %collective-permute-start.13 = (bf16[80,1664]{1,0:T(8,128)(2,1)S(1)}, bf16[80,1664]{1,0:T(8,128)(2,1)S(1)}, u32[]{:S(2)}, u32[]{:S(2)}) collective-permute-start(bf16[80,1664]{1,0:T(8,128)(2,1)S(1)} %collective-permute-done.5), channel_id=1, source_target_pairs={{0,4},{4,0},{8,12},{12,8},{16,20},{20,16},{24,28},{28,24},{1,5},{5... | collective-permute-start | bytes 798728 | tf_op jit(solution)/shard_map/ppermute | solution.py:154
  61.7 29.9 %collective-permute-start.16 = (bf16[5,384,256]{2,1,0:T(8,128)(2,1)S(1)}, bf16[5,384,256]{2,1,0:T(8,128)(2,1)S(1)}, u32[]{:S(2)}, u32[]{:S(2)}) collective-permute-start(bf16[5,384,256]{2,1,0:T(8,128)(2,1)S(1)} %maximum_select_fusion.refs_0_), channel_id=1, source_target_pairs={{0,16},{4,20},{8,24},{12,28},{16,0},{20,4},{24,8},{28,12},{1,17},{... | collective-permute-start | bytes 2949128 | tf_op jit(solution)/shard_map/ppermute | solution.py:154
  79.7 27.8 %collective-permute-start.18 = (bf16[5,384,256]{2,1,0:T(8,128)(2,1)S(1)}, bf16[5,384,256]{2,1,0:T(8,128)(2,1)S(1)}, u32[]{:S(2)}, u32[]{:S(2)}) collective-permute-start(bf16[5,384,256]{2,1,0:T(8,128)(2,1)S(1)} %collective-permute-done.17.refs_2_), channel_id=1, source_target_pairs={{0,16},{4,20},{8,24},{12,28},{16,0},{20,4},{24,8},{28,12},{1,17},{... | collective-permute-start | bytes 2949128 | tf_op jit(solution)/shard_map/ppermute | solution.py:154
  89.5 30.9 %collective-permute-start.31 = (bf16[5,384,128]{2,1,0:T(8,128)(2,1)S(1)}, bf16[5,384,128]{2,1,0:T(8,128)(2,1)S(1)}, u32[]{:S(2)}, u32[]{:S(2)}) collective-permute-start(bf16[5,384,128]{2,1,0:T(8,128)(2,1)S(1)} %get-tuple-element.20.w_ref), channel_id=1, source_target_pairs={{0,16},{4,20},{8,24},{12,28},{16,0},{20,4},{24,8},{28,12},{1,17},{... | collective-permute-start | bytes 1474568 | tf_op jit(solution)/shard_map/ppermute | solution.py:154
  91.1 36.5 %collective-permute-start.37 = (bf16[5,384,128]{2,1,0:T(8,128)(2,1)S(1)}, bf16[5,384,128]{2,1,0:T(8,128)(2,1)S(1)}, u32[]{:S(2)}, u32[]{:S(2)}) collective-permute-start(bf16[5,384,128]{2,1,0:T(8,128)(2,1)S(1)} %get-tuple-element.21.w_ref), channel_id=1, source_target_pairs={{0,16},{4,20},{8,24},{12,28},{16,0},{20,4},{24,8},{28,12},{1,17},{... | collective-permute-start | bytes 1474568 | tf_op jit(solution)/shard_map/ppermute | solution.py:154
  130.9 14.5 %collective-permute-start.27 = (bf16[320,384]{1,0:T(8,128)(2,1)S(1)}, bf16[320,384]{1,0:T(8,128)(2,1)S(1)}, u32[]{:S(2)}, u32[]{:S(2)}) collective-permute-start(bf16[320,384]{1,0:T(8,128)(2,1)S(1)} %slice.230), channel_id=1, source_target_pairs={{0,8},{4,12},{8,0},{12,4},{16,24},{20,28},{24,16},{28,20},{1,9},{5... | collective-permute-start | bytes 737288 | tf_op jit(solution)/shard_map/ppermute | solution.py:154
  131.6 16.9 %collective-permute-start.33 = (bf16[320,384]{1,0:T(8,128)(2,1)S(1)}, bf16[320,384]{1,0:T(8,128)(2,1)S(1)}, u32[]{:S(2)}, u32[]{:S(2)}) collective-permute-start(bf16[320,384]{1,0:T(8,128)(2,1)S(1)} %slice.229), channel_id=1, source_target_pairs={{0,8},{4,12},{8,0},{12,4},{16,24},{20,28},{24,16},{28,20},{1,9},{5... | collective-permute-start | bytes 737288 | tf_op jit(solution)/shard_map/ppermute | solution.py:154
  133.4 22.5 %collective-permute-start.39 = (bf16[320,384]{1,0:T(8,128)(2,1)S(1)}, bf16[320,384]{1,0:T(8,128)(2,1)S(1)}, u32[]{:S(2)}, u32[]{:S(2)}) collective-permute-start(bf16[320,384]{1,0:T(8,128)(2,1)S(1)} %slice.228), channel_id=1, source_target_pairs={{0,8},{4,12},{8,0},{12,4},{16,24},{20,28},{24,16},{28,20},{1,9},{5... | collective-permute-start | bytes 737288 | tf_op jit(solution)/shard_map/ppermute | solution.py:154
  138.1 18.8 %collective-permute-start.23 = (bf16[80,384]{1,0:T(8,128)(2,1)S(1)}, bf16[80,384]{1,0:T(8,128)(2,1)S(1)}, u32[]{:S(2)}, u32[]{:S(2)}) collective-permute-start(bf16[80,384]{1,0:T(8,128)(2,1)S(1)} %get-tuple-element.34), channel_id=1, source_target_pairs={{0,3},{1,0},{2,1},{3,2},{4,7},{5,4},{6,5},{7,6},{8,11},{9,8},{10,9... | collective-permute-start | bytes 184328 | tf_op jit(solution)/shard_map/ppermute | solution.py:157
  145.3 16.0 %collective-permute-start.24 = (bf16[80,384]{1,0:T(8,128)(2,1)S(1)}, bf16[80,384]{1,0:T(8,128)(2,1)S(1)}, u32[]{:S(2)}, u32[]{:S(2)}) collective-permute-start(bf16[80,384]{1,0:T(8,128)(2,1)S(1)} %get-tuple-element.36), channel_id=1, source_target_pairs={{0,2},{1,3},{2,0},{3,1},{4,6},{5,7},{6,4},{7,5},{8,10},{9,11},{10,... | collective-permute-start | bytes 184328 | tf_op jit(solution)/shard_map/ppermute | solution.py:157
  145.3 16.0 %collective-permute-start.25 = (bf16[80,384]{1,0:T(8,128)(2,1)S(1)}, bf16[80,384]{1,0:T(8,128)(2,1)S(1)}, u32[]{:S(2)}, u32[]{:S(2)}) collective-permute-start(bf16[80,384]{1,0:T(8,128)(2,1)S(1)} %get-tuple-element.35), channel_id=1, source_target_pairs={{0,1},{1,2},{2,3},{3,0},{4,5},{5,6},{6,7},{7,4},{8,9},{9,10},{10,1... | collective-permute-start | bytes 184328 | tf_op jit(solution)/shard_map/ppermute | solution.py:157
  148.5 14.4 %collective-permute-start.28 = (bf16[80,384]{1,0:T(8,128)(2,1)S(1)}, bf16[80,384]{1,0:T(8,128)(2,1)S(1)}, u32[]{:S(2)}, u32[]{:S(2)}) collective-permute-start(bf16[80,384]{1,0:T(8,128)(2,1)S(1)} %get-tuple-element.37), channel_id=1, source_target_pairs={{0,3},{1,0},{2,1},{3,2},{4,7},{5,4},{6,5},{7,6},{8,11},{9,8},{10,9... | collective-permute-start | bytes 184328 | tf_op jit(solution)/shard_map/ppermute | solution.py:157
  (26 other events, 261.2 us)

commit v2 on v1

--- a/solution.py
+++ b/solution.py
@@ -36,29 +36,43 @@
     return jnp.concatenate([jnp.pad(high, pad), jnp.pad(low, pad)], axis=1)
 
 
+def after(values, *others):
+    return lax.optimization_barrier((values, *others))[0]
+
+
 def swap_blocks(values, index, blocks):
-    lead = values.shape[:-1]
-    out = values.reshape(*lead, blocks, -1)
+    size = values.shape[1] // blocks
     bit = 1
     while bit < blocks:
-        order = [m ^ bit for m in range(blocks)]
-        swapped = jnp.concatenate([out[..., m : m + 1, :] for m in order], axis=-2)
-        out = jnp.where((index & bit) != 0, swapped, out)
+        swapped = jnp.concatenate(
+            [values[:, (m ^ bit) * size : ((m ^ bit) + 1) * size] for m in range(blocks)], axis=1
+        )
+        values = jnp.where((index & bit) != 0, swapped, values)
         bit *= 2
-    return out.reshape(values.shape)
-
-
-def up_kernel(rows, place_ref, x_ref, *refs):
-    own, nbr, out_ref = refs[:rows], refs[rows : 2 * rows], refs[2 * rows]
-    first = place_ref[0] == 0
-    zone = place_ref[1]
-    local = place_ref[2]
+    return values
+
+
+def up_kernel(rows, blocks, place_ref, *refs):
+    parts, pieces = refs[:blocks], refs[blocks : blocks + QUAD * rows]
+    out_ref, x_ref = refs[blocks + QUAD * rows :]
+    side, core, zone, local = (place_ref[i] for i in range(4))
     expert = pl.program_id(0)
     width = out_ref.shape[1]
+
+    @pl.when(expert == 0)
+    def _():
+        at = 0
+        for part in parts:
+            x_ref[at : at + part.shape[0], :] = part[...]
+            at += part.shape[0]
+
     acc = None
     for m in range(rows):
-        a, b = own[m][0], nbr[m][0]
-        w = jnp.concatenate([jnp.where(first, a, b), jnp.where(first, b, a)], axis=0)
+        own, mate, own_x, mate_x = (pieces[QUAD * m + i][0] for i in range(QUAD))
+        near = [jnp.where(core == 0, own, mate), jnp.where(core == 0, mate, own)]
+        far = [jnp.where(core == 0, own_x, mate_x), jnp.where(core == 0, mate_x, own_x)]
+        order = [jnp.where(side == 0, a, b) for a, b in zip(near + far, far + near)]
+        w = jnp.concatenate(order, axis=0)
         depth = w.shape[0]
         part = jnp.dot(
             x_ref[:, m * depth : (m + 1) * depth], w, preferred_element_type=jnp.float32
@@ -73,28 +87,30 @@
     out_ref[...] = (g / (1.0 + jnp.exp(-g)) * u * gate).astype(jnp.bfloat16)
 
 
-def up_call(place, x, own, nbr):
-    rows = len(own)
-    local, depth, cols = own[0].shape
-    tokens, lanes = x.shape
+def up_call(place, parts, pieces):
+    rows = len(pieces) // QUAD
+    local, depth, cols = pieces[0].shape
+    tokens, lanes = sum(v.shape[0] for v in parts), parts[0].shape[1]
     piece = pl.BlockSpec((1, depth, cols), lambda e, p: (e, 0, 0))
     return pl.pallas_call(
-        functools.partial(up_kernel, rows),
+        functools.partial(up_kernel, rows, len(parts)),
         grid_spec=pltpu.PrefetchScalarGridSpec(
             num_scalar_prefetch=1,
             grid=(local,),
-            in_specs=[pl.BlockSpec((tokens, lanes), lambda e, p: (0, 0))] + [piece] * (2 * rows),
+            in_specs=[pl.BlockSpec(v.shape, lambda e, p: (0, 0)) for v in parts]
+            + [piece] * len(pieces),
             out_specs=pl.BlockSpec((tokens, cols // 2), lambda e, p: (0, e)),
+            scratch_shapes=[pltpu.VMEM((tokens, lanes), jnp.bfloat16)],
         ),
         out_shape=jax.ShapeDtypeStruct((tokens, local * cols // 2), jnp.bfloat16),
-        compiler_params=pltpu.CompilerParams(vmem_limit_bytes=40 * 1024 * 1024),
+        compiler_params=pltpu.CompilerParams(vmem_limit_bytes=48 * 1024 * 1024),
         cost_estimate=pl.CostEstimate(
             flops=2 * tokens * lanes * local * cols,
             bytes_accessed=2 * (tokens * lanes + local * lanes * cols),
             transcendentals=tokens * local * cols // 2,
         ),
         name="up",
-    )(place, x, *own, *nbr)
+    )(place, *parts, *pieces)
 
 
 def down_kernel(h_ref, w_ref, out_ref):
@@ -153,33 +169,24 @@
     def flip(values, bit):
         return lax.ppermute(values, "dp", [(i, i ^ bit) for i in range(ranks)])
 
-    def shift(values, step):
-        return lax.ppermute(values, "expert", [(i, (i + step) % zones) for i in range(zones)])
-
-    def columns(values, offset):
-        return lax.dynamic_slice_in_dim(values, offset, part, axis=2)
+    def hop(values, bit):
+        return lax.ppermute(values, "expert", [(i, i ^ bit) for i in range(zones)])
 
     def quarter(values, c, s):
         blocks = values.shape[2] // hid
-        cuts = [columns(values, b * hid + (2 * c + s) * part) for b in range(blocks)]
+        cuts = [
+            lax.dynamic_slice_in_dim(values, b * hid + (2 * c + s) * part, part, axis=2)
+            for b in range(blocks)
+        ]
         return jnp.concatenate(cuts, axis=2) if blocks > 1 else cuts[0]
 
-    def spread(values):
+    def from_mate(values):
         away = jnp.concatenate([quarter(values, 1 - core, s) for s in range(2)], axis=2)
         got = flip(away, 1)
         size = got.shape[2] // 2
-        both = []
-        for s in (side, 1 - side):
-            mine = quarter(values, core, s)
-            theirs = lax.dynamic_slice_in_dim(got, s * size, size, axis=2)
-            both.append(
-                jnp.where(
-                    core == 0,
-                    jnp.concatenate([mine, theirs], axis=1),
-                    jnp.concatenate([theirs, mine], axis=1),
-                )
-            )
-        return both[0], flip(both[1], 2)
+        return [
+            lax.dynamic_slice_in_dim(got, s * size, size, axis=2) for s in (side, 1 - side)
+        ]
 
     def widen(pieces):
         bit = 1
@@ -188,12 +195,19 @@
             bit *= 2
         return pieces
 
-    gu_own, gu_nbr = spread(gate_up)
-    own, nbr = widen([gu_own]), widen([gu_nbr])
-    dn_own, dn_nbr = spread(down_weight)
-    halves = [
-        widen([jnp.where(side == j, dn_own, dn_nbr)]) for j in range(2)
-    ]
+    zone_bits = []
+    while 1 << len(zone_bits) < zones:
+        zone_bits.insert(0, 1 << len(zone_bits))
+
+    gu_mate, gu_mate_away = from_mate(gate_up)
+    gu_own = quarter(gate_up, core, side)
+    gu_own_x = flip(quarter(gate_up, core, 1 - side), 2)
+    gu_mate_x = flip(gu_mate_away, 2)
+    first = widen([gu_own])
+    second = widen([gu_mate])
+    third = widen([after(gu_own_x, first[-1])])
+    fourth = widen([after(gu_mate_x, second[-1])])
+    pieces = [p for group in zip(first, second, third, fourth) for p in group]
 
     mixed = residual.astype(jnp.float32) + jnp.dot(
         attended, out_weight, preferred_element_type=jnp.float32
@@ -203,15 +217,36 @@
     normed_in = normalize(stream_in, norm_gain).astype(jnp.bfloat16)
     gates = gate_lanes(slot_gates(routes, gate_logits, placement))
     sent = jnp.concatenate([swap_blocks(normed_in, row, rows), gates], axis=1)
-
-    column = [sent] + [shift(sent, k) for k in range(1, zones)]
-    beside = [flip(v, 2) for v in column]
-    chip = column + beside
-    mate = [flip(v, 1) for v in chip]
-    x = jnp.concatenate(chip + mate, axis=0)
-
-    place = jnp.stack([side, zone, jnp.int32(local)]).astype(jnp.int32)
-    hidden = up_call(place, x, own, nbr)
+    sent = after(sent, gu_own, gu_mate)
+    near = sent
+    for bit in zone_bits[:-1]:
+        near = jnp.concatenate([near, hop(near, bit)], axis=0)
+    far = hop(near, zone_bits[-1])
+    near_x = flip(near, 2)
+    far_x = flip(far, 2)
+    chip = [near, far, near_x, far_x]
+    parts = chip + [flip(v, 1) for v in chip]
+
+    dn_mate, dn_mate_away = from_mate(down_weight)
+    dn_own = quarter(down_weight, core, side)
+    dn_away = quarter(down_weight, core, 1 - side)
+
+    def pair(own, mate):
+        return jnp.where(
+            core == 0,
+            jnp.concatenate([own, mate], axis=1),
+            jnp.concatenate([mate, own], axis=1),
+        )
+
+    dn_near = pair(dn_own, dn_mate)
+    dn_far = flip(after(pair(dn_away, dn_mate_away), near_x), 2)
+    halves = []
+    for j, gate_piece in ((0, third), (1, fourth)):
+        half = jnp.where(side == j, dn_near, dn_far)
+        halves.append(widen([after(half, gate_piece[-1])]))
+
+    place = jnp.stack([side, core, zone, jnp.int32(local)]).astype(jnp.int32)
+    hidden = up_call(place, parts, pieces)
 
     count = zones * tok
     chunks = []
@@ -219,15 +254,13 @@
         for j in range(2):
             partial = down_call(hidden, halves[j][m])
             back = flip(partial[2 * count :], 1)
-            summed = (
-                partial[: 2 * count].astype(jnp.float32) + back.astype(jnp.float32)
-            )
-            back = flip(summed[count:].astype(jnp.bfloat16), 2)
-            summed = summed[:count] + back.astype(jnp.float32)
-            total = summed[:tok]
-            for k in range(1, zones):
-                piece = summed[k * tok : (k + 1) * tok].astype(jnp.bfloat16)
-                total = total + shift(piece, -k).astype(jnp.float32)
+            total = partial[: 2 * count].astype(jnp.float32) + back.astype(jnp.float32)
+            back = flip(total[count:].astype(jnp.bfloat16), 2)
+            total = total[:count] + back.astype(jnp.float32)
+            for bit in reversed(zone_bits):
+                size = total.shape[0] // 2
+                back = hop(total[size:].astype(jnp.bfloat16), bit)
+                total = total[:size] + back.astype(jnp.float32)
             chunks.append(total)
     branch = swap_blocks(jnp.concatenate(chunks, axis=1), row, rows)
     total = stream_in + branch

time: 178 us -> 167 us (0.938)
  waiting for transfers between devices: 70.6 us -> 91.7 us
  starting transfers between devices: 56.1 us -> 35.9 us
  local copies, waits for them, and re-layouts: 24.2 us -> 12.1 us
  Pallas kernels: 12.5 us -> 15.3 us
  other arithmetic: 9.9 us -> 7.42 us
    ppermute x15 -> x10, starting transfers between devices: 37 us -> 16.9 us  [hop(): return lax.ppermute(values, 'expert', [(i, i ^ bit) for i in range(zones)])]
    ppermute x28 -> x25, waiting for transfers between devices: 58.9 us -> 73.8 us  [flip(): return lax.ppermute(values, 'dp', [(i, i ^ bit) for i in range(ranks)])]
    unnamed x31 -> x39, local copies, waits for them, and re-layouts: 17.9 us -> 5.09 us
    ppermute x15 -> x10, waiting for transfers between devices: 11.7 us -> 17.9 us  [hop(): return lax.ppermute(values, 'expert', [(i, i ^ bit) for i in range(zones)])]
    pallas_call x1, Pallas kernels: 7.34 us -> 10.1 us  [up_call(): pl.pallas_call(functools.partial(up_kernel, rows, len(parts)), grid_spec=...]
    dynamic_slice x4, local copies, waits for them, and re-layouts: 3.7 us -> 6.21 us  [the longest x2 3.57 us: quarter(): lax.dynamic_slice_in_dim(values, b * hid + (2 * c + s) * part, part, axis=2)]
    ppermute x28 -> x25, starting transfers between devices: 19 us -> 19 us  [flip(): return lax.ppermute(values, 'dp', [(i, i ^ bit) for i in range(ranks)])]
  transfers between devices with their start and end apart: 43 -> 35, of which waited for: 14 -> 16; matrix products, arithmetic and copies ran while one was open for 14% -> 7% of each run, Pallas kernels for 7% -> 9%
where the time goes in v2:
time: 167 us
  waiting for transfers between devices  91.7 us (55%)
  starting transfers between devices  35.9 us (21%)
  Pallas kernels  15.3 us (9%)
  local copies, waits for them, and re-layouts  12.1 us (7%)
  other arithmetic  7.42 us (4%)
  matrix products  3.28 us (2%)
    ppermute x25, waiting for transfers between devices, flip(): return lax.ppermute(values, 'dp', [(i, i ^ bit) for i in range(ranks)])  73.8 us
    ppermute x25, starting transfers between devices, flip(): return lax.ppermute(values, 'dp', [(i, i ^ bit) for i in range(ranks)])  19 us
    ppermute x10, waiting for transfers between devices, hop(): return lax.ppermute(values, 'expert', [(i, i ^ bit) for i in range(zones)])  17.9 us
    ppermute x10, starting transfers between devices, hop(): return lax.ppermute(values, 'expert', [(i, i ^ bit) for i in range(zones)])  16.9 us
    pallas_call x1, Pallas kernels, up_call(): pl.pallas_call(functools.partial(up_kernel, rows, len(parts)), grid_spec=...  10.1 us
    pallas_call x4, Pallas kernels, down_call(): pl.pallas_call(down_kernel, grid=(steps,), in_specs=[pl.BlockSpec((tokens...  5.22 us
    unnamed x39, local copies, waits for them, and re-layouts  5.09 us
    dynamic_slice x2, local copies, waits for them, and re-layouts, quarter(): lax.dynamic_slice_in_dim(values, b * hid + (2 * c + s) * part, part, axis=2)  3.57 us
  transfers between devices with their start and end apart: 35, of which 16 were waited for; matrix products, arithmetic and copies ran while one was open for 7% of the time, Pallas kernels for 9%

profile of v2, /device:TPU:0, one launch (start us, length us, event | category | flops | bytes accessed | tf_op | source)
XLA Modules:
  0.0 167.0 jit_solution(6755996894283316600)
XLA Ops:
  0.7 2.6 %constant_dynamic-slice_fusion.8 = (bf16[5,192,128]{2,1,0:T(8,128)(2,1)}, bf16[5,192,128]{2,1,0:T(8,128)(2,1)S(1)}, bf16[5,192,128]{2,1,0:T(8,128)(2,1)S(1)}, bf...) fusion(bf16[5,192,1024]{2,1,0:T(8,128)(2,1)} %param.18, ...), kind=kLoop, calls=%fused_computation.61 | loop fusion | bytes 3932192 | tf_op jit(solution)/shard_map/dynamic_slice | solution.py:178
  5.2 3.3 %fusion = bf16[80,1536]{1,0:T(8,128)(2,1)S(1)} fusion(bf16[80,1536]{1,0:T(8,128)(2,1)S(1)} %copy-done, bf16[1536,1536]{1,0:T(8,128)(2,1)} %param.12, bf16[80,1536]{1,0:T(8,128)(2,1)S(1)} %copy-done.13), kind=kOutput, calls=%fused_computation.1 | convolution fusion | flops 377856000 | bytes 5455872 | tf_op jit(solution)/shard_map/dot_general | solution.py:212
  11.6 3.6 %collective-permute-start.1 = (bf16[80,1664]{1,0:T(8,128)(2,1)S(1)}, bf16[80,1664]{1,0:T(8,128)(2,1)S(1)}, u32[]{:S(2)}, u32[]{:S(2)}) collective-permute-start(bf16[80,1664]{1,0:T(8,128)(2,1)S(1)} %concatenate.43), channel_id=1, source_target_pairs={{0,2},{1,3},{2,0},{3,1},{4,6},{5,7},{6,4},{7,5},{8,10},{9,11},{10,... | collective-permute-start | bytes 798728 | tf_op jit(solution)/shard_map/ppermute | solution.py:173
  16.3 11.7 %collective-permute-done.1 = bf16[80,1664]{1,0:T(8,128)(2,1)S(1)} collective-permute-done((bf16[80,1664]{1,0:T(8,128)(2,1)S(1)}, bf16[80,1664]{1,0:T(8,128)(2,1)S(1)}, u32[]{:S(2)}, u32[]{:S(2)}) %collective-permute-start.1) | collective-permute-done | bytes 266272 | tf_op jit(solution)/shard_map/ppermute | solution.py:173
  34.1 1.8 %constant_dynamic-slice_fusion.2 = (bf16[5,192,128]{2,1,0:T(8,128)(2,1)}, bf16[5,192,128]{2,1,0:T(8,128)(2,1)S(1)}) fusion(bf16[5,192,256]{2,1,0:T(8,128)(2,1)} %collective-permute-done.15, s32[]{:T(128)S(6)} %select_n.130, s32[]{:T(128)S(6)} %select_n.133), kind=kLoop, calls=%fused_computation.55 | loop fusion | bytes 983048 | tf_op jit(solution)/shard_map/dynamic_slice | solution.py:188
  35.9 7.3 %collective-permute-done.11.refs_11_ = bf16[5,192,256]{2,1,0:T(8,128)(2,1)} collective-permute-done((bf16[5,192,256]{2,1,0:T(8,128)(2,1)}, bf16[5,192,256]{2,1,0:T(8,128)(2,1)}, u32[]{:S(2)}, u32[]{:S(2)}) %collective-permute-start.11) | collective-permute-done | bytes 491552 | tf_op jit(solution)/shard_map/ppermute | solution.py:170
  47.7 6.8 %collective-permute-done.3.refs_2_ = bf16[160,1664]{1,0:T(8,128)(2,1)S(1)} collective-permute-done((bf16[160,1664]{1,0:T(8,128)(2,1)S(1)}, bf16[160,1664]{1,0:T(8,128)(2,1)S(1)}, u32[]{:S(2)}, u32[]{:S(2)}) %collective-permute-start.3) | collective-permute-done | bytes 532512 | tf_op jit(solution)/shard_map/ppermute | solution.py:170
  56.0 9.1 %collective-permute-done.9.refs_10_ = bf16[5,192,256]{2,1,0:T(8,128)(2,1)} collective-permute-done((bf16[5,192,256]{2,1,0:T(8,128)(2,1)S(1)}, bf16[5,192,256]{2,1,0:T(8,128)(2,1)}, u32[]{:S(2)}, u32[]{:S(2)}) %collective-permute-start.9) | collective-permute-done | bytes 491552 | tf_op jit(solution)/shard_map/ppermute | solution.py:170
  67.3 9.2 %collective-permute-done.4.refs_3_ = bf16[160,1664]{1,0:T(8,128)(2,1)S(1)} collective-permute-done((bf16[160,1664]{1,0:T(8,128)(2,1)S(1)}, bf16[160,1664]{1,0:T(8,128)(2,1)S(1)}, u32[]{:S(2)}, u32[]{:S(2)}) %collective-permute-start.4) | collective-permute-done | bytes 532512 | tf_op jit(solution)/shard_map/ppermute | solution.py:170
  76.5 9.3 %collective-permute-done.16 = bf16[5,384,128]{2,1,0:T(8,128)(2,1)S(1)} collective-permute-done((bf16[5,384,128]{2,1,0:T(8,128)(2,1)S(1)}, bf16[5,384,128]{2,1,0:T(8,128)(2,1)S(1)}, u32[]{:S(2)}, u32[]{:S(2)}) %collective-permute-start.16) | collective-permute-done | bytes 491552 | tf_op jit(solution)/shard_map/ppermute | solution.py:170
  88.2 1.7 %broadcast_select_fusion.1 = (bf16[5,384,128]{2,1,0:T(8,128)(2,1)S(1)}, bf16[5,384,128]{2,1,0:T(8,128)(2,1)S(1)}) fusion(bf16[5,384,128]{2,1,0:T(8,128)(2,1)} %copy-done.12, pred[]{:T(512)S(6)} %eq.29, bf16[5,192,128]{2,1,0:T(8,128)(2,1)} %get-tuple-element.26, bf16[5,192,128]{2,1,0:T(8,128)(2,1)} %get-tuple-element.34, pred[]{:T(512)S(6)} %eq.30, pred[]{:T(512)S(6)} %eq.31), kind=kLoop, calls=%fused_computation.30 | loop fusion | flops 2703360 | bytes 1966083 | tf_op jit(solution)/shard_map/jit(_where)/select_n | solution.py:245
  89.9 9.0 %collective-permute-done.13.refs_14_ = bf16[5,192,256]{2,1,0:T(8,128)(2,1)} collective-permute-done((bf16[5,192,256]{2,1,0:T(8,128)(2,1)}, bf16[5,192,256]{2,1,0:T(8,128)(2,1)}, u32[]{:S(2)}, u32[]{:S(2)}) %collective-permute-start.13) | collective-permute-done | bytes 491552 | tf_op jit(solution)/shard_map/ppermute | solution.py:170
  101.0 10.1 %up.1.h_ref = bf16[1280,640]{1,0:T(8,128)(2,1)} custom-call(s32[4]{0:T(128)S(1)} %pad_add_fusion.place_ref, bf16[160,1664]{1,0:T(8,128)(2,1)S(1)} %constant_dynamic-update-slice_fusion.refs_0_, bf16[160,1664]{1,0:T(8,128)(2,1)S(1)} %collective-permute-done.2.refs_1_, bf16[160,1664]{1,0:T(8,128)(2,1)S(1)} %collective-permute-done.3.refs_2_, ...), custom_call_target="tpu_custom_call" | custom-call | flops 5452595200 | bytes 8519680 | tf_op jit(solution)/shard_map/up/pallas_call | solution.py:95
  111.1 2.0 %collective-permute-done.22.w_ref = bf16[5,384,128]{2,1,0:T(8,128)(2,1)S(1)} collective-permute-done((bf16[5,384,128]{2,1,0:T(8,128)(2,1)S(1)}, bf16[5,384,128]{2,1,0:T(8,128)(2,1)S(1)}, u32[]{:S(2)}, u32[]{:S(2)}) %collective-permute-start.22) | collective-permute-done | bytes 491552 | tf_op jit(solution)/shard_map/ppermute | solution.py:170
  116.0 4.6 %collective-permute-done.17.w_ref = bf16[5,384,128]{2,1,0:T(8,128)(2,1)S(1)} collective-permute-done((bf16[5,384,128]{2,1,0:T(8,128)(2,1)S(1)}, bf16[5,384,128]{2,1,0:T(8,128)(2,1)S(1)}, u32[]{:S(2)}, u32[]{:S(2)}) %collective-permute-start.17) | collective-permute-done | bytes 491552 | tf_op jit(solution)/shard_map/ppermute | solution.py:170
  128.0 1.6 collective-permute-start.32
  130.3 4.1 %collective-permute-done.24 = bf16[320,384]{1,0:T(8,128)(2,1)S(1)} collective-permute-done((bf16[320,384]{1,0:T(8,128)(2,1)S(1)}, bf16[320,384]{1,0:T(8,128)(2,1)S(1)}, u32[]{:S(2)}, u32[]{:S(2)}) %collective-permute-start.24) | collective-permute-done | bytes 245792 | tf_op jit(solution)/shard_map/ppermute | solution.py:170
  135.4 4.2 %collective-permute-done.19 = bf16[320,384]{1,0:T(8,128)(2,1)S(1)} collective-permute-done((bf16[320,384]{1,0:T(8,128)(2,1)S(1)}, bf16[320,384]{1,0:T(8,128)(2,1)S(1)}, u32[]{:S(2)}, u32[]{:S(2)}) %collective-permute-start.19) | collective-permute-done | bytes 245792 | tf_op jit(solution)/shard_map/ppermute | solution.py:170
  140.7 4.2 %collective-permute-done.32 = bf16[320,384]{1,0:T(8,128)(2,1)S(1)} collective-permute-done((bf16[320,384]{1,0:T(8,128)(2,1)S(1)}, bf16[320,384]{1,0:T(8,128)(2,1)S(1)}, u32[]{:S(2)}, u32[]{:S(2)}) %collective-permute-start.32) | collective-permute-done | bytes 245792 | tf_op jit(solution)/shard_map/ppermute | solution.py:170
  145.9 3.8 %collective-permute-done.28 = bf16[320,384]{1,0:T(8,128)(2,1)S(1)} collective-permute-done((bf16[320,384]{1,0:T(8,128)(2,1)S(1)}, bf16[320,384]{1,0:T(8,128)(2,1)S(1)}, u32[]{:S(2)}, u32[]{:S(2)}) %collective-permute-start.28) | collective-permute-done | bytes 245792 | tf_op jit(solution)/shard_map/ppermute | solution.py:170
  150.8 3.6 %collective-permute-start.26 = (bf16[80,384]{1,0:T(8,128)(2,1)S(1)}, bf16[80,384]{1,0:T(8,128)(2,1)S(1)}, u32[]{:S(2)}, u32[]{:S(2)}) collective-permute-start(bf16[80,384]{1,0:T(8,128)(2,1)S(1)} %slice.224), channel_id=1, source_target_pairs={{0,2},{1,3},{2,0},{3,1},{4,6},{5,7},{6,4},{7,5},{8,10},{9,11},{10,... | collective-permute-start | bytes 184328 | tf_op jit(solution)/shard_map/ppermute | solution.py:173
  154.6 3.0 %collective-permute-start.34 = (bf16[80,384]{1,0:T(8,128)(2,1)S(1)}, bf16[80,384]{1,0:T(8,128)(2,1)S(1)}, u32[]{:S(2)}, u32[]{:S(2)}) collective-permute-start(bf16[80,384]{1,0:T(8,128)(2,1)S(1)} %slice.222), channel_id=1, source_target_pairs={{0,2},{1,3},{2,0},{3,1},{4,6},{5,7},{6,4},{7,5},{8,10},{9,11},{10,... | collective-permute-start | bytes 184328 | tf_op jit(solution)/shard_map/ppermute | solution.py:173
  157.6 2.0 %collective-permute-start.30 = (bf16[80,384]{1,0:T(8,128)(2,1)S(1)}, bf16[80,384]{1,0:T(8,128)(2,1)S(1)}, u32[]{:S(2)}, u32[]{:S(2)}) collective-permute-start(bf16[80,384]{1,0:T(8,128)(2,1)S(1)} %slice.223), channel_id=1, source_target_pairs={{0,2},{1,3},{2,0},{3,1},{4,6},{5,7},{6,4},{7,5},{8,10},{9,11},{10,... | collective-permute-start | bytes 184328 | tf_op jit(solution)/shard_map/ppermute | solution.py:173
  159.7 4.7 %collective-permute-done.21 = bf16[80,384]{1,0:T(8,128)(2,1)S(1)} collective-permute-done((bf16[80,384]{1,0:T(8,128)(2,1)S(1)}, bf16[80,384]{1,0:T(8,128)(2,1)S(1)}, u32[]{:S(2)}, u32[]{:S(2)}) %collective-permute-start.21) | collective-permute-done | bytes 61472 | tf_op jit(solution)/shard_map/ppermute | solution.py:173
  (153 shorter events, 42.5 us)
Async XLA Ops:
  11.6 16.4 %collective-permute-start.1 = (bf16[80,1664]{1,0:T(8,128)(2,1)S(1)}, bf16[80,1664]{1,0:T(8,128)(2,1)S(1)}, u32[]{:S(2)}, u32[]{:S(2)}) collective-permute-start(bf16[80,1664]{1,0:T(8,128)(2,1)S(1)} %concatenate.43), channel_id=1, source_target_pairs={{0,2},{1,3},{2,0},{3,1},{4,6},{5,7},{6,4},{7,5},{8,10},{9,11},{10,... | collective-permute-start | bytes 798728 | tf_op jit(solution)/shard_map/ppermute | solution.py:173
  16.1 17.5 %collective-permute-start.15 = (bf16[5,192,256]{2,1,0:T(8,128)(2,1)}, bf16[5,192,256]{2,1,0:T(8,128)(2,1)}, u32[]{:S(2)}, u32[]{:S(2)}) collective-permute-start(bf16[5,192,256]{2,1,0:T(8,128)(2,1)} %pad_maximum_fusion.3), channel_id=1, source_target_pairs={{0,4},{4,0},{8,12},{12,8},{16,20},{20,16},{24,28},{28,24},{1,5},{5... | collective-permute-start | bytes 1474568 | tf_op jit(solution)/shard_map/ppermute | solution.py:170
  28.0 19.1 %collective-permute-start.2 = (bf16[160,1664]{1,0:T(8,128)(2,1)S(1)}, bf16[160,1664]{1,0:T(8,128)(2,1)S(1)}, u32[]{:S(2)}, u32[]{:S(2)}) collective-permute-start(bf16[160,1664]{1,0:T(8,128)(2,1)S(1)} %constant_dynamic-update-slice_fusion.refs_0_), channel_id=1, source_target_pairs={{0,1},{1,0},{2,3},{3,2},{4,5},{5,4},{6,7},{7,6},{8,9},{9,8},{10,11... | collective-permute-start | bytes 1597448 | tf_op jit(solution)/shard_map/ppermute | solution.py:173
  28.8 14.4 %collective-permute-start.11 = (bf16[5,192,256]{2,1,0:T(8,128)(2,1)}, bf16[5,192,256]{2,1,0:T(8,128)(2,1)}, u32[]{:S(2)}, u32[]{:S(2)}) collective-permute-start(bf16[5,192,256]{2,1,0:T(8,128)(2,1)} %get-tuple-element.30), channel_id=1, source_target_pairs={{0,8},{4,12},{8,0},{12,4},{16,24},{20,28},{24,16},{28,20},{1,9},{5... | collective-permute-start | bytes 1474568 | tf_op jit(solution)/shard_map/ppermute | solution.py:170
  30.3 14.4 %collective-permute-start.12 = (bf16[5,192,256]{2,1,0:T(8,128)(2,1)S(1)}, bf16[5,192,256]{2,1,0:T(8,128)(2,1)S(1)}, u32[]{:S(2)}, u32[]{:S(2)}) collective-permute-start(bf16[5,192,256]{2,1,0:T(8,128)(2,1)S(1)} %get-tuple-element.31.refs_9_), channel_id=1, source_target_pairs={{0,16},{4,20},{8,24},{12,28},{16,0},{20,4},{24,8},{28,12},{1,17},{... | collective-permute-start | bytes 1474568 | tf_op jit(solution)/shard_map/ppermute | solution.py:170
  31.8 22.7 %collective-permute-start.3 = (bf16[160,1664]{1,0:T(8,128)(2,1)S(1)}, bf16[160,1664]{1,0:T(8,128)(2,1)S(1)}, u32[]{:S(2)}, u32[]{:S(2)}) collective-permute-start(bf16[160,1664]{1,0:T(8,128)(2,1)S(1)} %constant_dynamic-update-slice_fusion.refs_0_), channel_id=1, source_target_pairs={{0,8},{4,12},{8,0},{12,4},{16,24},{20,28},{24,16},{28,20},{1,9},{5... | collective-permute-start | bytes 1597448 | tf_op jit(solution)/shard_map/ppermute | solution.py:170
  33.5 31.7 %collective-permute-start.10 = (bf16[5,192,256]{2,1,0:T(8,128)(2,1)S(1)}, bf16[5,192,256]{2,1,0:T(8,128)(2,1)S(1)}, u32[]{:S(2)}, u32[]{:S(2)}) collective-permute-start(bf16[5,192,256]{2,1,0:T(8,128)(2,1)S(1)} %pad_maximum_fusion.1.refs_8_), channel_id=1, source_target_pairs={{0,16},{4,20},{8,24},{12,28},{16,0},{20,4},{24,8},{28,12},{1,17},{... | collective-permute-start | bytes 1474568 | tf_op jit(solution)/shard_map/ppermute | solution.py:170
  43.3 21.9 %collective-permute-start.9 = (bf16[5,192,256]{2,1,0:T(8,128)(2,1)S(1)}, bf16[5,192,256]{2,1,0:T(8,128)(2,1)}, u32[]{:S(2)}, u32[]{:S(2)}) collective-permute-start(bf16[5,192,256]{2,1,0:T(8,128)(2,1)S(1)} %pad_maximum_fusion.2), channel_id=1, source_target_pairs={{0,8},{4,12},{8,0},{12,4},{16,24},{20,28},{24,16},{28,20},{1,9},{5... | collective-permute-start | bytes 1474568 | tf_op jit(solution)/shard_map/ppermute | solution.py:170
  45.5 21.0 %collective-permute-start.14 = (bf16[5,192,256]{2,1,0:T(8,128)(2,1)}, bf16[5,192,256]{2,1,0:T(8,128)(2,1)S(1)}, u32[]{:S(2)}, u32[]{:S(2)}) collective-permute-start(bf16[5,192,256]{2,1,0:T(8,128)(2,1)} %collective-permute-done.11.refs_11_), channel_id=1, source_target_pairs={{0,16},{4,20},{8,24},{12,28},{16,0},{20,4},{24,8},{28,12},{1,17},{... | collective-permute-start | bytes 1474568 | tf_op jit(solution)/shard_map/ppermute | solution.py:170
  47.1 29.5 %collective-permute-start.4 = (bf16[160,1664]{1,0:T(8,128)(2,1)S(1)}, bf16[160,1664]{1,0:T(8,128)(2,1)S(1)}, u32[]{:S(2)}, u32[]{:S(2)}) collective-permute-start(bf16[160,1664]{1,0:T(8,128)(2,1)S(1)} %collective-permute-done.2.refs_1_), channel_id=1, source_target_pairs={{0,8},{4,12},{8,0},{12,4},{16,24},{20,28},{24,16},{28,20},{1,9},{5... | collective-permute-start | bytes 1597448 | tf_op jit(solution)/shard_map/ppermute | solution.py:170
  54.6 31.2 %collective-permute-start.16 = (bf16[5,384,128]{2,1,0:T(8,128)(2,1)S(1)}, bf16[5,384,128]{2,1,0:T(8,128)(2,1)S(1)}, u32[]{:S(2)}, u32[]{:S(2)}) collective-permute-start(bf16[5,384,128]{2,1,0:T(8,128)(2,1)S(1)} %maximum_select_fusion.1), channel_id=1, source_target_pairs={{0,8},{4,12},{8,0},{12,4},{16,24},{20,28},{24,16},{28,20},{1,9},{5... | collective-permute-start | bytes 1474568 | tf_op jit(solution)/shard_map/ppermute | solution.py:170
  65.2 35.3 %collective-permute-start.5 = (bf16[160,1664]{1,0:T(8,128)(2,1)S(1)}, bf16[160,1664]{1,0:T(8,128)(2,1)}, u32[]{:S(2)}, u32[]{:S(2)}) collective-permute-start(bf16[160,1664]{1,0:T(8,128)(2,1)S(1)} %constant_dynamic-update-slice_fusion.refs_0_), channel_id=1, source_target_pairs={{0,4},{4,0},{8,12},{12,8},{16,20},{20,16},{24,28},{28,24},{1,5},{5... | collective-permute-start | bytes 1597448 | tf_op jit(solution)/shard_map/ppermute | solution.py:170
  66.0 34.9 %collective-permute-start.6 = (bf16[160,1664]{1,0:T(8,128)(2,1)S(1)}, bf16[160,1664]{1,0:T(8,128)(2,1)}, u32[]{:S(2)}, u32[]{:S(2)}) collective-permute-start(bf16[160,1664]{1,0:T(8,128)(2,1)S(1)} %collective-permute-done.2.refs_1_), channel_id=1, source_target_pairs={{0,4},{4,0},{8,12},{12,8},{16,20},{20,16},{24,28},{28,24},{1,5},{5... | collective-permute-start | bytes 1597448 | tf_op jit(solution)/shard_map/ppermute | solution.py:170
  67.3 33.6 %collective-permute-start.7 = (bf16[160,1664]{1,0:T(8,128)(2,1)S(1)}, bf16[160,1664]{1,0:T(8,128)(2,1)}, u32[]{:S(2)}, u32[]{:S(2)}) collective-permute-start(bf16[160,1664]{1,0:T(8,128)(2,1)S(1)} %collective-permute-done.3.refs_2_), channel_id=1, source_target_pairs={{0,4},{4,0},{8,12},{12,8},{16,20},{20,16},{24,28},{28,24},{1,5},{5... | collective-permute-start | bytes 1597448 | tf_op jit(solution)/shard_map/ppermute | solution.py:170
  76.5 24.5 %collective-permute-start.8 = (bf16[160,1664]{1,0:T(8,128)(2,1)S(1)}, bf16[160,1664]{1,0:T(8,128)(2,1)}, u32[]{:S(2)}, u32[]{:S(2)}) collective-permute-start(bf16[160,1664]{1,0:T(8,128)(2,1)S(1)} %collective-permute-done.4.refs_3_), channel_id=1, source_target_pairs={{0,4},{4,0},{8,12},{12,8},{16,20},{20,16},{24,28},{28,24},{1,5},{5... | collective-permute-start | bytes 1597448 | tf_op jit(solution)/shard_map/ppermute | solution.py:170
  86.6 12.3 %collective-permute-start.13 = (bf16[5,192,256]{2,1,0:T(8,128)(2,1)}, bf16[5,192,256]{2,1,0:T(8,128)(2,1)}, u32[]{:S(2)}, u32[]{:S(2)}) collective-permute-start(bf16[5,192,256]{2,1,0:T(8,128)(2,1)} %collective-permute-done.9.refs_10_), channel_id=1, source_target_pairs={{0,16},{4,20},{8,24},{12,28},{16,0},{20,4},{24,8},{28,12},{1,17},{... | collective-permute-start | bytes 1474568 | tf_op jit(solution)/shard_map/ppermute | solution.py:170
  98.9 14.2 %collective-permute-start.22 = (bf16[5,384,128]{2,1,0:T(8,128)(2,1)S(1)}, bf16[5,384,128]{2,1,0:T(8,128)(2,1)S(1)}, u32[]{:S(2)}, u32[]{:S(2)}) collective-permute-start(bf16[5,384,128]{2,1,0:T(8,128)(2,1)S(1)} %get-tuple-element.13.w_ref), channel_id=1, source_target_pairs={{0,16},{4,20},{8,24},{12,28},{16,0},{20,4},{24,8},{28,12},{1,17},{... | collective-permute-start | bytes 1474568 | tf_op jit(solution)/shard_map/ppermute | solution.py:170
  100.5 20.1 %collective-permute-start.17 = (bf16[5,384,128]{2,1,0:T(8,128)(2,1)S(1)}, bf16[5,384,128]{2,1,0:T(8,128)(2,1)S(1)}, u32[]{:S(2)}, u32[]{:S(2)}) collective-permute-start(bf16[5,384,128]{2,1,0:T(8,128)(2,1)S(1)} %get-tuple-element.12.w_ref), channel_id=1, source_target_pairs={{0,16},{4,20},{8,24},{12,28},{16,0},{20,4},{24,8},{28,12},{1,17},{... | collective-permute-start | bytes 1474568 | tf_op jit(solution)/shard_map/ppermute | solution.py:170
  127.2 12.4 %collective-permute-start.19 = (bf16[320,384]{1,0:T(8,128)(2,1)S(1)}, bf16[320,384]{1,0:T(8,128)(2,1)S(1)}, u32[]{:S(2)}, u32[]{:S(2)}) collective-permute-start(bf16[320,384]{1,0:T(8,128)(2,1)S(1)} %slice.217), channel_id=1, source_target_pairs={{0,8},{4,12},{8,0},{12,4},{16,24},{20,28},{24,16},{28,20},{1,9},{5... | collective-permute-start | bytes 737288 | tf_op jit(solution)/shard_map/ppermute | solution.py:170
  128.0 16.9 %collective-permute-start.32 = (bf16[320,384]{1,0:T(8,128)(2,1)S(1)}, bf16[320,384]{1,0:T(8,128)(2,1)S(1)}, u32[]{:S(2)}, u32[]{:S(2)}) collective-permute-start(bf16[320,384]{1,0:T(8,128)(2,1)S(1)} %slice.214), channel_id=1, source_target_pairs={{0,8},{4,12},{8,0},{12,4},{16,24},{20,28},{24,16},{28,20},{1,9},{5... | collective-permute-start | bytes 737288 | tf_op jit(solution)/shard_map/ppermute | solution.py:170
  129.7 20.0 %collective-permute-start.28 = (bf16[320,384]{1,0:T(8,128)(2,1)S(1)}, bf16[320,384]{1,0:T(8,128)(2,1)S(1)}, u32[]{:S(2)}, u32[]{:S(2)}) collective-permute-start(bf16[320,384]{1,0:T(8,128)(2,1)S(1)} %slice.215), channel_id=1, source_target_pairs={{0,8},{4,12},{8,0},{12,4},{16,24},{20,28},{24,16},{28,20},{1,9},{5... | collective-permute-start | bytes 737288 | tf_op jit(solution)/shard_map/ppermute | solution.py:170
  134.4 16.4 %collective-permute-start.25 = (bf16[160,384]{1,0:T(8,128)(2,1)S(1)}, bf16[160,384]{1,0:T(8,128)(2,1)S(1)}, u32[]{:S(2)}, u32[]{:S(2)}) collective-permute-start(bf16[160,384]{1,0:T(8,128)(2,1)S(1)} %slice.220), channel_id=1, source_target_pairs={{0,1},{1,0},{2,3},{3,2},{4,5},{5,4},{6,7},{7,6},{8,9},{9,8},{10,11... | collective-permute-start | bytes 368648 | tf_op jit(solution)/shard_map/ppermute | solution.py:173
  139.7 14.7 %collective-permute-start.20 = (bf16[160,384]{1,0:T(8,128)(2,1)S(1)}, bf16[160,384]{1,0:T(8,128)(2,1)S(1)}, u32[]{:S(2)}, u32[]{:S(2)}) collective-permute-start(bf16[160,384]{1,0:T(8,128)(2,1)S(1)} %slice.221), channel_id=1, source_target_pairs={{0,1},{1,0},{2,3},{3,2},{4,5},{5,4},{6,7},{7,6},{8,9},{9,8},{10,11... | collective-permute-start | bytes 368648 | tf_op jit(solution)/shard_map/ppermute | solution.py:173
  154.6 10.7 %collective-permute-start.34 = (bf16[80,384]{1,0:T(8,128)(2,1)S(1)}, bf16[80,384]{1,0:T(8,128)(2,1)S(1)}, u32[]{:S(2)}, u32[]{:S(2)}) collective-permute-start(bf16[80,384]{1,0:T(8,128)(2,1)S(1)} %slice.222), channel_id=1, source_target_pairs={{0,2},{1,3},{2,0},{3,1},{4,6},{5,7},{6,4},{7,5},{8,10},{9,11},{10,... | collective-permute-start | bytes 184328 | tf_op jit(solution)/shard_map/ppermute | solution.py:173
  (30 other events, 186.2 us)

commit v3 on v2

v3 whole, which is shorter than its diff:
```python
import functools

import jax
import jax.numpy as jnp
from jax import lax
from jax.experimental import pallas as pl
from jax.experimental.pallas import tpu as pltpu
from jax.sharding import PartitionSpec as P

EPS = 1e-06
LOGIT_SCALE = 0.5
LANES = 128
LOW = 64
QUAD = 4


def normalize(values, gain):
    return values * lax.rsqrt(jnp.mean(values * values, axis=-1, keepdims=True) + EPS) * gain


def after(values, *others):
    return lax.optimization_barrier((values, *others))[0]


def swap_blocks(values, index, blocks):
    size = values.shape[1] // blocks
    bit = 1
    while bit < blocks:
        swapped = jnp.concatenate(
            [values[:, (m ^ bit) * size : ((m ^ bit) + 1) * size] for m in range(blocks)], axis=1
        )
        values = jnp.where((index & bit) != 0, swapped, values)
        bit *= 2
    return values


def swap_lanes(values, index, blocks):
    width = values.shape[1]
    size = width // blocks
    lane = lax.broadcasted_iota(jnp.int32, values.shape, 1)
    bit = 1
    while bit < blocks:
        step = bit * size
        upper = (lane // step) % 2 == 1
        swapped = jnp.where(
            upper, pltpu.roll(values, step, 1), pltpu.roll(values, width - step, 1)
        )
        values = jnp.where((index & bit) != 0, swapped, values)
        bit *= 2
    return values


def front_kernel(
    rows,
    place_ref,
    att_ref,
    res_ref,
    w_ref,
    gain_ref,
    routes_ref,
    logits_ref,
    placed_ref,
    stream_ref,
    sent_ref,
    keep_ref,
):
    step = pl.program_id(0)
    cols = w_ref.shape[1]
    width = att_ref.shape[1]
    mixed = res_ref[...].astype(jnp.float32) + jnp.dot(
        att_ref[...], w_ref[...], preferred_element_type=jnp.float32
    )
    stored = mixed.astype(jnp.bfloat16)
    stream_ref[...] = stored
    keep_ref[:, pl.ds(pl.multiple_of(step * cols, cols), cols)] = stored.astype(jnp.float32)

    @pl.when(step == pl.num_programs(0) - 1)
    def _():
        normed = normalize(keep_ref[...], gain_ref[...])
        sent_ref[:, :width] = swap_lanes(normed, place_ref[4], rows).astype(jnp.bfloat16)
        scores = jnp.exp(logits_ref[...].astype(jnp.float32) * LOGIT_SCALE)
        gates = scores / jnp.sum(scores, axis=1, keepdims=True)
        routes = routes_ref[...]
        spread = jnp.zeros((gates.shape[0], LANES), jnp.float32)
        for k in range(gates.shape[1]):
            hit = routes[:, k : k + 1] == placed_ref[...]
            spread = jnp.where(hit, gates[:, k : k + 1], spread)
        high = spread.astype(jnp.bfloat16).astype(jnp.float32)
        lane = lax.broadcasted_iota(jnp.int32, spread.shape, 1)
        sent_ref[:, width:] = jnp.where(lane < LOW, high, spread - high).astype(jnp.bfloat16)


def front_call(place, rows, attended, residual, weight, gain, routes, logits, placement):
    tok, width = attended.shape
    steps = 4
    cols = width // steps
    padded = jnp.pad(placement, (0, LOW - placement.shape[0]), constant_values=-1)
    placed = jnp.concatenate([padded, padded])[None, :]
    whole = lambda shape: pl.BlockSpec(shape, lambda i, p: (0, 0))
    return pl.pallas_call(
        functools.partial(front_kernel, rows),
        grid_spec=pltpu.PrefetchScalarGridSpec(
            num_scalar_prefetch=1,
            grid=(steps,),
            in_specs=[
                whole((tok, width)),
                pl.BlockSpec((tok, cols), lambda i, p: (0, i)),
                pl.BlockSpec((width, cols), lambda i, p: (0, i)),
                whole((1, width)),
                whole(routes.shape),
                whole(logits.shape),
                whole((1, LANES)),
            ],
            out_specs=[
                pl.BlockSpec((tok, cols), lambda i, p: (0, i)),
                whole((tok, width + LANES)),
            ],
            scratch_shapes=[pltpu.VMEM((tok, width), jnp.float32)],
        ),
        out_shape=[
            jax.ShapeDtypeStruct((tok, width), jnp.bfloat16),
            jax.ShapeDtypeStruct((tok, width + LANES), jnp.bfloat16),
        ],
        compiler_params=pltpu.CompilerParams(vmem_limit_bytes=24 * 1024 * 1024),
        name="front",
    )(place, attended, residual, weight, gain[None, :], routes, logits, placed)


def cut_kernel(part, place_ref, w_ref, *out_refs):
    side, core = place_ref[0], place_ref[1]
    blocks = out_refs[0].shape[2] // part
    targets = [(core, side), (core, 1 - side), (1 - core, side), (1 - core, 1 - side)]
    for out_ref, (c, s) in zip(out_refs, targets):
        for b in range(blocks):
            at = pl.multiple_of(b * QUAD * part + (2 * c + s) * part, part)
            out_ref[:, :, b * part : (b + 1) * part] = w_ref[:, :, pl.ds(at, part)]


def cut_call(place, weight, part):
    local, depth, cols = weight.shape
    out = jax.ShapeDtypeStruct((local, depth, cols // QUAD), jnp.bfloat16)
    return pl.pallas_call(
        functools.partial(cut_kernel, part),
        grid_spec=pltpu.PrefetchScalarGridSpec(
            num_scalar_prefetch=1,
            grid=(local,),
            in_specs=[pl.BlockSpec((1, depth, cols), lambda e, p: (e, 0, 0))],
            out_specs=[pl.BlockSpec((1, depth, cols // QUAD), lambda e, p: (e, 0, 0))] * QUAD,
        ),
        out_shape=[out] * QUAD,
        name="cut",
    )(place, weight)


def up_kernel(rows, blocks, place_ref, *refs):
    parts, pieces = refs[:blocks], refs[blocks : blocks + QUAD * rows]
    out_ref, x_ref = refs[blocks + QUAD * rows :]
    side, core, zone, local = (place_ref[i] for i in range(4))
    expert = pl.program_id(0)
    width = out_ref.shape[1]

    @pl.when(expert == 0)
    def _():
        at = 0
        for part in parts:
            x_ref[at : at + part.shape[0], :] = part[...]
            at += part.shape[0]

    acc = None
    for m in range(rows):
        own, mate, own_x, mate_x = (pieces[QUAD * m + i][0] for i in range(QUAD))
        near = [jnp.where(core == 0, own, mate), jnp.where(core == 0, mate, own)]
        far = [jnp.where(core == 0, own_x, mate_x), jnp.where(core == 0, mate_x, own_x)]
        order = [jnp.where(side == 0, a, b) for a, b in zip(near + far, far + near)]
        w = jnp.concatenate(order, axis=0)
        depth = w.shape[0]
        part = jnp.dot(
            x_ref[:, m * depth : (m + 1) * depth], w, preferred_element_type=jnp.float32
        )
        acc = part if acc is None else acc + part
    feats = x_ref.shape[1] - LANES
    lane = lax.broadcasted_iota(jnp.int32, (LANES, width), 0)
    slot = zone * local + expert
    pick = jnp.where((lane == slot) | (lane == slot + LOW), 1.0, 0.0).astype(jnp.bfloat16)
    gate = jnp.dot(x_ref[:, feats:], pick, preferred_element_type=jnp.float32)
    g, u = acc[:, :width], acc[:, width:]
    out_ref[...] = (g / (1.0 + jnp.exp(-g)) * u * gate).astype(jnp.bfloat16)


def up_call(place, parts, pieces):
    rows = len(pieces) // QUAD
    local, depth, cols = pieces[0].shape
    tokens, lanes = sum(v.shape[0] for v in parts), parts[0].shape[1]
    piece = pl.BlockSpec((1, depth, cols), lambda e, p: (e, 0, 0))
    return pl.pallas_call(
        functools.partial(up_kernel, rows, len(parts)),
        grid_spec=pltpu.PrefetchScalarGridSpec(
            num_scalar_prefetch=1,
            grid=(local,),
            in_specs=[pl.BlockSpec(v.shape, lambda e, p: (0, 0)) for v in parts]
            + [piece] * len(pieces),
            out_specs=pl.BlockSpec((tokens, cols // 2), lambda e, p: (0, e)),
            scratch_shapes=[pltpu.VMEM((tokens, lanes), jnp.bfloat16)],
        ),
        out_shape=jax.ShapeDtypeStruct((tokens, local * cols // 2), jnp.bfloat16),
        compiler_params=pltpu.CompilerParams(vmem_limit_bytes=48 * 1024 * 1024),
        cost_estimate=pl.CostEstimate(
            flops=2 * tokens * lanes * local * cols,
            bytes_accessed=2 * (tokens * lanes + local * lanes * cols),
            transcendentals=tokens * local * cols // 2,
        ),
        name="up",
    )(place, *parts, *pieces)


def down_kernel(place_ref, h_ref, near_ref, far_ref, send_ref, keep_ref):
    side = place_ref[0]
    feats = near_ref.shape[1]
    parts = []
    for e in range(near_ref.shape[0]):
        near, far = near_ref[e], far_ref[e]
        parts.append([jnp.where(side == 0, near, far), jnp.where(side == 0, far, near)])

    def times(j):
        w = jnp.concatenate([p[j] for p in parts], axis=1)
        return lax.dot_general(
            h_ref[...], w, (((1,), (1,)), ((), ())), preferred_element_type=jnp.float32
        )

    @pl.when(pl.program_id(0) == 0)
    def _():
        for j in range(2):
            send_ref[:, j * feats : (j + 1) * feats] = times(j).astype(send_ref.dtype)

    @pl.when(pl.program_id(0) == 1)
    def _():
        for j in range(2):
            keep_ref[:, j * feats : (j + 1) * feats] = times(j)


def down_call(place, hidden, near, far):
    tokens, depth = hidden.shape
    local, feats, part = near.shape
    half = tokens // 2
    whole = pl.BlockSpec((local, feats, part), lambda i, p: (0, 0, 0))
    out = pl.BlockSpec((half, 2 * feats), lambda i, p: (0, 0))
    return pl.pallas_call(
        down_kernel,
        grid_spec=pltpu.PrefetchScalarGridSpec(
            num_scalar_prefetch=1,
            grid=(2,),
            in_specs=[pl.BlockSpec((half, depth), lambda i, p: (1 - i, 0)), whole, whole],
            out_specs=[out, out],
        ),
        out_shape=[
            jax.ShapeDtypeStruct((half, 2 * feats), jnp.bfloat16),
            jax.ShapeDtypeStruct((half, 2 * feats), jnp.float32),
        ],
        compiler_params=pltpu.CompilerParams(vmem_limit_bytes=40 * 1024 * 1024),
        cost_estimate=pl.CostEstimate(
            flops=4 * tokens * depth * feats,
            bytes_accessed=2 * (tokens * depth + 2 * depth * feats + 3 * tokens * feats),
            transcendentals=0,
        ),
        name="down",
    )(place, hidden, near, far)


def body(
    attended,
    residual,
    out_weight,
    norm_gain,
    final_gain,
    routes,
    gate_logits,
    placement,
    gate_up,
    down_weight,
):
    ranks = lax.axis_size("dp")
    zones = lax.axis_size("expert")
    rows = ranks // QUAD
    me = lax.axis_index("dp")
    zone = lax.axis_index("expert")
    core, side, row = me % 2, (me // 2) % 2, me // QUAD
    tok, width = attended.shape
    local, depth, _ = gate_up.shape
    hid = down_weight.shape[2]
    part = hid // QUAD

    def flip(values, bit):
        return lax.ppermute(values, "dp", [(i, i ^ bit) for i in range(ranks)])

    def hop(values, bit):
        return lax.ppermute(values, "expert", [(i, i ^ bit) for i in range(zones)])

    def widen(pieces):
        bit = 1
        while bit < rows:
            pieces = pieces + [flip(p, bit * QUAD) for p in pieces]
            bit *= 2
        return pieces

    zone_bits = []
    while 1 << len(zone_bits) < zones:
        zone_bits.insert(0, 1 << len(zone_bits))

    place = jnp.stack([side, core, zone, jnp.int32(local), row]).astype(jnp.int32)

    gu_own, gu_away, gu_to_mate, gu_to_mate_away = cut_call(place, gate_up, part)
    stored, sent = front_call(
        place, rows, after(attended, gu_own), residual, out_weight, norm_gain, routes, gate_logits, placement
    )
    stream_in = stored.astype(jnp.float32)
    gu_own_x = flip(gu_away, 2)
    first = widen([gu_own])
    gu_mate, gu_mate_away = flip(gu_to_mate, 1), flip(gu_to_mate_away, 1)
    gu_mate_x = flip(after(gu_mate_away, gu_own_x, first[-1]), 2)
    second = widen([after(gu_mate, first[-1], sent)])
    third = widen([after(gu_own_x, second[-1])])
    fourth = widen([after(gu_mate_x, third[-1])])
    pieces = [p for group in zip(first, second, third, fourth) for p in group]

    near = sent
    for bit in zone_bits[:-1]:
        near = jnp.concatenate([near, hop(near, bit)], axis=0)
    far = hop(near, zone_bits[-1])
    near_x = flip(after(near, gu_mate_x, second[-1]), 2)
    far_x = flip(after(far, near_x, third[-1]), 2)
    chip = [near, after(far, fourth[-1]), near_x, after(far_x, fourth[-1])]
    parts = chip + [flip(v, 1) for v in chip]

    dn_own, dn_away, dn_to_mate, dn_to_mate_away = cut_call(place, down_weight, part)
    dn_mate, dn_mate_away = flip(dn_to_mate, 1), flip(dn_to_mate_away, 1)

    def pair(own, mate):
        return jnp.where(
            core == 0,
            jnp.concatenate([own, mate], axis=1),
            jnp.concatenate([mate, own], axis=1),
        )

    dn_near = pair(dn_own, dn_mate)
    dn_far = flip(after(pair(dn_away, dn_mate_away), far_x), 2)
    dn_nears = widen([after(dn_near, fourth[-1])])
    hidden = after(up_call(place, parts, pieces), dn_nears[-1])
    dn_fars = widen([after(dn_far, dn_nears[-1], hidden)])

    count = zones * tok
    sums = []
    for m in range(rows):
        ready = after(hidden, *(v[1] for v in sums[-2:-1]))
        send, keep = down_call(place, ready, dn_nears[m], dn_fars[m])
        back = flip(send, 1)
        feats = send.shape[1] // 2
        for j in range(2):
            cols = slice(j * feats, (j + 1) * feats)
            total = keep[:, cols] + back[:, cols].astype(jnp.float32)
            away = total[count:].astype(jnp.bfloat16)
            crossed = flip(after(away, *(v[1] for v in sums[-2:-1])), 2)
            sums.append((total[:count], crossed))
    merged = [
        (jnp.concatenate([a[0], b[0]], axis=1), jnp.concatenate([a[1], b[1]], axis=1))
        for a, b in zip(sums[:-2:2], sums[1:-2:2])
    ]
    chunks = []
    for i, (total, crossed) in enumerate(merged + sums[-2:]):
        total = total + crossed.astype(jnp.float32)
        for bit in reversed(zone_bits):
            size = total.shape[0] // 2
            away = total[size:].astype(jnp.bfloat16)
            if i < len(merged) and bit == zone_bits[0]:
                away = after(away, sums[-2][1])
            total = total[:size] + hop(away, bit).astype(jnp.float32)
        chunks.append(total)
    branch = swap_blocks(jnp.concatenate(chunks, axis=1), row, rows)
    total = stream_in + branch
    return (total.astype(jnp.bfloat16), normalize(total, final_gain).astype(jnp.bfloat16))


def solution(mesh):
    tokens = P(("dp", "expert"), None)
    weights = P("expert", "dp", None)
    return jax.shard_map(
        body,
        mesh=mesh,
        in_specs=(tokens, tokens, P(), P(), P(), tokens, tokens, P(), weights, weights),
        out_specs=(tokens, tokens),
        check_vma=False,
    )
```

time: 167 us -> 141 us (0.84)
  waiting for transfers between devices: 91.7 us -> 62.7 us
  Pallas kernels: 15.3 us -> 29 us
  starting transfers between devices: 35.9 us -> 31 us
  matrix products: 3.28 us -> 0 us
  local copies, waits for them, and re-layouts: 12.1 us -> 9.32 us
    ppermute x25, waiting for transfers between devices: 73.8 us -> 35.4 us  [flip(): return lax.ppermute(values, 'dp', [(i, i ^ bit) for i in range(ranks)])]
    pallas_call x4 -> x5, Pallas kernels: 5.22 us -> 19 us  [the longest x2 9.86 us: cut_call(): pl.pallas_call(functools.partial(cut_kernel, part), grid_spec=pltpu.Prefe...]
    ppermute x10 -> x8, waiting for transfers between devices: 17.9 us -> 27.3 us  [hop(): return lax.ppermute(values, 'expert', [(i, i ^ bit) for i in range(zones)])]
    ppermute x10 -> x8, starting transfers between devices: 16.9 us -> 10.5 us  [hop(): return lax.ppermute(values, 'expert', [(i, i ^ bit) for i in range(zones)])]
    dynamic_slice x4 -> x0, local copies, waits for them, and re-layouts: 6.21 us -> none  [the longest x2 3.57 us: quarter(): lax.dynamic_slice_in_dim(values, b * hid + (2 * c + s) * part, part, axis=2)]
    dot_general x1 -> x0, matrix products: 3.28 us -> none  [body(): jnp.dot(attended, out_weight, preferred_element_type=jnp.float32)]
    concatenate x4 -> x0, other arithmetic: 3.16 us -> none  [the longest x2 1.94 us: from_mate(): jnp.concatenate([quarter(values, 1 - core, s) for s in range(2)], axis=2)]
    select_n x1 -> x2, other arithmetic: 0.13 us -> 3.01 us  [pair(): jnp.where(core == 0, jnp.concatenate([own, mate], axis=1), jnp.concatenat...]
  transfers between devices with their start and end apart: 35 -> 33, of which waited for: 16 -> 23; matrix products, arithmetic and copies ran while one was open for 7% -> 7% of each run, Pallas kernels for 9% -> 12%
where the time goes in v3:
time: 141 us; the launch traced here: 140 us
  waiting for transfers between devices  62.7 us (44%)
  starting transfers between devices  31 us (22%)
  Pallas kernels  29 us (21%)
  local copies, waits for them, and re-layouts  9.32 us (7%)
  other arithmetic  7.05 us (5%)
    ppermute x25, waiting for transfers between devices, flip(): return lax.ppermute(values, 'dp', [(i, i ^ bit) for i in range(ranks)])  35.4 us
    ppermute x8, waiting for transfers between devices, hop(): return lax.ppermute(values, 'expert', [(i, i ^ bit) for i in range(zones)])  27.3 us
    ppermute x25, starting transfers between devices, flip(): return lax.ppermute(values, 'dp', [(i, i ^ bit) for i in range(ranks)])  20.5 us
    ppermute x8, starting transfers between devices, hop(): return lax.ppermute(values, 'expert', [(i, i ^ bit) for i in range(zones)])  10.5 us
    pallas_call x1, Pallas kernels, up_call(): pl.pallas_call(functools.partial(up_kernel, rows, len(parts)), grid_spec=...  10 us
    pallas_call x2, Pallas kernels, cut_call(): pl.pallas_call(functools.partial(cut_kernel, part), grid_spec=pltpu.Prefe...  9.86 us
    pallas_call x2, Pallas kernels, down_call(): pl.pallas_call(down_kernel, grid_spec=pltpu.PrefetchScalarGridSpec(num_sc...  6.27 us
    unnamed x47, local copies, waits for them, and re-layouts  5.61 us
  transfers between devices with their start and end apart: 33, of which 23 were waited for; matrix products, arithmetic and copies ran while one was open for 7% of the time, Pallas kernels for 12%

profile of v3, /device:TPU:0, one launch (start us, length us, event | category | flops | bytes accessed | tf_op | source)
XLA Modules:
  0.0 140.2 jit_solution(841732800021320490)
XLA Ops:
  1.4 5.4 %cut.2 = (bf16[5,192,256]{2,1,0:T(8,128)(2,1)}, bf16[5,192,256]{2,1,0:T(8,128)(2,1)}, bf16[5,192,256]{2,1,0:T(8,128)(2,1)}, bf16[5,192,256]{2,1,0:T(8,128)(2,1)}) custom-call(s32[5]{0:T(128)} %stack.19.place_ref, bf16[5,192,1024]{2,1,0:T(8,128)(2,1)} %w_ref.3), custom_call_target="tpu_custom_call" | custom-call | tf_op jit(solution)/shard_map/cut/pallas_call | solution.py:142
  6.7 3.0 %collective-permute-start.4 = (bf16[5,192,256]{2,1,0:T(8,128)(2,1)}, bf16[5,192,256]{2,1,0:T(8,128)(2,1)S(1)}, u32[]{:S(2)}, u32[]{:S(2)}) collective-permute-start(bf16[5,192,256]{2,1,0:T(8,128)(2,1)} %get-tuple-element.33.refs_8_), channel_id=1, source_target_pairs={{0,16},{4,20},{8,24},{12,28},{16,0},{20,4},{24,8},{28,12},{1,17},{... | collective-permute-start | bytes 1474568 | tf_op jit(solution)/shard_map/ppermute | solution.py:293
  12.0 2.3 %copy-done = bf16[1536,1536]{1,0:T(8,128)(2,1)S(1)} copy-done((bf16[1536,1536]{1,0:T(8,128)(2,1)S(1)}, bf16[1536,1536]{1,0:T(8,128)(2,1)}, u32[]{:S(2)}) %copy-start) | copy-done | bytes 4718616
  14.3 2.9 %front.1 = (bf16[80,1536]{1,0:T(8,128)(2,1)S(1)}, bf16[80,1664]{1,0:T(8,128)(2,1)S(1)}) custom-call(s32[5]{0:T(128)S(1)} %copy-done.3, bf16[80,1536]{1,0:T(8,128)(2,1)S(1)} %copy-done.1, bf16[80,1536]{1,0:T(8,128)(2,1)S(1)} %copy-done.2, bf16[1536,1536]{1,0:T(8,128)(2,1)S(1)} %copy-done, f32[1,1536]{1,0:T(1,128)S(1)} %broadcast_in_dim.8.gain_ref, ...), custom_call_target="tpu_custom_call" | custom-call | tf_op jit(solution)/shard_map/front/pallas_call | solution.py:100
  17.3 2.7 %collective-permute-start = (bf16[80,1664]{1,0:T(8,128)(2,1)S(1)}, bf16[80,1664]{1,0:T(8,128)(2,1)S(1)}, u32[]{:S(2)}, u32[]{:S(2)}) collective-permute-start(bf16[80,1664]{1,0:T(8,128)(2,1)S(1)} %get-tuple-element.36), channel_id=1, source_target_pairs={{0,2},{1,3},{2,0},{3,1},{4,6},{5,7},{6,4},{7,5},{8,10},{9,11},{10,... | collective-permute-start | bytes 798728 | tf_op jit(solution)/shard_map/ppermute | solution.py:296
  21.1 1.8 %collective-permute-start.7 = (bf16[5,192,256]{2,1,0:T(8,128)(2,1)S(1)}, bf16[5,192,256]{2,1,0:T(8,128)(2,1)S(1)}, u32[]{:S(2)}, u32[]{:S(2)}) collective-permute-start(bf16[5,192,256]{2,1,0:T(8,128)(2,1)S(1)} %collective-permute-done.6.refs_9_), channel_id=1, source_target_pairs={{0,16},{4,20},{8,24},{12,28},{16,0},{20,4},{24,8},{28,12},{1,17},{... | collective-permute-start | bytes 1474568 | tf_op jit(solution)/shard_map/ppermute | solution.py:293
  25.1 6.9 %collective-permute-done = bf16[80,1664]{1,0:T(8,128)(2,1)S(1)} collective-permute-done((bf16[80,1664]{1,0:T(8,128)(2,1)S(1)}, bf16[80,1664]{1,0:T(8,128)(2,1)S(1)}, u32[]{:S(2)}, u32[]{:S(2)}) %collective-permute-start) | collective-permute-done | bytes 266272 | tf_op jit(solution)/shard_map/ppermute | solution.py:296
  34.4 1.7 %collective-permute-done.5.refs_11_ = bf16[5,192,256]{2,1,0:T(8,128)(2,1)} collective-permute-done((bf16[5,192,256]{2,1,0:T(8,128)(2,1)}, bf16[5,192,256]{2,1,0:T(8,128)(2,1)}, u32[]{:S(2)}, u32[]{:S(2)}) %collective-permute-start.5) | collective-permute-done | bytes 491552 | tf_op jit(solution)/shard_map/ppermute | solution.py:293
  38.1 6.9 %collective-permute-done.1.refs_1_ = bf16[160,1664]{1,0:T(8,128)(2,1)S(1)} collective-permute-done((bf16[160,1664]{1,0:T(8,128)(2,1)S(1)}, bf16[160,1664]{1,0:T(8,128)(2,1)S(1)}, u32[]{:S(2)}, u32[]{:S(2)}) %collective-permute-start.1) | collective-permute-done | bytes 532512 | tf_op jit(solution)/shard_map/ppermute | solution.py:296
  45.1 3.7 %collective-permute-done.8.refs_14_ = bf16[5,192,256]{2,1,0:T(8,128)(2,1)S(1)} collective-permute-done((bf16[5,192,256]{2,1,0:T(8,128)(2,1)S(1)}, bf16[5,192,256]{2,1,0:T(8,128)(2,1)S(1)}, u32[]{:S(2)}, u32[]{:S(2)}) %collective-permute-start.8) | collective-permute-done | bytes 491552 | tf_op jit(solution)/shard_map/ppermute | solution.py:293
  50.8 4.5 %cut.3 = (bf16[5,192,128]{2,1,0:T(8,128)(2,1)}, bf16[5,192,128]{2,1,0:T(8,128)(2,1)}, bf16[5,192,128]{2,1,0:T(8,128)(2,1)}, bf16[5,192,128]{2,1,0:T(8,128)(2,1)}) custom-call(s32[5]{0:T(128)} %stack.19.place_ref, bf16[5,192,512]{2,1,0:T(8,128)(2,1)} %w_ref.5), custom_call_target="tpu_custom_call" | custom-call | tf_op jit(solution)/shard_map/cut/pallas_call | solution.py:142
  55.9 4.5 %collective-permute-done.9.refs_15_ = bf16[5,192,256]{2,1,0:T(8,128)(2,1)} collective-permute-done((bf16[5,192,256]{2,1,0:T(8,128)(2,1)}, bf16[5,192,256]{2,1,0:T(8,128)(2,1)}, u32[]{:S(2)}, u32[]{:S(2)}) %collective-permute-start.9) | collective-permute-done | bytes 491552 | tf_op jit(solution)/shard_map/ppermute | solution.py:293
  66.8 10.0 %up.1.h_ref = bf16[1280,640]{1,0:T(8,128)(2,1)} custom-call(s32[5]{0:T(128)S(1)} %copy-done.4, bf16[160,1664]{1,0:T(8,128)(2,1)S(1)} %constant_dynamic-update-slice_fusion.refs_0_, bf16[160,1664]{1,0:T(8,128)(2,1)S(1)} %collective-permute-done.1.refs_1_, bf16[160,1664]{1,0:T(8,128)(2,1)S(1)} %collective-permute-done.10.refs_2_, ...), custom_call_target="tpu_custom_call" | custom-call | flops 5452595200 | bytes 8519680 | tf_op jit(solution)/shard_map/up/pallas_call | solution.py:195
  80.1 3.1 %down.2 = (bf16[640,768]{1,0:T(8,128)(2,1)S(1)}, f32[640,768]{1,0:T(8,128)S(1)}) custom-call(s32[5]{0:T(128)S(1)} %copy-done.4, bf16[1280,640]{1,0:T(8,128)(2,1)S(1)} %copy-done.14, bf16[5,384,128]{2,1,0:T(8,128)(2,1)S(1)} %maximum_select_fusion.near_ref, bf16[5,384,128]{2,1,0:T(8,128)(2,1)S(1)} %collective-permute-done.19.far_ref), custom_call_target="tpu_custom_call" | custom-call | flops 1258291200 | bytes 5570560 | tf_op jit(solution)/shard_map/down/pallas_call | solution.py:247
  87.2 7.0 %collective-permute-done.21 = bf16[320,384]{1,0:T(8,128)(2,1)S(1)} collective-permute-done((bf16[320,384]{1,0:T(8,128)(2,1)S(1)}, bf16[320,384]{1,0:T(8,128)(2,1)S(1)}, u32[]{:S(2)}, u32[]{:S(2)}) %collective-permute-start.21) | collective-permute-done | bytes 245792 | tf_op jit(solution)/shard_map/ppermute | solution.py:293
  94.2 2.8 %collective-permute-done.22.far_ref = bf16[5,384,128]{2,1,0:T(8,128)(2,1)S(1)} collective-permute-done((bf16[5,384,128]{2,1,0:T(8,128)(2,1)S(1)}, bf16[5,384,128]{2,1,0:T(8,128)(2,1)S(1)}, u32[]{:S(2)}, u32[]{:S(2)}) %collective-permute-start.22) | collective-permute-done | bytes 491552 | tf_op jit(solution)/shard_map/ppermute | solution.py:293
  97.0 3.1 %down.3 = (bf16[640,768]{1,0:T(8,128)(2,1)S(1)}, f32[640,768]{1,0:T(8,128)S(1)}) custom-call(s32[5]{0:T(128)S(1)} %copy-done.4, bf16[1280,640]{1,0:T(8,128)(2,1)S(1)} %copy-done.14, bf16[5,384,128]{2,1,0:T(8,128)(2,1)S(1)} %collective-permute-done.17.near_ref, bf16[5,384,128]{2,1,0:T(8,128)(2,1)S(1)} %collective-permute-done.22.far_ref), custom_call_target="tpu_custom_call" | custom-call | flops 1258291200 | bytes 5570560 | tf_op jit(solution)/shard_map/down/pallas_call | solution.py:247
  104.1 5.5 %collective-permute-done.27 = bf16[320,384]{1,0:T(8,128)(2,1)} collective-permute-done((bf16[320,384]{1,0:T(8,128)(2,1)}, bf16[320,384]{1,0:T(8,128)(2,1)}, u32[]{:S(2)}, u32[]{:S(2)}) %collective-permute-start.27) | collective-permute-done | bytes 245792 | tf_op jit(solution)/shard_map/ppermute | solution.py:293
  114.9 3.5 %collective-permute-done.31 = bf16[160,768]{1,0:T(8,128)(2,1)S(1)} collective-permute-done((bf16[160,768]{1,0:T(8,128)(2,1)S(1)}, bf16[160,768]{1,0:T(8,128)(2,1)S(1)}, u32[]{:S(2)}, u32[]{:S(2)}) %collective-permute-start.31) | collective-permute-done | bytes 245792 | tf_op jit(solution)/shard_map/ppermute | solution.py:296
  119.5 2.1 %collective-permute-done.24 = bf16[320,384]{1,0:T(8,128)(2,1)S(1)} collective-permute-done((bf16[320,384]{1,0:T(8,128)(2,1)S(1)}, bf16[320,384]{1,0:T(8,128)(2,1)S(1)}, u32[]{:S(2)}, u32[]{:S(2)}) %collective-permute-start.24) | collective-permute-done | bytes 245792 | tf_op jit(solution)/shard_map/ppermute | solution.py:293
  121.6 3.0 %collective-permute-start.32 = (bf16[80,768]{1,0:T(8,128)(2,1)S(1)}, bf16[80,768]{1,0:T(8,128)(2,1)S(1)}, u32[]{:S(2)}, u32[]{:S(2)}) collective-permute-start(bf16[80,768]{1,0:T(8,128)(2,1)S(1)} %slice.179), channel_id=1, source_target_pairs={{0,2},{1,3},{2,0},{3,1},{4,6},{5,7},{6,4},{7,5},{8,10},{9,11},{10,... | collective-permute-start | bytes 368648 | tf_op jit(solution)/shard_map/ppermute | solution.py:296
  127.0 4.8 %collective-permute-done.25 = bf16[160,384]{1,0:T(8,128)(2,1)S(1)} collective-permute-done((bf16[160,384]{1,0:T(8,128)(2,1)S(1)}, bf16[160,384]{1,0:T(8,128)(2,1)S(1)}, u32[]{:S(2)}, u32[]{:S(2)}) %collective-permute-start.25) | collective-permute-done | bytes 122912 | tf_op jit(solution)/shard_map/ppermute | solution.py:296
  133.2 1.8 %collective-permute-start.30 = (bf16[80,384]{1,0:T(8,128)(2,1)S(1)}, bf16[80,384]{1,0:T(8,128)(2,1)S(1)}, u32[]{:S(2)}, u32[]{:S(2)}) collective-permute-start(bf16[80,384]{1,0:T(8,128)(2,1)S(1)} %slice.182), channel_id=1, source_target_pairs={{0,2},{1,3},{2,0},{3,1},{4,6},{5,7},{6,4},{7,5},{8,10},{9,11},{10,... | collective-permute-start | bytes 184328 | tf_op jit(solution)/shard_map/ppermute | solution.py:296
  135.1 2.7 %collective-permute-done.26 = bf16[80,384]{1,0:T(8,128)(2,1)S(1)} collective-permute-done((bf16[80,384]{1,0:T(8,128)(2,1)S(1)}, bf16[80,384]{1,0:T(8,128)(2,1)S(1)}, u32[]{:S(2)}, u32[]{:S(2)}) %collective-permute-start.26) | collective-permute-done | bytes 61472 | tf_op jit(solution)/shard_map/ppermute | solution.py:296
  (128 shorter events, 43.4 us)
Async XLA Ops:
  6.7 14.4 %collective-permute-start.4 = (bf16[5,192,256]{2,1,0:T(8,128)(2,1)}, bf16[5,192,256]{2,1,0:T(8,128)(2,1)S(1)}, u32[]{:S(2)}, u32[]{:S(2)}) collective-permute-start(bf16[5,192,256]{2,1,0:T(8,128)(2,1)} %get-tuple-element.33.refs_8_), channel_id=1, source_target_pairs={{0,16},{4,20},{8,24},{12,28},{16,0},{20,4},{24,8},{28,12},{1,17},{... | collective-permute-start | bytes 1474568 | tf_op jit(solution)/shard_map/ppermute | solution.py:293
  9.7 11.4 %collective-permute-start.6 = (bf16[5,192,256]{2,1,0:T(8,128)(2,1)}, bf16[5,192,256]{2,1,0:T(8,128)(2,1)S(1)}, u32[]{:S(2)}, u32[]{:S(2)}) collective-permute-start(bf16[5,192,256]{2,1,0:T(8,128)(2,1)} %get-tuple-element.40), channel_id=1, source_target_pairs={{0,4},{4,0},{8,12},{12,8},{16,20},{20,16},{24,28},{28,24},{1,5},{5... | collective-permute-start | bytes 1474568 | tf_op jit(solution)/shard_map/ppermute | solution.py:293
  9.7 13.2 %collective-permute-start.2 = (bf16[5,192,256]{2,1,0:T(8,128)(2,1)}, bf16[5,192,256]{2,1,0:T(8,128)(2,1)}, u32[]{:S(2)}, u32[]{:S(2)}) collective-permute-start(bf16[5,192,256]{2,1,0:T(8,128)(2,1)} %get-tuple-element.37), channel_id=1, source_target_pairs={{0,4},{4,0},{8,12},{12,8},{16,20},{20,16},{24,28},{28,24},{1,5},{5... | collective-permute-start | bytes 1474568 | tf_op jit(solution)/shard_map/ppermute | solution.py:293
  10.2 13.3 %collective-permute-start.3 = (bf16[5,192,256]{2,1,0:T(8,128)(2,1)}, bf16[5,192,256]{2,1,0:T(8,128)(2,1)S(1)}, u32[]{:S(2)}, u32[]{:S(2)}) collective-permute-start(bf16[5,192,256]{2,1,0:T(8,128)(2,1)} %get-tuple-element.38), channel_id=1, source_target_pairs={{0,8},{4,12},{8,0},{12,4},{16,24},{20,28},{24,16},{28,20},{1,9},{5... | collective-permute-start | bytes 1474568 | tf_op jit(solution)/shard_map/ppermute | solution.py:293
  17.3 14.7 %collective-permute-start = (bf16[80,1664]{1,0:T(8,128)(2,1)S(1)}, bf16[80,1664]{1,0:T(8,128)(2,1)S(1)}, u32[]{:S(2)}, u32[]{:S(2)}) collective-permute-start(bf16[80,1664]{1,0:T(8,128)(2,1)S(1)} %get-tuple-element.36), channel_id=1, source_target_pairs={{0,2},{1,3},{2,0},{3,1},{4,6},{5,7},{6,4},{7,5},{8,10},{9,11},{10,... | collective-permute-start | bytes 798728 | tf_op jit(solution)/shard_map/ppermute | solution.py:296
  21.1 12.5 %collective-permute-start.7 = (bf16[5,192,256]{2,1,0:T(8,128)(2,1)S(1)}, bf16[5,192,256]{2,1,0:T(8,128)(2,1)S(1)}, u32[]{:S(2)}, u32[]{:S(2)}) collective-permute-start(bf16[5,192,256]{2,1,0:T(8,128)(2,1)S(1)} %collective-permute-done.6.refs_9_), channel_id=1, source_target_pairs={{0,16},{4,20},{8,24},{12,28},{16,0},{20,4},{24,8},{28,12},{1,17},{... | collective-permute-start | bytes 1474568 | tf_op jit(solution)/shard_map/ppermute | solution.py:293
  23.5 12.6 %collective-permute-start.5 = (bf16[5,192,256]{2,1,0:T(8,128)(2,1)}, bf16[5,192,256]{2,1,0:T(8,128)(2,1)}, u32[]{:S(2)}, u32[]{:S(2)}) collective-permute-start(bf16[5,192,256]{2,1,0:T(8,128)(2,1)} %collective-permute-done.2), channel_id=1, source_target_pairs={{0,8},{4,12},{8,0},{12,4},{16,24},{20,28},{24,16},{28,20},{1,9},{5... | collective-permute-start | bytes 1474568 | tf_op jit(solution)/shard_map/ppermute | solution.py:293
  32.0 13.0 %collective-permute-start.1 = (bf16[160,1664]{1,0:T(8,128)(2,1)S(1)}, bf16[160,1664]{1,0:T(8,128)(2,1)S(1)}, u32[]{:S(2)}, u32[]{:S(2)}) collective-permute-start(bf16[160,1664]{1,0:T(8,128)(2,1)S(1)} %constant_dynamic-update-slice_fusion.refs_0_), channel_id=1, source_target_pairs={{0,1},{1,0},{2,3},{3,2},{4,5},{5,4},{6,7},{7,6},{8,9},{9,8},{10,11... | collective-permute-start | bytes 1597448 | tf_op jit(solution)/shard_map/ppermute | solution.py:296
  36.1 13.4 %collective-permute-start.10 = (bf16[160,1664]{1,0:T(8,128)(2,1)S(1)}, bf16[160,1664]{1,0:T(8,128)(2,1)S(1)}, u32[]{:S(2)}, u32[]{:S(2)}) collective-permute-start(bf16[160,1664]{1,0:T(8,128)(2,1)S(1)} %constant_dynamic-update-slice_fusion.refs_0_), channel_id=1, source_target_pairs={{0,8},{4,12},{8,0},{12,4},{16,24},{20,28},{24,16},{28,20},{1,9},{5... | collective-permute-start | bytes 1597448 | tf_op jit(solution)/shard_map/ppermute | solution.py:293
  37.6 11.1 %collective-permute-start.8 = (bf16[5,192,256]{2,1,0:T(8,128)(2,1)S(1)}, bf16[5,192,256]{2,1,0:T(8,128)(2,1)S(1)}, u32[]{:S(2)}, u32[]{:S(2)}) collective-permute-start(bf16[5,192,256]{2,1,0:T(8,128)(2,1)S(1)} %collective-permute-done.3.refs_10_), channel_id=1, source_target_pairs={{0,16},{4,20},{8,24},{12,28},{16,0},{20,4},{24,8},{28,12},{1,17},{... | collective-permute-start | bytes 1474568 | tf_op jit(solution)/shard_map/ppermute | solution.py:293
  49.5 11.0 %collective-permute-start.11 = (bf16[160,1664]{1,0:T(8,128)(2,1)S(1)}, bf16[160,1664]{1,0:T(8,128)(2,1)S(1)}, u32[]{:S(2)}, u32[]{:S(2)}) collective-permute-start(bf16[160,1664]{1,0:T(8,128)(2,1)S(1)} %collective-permute-done.1.refs_1_), channel_id=1, source_target_pairs={{0,8},{4,12},{8,0},{12,4},{16,24},{20,28},{24,16},{28,20},{1,9},{5... | collective-permute-start | bytes 1597448 | tf_op jit(solution)/shard_map/ppermute | solution.py:293
  50.0 10.3 %collective-permute-start.9 = (bf16[5,192,256]{2,1,0:T(8,128)(2,1)}, bf16[5,192,256]{2,1,0:T(8,128)(2,1)}, u32[]{:S(2)}, u32[]{:S(2)}) collective-permute-start(bf16[5,192,256]{2,1,0:T(8,128)(2,1)} %collective-permute-done.5.refs_11_), channel_id=1, source_target_pairs={{0,16},{4,20},{8,24},{12,28},{16,0},{20,4},{24,8},{28,12},{1,17},{... | collective-permute-start | bytes 1474568 | tf_op jit(solution)/shard_map/ppermute | solution.py:293
  55.3 10.4 %collective-permute-start.12 = (bf16[160,1664]{1,0:T(8,128)(2,1)S(1)}, bf16[160,1664]{1,0:T(8,128)(2,1)}, u32[]{:S(2)}, u32[]{:S(2)}) collective-permute-start(bf16[160,1664]{1,0:T(8,128)(2,1)S(1)} %constant_dynamic-update-slice_fusion.refs_0_), channel_id=1, source_target_pairs={{0,4},{4,0},{8,12},{12,8},{16,20},{20,16},{24,28},{28,24},{1,5},{5... | collective-permute-start | bytes 1597448 | tf_op jit(solution)/shard_map/ppermute | solution.py:293
  55.8 10.9 %collective-permute-start.14 = (bf16[160,1664]{1,0:T(8,128)(2,1)S(1)}, bf16[160,1664]{1,0:T(8,128)(2,1)}, u32[]{:S(2)}, u32[]{:S(2)}) collective-permute-start(bf16[160,1664]{1,0:T(8,128)(2,1)S(1)} %collective-permute-done.10.refs_2_), channel_id=1, source_target_pairs={{0,4},{4,0},{8,12},{12,8},{16,20},{20,16},{24,28},{28,24},{1,5},{5... | collective-permute-start | bytes 1597448 | tf_op jit(solution)/shard_map/ppermute | solution.py:293
  64.7 13.3 %collective-permute-start.17 = (bf16[5,384,128]{2,1,0:T(8,128)(2,1)S(1)}, bf16[5,384,128]{2,1,0:T(8,128)(2,1)S(1)}, u32[]{:S(2)}, u32[]{:S(2)}) collective-permute-start(bf16[5,384,128]{2,1,0:T(8,128)(2,1)S(1)} %maximum_select_fusion.near_ref), channel_id=1, source_target_pairs={{0,16},{4,20},{8,24},{12,28},{16,0},{20,4},{24,8},{28,12},{1,17},{... | collective-permute-start | bytes 1474568 | tf_op jit(solution)/shard_map/ppermute | solution.py:293
  65.7 13.0 %collective-permute-start.19 = (bf16[5,384,128]{2,1,0:T(8,128)(2,1)S(1)}, bf16[5,384,128]{2,1,0:T(8,128)(2,1)S(1)}, u32[]{:S(2)}, u32[]{:S(2)}) collective-permute-start(bf16[5,384,128]{2,1,0:T(8,128)(2,1)S(1)} %maximum_select_fusion.1), channel_id=1, source_target_pairs={{0,8},{4,12},{8,0},{12,4},{16,24},{20,28},{24,16},{28,20},{1,9},{5... | collective-permute-start | bytes 1474568 | tf_op jit(solution)/shard_map/ppermute | solution.py:293
  83.3 13.6 %collective-permute-start.22 = (bf16[5,384,128]{2,1,0:T(8,128)(2,1)S(1)}, bf16[5,384,128]{2,1,0:T(8,128)(2,1)S(1)}, u32[]{:S(2)}, u32[]{:S(2)}) collective-permute-start(bf16[5,384,128]{2,1,0:T(8,128)(2,1)S(1)} %collective-permute-done.19.far_ref), channel_id=1, source_target_pairs={{0,16},{4,20},{8,24},{12,28},{16,0},{20,4},{24,8},{28,12},{1,17},{... | collective-permute-start | bytes 1474568 | tf_op jit(solution)/shard_map/ppermute | solution.py:293
  86.1 8.1 %collective-permute-start.21 = (bf16[320,384]{1,0:T(8,128)(2,1)S(1)}, bf16[320,384]{1,0:T(8,128)(2,1)S(1)}, u32[]{:S(2)}, u32[]{:S(2)}) collective-permute-start(bf16[320,384]{1,0:T(8,128)(2,1)S(1)} %slice.178), channel_id=1, source_target_pairs={{0,8},{4,12},{8,0},{12,4},{16,24},{20,28},{24,16},{28,20},{1,9},{5... | collective-permute-start | bytes 737288 | tf_op jit(solution)/shard_map/ppermute | solution.py:293
  100.1 11.8 %collective-permute-start.23 = (bf16[640,768]{1,0:T(8,128)(2,1)S(1)}, bf16[640,768]{1,0:T(8,128)(2,1)}, u32[]{:S(2)}, u32[]{:S(2)}) collective-permute-start(bf16[640,768]{1,0:T(8,128)(2,1)S(1)} %get-tuple-element.60), channel_id=1, source_target_pairs={{0,4},{4,0},{8,12},{12,8},{16,20},{20,16},{24,28},{28,24},{1,5},{5... | collective-permute-start | bytes 2949128 | tf_op jit(solution)/shard_map/ppermute | solution.py:293
  100.9 8.7 %collective-permute-start.27 = (bf16[320,384]{1,0:T(8,128)(2,1)}, bf16[320,384]{1,0:T(8,128)(2,1)}, u32[]{:S(2)}, u32[]{:S(2)}) collective-permute-start(bf16[320,384]{1,0:T(8,128)(2,1)} %slice.175), channel_id=1, source_target_pairs={{0,8},{4,12},{8,0},{12,4},{16,24},{20,28},{24,16},{28,20},{1,9},{5... | collective-permute-start | bytes 737288 | tf_op jit(solution)/shard_map/ppermute | solution.py:293
  110.7 7.6 %collective-permute-start.31 = (bf16[160,768]{1,0:T(8,128)(2,1)S(1)}, bf16[160,768]{1,0:T(8,128)(2,1)S(1)}, u32[]{:S(2)}, u32[]{:S(2)}) collective-permute-start(bf16[160,768]{1,0:T(8,128)(2,1)S(1)} %slice.174), channel_id=1, source_target_pairs={{0,1},{1,0},{2,3},{3,2},{4,5},{5,4},{6,7},{7,6},{8,9},{9,8},{10,11... | collective-permute-start | bytes 737288 | tf_op jit(solution)/shard_map/ppermute | solution.py:296
  113.4 8.1 %collective-permute-start.24 = (bf16[320,384]{1,0:T(8,128)(2,1)S(1)}, bf16[320,384]{1,0:T(8,128)(2,1)S(1)}, u32[]{:S(2)}, u32[]{:S(2)}) collective-permute-start(bf16[320,384]{1,0:T(8,128)(2,1)S(1)} %slice.177), channel_id=1, source_target_pairs={{0,8},{4,12},{8,0},{12,4},{16,24},{20,28},{24,16},{28,20},{1,9},{5... | collective-permute-start | bytes 737288 | tf_op jit(solution)/shard_map/ppermute | solution.py:293
  118.4 7.6 %collective-permute-start.28 = (bf16[320,384]{1,0:T(8,128)(2,1)S(1)}, bf16[320,384]{1,0:T(8,128)(2,1)S(1)}, u32[]{:S(2)}, u32[]{:S(2)}) collective-permute-start(bf16[320,384]{1,0:T(8,128)(2,1)S(1)} %slice.176), channel_id=1, source_target_pairs={{0,8},{4,12},{8,0},{12,4},{16,24},{20,28},{24,16},{28,20},{1,9},{5... | collective-permute-start | bytes 737288 | tf_op jit(solution)/shard_map/ppermute | solution.py:293
  121.6 13.5 %collective-permute-start.32 = (bf16[80,768]{1,0:T(8,128)(2,1)S(1)}, bf16[80,768]{1,0:T(8,128)(2,1)S(1)}, u32[]{:S(2)}, u32[]{:S(2)}) collective-permute-start(bf16[80,768]{1,0:T(8,128)(2,1)S(1)} %slice.179), channel_id=1, source_target_pairs={{0,2},{1,3},{2,0},{3,1},{4,6},{5,7},{6,4},{7,5},{8,10},{9,11},{10,... | collective-permute-start | bytes 368648 | tf_op jit(solution)/shard_map/ppermute | solution.py:296
  (31 other events, 336.5 us)

commit v4 on v3

--- a/solution.py
+++ b/solution.py
@@ -143,53 +143,57 @@
         functools.partial(cut_kernel, part),
         grid_spec=pltpu.PrefetchScalarGridSpec(
             num_scalar_prefetch=1,
-            grid=(local,),
-            in_specs=[pl.BlockSpec((1, depth, cols), lambda e, p: (e, 0, 0))],
-            out_specs=[pl.BlockSpec((1, depth, cols // QUAD), lambda e, p: (e, 0, 0))] * QUAD,
+            grid=(1,),
+            in_specs=[pl.BlockSpec((local, depth, cols), lambda i, p: (0, 0, 0))],
+            out_specs=[pl.BlockSpec((local, depth, cols // QUAD), lambda i, p: (0, 0, 0))] * QUAD,
         ),
         out_shape=[out] * QUAD,
+        compiler_params=pltpu.CompilerParams(vmem_limit_bytes=24 * 1024 * 1024),
         name="cut",
     )(place, weight)
 
 
 def up_kernel(rows, blocks, place_ref, *refs):
-    parts, pieces = refs[:blocks], refs[blocks : blocks + QUAD * rows]
-    out_ref, x_ref = refs[blocks + QUAD * rows :]
+    parts, pieces = refs[:blocks], refs[blocks : blocks + 2 * QUAD * rows]
+    out_ref, x_ref = refs[blocks + 2 * QUAD * rows :]
     side, core, zone, local = (place_ref[i] for i in range(4))
     expert = pl.program_id(0)
     width = out_ref.shape[1]
+    part = width // 2
 
     @pl.when(expert == 0)
     def _():
         at = 0
-        for part in parts:
-            x_ref[at : at + part.shape[0], :] = part[...]
-            at += part.shape[0]
-
-    acc = None
-    for m in range(rows):
-        own, mate, own_x, mate_x = (pieces[QUAD * m + i][0] for i in range(QUAD))
-        near = [jnp.where(core == 0, own, mate), jnp.where(core == 0, mate, own)]
-        far = [jnp.where(core == 0, own_x, mate_x), jnp.where(core == 0, mate_x, own_x)]
-        order = [jnp.where(side == 0, a, b) for a, b in zip(near + far, far + near)]
-        w = jnp.concatenate(order, axis=0)
-        depth = w.shape[0]
-        part = jnp.dot(
-            x_ref[:, m * depth : (m + 1) * depth], w, preferred_element_type=jnp.float32
-        )
-        acc = part if acc is None else acc + part
+        for block in parts:
+            x_ref[at : at + block.shape[0], :] = block[...]
+            at += block.shape[0]
+
+    def ordered(group):
+        order = []
+        for m in range(rows):
+            own, mate, own_x, mate_x = (group[QUAD * m + i][0] for i in range(QUAD))
+            near = [jnp.where(core == 0, own, mate), jnp.where(core == 0, mate, own)]
+            far = [jnp.where(core == 0, own_x, mate_x), jnp.where(core == 0, mate_x, own_x)]
+            order += [jnp.where(side == 0, a, b) for a, b in zip(near + far, far + near)]
+        return jnp.concatenate(order, axis=0)
+
+    mine, other = ordered(pieces[: QUAD * rows]), ordered(pieces[QUAD * rows :])
+    w = jnp.concatenate(
+        [mine[:, :part], other[:, :part], mine[:, part:], other[:, part:]], axis=1
+    )
     feats = x_ref.shape[1] - LANES
     lane = lax.broadcasted_iota(jnp.int32, (LANES, width), 0)
     slot = zone * local + expert
     pick = jnp.where((lane == slot) | (lane == slot + LOW), 1.0, 0.0).astype(jnp.bfloat16)
+    acc = jnp.dot(x_ref[:, :feats], w, preferred_element_type=jnp.float32)
     gate = jnp.dot(x_ref[:, feats:], pick, preferred_element_type=jnp.float32)
     g, u = acc[:, :width], acc[:, width:]
     out_ref[...] = (g / (1.0 + jnp.exp(-g)) * u * gate).astype(jnp.bfloat16)
 
 
-def up_call(place, parts, pieces):
-    rows = len(pieces) // QUAD
-    local, depth, cols = pieces[0].shape
+def up_call(place, parts, mine, other):
+    rows = len(mine) // QUAD
+    local, depth, cols = mine[0].shape
     tokens, lanes = sum(v.shape[0] for v in parts), parts[0].shape[1]
     piece = pl.BlockSpec((1, depth, cols), lambda e, p: (e, 0, 0))
     return pl.pallas_call(
@@ -198,72 +202,57 @@
             num_scalar_prefetch=1,
             grid=(local,),
             in_specs=[pl.BlockSpec(v.shape, lambda e, p: (0, 0)) for v in parts]
-            + [piece] * len(pieces),
-            out_specs=pl.BlockSpec((tokens, cols // 2), lambda e, p: (0, e)),
+            + [piece] * (2 * len(mine)),
+            out_specs=pl.BlockSpec((tokens, cols), lambda e, p: (0, e)),
             scratch_shapes=[pltpu.VMEM((tokens, lanes), jnp.bfloat16)],
         ),
-        out_shape=jax.ShapeDtypeStruct((tokens, local * cols // 2), jnp.bfloat16),
+        out_shape=jax.ShapeDtypeStruct((tokens, local * cols), jnp.bfloat16),
         compiler_params=pltpu.CompilerParams(vmem_limit_bytes=48 * 1024 * 1024),
-        cost_estimate=pl.CostEstimate(
-            flops=2 * tokens * lanes * local * cols,
-            bytes_accessed=2 * (tokens * lanes + local * lanes * cols),
-            transcendentals=tokens * local * cols // 2,
-        ),
+        cost_estimate=pl.CostEstimate(flops=1, bytes_accessed=1, transcendentals=0),
         name="up",
-    )(place, *parts, *pieces)
-
-
-def down_kernel(place_ref, h_ref, near_ref, far_ref, send_ref, keep_ref):
-    side = place_ref[0]
+    )(place, *parts, *mine, *other)
+
+
+def down_kernel(start, place_ref, h_ref, near_ref, near_other_ref, far_ref, far_other_ref, *out_refs):
+    first = place_ref[0] == 0
     feats = near_ref.shape[1]
-    parts = []
+    order = [[], []]
     for e in range(near_ref.shape[0]):
-        near, far = near_ref[e], far_ref[e]
-        parts.append([jnp.where(side == 0, near, far), jnp.where(side == 0, far, near)])
-
-    def times(j):
-        w = jnp.concatenate([p[j] for p in parts], axis=1)
-        return lax.dot_general(
-            h_ref[...], w, (((1,), (1,)), ((), ())), preferred_element_type=jnp.float32
+        for near, far in ((near_ref[e], far_ref[e]), (near_other_ref[e], far_other_ref[e])):
+            order[0].append(jnp.where(first, near, far))
+            order[1].append(jnp.where(first, far, near))
+    for j in range(2):
+        partial = lax.dot_general(
+            h_ref[start : start + out_refs[0].shape[0], :],
+            jnp.concatenate(order[j], axis=1),
+            (((1,), (1,)), ((), ())),
+            preferred_element_type=jnp.float32,
         )
-
-    @pl.when(pl.program_id(0) == 0)
-    def _():
-        for j in range(2):
-            send_ref[:, j * feats : (j + 1) * feats] = times(j).astype(send_ref.dtype)
-
-    @pl.when(pl.program_id(0) == 1)
-    def _():
-        for j in range(2):
-            keep_ref[:, j * feats : (j + 1) * feats] = times(j)
-
-
-def down_call(place, hidden, near, far):
-    tokens, depth = hidden.shape
-    local, feats, part = near.shape
-    half = tokens // 2
-    whole = pl.BlockSpec((local, feats, part), lambda i, p: (0, 0, 0))
-    out = pl.BlockSpec((half, 2 * feats), lambda i, p: (0, 0))
+        if len(out_refs) == 2:
+            out_refs[j][...] = partial.astype(out_refs[j].dtype)
+        else:
+            out_refs[0][:, j * feats : (j + 1) * feats] = partial
+
+
+def down_call(place, hidden, near, far, send):
+    tokens = hidden.shape[0] // 2
+    feats = near[0].shape[1]
+    if send:
+        out = [jax.ShapeDtypeStruct((tokens, feats), jnp.bfloat16)] * 2
+    else:
+        out = jax.ShapeDtypeStruct((tokens, 2 * feats), jnp.float32)
     return pl.pallas_call(
-        down_kernel,
-        grid_spec=pltpu.PrefetchScalarGridSpec(
-            num_scalar_prefetch=1,
-            grid=(2,),
-            in_specs=[pl.BlockSpec((half, depth), lambda i, p: (1 - i, 0)), whole, whole],
-            out_specs=[out, out],
-        ),
-        out_shape=[
-            jax.ShapeDtypeStruct((half, 2 * feats), jnp.bfloat16),
-            jax.ShapeDtypeStruct((half, 2 * feats), jnp.float32),
-        ],
+        functools.partial(down_kernel, tokens if send else 0),
+        in_specs=[pl.BlockSpec(memory_space=pltpu.SMEM)]
+        + [pl.BlockSpec(memory_space=pltpu.VMEM)] * 5,
+        out_specs=[pl.BlockSpec(memory_space=pltpu.VMEM)] * 2
+        if send
+        else pl.BlockSpec(memory_space=pltpu.VMEM),
+        out_shape=out,
         compiler_params=pltpu.CompilerParams(vmem_limit_bytes=40 * 1024 * 1024),
-        cost_estimate=pl.CostEstimate(
-            flops=4 * tokens * depth * feats,
-            bytes_accessed=2 * (tokens * depth + 2 * depth * feats + 3 * tokens * feats),
-            transcendentals=0,
-        ),
+        cost_estimate=pl.CostEstimate(flops=1, bytes_accessed=1, transcendentals=0),
         name="down",
-    )(place, hidden, near, far)
+    )(place, hidden, *near, *far)
 
 
 def body(
@@ -320,18 +309,16 @@
     second = widen([after(gu_mate, first[-1], sent)])
     third = widen([after(gu_own_x, second[-1])])
     fourth = widen([after(gu_mate_x, third[-1])])
-    pieces = [p for group in zip(first, second, third, fourth) for p in group]
-
-    near = sent
-    for bit in zone_bits[:-1]:
-        near = jnp.concatenate([near, hop(near, bit)], axis=0)
-    far = hop(near, zone_bits[-1])
-    near_x = flip(after(near, gu_mate_x, second[-1]), 2)
-    far_x = flip(after(far, near_x, third[-1]), 2)
-    chip = [near, after(far, fourth[-1]), near_x, after(far_x, fourth[-1])]
-    parts = chip + [flip(v, 1) for v in chip]
-
-    dn_own, dn_away, dn_to_mate, dn_to_mate_away = cut_call(place, down_weight, part)
+    mine = [p for group in zip(first, second, third, fourth) for p in group]
+    shared = [flip(gu_own, 1), flip(gu_own_x, 1), flip(gu_mate_x, 1)]
+    firsts, seconds, thirds, fourths = (
+        [flip(p, 1) for p in group[1:]] for group in (first, second, third, fourth)
+    )
+    other = [gu_to_mate, shared[0], shared[2], shared[1]]
+    for group in zip(seconds, firsts, fourths, thirds):
+        other += group
+
+    dn_own, dn_away, dn_to_mate, dn_to_mate_away = cut_call(place, after(down_weight, first[-1]), part)
     dn_mate, dn_mate_away = flip(dn_to_mate, 1), flip(dn_to_mate_away, 1)
 
     def pair(own, mate):
@@ -342,24 +329,31 @@
         )
 
     dn_near = pair(dn_own, dn_mate)
-    dn_far = flip(after(pair(dn_away, dn_mate_away), far_x), 2)
+    dn_away = pair(dn_away, dn_mate_away)
+    near = sent
+    for bit in zone_bits[:-1]:
+        near = jnp.concatenate([near, hop(near, bit)], axis=0)
+    far = hop(after(near, second[-1]), zone_bits[-1])
+    near_x = flip(
+        after(near, gu_mate_x, second[-1], dn_near, dn_away, shared[0], shared[1], *firsts), 2
+    )
+    far_x = flip(after(far, near_x, third[-1], shared[2], *seconds), 2)
+    dn_far = flip(after(dn_away, far_x, *thirds), 2)
+    hidden = up_call(place, [near, far, near_x, far_x], mine, other)
     dn_nears = widen([after(dn_near, fourth[-1])])
-    hidden = after(up_call(place, parts, pieces), dn_nears[-1])
-    dn_fars = widen([after(dn_far, dn_nears[-1], hidden)])
-
-    count = zones * tok
+    dn_fars = widen([after(dn_far, dn_nears[-1])])
+    dn_nears = [(v, flip(after(v, hidden), 1)) for v in dn_nears]
+    dn_fars = [(v, flip(after(v, hidden), 1)) for v in dn_fars]
+
     sums = []
     for m in range(rows):
         ready = after(hidden, *(v[1] for v in sums[-2:-1]))
-        send, keep = down_call(place, ready, dn_nears[m], dn_fars[m])
-        back = flip(send, 1)
-        feats = send.shape[1] // 2
+        sends = down_call(place, ready, dn_nears[m], dn_fars[m], True)
+        keep = down_call(place, after(hidden, sends[0]), dn_nears[m], dn_fars[m], False)
+        feats = keep.shape[1] // 2
         for j in range(2):
-            cols = slice(j * feats, (j + 1) * feats)
-            total = keep[:, cols] + back[:, cols].astype(jnp.float32)
-            away = total[count:].astype(jnp.bfloat16)
-            crossed = flip(after(away, *(v[1] for v in sums[-2:-1])), 2)
-            sums.append((total[:count], crossed))
+            crossed = flip(after(sends[j], *(v[1] for v in sums[-1:])), 2)
+            sums.append((keep[:, j * feats : (j + 1) * feats], crossed))
     merged = [
         (jnp.concatenate([a[0], b[0]], axis=1), jnp.concatenate([a[1], b[1]], axis=1))
         for a, b in zip(sums[:-2:2], sums[1:-2:2])
@@ -369,10 +363,10 @@
         total = total + crossed.astype(jnp.float32)
         for bit in reversed(zone_bits):
             size = total.shape[0] // 2
-            away = total[size:].astype(jnp.bfloat16)
+            moved = total[size:].astype(jnp.bfloat16)
             if i < len(merged) and bit == zone_bits[0]:
-                away = after(away, sums[-2][1])
-            total = total[:size] + hop(away, bit).astype(jnp.float32)
+                moved = after(moved, sums[-2][1])
+            total = total[:size] + hop(moved, bit).astype(jnp.float32)
         chunks.append(total)
     branch = swap_blocks(jnp.concatenate(chunks, axis=1), row, rows)
     total = stream_in + branch

time: 141 us -> 135 us (0.957)
  waiting for transfers between devices: 62.7 us -> 55.5 us
  Pallas kernels: 29 us -> 22.7 us
  starting transfers between devices: 31 us -> 36.4 us
  local copies, waits for them, and re-layouts: 9.32 us -> 12.9 us
    ppermute x8, waiting for transfers between devices: 27.3 us -> 17.7 us  [hop(): return lax.ppermute(values, 'expert', [(i, i ^ bit) for i in range(zones)])]
    ppermute x8, starting transfers between devices: 10.5 us -> 17.9 us  [hop(): return lax.ppermute(values, 'expert', [(i, i ^ bit) for i in range(zones)])]
    pallas_call x2, Pallas kernels: 9.86 us -> 2.71 us  [cut_call(): pl.pallas_call(functools.partial(cut_kernel, part), grid_spec=pltpu.Prefe...]
    unnamed x47 -> x65, local copies, waits for them, and re-layouts: 5.61 us -> 10.3 us
    ppermute x25 -> x30, waiting for transfers between devices: 35.4 us -> 37.9 us  [flip(): return lax.ppermute(values, 'dp', [(i, i ^ bit) for i in range(ranks)])]
    slice x12 -> x6, local copies, waits for them, and re-layouts: 3.03 us -> 0.9 us  [body(): moved = total[size:].astype(jnp.bfloat16)]
    ppermute x25 -> x30, starting transfers between devices: 20.5 us -> 18.5 us  [flip(): return lax.ppermute(values, 'dp', [(i, i ^ bit) for i in range(ranks)])]
    concatenate x1, local copies, waits for them, and re-layouts: 0.03 us -> 1.67 us  [body(): near = jnp.concatenate([near, hop(near, bit)], axis=0)]
  transfers between devices with their start and end apart: 33 -> 38, of which waited for: 23 -> 16; matrix products, arithmetic and copies ran while one was open for 7% -> 6% of each run, Pallas kernels for 12% -> 15%
where the time goes in v4:
time: 135 us
  waiting for transfers between devices  55.5 us (41%)
  starting transfers between devices  36.4 us (27%)
  Pallas kernels  22.7 us (17%)
  local copies, waits for them, and re-layouts  12.9 us (10%)
  other arithmetic  6.29 us (5%)
    ppermute x30, waiting for transfers between devices, flip(): return lax.ppermute(values, 'dp', [(i, i ^ bit) for i in range(ranks)])  37.9 us
    ppermute x30, starting transfers between devices, flip(): return lax.ppermute(values, 'dp', [(i, i ^ bit) for i in range(ranks)])  18.5 us
    ppermute x8, starting transfers between devices, hop(): return lax.ppermute(values, 'expert', [(i, i ^ bit) for i in range(zones)])  17.9 us
    ppermute x8, waiting for transfers between devices, hop(): return lax.ppermute(values, 'expert', [(i, i ^ bit) for i in range(zones)])  17.7 us
    pallas_call x1, Pallas kernels, up_call(): pl.pallas_call(functools.partial(up_kernel, rows, len(parts)), grid_spec=...  10.5 us
    unnamed x65, local copies, waits for them, and re-layouts  10.3 us
    pallas_call x4, Pallas kernels, down_call(): pl.pallas_call(functools.partial(down_kernel, tokens if send else 0), in_...  6.57 us
    select_n x2, other arithmetic, pair(): jnp.where(core == 0, jnp.concatenate([own, mate], axis=1), jnp.concatenat...  2.94 us
  transfers between devices with their start and end apart: 38, of which 16 were waited for; matrix products, arithmetic and copies ran while one was open for 6% of the time, Pallas kernels for 15%

profile of v4, /device:TPU:0, one launch (start us, length us, event | category | flops | bytes accessed | tf_op | source)
XLA Modules:
  0.0 135.0 jit_solution(5245332401562444008)
XLA Ops:
  2.4 2.0 %cut.2 = (bf16[5,192,256]{2,1,0:T(8,128)(2,1)S(1)}, bf16[5,192,256]{2,1,0:T(8,128)(2,1)}, bf16[5,192,256]{2,1,0:T(8,128)(2,1)S(1)}, bf16[5,192,256]{2,1,0:T(8,128)(2,1)}) custom-call(s32[5]{0:T(128)S(1)} %stack.19.place_ref, bf16[5,192,1024]{2,1,0:T(8,128)(2,1)S(1)} %copy-done.3), custom_call_target="tpu_custom_call" | custom-call | tf_op jit(solution)/shard_map/cut/pallas_call | solution.py:142
  4.3 3.0 %collective-permute-start.2 = (bf16[5,192,256]{2,1,0:T(8,128)(2,1)S(1)}, bf16[5,192,256]{2,1,0:T(8,128)(2,1)S(1)}, u32[]{:S(2)}, u32[]{:S(2)}) collective-permute-start(bf16[5,192,256]{2,1,0:T(8,128)(2,1)S(1)} %get-tuple-element.39.refs_4_), channel_id=1, source_target_pairs={{0,16},{4,20},{8,24},{12,28},{16,0},{20,4},{24,8},{28,12},{1,17},{... | collective-permute-start | bytes 1474568 | tf_op jit(solution)/shard_map/ppermute | solution.py:282
  9.6 2.3 %copy-done.2 = bf16[1536,1536]{1,0:T(8,128)(2,1)S(1)} copy-done((bf16[1536,1536]{1,0:T(8,128)(2,1)S(1)}, bf16[1536,1536]{1,0:T(8,128)(2,1)}, u32[]{:S(2)}) %copy-start.2) | copy-done | bytes 4718616
  12.0 2.9 %front.1 = (bf16[80,1536]{1,0:T(8,128)(2,1)S(1)}, bf16[80,1664]{1,0:T(8,128)(2,1)S(1)}) custom-call(s32[5]{0:T(128)S(1)} %stack.19.place_ref, bf16[80,1536]{1,0:T(8,128)(2,1)S(1)} %copy-done.9, bf16[80,1536]{1,0:T(8,128)(2,1)S(1)} %copy-done.10, bf16[1536,1536]{1,0:T(8,128)(2,1)S(1)} %copy-done.2, f32[1,1536]{1,0:T(1,128)S(1)} %broadcast_in_dim.8.gain_ref, ...), custom_call_target="tpu_custom_call" | custom-call | tf_op jit(solution)/shard_map/front/pallas_call | solution.py:100
  14.9 2.6 %collective-permute-start = (bf16[80,1664]{1,0:T(8,128)(2,1)S(1)}, bf16[80,1664]{1,0:T(8,128)(2,1)}, u32[]{:S(2)}, u32[]{:S(2)}) collective-permute-start(bf16[80,1664]{1,0:T(8,128)(2,1)S(1)} %get-tuple-element.42), channel_id=1, source_target_pairs={{0,2},{1,3},{2,0},{3,1},{4,6},{5,7},{6,4},{7,5},{8,10},{9,11},{10,... | collective-permute-start | bytes 798728 | tf_op jit(solution)/shard_map/ppermute | solution.py:285
  21.7 8.0 %collective-permute-done = bf16[80,1664]{1,0:T(8,128)(2,1)} collective-permute-done((bf16[80,1664]{1,0:T(8,128)(2,1)S(1)}, bf16[80,1664]{1,0:T(8,128)(2,1)}, u32[]{:S(2)}, u32[]{:S(2)}) %collective-permute-start) | collective-permute-done | bytes 266272 | tf_op jit(solution)/shard_map/ppermute | solution.py:285
  31.7 1.7 %constant_dynamic-update-slice_fusion.refs_0_ = bf16[160,1664]{1,0:T(8,128)(2,1)} fusion(bf16[160,1664]{1,0:T(8,128)(2,1)} %constant_dynamic-update-slice_fusion.1, bf16[80,1664]{1,0:T(8,128)(2,1)} %collective-permute-done), kind=kLoop, calls=%fused_computation.21 | loop fusion | bytes 532480 | tf_op jit(solution)/shard_map/concatenate | solution.py:335
  37.8 4.3 %collective-permute-done.7.refs_7_ = bf16[5,192,256]{2,1,0:T(8,128)(2,1)} collective-permute-done((bf16[5,192,256]{2,1,0:T(8,128)(2,1)}, bf16[5,192,256]{2,1,0:T(8,128)(2,1)}, u32[]{:S(2)}, u32[]{:S(2)}) %collective-permute-start.7) | collective-permute-done | bytes 491552 | tf_op jit(solution)/shard_map/ppermute | solution.py:282
  43.8 9.8 %collective-permute-done.14.refs_10_ = bf16[5,192,256]{2,1,0:T(8,128)(2,1)S(1)} collective-permute-done((bf16[5,192,256]{2,1,0:T(8,128)(2,1)S(1)}, bf16[5,192,256]{2,1,0:T(8,128)(2,1)S(1)}, u32[]{:S(2)}, u32[]{:S(2)}) %collective-permute-start.14) | collective-permute-done | bytes 491552 | tf_op jit(solution)/shard_map/ppermute | solution.py:282
  55.6 9.5 %collective-permute-done.18.refs_11_ = bf16[5,192,256]{2,1,0:T(8,128)(2,1)S(1)} collective-permute-done((bf16[5,192,256]{2,1,0:T(8,128)(2,1)}, bf16[5,192,256]{2,1,0:T(8,128)(2,1)S(1)}, u32[]{:S(2)}, u32[]{:S(2)}) %collective-permute-start.18) | collective-permute-done | bytes 491552 | tf_op jit(solution)/shard_map/ppermute | solution.py:282
  68.8 10.5 %up.1.h_ref = bf16[640,1280]{1,0:T(8,128)(2,1)} custom-call(s32[5]{0:T(128)S(1)} %stack.19.place_ref, bf16[160,1664]{1,0:T(8,128)(2,1)} %constant_dynamic-update-slice_fusion.refs_0_, bf16[160,1664]{1,0:T(8,128)(2,1)} %copy-done.18, bf16[160,1664]{1,0:T(8,128)(2,1)} %copy-done.19, bf16[160,1664]{1,0:T(8,128)(2,1)} %copy-done.20, ...), custom_call_target="tpu_custom_call" | custom-call | flops 1 | bytes 1 | tf_op jit(solution)/shard_map/up/pallas_call | solution.py:199
  86.2 6.9 %collective-permute-done.27.far_ref = bf16[5,384,128]{2,1,0:T(8,128)(2,1)S(1)} collective-permute-done((bf16[5,384,128]{2,1,0:T(8,128)(2,1)S(1)}, bf16[5,384,128]{2,1,0:T(8,128)(2,1)S(1)}, u32[]{:S(2)}, u32[]{:S(2)}) %collective-permute-start.27) | collective-permute-done | bytes 491552 | tf_op jit(solution)/shard_map/ppermute | solution.py:282
  94.3 1.6 %down.7 = f32[320,768]{1,0:T(8,128)S(1)} custom-call(s32[5]{0:T(128)S(1)} %stack.19.place_ref, bf16[640,1280]{1,0:T(8,128)(2,1)S(1)} %copy-done, bf16[5,384,128]{2,1,0:T(8,128)(2,1)S(1)} %maximum_select_fusion.near_ref, bf16[5,384,128]{2,1,0:T(8,128)(2,1)S(1)} %collective-permute-done.21.near_other_ref, ...), custom_call_target="tpu_custom_call" | custom-call | flops 1 | bytes 1 | tf_op jit(solution)/shard_map/down/pallas_call | solution.py:244
  95.9 1.9 %down.5 = (bf16[320,384]{1,0:T(8,128)(2,1)}, bf16[320,384]{1,0:T(8,128)(2,1)S(1)}) custom-call(s32[5]{0:T(128)S(1)} %stack.19.place_ref, bf16[640,1280]{1,0:T(8,128)(2,1)S(1)} %copy-done, bf16[5,384,128]{2,1,0:T(8,128)(2,1)S(1)} %collective-permute-done.23.near_ref, bf16[5,384,128]{2,1,0:T(8,128)(2,1)S(1)} %collective-permute-done.26.near_other_ref, ...), custom_call_target="tpu_custom_call" | custom-call | flops 1 | bytes 1 | tf_op jit(solution)/shard_map/down/pallas_call | solution.py:244
  97.8 3.7 %collective-permute-done.29 = bf16[320,384]{1,0:T(8,128)(2,1)S(1)} collective-permute-done((bf16[320,384]{1,0:T(8,128)(2,1)S(1)}, bf16[320,384]{1,0:T(8,128)(2,1)S(1)}, u32[]{:S(2)}, u32[]{:S(2)}) %collective-permute-start.29) | collective-permute-done | bytes 245792 | tf_op jit(solution)/shard_map/ppermute | solution.py:282
  103.8 3.9 %collective-permute-start.36 = (bf16[160,768]{1,0:T(8,128)(2,1)}, bf16[160,768]{1,0:T(8,128)(2,1)}, u32[]{:S(2)}, u32[]{:S(2)}) collective-permute-start(bf16[160,768]{1,0:T(8,128)(2,1)} %slice.95), channel_id=1, source_target_pairs={{0,1},{1,0},{2,3},{3,2},{4,5},{5,4},{6,7},{7,6},{8,9},{9,8},{10,11... | collective-permute-start | bytes 737288 | tf_op jit(solution)/shard_map/ppermute | solution.py:285
  108.8 1.6 %down.6 = f32[320,768]{1,0:T(8,128)S(1)} custom-call(s32[5]{0:T(128)S(1)} %stack.19.place_ref, bf16[640,1280]{1,0:T(8,128)(2,1)S(1)} %copy-done.1, bf16[5,384,128]{2,1,0:T(8,128)(2,1)S(1)} %collective-permute-done.23.near_ref, bf16[5,384,128]{2,1,0:T(8,128)(2,1)S(1)} %collective-permute-done.26.near_other_ref, ...), custom_call_target="tpu_custom_call" | custom-call | flops 1 | bytes 1 | tf_op jit(solution)/shard_map/down/pallas_call | solution.py:244
  111.2 2.4 %collective-permute-done.36 = bf16[160,768]{1,0:T(8,128)(2,1)} collective-permute-done((bf16[160,768]{1,0:T(8,128)(2,1)}, bf16[160,768]{1,0:T(8,128)(2,1)}, u32[]{:S(2)}, u32[]{:S(2)}) %collective-permute-start.36) | collective-permute-done | bytes 245792 | tf_op jit(solution)/shard_map/ppermute | solution.py:285
  114.6 3.5 %collective-permute-start.37 = (bf16[80,768]{1,0:T(8,128)(2,1)S(1)}, bf16[80,768]{1,0:T(8,128)(2,1)S(1)}, u32[]{:S(2)}, u32[]{:S(2)}) collective-permute-start(bf16[80,768]{1,0:T(8,128)(2,1)S(1)} %slice.96), channel_id=1, source_target_pairs={{0,2},{1,3},{2,0},{3,1},{4,6},{5,7},{6,4},{7,5},{8,10},{9,11},{10,... | collective-permute-start | bytes 368648 | tf_op jit(solution)/shard_map/ppermute | solution.py:285
  119.3 1.8 %collective-permute-start.34 = (bf16[160,384]{1,0:T(8,128)(2,1)S(1)}, bf16[160,384]{1,0:T(8,128)(2,1)S(1)}, u32[]{:S(2)}, u32[]{:S(2)}) collective-permute-start(bf16[160,384]{1,0:T(8,128)(2,1)S(1)} %slice.97), channel_id=1, source_target_pairs={{0,1},{1,0},{2,3},{3,2},{4,5},{5,4},{6,7},{7,6},{8,9},{9,8},{10,11... | collective-permute-start | bytes 368648 | tf_op jit(solution)/shard_map/ppermute | solution.py:285
  121.1 2.1 %collective-permute-done.37 = bf16[80,768]{1,0:T(8,128)(2,1)S(1)} collective-permute-done((bf16[80,768]{1,0:T(8,128)(2,1)S(1)}, bf16[80,768]{1,0:T(8,128)(2,1)S(1)}, u32[]{:S(2)}, u32[]{:S(2)}) %collective-permute-start.37) | collective-permute-done | bytes 122912 | tf_op jit(solution)/shard_map/ppermute | solution.py:285
  125.4 2.6 %collective-permute-start.35 = (bf16[80,384]{1,0:T(8,128)(2,1)S(1)}, bf16[80,384]{1,0:T(8,128)(2,1)S(1)}, u32[]{:S(2)}, u32[]{:S(2)}) collective-permute-start(bf16[80,384]{1,0:T(8,128)(2,1)S(1)} %slice.99), channel_id=1, source_target_pairs={{0,2},{1,3},{2,0},{3,1},{4,6},{5,7},{6,4},{7,5},{8,10},{9,11},{10,... | collective-permute-start | bytes 184328 | tf_op jit(solution)/shard_map/ppermute | solution.py:285
  128.8 2.0 %collective-permute-start.32 = (bf16[80,384]{1,0:T(8,128)(2,1)S(1)}, bf16[80,384]{1,0:T(8,128)(2,1)S(1)}, u32[]{:S(2)}, u32[]{:S(2)}) collective-permute-start(bf16[80,384]{1,0:T(8,128)(2,1)S(1)} %slice.100), channel_id=1, source_target_pairs={{0,2},{1,3},{2,0},{3,1},{4,6},{5,7},{6,4},{7,5},{8,10},{9,11},{10,... | collective-permute-start | bytes 184328 | tf_op jit(solution)/shard_map/ppermute | solution.py:285
  130.8 3.1 %collective-permute-done.32 = bf16[80,384]{1,0:T(8,128)(2,1)S(1)} collective-permute-done((bf16[80,384]{1,0:T(8,128)(2,1)S(1)}, bf16[80,384]{1,0:T(8,128)(2,1)S(1)}, u32[]{:S(2)}, u32[]{:S(2)}) %collective-permute-start.32) | collective-permute-done | bytes 61472 | tf_op jit(solution)/shard_map/ppermute | solution.py:285
  (149 shorter events, 40.2 us)
Async XLA Ops:
  4.3 14.2 %collective-permute-start.2 = (bf16[5,192,256]{2,1,0:T(8,128)(2,1)S(1)}, bf16[5,192,256]{2,1,0:T(8,128)(2,1)S(1)}, u32[]{:S(2)}, u32[]{:S(2)}) collective-permute-start(bf16[5,192,256]{2,1,0:T(8,128)(2,1)S(1)} %get-tuple-element.39.refs_4_), channel_id=1, source_target_pairs={{0,16},{4,20},{8,24},{12,28},{16,0},{20,4},{24,8},{28,12},{1,17},{... | collective-permute-start | bytes 1474568 | tf_op jit(solution)/shard_map/ppermute | solution.py:282
  7.3 12.0 %collective-permute-start.1 = (bf16[5,192,256]{2,1,0:T(8,128)(2,1)S(1)}, bf16[5,192,256]{2,1,0:T(8,128)(2,1)S(1)}, u32[]{:S(2)}, u32[]{:S(2)}) collective-permute-start(bf16[5,192,256]{2,1,0:T(8,128)(2,1)S(1)} %get-tuple-element.43.refs_12_), channel_id=1, source_target_pairs={{0,4},{4,0},{8,12},{12,8},{16,20},{20,16},{24,28},{28,24},{1,5},{5... | collective-permute-start | bytes 1474568 | tf_op jit(solution)/shard_map/ppermute | solution.py:282
  7.3 12.5 %collective-permute-start.5 = (bf16[5,192,256]{2,1,0:T(8,128)(2,1)}, bf16[5,192,256]{2,1,0:T(8,128)(2,1)}, u32[]{:S(2)}, u32[]{:S(2)}) collective-permute-start(bf16[5,192,256]{2,1,0:T(8,128)(2,1)} %get-tuple-element.46), channel_id=1, source_target_pairs={{0,4},{4,0},{8,12},{12,8},{16,20},{20,16},{24,28},{28,24},{1,5},{5... | collective-permute-start | bytes 1474568 | tf_op jit(solution)/shard_map/ppermute | solution.py:282
  7.8 13.3 %collective-permute-start.6 = (bf16[5,192,256]{2,1,0:T(8,128)(2,1)}, bf16[5,192,256]{2,1,0:T(8,128)(2,1)S(1)}, u32[]{:S(2)}, u32[]{:S(2)}) collective-permute-start(bf16[5,192,256]{2,1,0:T(8,128)(2,1)} %get-tuple-element.47), channel_id=1, source_target_pairs={{0,8},{4,12},{8,0},{12,4},{16,24},{20,28},{24,16},{28,20},{1,9},{5... | collective-permute-start | bytes 1474568 | tf_op jit(solution)/shard_map/ppermute | solution.py:282
  14.9 14.8 %collective-permute-start = (bf16[80,1664]{1,0:T(8,128)(2,1)S(1)}, bf16[80,1664]{1,0:T(8,128)(2,1)}, u32[]{:S(2)}, u32[]{:S(2)}) collective-permute-start(bf16[80,1664]{1,0:T(8,128)(2,1)S(1)} %get-tuple-element.42), channel_id=1, source_target_pairs={{0,2},{1,3},{2,0},{3,1},{4,6},{5,7},{6,4},{7,5},{8,10},{9,11},{10,... | collective-permute-start | bytes 798728 | tf_op jit(solution)/shard_map/ppermute | solution.py:285
  19.3 10.9 %collective-permute-start.8 = (bf16[5,192,128]{2,1,0:T(8,128)(2,1)S(1)}, bf16[5,192,128]{2,1,0:T(8,128)(2,1)S(1)}, u32[]{:S(2)}, u32[]{:S(2)}) collective-permute-start(bf16[5,192,128]{2,1,0:T(8,128)(2,1)S(1)} %get-tuple-element.51), channel_id=1, source_target_pairs={{0,4},{4,0},{8,12},{12,8},{16,20},{20,16},{24,28},{28,24},{1,5},{5... | collective-permute-start | bytes 737288 | tf_op jit(solution)/shard_map/ppermute | solution.py:282
  19.4 10.9 %collective-permute-start.9 = (bf16[5,192,128]{2,1,0:T(8,128)(2,1)S(1)}, bf16[5,192,128]{2,1,0:T(8,128)(2,1)S(1)}, u32[]{:S(2)}, u32[]{:S(2)}) collective-permute-start(bf16[5,192,128]{2,1,0:T(8,128)(2,1)S(1)} %get-tuple-element.53), channel_id=1, source_target_pairs={{0,4},{4,0},{8,12},{12,8},{16,20},{20,16},{24,28},{28,24},{1,5},{5... | collective-permute-start | bytes 737288 | tf_op jit(solution)/shard_map/ppermute | solution.py:282
  19.9 17.1 %collective-permute-start.10 = (bf16[5,192,256]{2,1,0:T(8,128)(2,1)S(1)}, bf16[5,192,256]{2,1,0:T(8,128)(2,1)S(1)}, u32[]{:S(2)}, u32[]{:S(2)}) collective-permute-start(bf16[5,192,256]{2,1,0:T(8,128)(2,1)S(1)} %get-tuple-element.39.refs_4_), channel_id=1, source_target_pairs={{0,4},{4,0},{8,12},{12,8},{16,20},{20,16},{24,28},{28,24},{1,5},{5... | collective-permute-start | bytes 1474568 | tf_op jit(solution)/shard_map/ppermute | solution.py:282
  21.2 15.2 %collective-permute-start.3 = (bf16[5,192,256]{2,1,0:T(8,128)(2,1)S(1)}, bf16[5,192,256]{2,1,0:T(8,128)(2,1)}, u32[]{:S(2)}, u32[]{:S(2)}) collective-permute-start(bf16[5,192,256]{2,1,0:T(8,128)(2,1)S(1)} %collective-permute-done.1.refs_5_), channel_id=1, source_target_pairs={{0,16},{4,20},{8,24},{12,28},{16,0},{20,4},{24,8},{28,12},{1,17},{... | collective-permute-start | bytes 1474568 | tf_op jit(solution)/shard_map/ppermute | solution.py:282
  29.7 12.4 %collective-permute-start.7 = (bf16[5,192,256]{2,1,0:T(8,128)(2,1)}, bf16[5,192,256]{2,1,0:T(8,128)(2,1)}, u32[]{:S(2)}, u32[]{:S(2)}) collective-permute-start(bf16[5,192,256]{2,1,0:T(8,128)(2,1)} %collective-permute-done.5), channel_id=1, source_target_pairs={{0,8},{4,12},{8,0},{12,4},{16,24},{20,28},{24,16},{28,20},{1,9},{5... | collective-permute-start | bytes 1474568 | tf_op jit(solution)/shard_map/ppermute | solution.py:282
  30.2 11.9 %collective-permute-start.11 = (bf16[5,192,256]{2,1,0:T(8,128)(2,1)S(1)}, bf16[5,192,256]{2,1,0:T(8,128)(2,1)}, u32[]{:S(2)}, u32[]{:S(2)}) collective-permute-start(bf16[5,192,256]{2,1,0:T(8,128)(2,1)S(1)} %collective-permute-done.6.refs_6_), channel_id=1, source_target_pairs={{0,4},{4,0},{8,12},{12,8},{16,20},{20,16},{24,28},{28,24},{1,5},{5... | collective-permute-start | bytes 1474568 | tf_op jit(solution)/shard_map/ppermute | solution.py:282
  30.3 11.8 %collective-permute-start.12 = (bf16[5,192,256]{2,1,0:T(8,128)(2,1)S(1)}, bf16[5,192,256]{2,1,0:T(8,128)(2,1)}, u32[]{:S(2)}, u32[]{:S(2)}) collective-permute-start(bf16[5,192,256]{2,1,0:T(8,128)(2,1)S(1)} %collective-permute-done.2.refs_8_), channel_id=1, source_target_pairs={{0,4},{4,0},{8,12},{12,8},{16,20},{20,16},{24,28},{28,24},{1,5},{5... | collective-permute-start | bytes 1474568 | tf_op jit(solution)/shard_map/ppermute | solution.py:282
  36.3 17.2 %collective-permute-start.4 = (bf16[160,1664]{1,0:T(8,128)(2,1)S(1)}, bf16[160,1664]{1,0:T(8,128)(2,1)S(1)}, u32[]{:S(2)}, u32[]{:S(2)}) collective-permute-start(bf16[160,1664]{1,0:T(8,128)(2,1)S(1)} %copy-done.17), channel_id=1, source_target_pairs={{0,1},{1,0},{2,3},{3,2},{4,5},{5,4},{6,7},{7,6},{8,9},{9,8},{10,11... | collective-permute-start | bytes 1597448 | tf_op jit(solution)/shard_map/ppermute | solution.py:285
  42.1 12.3 %collective-permute-start.13 = (bf16[160,1664]{1,0:T(8,128)(2,1)S(1)}, bf16[160,1664]{1,0:T(8,128)(2,1)S(1)}, u32[]{:S(2)}, u32[]{:S(2)}) collective-permute-start(bf16[160,1664]{1,0:T(8,128)(2,1)S(1)} %copy-done.17), channel_id=1, source_target_pairs={{0,8},{4,12},{8,0},{12,4},{16,24},{20,28},{24,16},{28,20},{1,9},{5... | collective-permute-start | bytes 1597448 | tf_op jit(solution)/shard_map/ppermute | solution.py:282
  42.6 10.9 %collective-permute-start.14 = (bf16[5,192,256]{2,1,0:T(8,128)(2,1)S(1)}, bf16[5,192,256]{2,1,0:T(8,128)(2,1)S(1)}, u32[]{:S(2)}, u32[]{:S(2)}) collective-permute-start(bf16[5,192,256]{2,1,0:T(8,128)(2,1)S(1)} %collective-permute-done.6.refs_6_), channel_id=1, source_target_pairs={{0,16},{4,20},{8,24},{12,28},{16,0},{20,4},{24,8},{28,12},{1,17},{... | collective-permute-start | bytes 1474568 | tf_op jit(solution)/shard_map/ppermute | solution.py:282
  43.2 10.3 %collective-permute-start.15 = (bf16[5,192,256]{2,1,0:T(8,128)(2,1)}, bf16[5,192,256]{2,1,0:T(8,128)(2,1)S(1)}, u32[]{:S(2)}, u32[]{:S(2)}) collective-permute-start(bf16[5,192,256]{2,1,0:T(8,128)(2,1)} %collective-permute-done.7.refs_7_), channel_id=1, source_target_pairs={{0,4},{4,0},{8,12},{12,8},{16,20},{20,16},{24,28},{28,24},{1,5},{5... | collective-permute-start | bytes 1474568 | tf_op jit(solution)/shard_map/ppermute | solution.py:282
  43.2 10.3 %collective-permute-start.16 = (bf16[5,192,256]{2,1,0:T(8,128)(2,1)}, bf16[5,192,256]{2,1,0:T(8,128)(2,1)S(1)}, u32[]{:S(2)}, u32[]{:S(2)}) collective-permute-start(bf16[5,192,256]{2,1,0:T(8,128)(2,1)} %collective-permute-done.3.refs_9_), channel_id=1, source_target_pairs={{0,4},{4,0},{8,12},{12,8},{16,20},{20,16},{24,28},{28,24},{1,5},{5... | collective-permute-start | bytes 1474568 | tf_op jit(solution)/shard_map/ppermute | solution.py:282
  54.3 11.5 %collective-permute-start.17 = (bf16[160,1664]{1,0:T(8,128)(2,1)S(1)}, bf16[160,1664]{1,0:T(8,128)(2,1)S(1)}, u32[]{:S(2)}, u32[]{:S(2)}) collective-permute-start(bf16[160,1664]{1,0:T(8,128)(2,1)S(1)} %collective-permute-done.4.refs_1_), channel_id=1, source_target_pairs={{0,8},{4,12},{8,0},{12,4},{16,24},{20,28},{24,16},{28,20},{1,9},{5... | collective-permute-start | bytes 1597448 | tf_op jit(solution)/shard_map/ppermute | solution.py:282
  55.1 10.0 %collective-permute-start.18 = (bf16[5,192,256]{2,1,0:T(8,128)(2,1)}, bf16[5,192,256]{2,1,0:T(8,128)(2,1)S(1)}, u32[]{:S(2)}, u32[]{:S(2)}) collective-permute-start(bf16[5,192,256]{2,1,0:T(8,128)(2,1)} %collective-permute-done.7.refs_7_), channel_id=1, source_target_pairs={{0,16},{4,20},{8,24},{12,28},{16,0},{20,4},{24,8},{28,12},{1,17},{... | collective-permute-start | bytes 1474568 | tf_op jit(solution)/shard_map/ppermute | solution.py:282
  55.6 10.2 %collective-permute-start.20 = (bf16[5,192,256]{2,1,0:T(8,128)(2,1)S(1)}, bf16[5,192,256]{2,1,0:T(8,128)(2,1)S(1)}, u32[]{:S(2)}, u32[]{:S(2)}) collective-permute-start(bf16[5,192,256]{2,1,0:T(8,128)(2,1)S(1)} %collective-permute-done.14.refs_10_), channel_id=1, source_target_pairs={{0,4},{4,0},{8,12},{12,8},{16,20},{20,16},{24,28},{28,24},{1,5},{5... | collective-permute-start | bytes 1474568 | tf_op jit(solution)/shard_map/ppermute | solution.py:282
  65.1 14.3 %collective-permute-start.23 = (bf16[5,384,128]{2,1,0:T(8,128)(2,1)S(1)}, bf16[5,384,128]{2,1,0:T(8,128)(2,1)S(1)}, u32[]{:S(2)}, u32[]{:S(2)}) collective-permute-start(bf16[5,384,128]{2,1,0:T(8,128)(2,1)S(1)} %maximum_select_fusion.near_ref), channel_id=1, source_target_pairs={{0,16},{4,20},{8,24},{12,28},{16,0},{20,4},{24,8},{28,12},{1,17},{... | collective-permute-start | bytes 1474568 | tf_op jit(solution)/shard_map/ppermute | solution.py:282
  65.8 13.6 %collective-permute-start.22 = (bf16[5,384,128]{2,1,0:T(8,128)(2,1)S(1)}, bf16[5,384,128]{2,1,0:T(8,128)(2,1)S(1)}, u32[]{:S(2)}, u32[]{:S(2)}) collective-permute-start(bf16[5,384,128]{2,1,0:T(8,128)(2,1)S(1)} %maximum_select_fusion.1), channel_id=1, source_target_pairs={{0,8},{4,12},{8,0},{12,4},{16,24},{20,28},{24,16},{28,20},{1,9},{5... | collective-permute-start | bytes 1474568 | tf_op jit(solution)/shard_map/ppermute | solution.py:282
  79.8 13.3 %collective-permute-start.27 = (bf16[5,384,128]{2,1,0:T(8,128)(2,1)S(1)}, bf16[5,384,128]{2,1,0:T(8,128)(2,1)S(1)}, u32[]{:S(2)}, u32[]{:S(2)}) collective-permute-start(bf16[5,384,128]{2,1,0:T(8,128)(2,1)S(1)} %collective-permute-done.22.far_ref), channel_id=1, source_target_pairs={{0,16},{4,20},{8,24},{12,28},{16,0},{20,4},{24,8},{28,12},{1,17},{... | collective-permute-start | bytes 1474568 | tf_op jit(solution)/shard_map/ppermute | solution.py:282
  81.3 14.6 %collective-permute-start.26 = (bf16[5,384,128]{2,1,0:T(8,128)(2,1)S(1)}, bf16[5,384,128]{2,1,0:T(8,128)(2,1)S(1)}, u32[]{:S(2)}, u32[]{:S(2)}) collective-permute-start(bf16[5,384,128]{2,1,0:T(8,128)(2,1)S(1)} %collective-permute-done.23.near_ref), channel_id=1, source_target_pairs={{0,4},{4,0},{8,12},{12,8},{16,20},{20,16},{24,28},{28,24},{1,5},{5... | collective-permute-start | bytes 1474568 | tf_op jit(solution)/shard_map/ppermute | solution.py:282
  (45 other events, 261.1 us)

commit v5 on v4

--- a/solution.py
+++ b/solution.py
@@ -20,6 +20,10 @@
 
 def after(values, *others):
     return lax.optimization_barrier((values, *others))[0]
+
+
+def after_all(values, *others):
+    return lax.optimization_barrier((*values, *others))[: len(values)]
 
 
 def swap_blocks(values, index, blocks):
@@ -61,7 +65,8 @@
     logits_ref,
     placed_ref,
     stream_ref,
-    sent_ref,
+    head_ref,
+    tail_ref,
     keep_ref,
 ):
     step = pl.program_id(0)
@@ -77,7 +82,10 @@
     @pl.when(step == pl.num_programs(0) - 1)
     def _():
         normed = normalize(keep_ref[...], gain_ref[...])
-        sent_ref[:, :width] = swap_lanes(normed, place_ref[4], rows).astype(jnp.bfloat16)
+        moved = swap_lanes(normed, place_ref[4], rows).astype(jnp.bfloat16)
+        half = width // 2
+        head_ref[:, :half] = moved[:, :half]
+        tail_ref[...] = moved[:, half:]
         scores = jnp.exp(logits_ref[...].astype(jnp.float32) * LOGIT_SCALE)
         gates = scores / jnp.sum(scores, axis=1, keepdims=True)
         routes = routes_ref[...]
@@ -87,7 +95,7 @@
             spread = jnp.where(hit, gates[:, k : k + 1], spread)
         high = spread.astype(jnp.bfloat16).astype(jnp.float32)
         lane = lax.broadcasted_iota(jnp.int32, spread.shape, 1)
-        sent_ref[:, width:] = jnp.where(lane < LOW, high, spread - high).astype(jnp.bfloat16)
+        head_ref[:, half:] = jnp.where(lane < LOW, high, spread - high).astype(jnp.bfloat16)
 
 
 def front_call(place, rows, attended, residual, weight, gain, routes, logits, placement):
@@ -113,13 +121,15 @@
             ],
             out_specs=[
                 pl.BlockSpec((tok, cols), lambda i, p: (0, i)),
-                whole((tok, width + LANES)),
+                whole((tok, width // 2 + LANES)),
+                whole((tok, width // 2)),
             ],
             scratch_shapes=[pltpu.VMEM((tok, width), jnp.float32)],
         ),
         out_shape=[
             jax.ShapeDtypeStruct((tok, width), jnp.bfloat16),
-            jax.ShapeDtypeStruct((tok, width + LANES), jnp.bfloat16),
+            jax.ShapeDtypeStruct((tok, width // 2 + LANES), jnp.bfloat16),
+            jax.ShapeDtypeStruct((tok, width // 2), jnp.bfloat16),
         ],
         compiler_params=pltpu.CompilerParams(vmem_limit_bytes=24 * 1024 * 1024),
         name="front",
@@ -153,64 +163,70 @@
     )(place, weight)
 
 
-def up_kernel(rows, blocks, place_ref, *refs):
-    parts, pieces = refs[:blocks], refs[blocks : blocks + 2 * QUAD * rows]
-    out_ref, x_ref = refs[blocks + 2 * QUAD * rows :]
-    side, core, zone, local = (place_ref[i] for i in range(4))
-    expert = pl.program_id(0)
-    width = out_ref.shape[1]
+def up_kernel(rows, heads, tails, tok, place_ref, *refs):
+    head, tail = refs[:heads], refs[heads : heads + tails]
+    pieces = refs[heads + tails : heads + tails + 2 * QUAD * rows]
+    out_ref, x_ref = refs[heads + tails + 2 * QUAD * rows :]
+    side, core, zone = (place_ref[i] for i in range(3))
+    local, _, width = pieces[0].shape
     part = width // 2
-
-    @pl.when(expert == 0)
-    def _():
-        at = 0
-        for block in parts:
-            x_ref[at : at + block.shape[0], :] = block[...]
-            at += block.shape[0]
-
-    def ordered(group):
+    half = tail[0].shape[1]
+    blocks = x_ref.shape[0] // tok
+
+    at = 0
+    for block in head:
+        some = slice(at, at + block.shape[0])
+        x_ref[some, :half] = block[:, :half]
+        x_ref[some, 2 * half :] = block[:, half:]
+        at += block.shape[0]
+    at = 0
+    for block in tail:
+        for i in range(block.shape[0] // tok):
+            to = (at % 2) * (blocks // 2) + at // 2
+            x_ref[to * tok : (to + 1) * tok, half : 2 * half] = block[i * tok : (i + 1) * tok, :]
+            at += 1
+
+    def ordered(group, e):
         order = []
         for m in range(rows):
-            own, mate, own_x, mate_x = (group[QUAD * m + i][0] for i in range(QUAD))
+            own, mate, own_x, mate_x = (group[QUAD * m + i][e] for i in range(QUAD))
             near = [jnp.where(core == 0, own, mate), jnp.where(core == 0, mate, own)]
             far = [jnp.where(core == 0, own_x, mate_x), jnp.where(core == 0, mate_x, own_x)]
             order += [jnp.where(side == 0, a, b) for a, b in zip(near + far, far + near)]
         return jnp.concatenate(order, axis=0)
 
-    mine, other = ordered(pieces[: QUAD * rows]), ordered(pieces[QUAD * rows :])
-    w = jnp.concatenate(
-        [mine[:, :part], other[:, :part], mine[:, part:], other[:, part:]], axis=1
-    )
-    feats = x_ref.shape[1] - LANES
     lane = lax.broadcasted_iota(jnp.int32, (LANES, width), 0)
-    slot = zone * local + expert
-    pick = jnp.where((lane == slot) | (lane == slot + LOW), 1.0, 0.0).astype(jnp.bfloat16)
-    acc = jnp.dot(x_ref[:, :feats], w, preferred_element_type=jnp.float32)
-    gate = jnp.dot(x_ref[:, feats:], pick, preferred_element_type=jnp.float32)
-    g, u = acc[:, :width], acc[:, width:]
-    out_ref[...] = (g / (1.0 + jnp.exp(-g)) * u * gate).astype(jnp.bfloat16)
-
-
-def up_call(place, parts, mine, other):
-    rows = len(mine) // QUAD
-    local, depth, cols = mine[0].shape
-    tokens, lanes = sum(v.shape[0] for v in parts), parts[0].shape[1]
-    piece = pl.BlockSpec((1, depth, cols), lambda e, p: (e, 0, 0))
+    for e in range(local):
+        mine, other = ordered(pieces[: QUAD * rows], e), ordered(pieces[QUAD * rows :], e)
+        w = jnp.concatenate(
+            [mine[:, :part], other[:, :part], mine[:, part:], other[:, part:]], axis=1
+        )
+        slot = zone * local + e
+        pick = jnp.where((lane == slot) | (lane == slot + LOW), 1.0, 0.0).astype(jnp.bfloat16)
+        acc = jnp.dot(x_ref[:, : 2 * half], w, preferred_element_type=jnp.float32)
+        gate = jnp.dot(x_ref[:, 2 * half :], pick, preferred_element_type=jnp.float32)
+        g, u = acc[:, :width], acc[:, width:]
+        out_ref[:, e * width : (e + 1) * width] = (
+            g / (1.0 + jnp.exp(-g)) * u * gate
+        ).astype(jnp.bfloat16)
+
+
+def up_call(place, tok, head, tail, mine, other):
+    local, _, cols = mine[0].shape
+    tokens = sum(v.shape[0] for v in head)
+    lanes = head[0].shape[1] + tail[0].shape[1]
+    count = len(head) + len(tail) + len(mine) + len(other)
     return pl.pallas_call(
-        functools.partial(up_kernel, rows, len(parts)),
-        grid_spec=pltpu.PrefetchScalarGridSpec(
-            num_scalar_prefetch=1,
-            grid=(local,),
-            in_specs=[pl.BlockSpec(v.shape, lambda e, p: (0, 0)) for v in parts]
-            + [piece] * (2 * len(mine)),
-            out_specs=pl.BlockSpec((tokens, cols), lambda e, p: (0, e)),
-            scratch_shapes=[pltpu.VMEM((tokens, lanes), jnp.bfloat16)],
-        ),
+        functools.partial(up_kernel, len(mine) // QUAD, len(head), len(tail), tok),
+        in_specs=[pl.BlockSpec(memory_space=pltpu.SMEM)]
+        + [pl.BlockSpec(memory_space=pltpu.VMEM)] * count,
+        out_specs=pl.BlockSpec(memory_space=pltpu.VMEM),
+        scratch_shapes=[pltpu.VMEM((tokens, lanes), jnp.bfloat16)],
         out_shape=jax.ShapeDtypeStruct((tokens, local * cols), jnp.bfloat16),
         compiler_params=pltpu.CompilerParams(vmem_limit_bytes=48 * 1024 * 1024),
         cost_estimate=pl.CostEstimate(flops=1, bytes_accessed=1, transcendentals=0),
         name="up",
-    )(place, *parts, *mine, *other)
+    )(place, *head, *tail, *mine, *other)
 
 
 def down_kernel(start, place_ref, h_ref, near_ref, near_other_ref, far_ref, far_other_ref, *out_refs):
@@ -231,23 +247,19 @@
         if len(out_refs) == 2:
             out_refs[j][...] = partial.astype(out_refs[j].dtype)
         else:
-            out_refs[0][:, j * feats : (j + 1) * feats] = partial
-
-
-def down_call(place, hidden, near, far, send):
+            out_refs[0][:, j * feats : (j + 1) * feats] = partial.astype(out_refs[0].dtype)
+
+
+def down_call(place, hidden, near, far, send, parts):
     tokens = hidden.shape[0] // 2
-    feats = near[0].shape[1]
-    if send:
-        out = [jax.ShapeDtypeStruct((tokens, feats), jnp.bfloat16)] * 2
-    else:
-        out = jax.ShapeDtypeStruct((tokens, 2 * feats), jnp.float32)
+    feats = 2 * near[0].shape[1] // parts
+    kind = jnp.bfloat16 if send else jnp.float32
+    out = [jax.ShapeDtypeStruct((tokens, feats), kind)] * parts
     return pl.pallas_call(
         functools.partial(down_kernel, tokens if send else 0),
         in_specs=[pl.BlockSpec(memory_space=pltpu.SMEM)]
         + [pl.BlockSpec(memory_space=pltpu.VMEM)] * 5,
-        out_specs=[pl.BlockSpec(memory_space=pltpu.VMEM)] * 2
-        if send
-        else pl.BlockSpec(memory_space=pltpu.VMEM),
+        out_specs=[pl.BlockSpec(memory_space=pltpu.VMEM)] * parts,
         out_shape=out,
         compiler_params=pltpu.CompilerParams(vmem_limit_bytes=40 * 1024 * 1024),
         cost_estimate=pl.CostEstimate(flops=1, bytes_accessed=1, transcendentals=0),
@@ -298,17 +310,23 @@
     place = jnp.stack([side, core, zone, jnp.int32(local), row]).astype(jnp.int32)
 
     gu_own, gu_away, gu_to_mate, gu_to_mate_away = cut_call(place, gate_up, part)
-    stored, sent = front_call(
+    stored, head, tail = front_call(
         place, rows, after(attended, gu_own), residual, out_weight, norm_gain, routes, gate_logits, placement
     )
     stream_in = stored.astype(jnp.float32)
     gu_own_x = flip(gu_away, 2)
     first = widen([gu_own])
     gu_mate, gu_mate_away = flip(gu_to_mate, 1), flip(gu_to_mate_away, 1)
-    gu_mate_x = flip(after(gu_mate_away, gu_own_x, first[-1]), 2)
-    second = widen([after(gu_mate, first[-1], sent)])
-    third = widen([after(gu_own_x, second[-1])])
-    fourth = widen([after(gu_mate_x, third[-1])])
+    gu_mate_x = flip(gu_mate_away, 2)
+    near = after(head, gu_mate, gu_mate_away)
+    second = widen([after(gu_mate, head)])
+    hops = []
+    for bit in zone_bits[:-1]:
+        hops.append(hop(near, bit))
+        near = jnp.concatenate([near, hops[-1]], axis=0)
+    gu_own_x, *first[1:] = after_all([gu_own_x, *first[1:]], hops[0])
+    third = widen([gu_own_x])
+    fourth = widen([after(gu_mate_x, second[-1])])
     mine = [p for group in zip(first, second, third, fourth) for p in group]
     shared = [flip(gu_own, 1), flip(gu_own_x, 1), flip(gu_mate_x, 1)]
     firsts, seconds, thirds, fourths = (
@@ -318,7 +336,9 @@
     for group in zip(seconds, firsts, fourths, thirds):
         other += group
 
-    dn_own, dn_away, dn_to_mate, dn_to_mate_away = cut_call(place, after(down_weight, first[-1]), part)
+    dn_own, dn_away, dn_to_mate, dn_to_mate_away = cut_call(
+        place, after(down_weight, first[-1]), part
+    )
     dn_mate, dn_mate_away = flip(dn_to_mate, 1), flip(dn_to_mate_away, 1)
 
     def pair(own, mate):
@@ -330,44 +350,40 @@
 
     dn_near = pair(dn_own, dn_mate)
     dn_away = pair(dn_away, dn_mate_away)
-    near = sent
+
+    both = jnp.concatenate([tail, flip(tail, 2)], axis=0)
     for bit in zone_bits[:-1]:
-        near = jnp.concatenate([near, hop(near, bit)], axis=0)
-    far = hop(after(near, second[-1]), zone_bits[-1])
-    near_x = flip(
-        after(near, gu_mate_x, second[-1], dn_near, dn_away, shared[0], shared[1], *firsts), 2
-    )
-    far_x = flip(after(far, near_x, third[-1], shared[2], *seconds), 2)
+        received = hop(after(both, hops[0]), bit)
+        both = jnp.concatenate([both, received], axis=0)
+    both_far = hop(both, zone_bits[-1])
+
+    far = hop(after(near, second[-1], gu_mate_x), zone_bits[-1])
+    near_x = flip(after(near, second[-1], received, shared[0], shared[1], *firsts), 2)
+    far_x = flip(after(far, near_x, third[-1], dn_near, dn_away, shared[2], *seconds), 2)
+
     dn_far = flip(after(dn_away, far_x, *thirds), 2)
-    hidden = up_call(place, [near, far, near_x, far_x], mine, other)
-    dn_nears = widen([after(dn_near, fourth[-1])])
-    dn_fars = widen([after(dn_far, dn_nears[-1])])
+
+    hidden = up_call(place, tok, [near, far, near_x, far_x], [both, both_far], mine, other)
+    dn_nears = widen([after(dn_near, third[-1])])
+    hidden = after(hidden, dn_nears[-1])
+    dn_fars = widen([after(dn_far, fourth[-1])])
     dn_nears = [(v, flip(after(v, hidden), 1)) for v in dn_nears]
     dn_fars = [(v, flip(after(v, hidden), 1)) for v in dn_fars]
 
-    sums = []
+    chunks, crossed = [], None
     for m in range(rows):
-        ready = after(hidden, *(v[1] for v in sums[-2:-1]))
-        sends = down_call(place, ready, dn_nears[m], dn_fars[m], True)
-        keep = down_call(place, after(hidden, sends[0]), dn_nears[m], dn_fars[m], False)
-        feats = keep.shape[1] // 2
-        for j in range(2):
-            crossed = flip(after(sends[j], *(v[1] for v in sums[-1:])), 2)
-            sums.append((keep[:, j * feats : (j + 1) * feats], crossed))
-    merged = [
-        (jnp.concatenate([a[0], b[0]], axis=1), jnp.concatenate([a[1], b[1]], axis=1))
-        for a, b in zip(sums[:-2:2], sums[1:-2:2])
-    ]
-    chunks = []
-    for i, (total, crossed) in enumerate(merged + sums[-2:]):
-        total = total + crossed.astype(jnp.float32)
-        for bit in reversed(zone_bits):
-            size = total.shape[0] // 2
-            moved = total[size:].astype(jnp.bfloat16)
-            if i < len(merged) and bit == zone_bits[0]:
-                moved = after(moved, sums[-2][1])
-            total = total[:size] + hop(moved, bit).astype(jnp.float32)
-        chunks.append(total)
+        parts = 2 if m == rows - 1 else 1
+        ready = hidden if crossed is None else after(hidden, crossed)
+        sends = down_call(place, ready, dn_nears[m], dn_fars[m], True, parts)
+        keeps = down_call(place, after(hidden, sends[0]), dn_nears[m], dn_fars[m], False, parts)
+        for send, keep in zip(sends, keeps):
+            crossed = flip(send, 2)
+            total = keep + crossed.astype(jnp.float32)
+            for bit in reversed(zone_bits):
+                size = total.shape[0] // 2
+                moved = total[size:].astype(jnp.bfloat16)
+                total = total[:size] + hop(moved, bit).astype(jnp.float32)
+            chunks.append(total)
     branch = swap_blocks(jnp.concatenate(chunks, axis=1), row, rows)
     total = stream_in + branch
     return (total.astype(jnp.bfloat16), normalize(total, final_gain).astype(jnp.bfloat16))

time: 135 us -> 137 us (1.015)
  starting transfers between devices: 36.4 us -> 43.6 us
  local copies, waits for them, and re-layouts: 12.9 us -> 10.6 us
  waiting for transfers between devices: 55.5 us -> 53.6 us
    ppermute x30, waiting for transfers between devices: 37.9 us -> 27.6 us  [flip(): return lax.ppermute(values, 'dp', [(i, i ^ bit) for i in range(ranks)])]
    ppermute x8 -> x10, waiting for transfers between devices: 17.7 us -> 26.1 us  [hop(): return lax.ppermute(values, 'expert', [(i, i ^ bit) for i in range(zones)])]
    ppermute x30, starting transfers between devices: 18.5 us -> 23.3 us  [flip(): return lax.ppermute(values, 'dp', [(i, i ^ bit) for i in range(ranks)])]
    ppermute x8 -> x10, starting transfers between devices: 17.9 us -> 20.3 us  [hop(): return lax.ppermute(values, 'expert', [(i, i ^ bit) for i in range(zones)])]
    concatenate x1 -> x2, local copies, waits for them, and re-layouts: 1.67 us -> 0.04 us  [the longest x1 0.02 us: body(): near = jnp.concatenate([near, hops[-1]], axis=0)]
    unnamed x65 -> x55, local copies, waits for them, and re-layouts: 10.3 us -> 9.66 us
  transfers between devices with their start and end apart: 38 -> 40, of which waited for: 16 -> 17; matrix products, arithmetic and copies ran while one was open for 6% -> 4% of each run, Pallas kernels for 15% -> 15%
where the time goes in v5:
time: 137 us
  waiting for transfers between devices  53.6 us (39%)
  starting transfers between devices  43.6 us (32%)
  Pallas kernels  22.5 us (16%)
  local copies, waits for them, and re-layouts  10.6 us (8%)
  other arithmetic  5.3 us (4%)
    ppermute x30, waiting for transfers between devices, flip(): return lax.ppermute(values, 'dp', [(i, i ^ bit) for i in range(ranks)])  27.6 us
    ppermute x10, waiting for transfers between devices, hop(): return lax.ppermute(values, 'expert', [(i, i ^ bit) for i in range(zones)])  26.1 us
    ppermute x30, starting transfers between devices, flip(): return lax.ppermute(values, 'dp', [(i, i ^ bit) for i in range(ranks)])  23.3 us
    ppermute x10, starting transfers between devices, hop(): return lax.ppermute(values, 'expert', [(i, i ^ bit) for i in range(zones)])  20.3 us
    pallas_call x1, Pallas kernels, up_call(): pl.pallas_call(functools.partial(up_kernel, len(mine) // QUAD, len(head),...  9.75 us
    unnamed x55, local copies, waits for them, and re-layouts  9.66 us
    pallas_call x4, Pallas kernels, down_call(): pl.pallas_call(functools.partial(down_kernel, tokens if send else 0), in_...  7.25 us
    pallas_call x1, Pallas kernels, front_call(): pl.pallas_call(functools.partial(front_kernel, rows), grid_spec=pltpu.Pre...  2.91 us
  transfers between devices with their start and end apart: 40, of which 17 were waited for; matrix products, arithmetic and copies ran while one was open for 4% of the time, Pallas kernels for 15%

profile of v5, /device:TPU:0, one launch (start us, length us, event | category | flops | bytes accessed | tf_op | source)
XLA Modules:
  0.0 136.7 jit_solution(4907229381197125077)
XLA Ops:
  4.7 2.9 %collective-permute-start.9 = (bf16[5,192,256]{2,1,0:T(8,128)(2,1)}, bf16[5,192,256]{2,1,0:T(8,128)(2,1)S(1)}, u32[]{:S(2)}, u32[]{:S(2)}) collective-permute-start(bf16[5,192,256]{2,1,0:T(8,128)(2,1)} %get-tuple-element.50), channel_id=1, source_target_pairs={{0,8},{4,12},{8,0},{12,4},{16,24},{20,28},{24,16},{28,20},{1,9},{5... | collective-permute-start | bytes 1474568 | tf_op jit(solution)/shard_map/ppermute | solution.py:294
  10.1 2.3 %copy-done.2 = bf16[1536,1536]{1,0:T(8,128)(2,1)S(1)} copy-done((bf16[1536,1536]{1,0:T(8,128)(2,1)S(1)}, bf16[1536,1536]{1,0:T(8,128)(2,1)}, u32[]{:S(2)}) %copy-start.2) | copy-done | bytes 4718616
  13.4 2.9 %front.1 = (bf16[80,1536]{1,0:T(8,128)(2,1)S(1)}, bf16[80,896]{1,0:T(8,128)(2,1)S(1)}, bf16[80,768]{1,0:T(8,128)(2,1)S(1)}) custom-call(s32[5]{0:T(128)S(1)} %stack.19.place_ref, bf16[80,1536]{1,0:T(8,128)(2,1)S(1)} %copy-done.8, bf16[80,1536]{1,0:T(8,128)(2,1)S(1)} %copy-done.9, bf16[1536,1536]{1,0:T(8,128)(2,1)S(1)} %copy-done.2, ...), custom_call_target="tpu_custom_call" | custom-call | tf_op jit(solution)/shard_map/front/pallas_call | solution.py:108
  17.9 2.0 %collective-permute-done.9.refs_8_ = bf16[5,192,256]{2,1,0:T(8,128)(2,1)S(1)} collective-permute-done((bf16[5,192,256]{2,1,0:T(8,128)(2,1)}, bf16[5,192,256]{2,1,0:T(8,128)(2,1)S(1)}, u32[]{:S(2)}, u32[]{:S(2)}) %collective-permute-start.9) | collective-permute-done | bytes 491552 | tf_op jit(solution)/shard_map/ppermute | solution.py:294
  19.9 3.2 %collective-permute-start.2 = (bf16[80,896]{1,0:T(8,128)(2,1)S(1)}, bf16[80,896]{1,0:T(8,128)(2,1)S(1)}, u32[]{:S(2)}, u32[]{:S(2)}) collective-permute-start(bf16[80,896]{1,0:T(8,128)(2,1)S(1)} %get-tuple-element.45), channel_id=1, source_target_pairs={{0,2},{1,3},{2,0},{3,1},{4,6},{5,7},{6,4},{7,5},{8,10},{9,11},{10,... | collective-permute-start | bytes 430088 | tf_op jit(solution)/shard_map/ppermute | solution.py:297
  24.5 3.8 %collective-permute-done.2 = bf16[80,896]{1,0:T(8,128)(2,1)S(1)} collective-permute-done((bf16[80,896]{1,0:T(8,128)(2,1)S(1)}, bf16[80,896]{1,0:T(8,128)(2,1)S(1)}, u32[]{:S(2)}, u32[]{:S(2)}) %collective-permute-start.2) | collective-permute-done | bytes 143392 | tf_op jit(solution)/shard_map/ppermute | solution.py:297
  28.3 4.1 %collective-permute-done.6 = bf16[80,768]{1,0:T(8,128)(2,1)S(1)} collective-permute-done((bf16[80,768]{1,0:T(8,128)(2,1)S(1)}, bf16[80,768]{1,0:T(8,128)(2,1)S(1)}, u32[]{:S(2)}, u32[]{:S(2)}) %collective-permute-start.6) | collective-permute-done | bytes 122912 | tf_op jit(solution)/shard_map/ppermute | solution.py:294
  32.4 2.9 %collective-permute-start.7 = (bf16[160,768]{1,0:T(8,128)(2,1)S(1)}, bf16[160,768]{1,0:T(8,128)(2,1)S(1)}, u32[]{:S(2)}, u32[]{:S(2)}) collective-permute-start(bf16[160,768]{1,0:T(8,128)(2,1)S(1)} %pad_maximum_fusion), channel_id=1, source_target_pairs={{0,2},{1,3},{2,0},{3,1},{4,6},{5,7},{6,4},{7,5},{8,10},{9,11},{10,... | collective-permute-start | bytes 737288 | tf_op jit(solution)/shard_map/ppermute | solution.py:297
  38.3 8.9 %collective-permute-done.7 = bf16[160,768]{1,0:T(8,128)(2,1)S(1)} collective-permute-done((bf16[160,768]{1,0:T(8,128)(2,1)S(1)}, bf16[160,768]{1,0:T(8,128)(2,1)S(1)}, u32[]{:S(2)}, u32[]{:S(2)}) %collective-permute-start.7) | collective-permute-done | bytes 245792 | tf_op jit(solution)/shard_map/ppermute | solution.py:297
  52.7 3.2 %collective-permute-done.5.refs_1_ = bf16[160,896]{1,0:T(8,128)(2,1)} collective-permute-done((bf16[160,896]{1,0:T(8,128)(2,1)S(1)}, bf16[160,896]{1,0:T(8,128)(2,1)}, u32[]{:S(2)}, u32[]{:S(2)}) %collective-permute-start.5) | collective-permute-done | bytes 286752 | tf_op jit(solution)/shard_map/ppermute | solution.py:297
  61.6 2.7 %collective-permute-done.21.refs_13_ = bf16[5,192,256]{2,1,0:T(8,128)(2,1)S(1)} collective-permute-done((bf16[5,192,256]{2,1,0:T(8,128)(2,1)}, bf16[5,192,256]{2,1,0:T(8,128)(2,1)S(1)}, u32[]{:S(2)}, u32[]{:S(2)}) %collective-permute-start.21) | collective-permute-done | bytes 491552 | tf_op jit(solution)/shard_map/ppermute | solution.py:294
  65.9 2.5 %collective-permute-done.19.refs_3_ = bf16[160,896]{1,0:T(8,128)(2,1)S(1)} collective-permute-done((bf16[160,896]{1,0:T(8,128)(2,1)}, bf16[160,896]{1,0:T(8,128)(2,1)S(1)}, u32[]{:S(2)}, u32[]{:S(2)}) %collective-permute-start.19) | collective-permute-done | bytes 286752 | tf_op jit(solution)/shard_map/ppermute | solution.py:294
  69.8 4.0 %collective-permute-done.20.refs_5_ = bf16[320,768]{1,0:T(8,128)(2,1)S(1)} collective-permute-done((bf16[320,768]{1,0:T(8,128)(2,1)S(1)}, bf16[320,768]{1,0:T(8,128)(2,1)S(1)}, u32[]{:S(2)}, u32[]{:S(2)}) %collective-permute-start.20) | collective-permute-done | bytes 491552 | tf_op jit(solution)/shard_map/ppermute | solution.py:297
  75.7 9.7 %up.1.h_ref = bf16[640,1280]{1,0:T(8,128)(2,1)} custom-call(s32[5]{0:T(128)S(1)} %stack.19.place_ref, bf16[160,896]{1,0:T(8,128)(2,1)S(1)} %constant_dynamic-update-slice_fusion.refs_0_, bf16[160,896]{1,0:T(8,128)(2,1)} %collective-permute-done.5.refs_1_, bf16[160,896]{1,0:T(8,128)(2,1)} %collective-permute-done.13.refs_2_, ...), custom_call_target="tpu_custom_call" | custom-call | flops 1 | bytes 1 | tf_op jit(solution)/shard_map/up/pallas_call | solution.py:219
  91.7 7.5 %collective-permute-done.30.far_ref = bf16[5,384,128]{2,1,0:T(8,128)(2,1)S(1)} collective-permute-done((bf16[5,384,128]{2,1,0:T(8,128)(2,1)S(1)}, bf16[5,384,128]{2,1,0:T(8,128)(2,1)S(1)}, u32[]{:S(2)}, u32[]{:S(2)}) %collective-permute-start.30) | collective-permute-done | bytes 491552 | tf_op jit(solution)/shard_map/ppermute | solution.py:294
  100.7 3.6 %collective-permute-done.28 = bf16[320,768]{1,0:T(8,128)(2,1)S(1)} collective-permute-done((bf16[320,768]{1,0:T(8,128)(2,1)S(1)}, bf16[320,768]{1,0:T(8,128)(2,1)S(1)}, u32[]{:S(2)}, u32[]{:S(2)}) %collective-permute-start.28) | collective-permute-done | bytes 491552 | tf_op jit(solution)/shard_map/ppermute | solution.py:294
  107.1 2.1 %down.5 = (bf16[320,384]{1,0:T(8,128)(2,1)S(1)}, bf16[320,384]{1,0:T(8,128)(2,1)S(1)}) custom-call(s32[5]{0:T(128)S(1)} %stack.19.place_ref, bf16[640,1280]{1,0:T(8,128)(2,1)S(1)} %copy-done.1, bf16[5,384,128]{2,1,0:T(8,128)(2,1)S(1)} %collective-permute-done.24.near_ref, bf16[5,384,128]{2,1,0:T(8,128)(2,1)S(1)} %collective-permute-done.29.near_other_ref, ...), custom_call_target="tpu_custom_call" | custom-call | flops 1 | bytes 1 | tf_op jit(solution)/shard_map/down/pallas_call | solution.py:258
  111.3 2.1 %down.6 = (f32[320,384]{1,0:T(8,128)S(1)}, f32[320,384]{1,0:T(8,128)S(1)}) custom-call(s32[5]{0:T(128)S(1)} %stack.19.place_ref, bf16[640,1280]{1,0:T(8,128)(2,1)S(1)} %copy-done.1, bf16[5,384,128]{2,1,0:T(8,128)(2,1)S(1)} %collective-permute-done.24.near_ref, bf16[5,384,128]{2,1,0:T(8,128)(2,1)S(1)} %collective-permute-done.29.near_other_ref, ...), custom_call_target="tpu_custom_call" | custom-call | flops 1 | bytes 1 | tf_op jit(solution)/shard_map/down/pallas_call | solution.py:258
  114.6 3.3 %collective-permute-start.39 = (bf16[80,768]{1,0:T(8,128)(2,1)S(1)}, bf16[80,768]{1,0:T(8,128)(2,1)S(1)}, u32[]{:S(2)}, u32[]{:S(2)}) collective-permute-start(bf16[80,768]{1,0:T(8,128)(2,1)S(1)} %slice.81), channel_id=1, source_target_pairs={{0,2},{1,3},{2,0},{3,1},{4,6},{5,7},{6,4},{7,5},{8,10},{9,11},{10,... | collective-permute-start | bytes 368648 | tf_op jit(solution)/shard_map/ppermute | solution.py:297
  117.8 3.6 %collective-permute-done.35 = bf16[320,384]{1,0:T(8,128)(2,1)S(1)} collective-permute-done((bf16[320,384]{1,0:T(8,128)(2,1)S(1)}, bf16[320,384]{1,0:T(8,128)(2,1)S(1)}, u32[]{:S(2)}, u32[]{:S(2)}) %collective-permute-start.35) | collective-permute-done | bytes 245792 | tf_op jit(solution)/shard_map/ppermute | solution.py:294
  123.7 2.7 %collective-permute-done.36 = bf16[160,384]{1,0:T(8,128)(2,1)S(1)} collective-permute-done((bf16[160,384]{1,0:T(8,128)(2,1)S(1)}, bf16[160,384]{1,0:T(8,128)(2,1)S(1)}, u32[]{:S(2)}, u32[]{:S(2)}) %collective-permute-start.36) | collective-permute-done | bytes 122912 | tf_op jit(solution)/shard_map/ppermute | solution.py:297
  126.5 3.9 %collective-permute-start.37 = (bf16[80,384]{1,0:T(8,128)(2,1)S(1)}, bf16[80,384]{1,0:T(8,128)(2,1)S(1)}, u32[]{:S(2)}, u32[]{:S(2)}) collective-permute-start(bf16[80,384]{1,0:T(8,128)(2,1)S(1)} %slice.84), channel_id=1, source_target_pairs={{0,2},{1,3},{2,0},{3,1},{4,6},{5,7},{6,4},{7,5},{8,10},{9,11},{10,... | collective-permute-start | bytes 184328 | tf_op jit(solution)/shard_map/ppermute | solution.py:297
  130.4 1.9 %collective-permute-start.34 = (bf16[80,384]{1,0:T(8,128)(2,1)S(1)}, bf16[80,384]{1,0:T(8,128)(2,1)S(1)}, u32[]{:S(2)}, u32[]{:S(2)}) collective-permute-start(bf16[80,384]{1,0:T(8,128)(2,1)S(1)} %slice.85), channel_id=1, source_target_pairs={{0,2},{1,3},{2,0},{3,1},{4,6},{5,7},{6,4},{7,5},{8,10},{9,11},{10,... | collective-permute-start | bytes 184328 | tf_op jit(solution)/shard_map/ppermute | solution.py:297
  133.0 2.6 %collective-permute-done.34 = bf16[80,384]{1,0:T(8,128)(2,1)S(1)} collective-permute-done((bf16[80,384]{1,0:T(8,128)(2,1)S(1)}, bf16[80,384]{1,0:T(8,128)(2,1)S(1)}, u32[]{:S(2)}, u32[]{:S(2)}) %collective-permute-start.34) | collective-permute-done | bytes 61472 | tf_op jit(solution)/shard_map/ppermute | solution.py:297
  (146 shorter events, 47.2 us)
Async XLA Ops:
  4.6 11.6 %collective-permute-start = (bf16[5,192,256]{2,1,0:T(8,128)(2,1)S(1)}, bf16[5,192,256]{2,1,0:T(8,128)(2,1)S(1)}, u32[]{:S(2)}, u32[]{:S(2)}) collective-permute-start(bf16[5,192,256]{2,1,0:T(8,128)(2,1)S(1)} %get-tuple-element.43.refs_14_), channel_id=1, source_target_pairs={{0,4},{4,0},{8,12},{12,8},{16,20},{20,16},{24,28},{28,24},{1,5},{5... | collective-permute-start | bytes 1474568 | tf_op jit(solution)/shard_map/ppermute | solution.py:294
  4.7 15.2 %collective-permute-start.9 = (bf16[5,192,256]{2,1,0:T(8,128)(2,1)}, bf16[5,192,256]{2,1,0:T(8,128)(2,1)S(1)}, u32[]{:S(2)}, u32[]{:S(2)}) collective-permute-start(bf16[5,192,256]{2,1,0:T(8,128)(2,1)} %get-tuple-element.50), channel_id=1, source_target_pairs={{0,8},{4,12},{8,0},{12,4},{16,24},{20,28},{24,16},{28,20},{1,9},{5... | collective-permute-start | bytes 1474568 | tf_op jit(solution)/shard_map/ppermute | solution.py:294
  7.6 15.4 %collective-permute-start.10 = (bf16[5,192,256]{2,1,0:T(8,128)(2,1)S(1)}, bf16[5,192,256]{2,1,0:T(8,128)(2,1)S(1)}, u32[]{:S(2)}, u32[]{:S(2)}) collective-permute-start(bf16[5,192,256]{2,1,0:T(8,128)(2,1)S(1)} %get-tuple-element.39.refs_6_), channel_id=1, source_target_pairs={{0,16},{4,20},{8,24},{12,28},{16,0},{20,4},{24,8},{28,12},{1,17},{... | collective-permute-start | bytes 1474568 | tf_op jit(solution)/shard_map/ppermute | solution.py:294
  9.2 23.3 %collective-permute-start.8 = (bf16[5,192,256]{2,1,0:T(8,128)(2,1)S(1)}, bf16[5,192,256]{2,1,0:T(8,128)(2,1)}, u32[]{:S(2)}, u32[]{:S(2)}) collective-permute-start(bf16[5,192,256]{2,1,0:T(8,128)(2,1)S(1)} %get-tuple-element.39.refs_6_), channel_id=1, source_target_pairs={{0,4},{4,0},{8,12},{12,8},{16,20},{20,16},{24,28},{28,24},{1,5},{5... | collective-permute-start | bytes 1474568 | tf_op jit(solution)/shard_map/ppermute | solution.py:294
  9.2 26.9 %collective-permute-start.4 = (bf16[5,192,256]{2,1,0:T(8,128)(2,1)}, bf16[5,192,256]{2,1,0:T(8,128)(2,1)}, u32[]{:S(2)}, u32[]{:S(2)}) collective-permute-start(bf16[5,192,256]{2,1,0:T(8,128)(2,1)} %collective-permute-done.1), channel_id=1, source_target_pairs={{0,8},{4,12},{8,0},{12,4},{16,24},{20,28},{24,16},{28,20},{1,9},{5... | collective-permute-start | bytes 1474568 | tf_op jit(solution)/shard_map/ppermute | solution.py:294
  16.3 20.1 %collective-permute-start.3 = (bf16[5,192,256]{2,1,0:T(8,128)(2,1)S(1)}, bf16[5,192,256]{2,1,0:T(8,128)(2,1)S(1)}, u32[]{:S(2)}, u32[]{:S(2)}) collective-permute-start(bf16[5,192,256]{2,1,0:T(8,128)(2,1)S(1)} %collective-permute-done.refs_7_), channel_id=1, source_target_pairs={{0,16},{4,20},{8,24},{12,28},{16,0},{20,4},{24,8},{28,12},{1,17},{... | collective-permute-start | bytes 1474568 | tf_op jit(solution)/shard_map/ppermute | solution.py:294
  28.3 19.7 %collective-permute-start.11 = (bf16[5,192,256]{2,1,0:T(8,128)(2,1)S(1)}, bf16[5,192,256]{2,1,0:T(8,128)(2,1)S(1)}, u32[]{:S(2)}, u32[]{:S(2)}) collective-permute-start(bf16[5,192,256]{2,1,0:T(8,128)(2,1)S(1)} %collective-permute-done.9.refs_8_), channel_id=1, source_target_pairs={{0,4},{4,0},{8,12},{12,8},{16,20},{20,16},{24,28},{28,24},{1,5},{5... | collective-permute-start | bytes 1474568 | tf_op jit(solution)/shard_map/ppermute | solution.py:294
  32.4 16.1 %collective-permute-start.12 = (bf16[5,192,256]{2,1,0:T(8,128)(2,1)S(1)}, bf16[5,192,256]{2,1,0:T(8,128)(2,1)S(1)}, u32[]{:S(2)}, u32[]{:S(2)}) collective-permute-start(bf16[5,192,256]{2,1,0:T(8,128)(2,1)S(1)} %collective-permute-done.10.refs_10_), channel_id=1, source_target_pairs={{0,4},{4,0},{8,12},{12,8},{16,20},{20,16},{24,28},{28,24},{1,5},{5... | collective-permute-start | bytes 1474568 | tf_op jit(solution)/shard_map/ppermute | solution.py:294
  32.4 14.8 %collective-permute-start.7 = (bf16[160,768]{1,0:T(8,128)(2,1)S(1)}, bf16[160,768]{1,0:T(8,128)(2,1)S(1)}, u32[]{:S(2)}, u32[]{:S(2)}) collective-permute-start(bf16[160,768]{1,0:T(8,128)(2,1)S(1)} %pad_maximum_fusion), channel_id=1, source_target_pairs={{0,2},{1,3},{2,0},{3,1},{4,6},{5,7},{6,4},{7,5},{8,10},{9,11},{10,... | collective-permute-start | bytes 737288 | tf_op jit(solution)/shard_map/ppermute | solution.py:297
  36.1 11.9 %collective-permute-start.15 = (bf16[5,192,128]{2,1,0:T(8,128)(2,1)S(1)}, bf16[5,192,128]{2,1,0:T(8,128)(2,1)}, u32[]{:S(2)}, u32[]{:S(2)}) collective-permute-start(bf16[5,192,128]{2,1,0:T(8,128)(2,1)S(1)} %get-tuple-element.56), channel_id=1, source_target_pairs={{0,4},{4,0},{8,12},{12,8},{16,20},{20,16},{24,28},{28,24},{1,5},{5... | collective-permute-start | bytes 737288 | tf_op jit(solution)/shard_map/ppermute | solution.py:294
  36.8 14.4 %collective-permute-start.14 = (bf16[5,192,256]{2,1,0:T(8,128)(2,1)S(1)}, bf16[5,192,256]{2,1,0:T(8,128)(2,1)}, u32[]{:S(2)}, u32[]{:S(2)}) collective-permute-start(bf16[5,192,256]{2,1,0:T(8,128)(2,1)S(1)} %collective-permute-done.9.refs_8_), channel_id=1, source_target_pairs={{0,16},{4,20},{8,24},{12,28},{16,0},{20,4},{24,8},{28,12},{1,17},{... | collective-permute-start | bytes 1474568 | tf_op jit(solution)/shard_map/ppermute | solution.py:294
  48.0 10.8 %collective-permute-start.17 = (bf16[5,192,256]{2,1,0:T(8,128)(2,1)}, bf16[5,192,256]{2,1,0:T(8,128)(2,1)}, u32[]{:S(2)}, u32[]{:S(2)}) collective-permute-start(bf16[5,192,256]{2,1,0:T(8,128)(2,1)} %collective-permute-done.4.refs_9_), channel_id=1, source_target_pairs={{0,4},{4,0},{8,12},{12,8},{16,20},{20,16},{24,28},{28,24},{1,5},{5... | collective-permute-start | bytes 1474568 | tf_op jit(solution)/shard_map/ppermute | solution.py:294
  48.5 10.4 %collective-permute-start.18 = (bf16[5,192,256]{2,1,0:T(8,128)(2,1)S(1)}, bf16[5,192,256]{2,1,0:T(8,128)(2,1)}, u32[]{:S(2)}, u32[]{:S(2)}) collective-permute-start(bf16[5,192,256]{2,1,0:T(8,128)(2,1)S(1)} %collective-permute-done.3.refs_11_), channel_id=1, source_target_pairs={{0,4},{4,0},{8,12},{12,8},{16,20},{20,16},{24,28},{28,24},{1,5},{5... | collective-permute-start | bytes 1474568 | tf_op jit(solution)/shard_map/ppermute | solution.py:294
  51.2 13.2 %collective-permute-start.21 = (bf16[5,192,256]{2,1,0:T(8,128)(2,1)}, bf16[5,192,256]{2,1,0:T(8,128)(2,1)S(1)}, u32[]{:S(2)}, u32[]{:S(2)}) collective-permute-start(bf16[5,192,256]{2,1,0:T(8,128)(2,1)} %collective-permute-done.4.refs_9_), channel_id=1, source_target_pairs={{0,16},{4,20},{8,24},{12,28},{16,0},{20,4},{24,8},{28,12},{1,17},{... | collective-permute-start | bytes 1474568 | tf_op jit(solution)/shard_map/ppermute | solution.py:294
  55.9 10.0 %collective-permute-start.23 = (bf16[5,192,256]{2,1,0:T(8,128)(2,1)}, bf16[5,192,256]{2,1,0:T(8,128)(2,1)S(1)}, u32[]{:S(2)}, u32[]{:S(2)}) collective-permute-start(bf16[5,192,256]{2,1,0:T(8,128)(2,1)} %collective-permute-done.14.refs_12_), channel_id=1, source_target_pairs={{0,4},{4,0},{8,12},{12,8},{16,20},{20,16},{24,28},{28,24},{1,5},{5... | collective-permute-start | bytes 1474568 | tf_op jit(solution)/shard_map/ppermute | solution.py:294
  60.4 13.4 %collective-permute-start.20 = (bf16[320,768]{1,0:T(8,128)(2,1)S(1)}, bf16[320,768]{1,0:T(8,128)(2,1)S(1)}, u32[]{:S(2)}, u32[]{:S(2)}) collective-permute-start(bf16[320,768]{1,0:T(8,128)(2,1)S(1)} %constant_dynamic-update-slice_fusion.2.refs_4_), channel_id=1, source_target_pairs={{0,1},{1,0},{2,3},{3,2},{4,5},{5,4},{6,7},{7,6},{8,9},{9,8},{10,11... | collective-permute-start | bytes 1474568 | tf_op jit(solution)/shard_map/ppermute | solution.py:297
  64.4 21.1 %collective-permute-start.24 = (bf16[5,384,128]{2,1,0:T(8,128)(2,1)S(1)}, bf16[5,384,128]{2,1,0:T(8,128)(2,1)S(1)}, u32[]{:S(2)}, u32[]{:S(2)}) collective-permute-start(bf16[5,384,128]{2,1,0:T(8,128)(2,1)S(1)} %maximum_select_fusion.near_ref), channel_id=1, source_target_pairs={{0,16},{4,20},{8,24},{12,28},{16,0},{20,4},{24,8},{28,12},{1,17},{... | collective-permute-start | bytes 1474568 | tf_op jit(solution)/shard_map/ppermute | solution.py:294
  68.4 17.0 %collective-permute-start.26 = (bf16[5,384,128]{2,1,0:T(8,128)(2,1)S(1)}, bf16[5,384,128]{2,1,0:T(8,128)(2,1)S(1)}, u32[]{:S(2)}, u32[]{:S(2)}) collective-permute-start(bf16[5,384,128]{2,1,0:T(8,128)(2,1)S(1)} %maximum_select_fusion.1), channel_id=1, source_target_pairs={{0,8},{4,12},{8,0},{12,4},{16,24},{20,28},{24,16},{28,20},{1,9},{5... | collective-permute-start | bytes 1474568 | tf_op jit(solution)/shard_map/ppermute | solution.py:294
  85.9 13.2 %collective-permute-start.30 = (bf16[5,384,128]{2,1,0:T(8,128)(2,1)S(1)}, bf16[5,384,128]{2,1,0:T(8,128)(2,1)S(1)}, u32[]{:S(2)}, u32[]{:S(2)}) collective-permute-start(bf16[5,384,128]{2,1,0:T(8,128)(2,1)S(1)} %collective-permute-done.26.far_ref), channel_id=1, source_target_pairs={{0,16},{4,20},{8,24},{12,28},{16,0},{20,4},{24,8},{28,12},{1,17},{... | collective-permute-start | bytes 1474568 | tf_op jit(solution)/shard_map/ppermute | solution.py:294
  91.0 13.3 %collective-permute-start.28 = (bf16[320,768]{1,0:T(8,128)(2,1)S(1)}, bf16[320,768]{1,0:T(8,128)(2,1)S(1)}, u32[]{:S(2)}, u32[]{:S(2)}) collective-permute-start(bf16[320,768]{1,0:T(8,128)(2,1)S(1)} %down.4), channel_id=1, source_target_pairs={{0,8},{4,12},{8,0},{12,4},{16,24},{20,28},{24,16},{28,20},{1,9},{5... | collective-permute-start | bytes 1474568 | tf_op jit(solution)/shard_map/ppermute | solution.py:294
  91.7 15.5 %collective-permute-start.29 = (bf16[5,384,128]{2,1,0:T(8,128)(2,1)S(1)}, bf16[5,384,128]{2,1,0:T(8,128)(2,1)S(1)}, u32[]{:S(2)}, u32[]{:S(2)}) collective-permute-start(bf16[5,384,128]{2,1,0:T(8,128)(2,1)S(1)} %collective-permute-done.24.near_ref), channel_id=1, source_target_pairs={{0,4},{4,0},{8,12},{12,8},{16,20},{20,16},{24,28},{28,24},{1,5},{5... | collective-permute-start | bytes 1474568 | tf_op jit(solution)/shard_map/ppermute | solution.py:294
  109.2 13.3 %collective-permute-start.32 = (bf16[320,384]{1,0:T(8,128)(2,1)S(1)}, bf16[320,384]{1,0:T(8,128)(2,1)S(1)}, u32[]{:S(2)}, u32[]{:S(2)}) collective-permute-start(bf16[320,384]{1,0:T(8,128)(2,1)S(1)} %get-tuple-element.70), channel_id=1, source_target_pairs={{0,8},{4,12},{8,0},{12,4},{16,24},{20,28},{24,16},{28,20},{1,9},{5... | collective-permute-start | bytes 737288 | tf_op jit(solution)/shard_map/ppermute | solution.py:294
  109.8 11.6 %collective-permute-start.35 = (bf16[320,384]{1,0:T(8,128)(2,1)S(1)}, bf16[320,384]{1,0:T(8,128)(2,1)S(1)}, u32[]{:S(2)}, u32[]{:S(2)}) collective-permute-start(bf16[320,384]{1,0:T(8,128)(2,1)S(1)} %get-tuple-element.74), channel_id=1, source_target_pairs={{0,8},{4,12},{8,0},{12,4},{16,24},{20,28},{24,16},{28,20},{1,9},{5... | collective-permute-start | bytes 737288 | tf_op jit(solution)/shard_map/ppermute | solution.py:294
  114.6 17.8 %collective-permute-start.39 = (bf16[80,768]{1,0:T(8,128)(2,1)S(1)}, bf16[80,768]{1,0:T(8,128)(2,1)S(1)}, u32[]{:S(2)}, u32[]{:S(2)}) collective-permute-start(bf16[80,768]{1,0:T(8,128)(2,1)S(1)} %slice.81), channel_id=1, source_target_pairs={{0,2},{1,3},{2,0},{3,1},{4,6},{5,7},{6,4},{7,5},{8,10},{9,11},{10,... | collective-permute-start | bytes 368648 | tf_op jit(solution)/shard_map/ppermute | solution.py:297
  (41 other events, 288.2 us)

commit v6 on v5

v6 whole, which is shorter than its diff:
```python
import functools

import jax
import jax.numpy as jnp
from jax import lax
from jax.experimental import pallas as pl
from jax.experimental.pallas import tpu as pltpu
from jax.sharding import PartitionSpec as P

EPS = 1e-06
LOGIT_SCALE = 0.5
LANES = 128
LOW = 64
QUAD = 4


def normalize(values, gain):
    return values * lax.rsqrt(jnp.mean(values * values, axis=-1, keepdims=True) + EPS) * gain


def after(values, *others):
    return lax.optimization_barrier((values, *others))[0]


def after_all(values, *others):
    return lax.optimization_barrier((*values, *others))[: len(values)]


def swap_blocks(values, index, blocks):
    size = values.shape[1] // blocks
    bit = 1
    while bit < blocks:
        swapped = jnp.concatenate(
            [values[:, (m ^ bit) * size : ((m ^ bit) + 1) * size] for m in range(blocks)], axis=1
        )
        values = jnp.where((index & bit) != 0, swapped, values)
        bit *= 2
    return values


def swap_lanes(values, index, blocks):
    width = values.shape[1]
    size = width // blocks
    lane = lax.broadcasted_iota(jnp.int32, values.shape, 1)
    bit = 1
    while bit < blocks:
        step = bit * size
        upper = (lane // step) % 2 == 1
        swapped = jnp.where(
            upper, pltpu.roll(values, step, 1), pltpu.roll(values, width - step, 1)
        )
        values = jnp.where((index & bit) != 0, swapped, values)
        bit *= 2
    return values


def cut(part, side, core, weight, outs):
    blocks = outs[0].shape[2] // part
    targets = [(core, side), (core, 1 - side), (1 - core, side), (1 - core, 1 - side)]
    for out_ref, (c, s) in zip(outs, targets):
        for b in range(blocks):
            at = pl.multiple_of(b * QUAD * part + (2 * c + s) * part, part)
            out_ref[:, :, b * part : (b + 1) * part] = weight[:, :, pl.ds(at, part)]


def front_kernel(
    ranks,
    part,
    place_ref,
    att_ref,
    res_ref,
    gain_ref,
    routes_ref,
    logits_ref,
    placed_ref,
    w_hbm,
    gu_hbm,
    stream_ref,
    sent_ref,
    own_ref,
    away_ref,
    mate_ref,
    mate_away_ref,
    w_ref,
    gu_ref,
    keep_ref,
    sems,
):
    steps = w_ref.shape[0]
    width, cols = w_ref.shape[1:]
    load = pltpu.make_async_copy(gu_hbm, gu_ref, sems.at[steps])
    load.start()
    loads = []
    for i in range(steps):
        loads.append(
            pltpu.make_async_copy(w_hbm.at[:, i * cols : (i + 1) * cols], w_ref.at[i], sems.at[i])
        )
        loads[-1].start()

    load.wait()
    cut(part, place_ref[0], place_ref[1], gu_ref, (own_ref, away_ref, mate_ref, mate_away_ref))

    for i in range(steps):
        some = slice(i * cols, (i + 1) * cols)
        loads[i].wait()
        mixed = res_ref[:, some].astype(jnp.float32) + jnp.dot(
            att_ref[...], w_ref[i], preferred_element_type=jnp.float32
        )
        stored = mixed.astype(jnp.bfloat16)
        stream_ref[:, some] = stored
        keep_ref[:, some] = stored.astype(jnp.float32)

    normed = normalize(keep_ref[...], gain_ref[...])
    sent_ref[:, :width] = swap_lanes(normed, place_ref[3], ranks).astype(jnp.bfloat16)
    scores = jnp.exp(logits_ref[...].astype(jnp.float32) * LOGIT_SCALE)
    gates = scores / jnp.sum(scores, axis=1, keepdims=True)
    routes = routes_ref[...]
    spread = jnp.zeros((gates.shape[0], LANES), jnp.float32)
    for k in range(gates.shape[1]):
        hit = routes[:, k : k + 1] == placed_ref[...]
        spread = jnp.where(hit, gates[:, k : k + 1], spread)
    high = spread.astype(jnp.bfloat16).astype(jnp.float32)
    lane = lax.broadcasted_iota(jnp.int32, spread.shape, 1)
    sent_ref[:, width:] = jnp.where(lane < LOW, high, spread - high).astype(jnp.bfloat16)


def front_call(
    place, ranks, part, attended, residual, weight, gain, routes, logits, placement, gate_up
):
    tok, width = attended.shape
    local, depth, cols = gate_up.shape
    steps = 4
    padded = jnp.pad(placement, (0, LOW - placement.shape[0]), constant_values=-1)
    placed = jnp.concatenate([padded, padded])[None, :]
    vmem = pl.BlockSpec(memory_space=pltpu.VMEM)
    hbm = pl.BlockSpec(memory_space=pl.ANY)
    return pl.pallas_call(
        functools.partial(front_kernel, ranks, part),
        in_specs=[pl.BlockSpec(memory_space=pltpu.SMEM)] + [vmem] * 6 + [hbm] * 2,
        out_specs=[vmem] * 6,
        out_shape=[
            jax.ShapeDtypeStruct((tok, width), jnp.bfloat16),
            jax.ShapeDtypeStruct((tok, width + LANES), jnp.bfloat16),
        ]
        + [jax.ShapeDtypeStruct((local, depth, cols // QUAD), jnp.bfloat16)] * QUAD,
        scratch_shapes=[
            pltpu.VMEM((steps, width, width // steps), jnp.bfloat16),
            pltpu.VMEM(gate_up.shape, jnp.bfloat16),
            pltpu.VMEM((tok, width), jnp.float32),
            pltpu.SemaphoreType.DMA((steps + 1,)),
        ],
        compiler_params=pltpu.CompilerParams(vmem_limit_bytes=48 * 1024 * 1024),
        cost_estimate=pl.CostEstimate(flops=1, bytes_accessed=1, transcendentals=0),
        name="front",
    )(place, attended, residual, gain[None, :], routes, logits, placed, weight, gate_up)


def cut_kernel(part, place_ref, w_ref, *out_refs):
    cut(part, place_ref[0], place_ref[1], w_ref, out_refs)


def cut_call(place, weight, part):
    local, depth, cols = weight.shape
    out = jax.ShapeDtypeStruct((local, depth, cols // QUAD), jnp.bfloat16)
    return pl.pallas_call(
        functools.partial(cut_kernel, part),
        in_specs=[pl.BlockSpec(memory_space=pltpu.SMEM), pl.BlockSpec(memory_space=pltpu.VMEM)],
        out_specs=[pl.BlockSpec(memory_space=pltpu.VMEM)] * QUAD,
        out_shape=[out] * QUAD,
        compiler_params=pltpu.CompilerParams(vmem_limit_bytes=24 * 1024 * 1024),
        cost_estimate=pl.CostEstimate(flops=1, bytes_accessed=1, transcendentals=0),
        name="cut",
    )(place, weight)


def up_kernel(rows, count, place_ref, *refs):
    here, away = refs[:count], refs[count : 2 * count]
    pieces = refs[2 * count : 2 * count + 2 * QUAD * rows]
    out_ref, x_ref = refs[2 * count + 2 * QUAD * rows :]
    zone = place_ref[2]
    local, _, width = pieces[0].shape
    part = width // 2
    tok = here[0].shape[0]
    feats = x_ref.shape[1] - LANES
    half = feats // (2 * rows)

    for i in range(count):
        x_ref[i * tok : (i + 1) * tok, :] = here[i][...]
        some = slice((count + i) * tok, (count + i + 1) * tok)
        for j in range(2 * rows):
            to, come = j * half, (j ^ 1) * half
            x_ref[some, to : to + half] = away[i][:, come : come + half]
        x_ref[some, feats:] = away[i][:, feats:]

    lane = lax.broadcasted_iota(jnp.int32, (LANES, width), 0)
    for e in range(local):
        mine, other = (
            jnp.concatenate([p[e] for p in pieces[i * QUAD * rows : (i + 1) * QUAD * rows]], axis=0)
            for i in range(2)
        )
        w = jnp.concatenate(
            [mine[:, :part], other[:, :part], mine[:, part:], other[:, part:]], axis=1
        )
        slot = zone * local + e
        pick = jnp.where((lane == slot) | (lane == slot + LOW), 0.5, 0.0).astype(jnp.bfloat16)
        acc = jnp.dot(x_ref[:, :feats], w, preferred_element_type=jnp.float32)
        gate = jnp.dot(x_ref[:, feats:], pick, preferred_element_type=jnp.float32)
        g, u = acc[:, :width], acc[:, width:]
        out_ref[:, e * width : (e + 1) * width] = (
            (g + g * jnp.tanh(0.5 * g)) * (u * gate)
        ).astype(jnp.bfloat16)


def up_call(place, here, away, mine, other):
    local, _, cols = mine[0].shape
    tok, lanes = here[0].shape
    tokens = 2 * len(here) * tok
    operands = [*here, *away, *mine, *other]
    return pl.pallas_call(
        functools.partial(up_kernel, len(mine) // QUAD, len(here)),
        in_specs=[pl.BlockSpec(memory_space=pltpu.SMEM)]
        + [pl.BlockSpec(memory_space=pltpu.VMEM)] * len(operands),
        out_specs=pl.BlockSpec(memory_space=pltpu.VMEM),
        scratch_shapes=[pltpu.VMEM((tokens, lanes), jnp.bfloat16)],
        out_shape=jax.ShapeDtypeStruct((tokens, local * cols), jnp.bfloat16),
        compiler_params=pltpu.CompilerParams(vmem_limit_bytes=48 * 1024 * 1024),
        cost_estimate=pl.CostEstimate(flops=1, bytes_accessed=1, transcendentals=0),
        name="up",
    )(place, *operands)


def product(hidden, mine, other):
    w = [part[e] for e in range(mine.shape[0]) for part in (mine, other)]
    return lax.dot_general(
        hidden,
        jnp.concatenate(w, axis=1),
        (((1,), (1,)), ((), ())),
        preferred_element_type=jnp.float32,
    )


def down_kernel(start, h_ref, near_ref, near_other_ref, far_ref, far_other_ref, *out_refs):
    rows = out_refs[0].shape[0]
    feats = near_ref.shape[1]
    hidden = h_ref[start : start + rows, :]
    for j, pair in enumerate(((near_ref, near_other_ref), (far_ref, far_other_ref))):
        partial = product(hidden, *pair)
        if len(out_refs) == 2:
            out_refs[j][...] = partial.astype(out_refs[j].dtype)
        else:
            out_refs[0][:, j * feats : (j + 1) * feats] = partial.astype(out_refs[0].dtype)


def down_call(hidden, near, far, send, parts):
    tokens = hidden.shape[0] // 2
    feats = 2 * near[0].shape[1] // parts
    kind = jnp.bfloat16 if send else jnp.float32
    out = [jax.ShapeDtypeStruct((tokens, feats), kind)] * parts
    return pl.pallas_call(
        functools.partial(down_kernel, tokens if send else 0),
        in_specs=[pl.BlockSpec(memory_space=pltpu.VMEM)] * 5,
        out_specs=[pl.BlockSpec(memory_space=pltpu.VMEM)] * parts,
        out_shape=out,
        compiler_params=pltpu.CompilerParams(vmem_limit_bytes=40 * 1024 * 1024),
        cost_estimate=pl.CostEstimate(flops=1, bytes_accessed=1, transcendentals=0),
        name="down",
    )(hidden, *near, *far)


def body(
    attended,
    residual,
    out_weight,
    norm_gain,
    final_gain,
    routes,
    gate_logits,
    placement,
    gate_up,
    down_weight,
):
    ranks = lax.axis_size("dp")
    zones = lax.axis_size("expert")
    rows = ranks // QUAD
    me = lax.axis_index("dp")
    zone = lax.axis_index("expert")
    core, side = me % 2, (me // 2) % 2
    hid = down_weight.shape[2]
    part = hid // QUAD

    def flip(values, bit):
        return lax.ppermute(values, "dp", [(i, i ^ bit) for i in range(ranks)])

    def hop(values, bit):
        return lax.ppermute(values, "expert", [(i, i ^ bit) for i in range(zones)])

    def widen(pieces):
        bit = 1
        while bit < rows:
            pieces = pieces + [flip(p, bit * QUAD) for p in pieces]
            bit *= 2
        return pieces

    zone_bits = []
    while 1 << len(zone_bits) < zones:
        zone_bits.append(1 << len(zone_bits))
    place = jnp.stack([side, core, zone, me]).astype(jnp.int32)

    stored, sent, gu_own, gu_away, gu_to_mate, gu_to_mate_away = front_call(
        place,
        ranks,
        part,
        attended,
        residual,
        out_weight,
        norm_gain,
        routes,
        gate_logits,
        placement,
        gate_up,
    )
    stream_in = stored.astype(jnp.float32)
    gu_own_x = flip(gu_away, 2)
    first = widen([gu_own])
    gu_mate, gu_mate_away = flip(gu_to_mate, 1), flip(gu_to_mate_away, 1)
    near = [sent]
    for bit in reversed(zone_bits[1:]):
        near = near + [hop(v, bit) for v in near]
    gu_own, gu_own_x, gu_mate, gu_mate_away, *both = after_all(
        [gu_own, gu_own_x, gu_mate, gu_mate_away, *first[1:], *near]
    )
    first, near = [gu_own, *both[: rows - 1]], both[rows - 1 :]
    gu_mate_x = flip(gu_mate_away, 2)
    second = widen([gu_mate])
    far = [hop(v, 1) for v in near]
    shared = [flip(gu_own, 1), flip(gu_own_x, 1)]
    firsts = [flip(p, 1) for p in first[1:]]
    gu_own_x, gu_mate, gu_mate_x, *both = after_all(
        [gu_own_x, gu_mate, gu_mate_x, *second[1:], *near, *far], *shared, *firsts
    )
    second, near, far = (
        [gu_mate, *both[: rows - 1]],
        both[rows - 1 : rows - 1 + len(near)],
        both[rows - 1 + len(near) :],
    )
    near_x = [flip(v, 2) for v in near]
    third = widen([gu_own_x])
    shared.append(flip(gu_mate_x, 1))
    seconds = [flip(p, 1) for p in second[1:]]
    gu_own_x, gu_mate_x, *both = after_all(
        [gu_own_x, gu_mate_x, *third[1:], *near_x, *far], shared[-1], *seconds
    )
    third, near_x, far = (
        [gu_own_x, *both[: rows - 1]],
        both[rows - 1 : rows - 1 + len(near)],
        both[rows - 1 + len(near) :],
    )
    far_x = [flip(v, 2) for v in far]
    fourth = widen([gu_mate_x])
    thirds = [flip(p, 1) for p in third[1:]]
    fourths = [flip(p, 1) for p in fourth[1:]]
    here, away = near + far, near_x + far_x
    mine = [p for group in zip(first, second, third, fourth) for p in group]
    other = [gu_to_mate, shared[0], shared[2], shared[1]]
    for group in zip(seconds, firsts, fourths, thirds):
        other += group

    dn_own, dn_away, dn_to_mate, dn_to_mate_away = cut_call(
        place, after(down_weight, first[-1]), part
    )
    dn_mate, dn_mate_away = flip(dn_to_mate, 1), flip(dn_to_mate_away, 1)

    def pair(own, mate):
        return jnp.where(
            core == 0,
            jnp.concatenate([own, mate], axis=1),
            jnp.concatenate([mate, own], axis=1),
        )

    dn_near, dn_away = pair(dn_own, dn_mate), pair(dn_away, dn_mate_away)
    dn_near_other = flip(dn_near, 1)

    dn_far = flip(after(dn_away, *far_x, fourth[-1], dn_near_other, *thirds), 2)
    hidden = up_call(place, here, away, mine, other)
    dn_nears = widen([after(dn_near, *far_x, fourth[-1])])
    hidden = after(hidden, dn_nears[-1])
    dn_fars = widen([after(dn_far, fourth[-1])])
    nears = [(dn_near, dn_near_other)] + [(v, flip(after(v, hidden), 1)) for v in dn_nears[1:]]
    fars = [(v, flip(after(v, hidden), 1)) for v in dn_fars]

    chunks, crossed = [], None
    for m in range(rows):
        parts = 2 if m == rows - 1 else 1
        ready = hidden if crossed is None else after(hidden, crossed)
        sends = down_call(ready, nears[m], fars[m], True, parts)
        keeps = down_call(after(hidden, sends[0]), nears[m], fars[m], False, parts)
        for i, keep in enumerate(keeps):
            crossed = flip(sends[parts - 1 - i], 2)
            if parts == 1:
                size = crossed.shape[1] // 2
                total = keep + jnp.concatenate(
                    [crossed[:, size:], crossed[:, :size]], axis=1
                ).astype(jnp.float32)
            else:
                total = keep + crossed.astype(jnp.float32)
            for bit in zone_bits:
                size = total.shape[0] // 2
                moved = total[size:].astype(jnp.bfloat16)
                total = total[:size] + hop(moved, bit).astype(jnp.float32)
            chunks.append(total)
    branch = swap_blocks(jnp.concatenate(chunks, axis=1), me // 2, 2 * rows)
    total = stream_in + branch
    return (total.astype(jnp.bfloat16), normalize(total, final_gain).astype(jnp.bfloat16))


def solution(mesh):
    tokens = P(("dp", "expert"), None)
    weights = P("expert", "dp", None)
    return jax.shard_map(
        body,
        mesh=mesh,
        in_specs=(tokens, tokens, P(), P(), P(), tokens, tokens, P(), weights, weights),
        out_specs=(tokens, tokens),
        check_vma=False,
    )
```

time: 137 us -> 143 us (1.044)
  local copies, waits for them, and re-layouts: 10.6 us -> 18.7 us
  starting transfers between devices: 43.6 us -> 35.8 us
  waiting for transfers between devices: 53.6 us -> 60.7 us
    ppermute x30 -> x31, waiting for transfers between devices: 27.6 us -> 34.3 us  [flip(): return lax.ppermute(values, 'dp', [(i, i ^ bit) for i in range(ranks)])]
    unnamed x55 -> x66, local copies, waits for them, and re-layouts: 9.66 us -> 16.1 us
    ppermute x30 -> x31, starting transfers between devices: 23.3 us -> 18.4 us  [flip(): return lax.ppermute(values, 'dp', [(i, i ^ bit) for i in range(ranks)])]
    ppermute x10 -> x9, starting transfers between devices: 20.3 us -> 17.4 us  [hop(): return lax.ppermute(values, 'expert', [(i, i ^ bit) for i in range(zones)])]
    ppermute x10 -> x9, waiting for transfers between devices: 26.1 us -> 26.4 us  [hop(): return lax.ppermute(values, 'expert', [(i, i ^ bit) for i in range(zones)])]
    pallas_call x4 -> x3, Pallas kernels: 15.2 us -> 14.9 us  [the longest x1 9.44 us: up_call(): pl.pallas_call(functools.partial(up_kernel, len(mine) // QUAD, len(here))...]
  transfers between devices with their start and end apart: 40 -> 40, of which waited for: 17 -> 18; matrix products, arithmetic and copies ran while one was open for 4% -> 3% of each run, Pallas kernels for 15% -> 11%
where the time goes in v6:
time: 143 us
  waiting for transfers between devices  60.7 us (42%)
  starting transfers between devices  35.8 us (25%)
  Pallas kernels  22.1 us (15%)
  local copies, waits for them, and re-layouts  18.7 us (13%)
  other arithmetic  4.21 us (3%)
    ppermute x31, waiting for transfers between devices, flip(): return lax.ppermute(values, 'dp', [(i, i ^ bit) for i in range(ranks)])  34.3 us
    ppermute x9, waiting for transfers between devices, hop(): return lax.ppermute(values, 'expert', [(i, i ^ bit) for i in range(zones)])  26.4 us
    ppermute x31, starting transfers between devices, flip(): return lax.ppermute(values, 'dp', [(i, i ^ bit) for i in range(ranks)])  18.4 us
    ppermute x9, starting transfers between devices, hop(): return lax.ppermute(values, 'expert', [(i, i ^ bit) for i in range(zones)])  17.4 us
    unnamed x66, local copies, waits for them, and re-layouts  16.1 us
    pallas_call x1, Pallas kernels, up_call(): pl.pallas_call(functools.partial(up_kernel, len(mine) // QUAD, len(here))...  9.44 us
    pallas_call x4, Pallas kernels, down_call(): pl.pallas_call(functools.partial(down_kernel, tokens if send else 0), in_...  7.23 us
    pallas_call x1, Pallas kernels, front_call(): pl.pallas_call(functools.partial(front_kernel, ranks, part), in_specs=[pl...  4.04 us
  transfers between devices with their start and end apart: 40, of which 18 were waited for; matrix products, arithmetic and copies ran while one was open for 3% of the time, Pallas kernels for 11%

profile of v6, /device:TPU:0, one launch (start us, length us, event | category | flops | bytes accessed | tf_op | source)
XLA Modules:
  0.0 142.6 jit_solution(7324111977412619141)
XLA Ops:
  3.7 1.5 %copy-done.2 = bf16[5,192,1024]{2,1,0:T(8,128)(2,1)S(1)} copy-done((bf16[5,192,1024]{2,1,0:T(8,128)(2,1)S(1)}, bf16[5,192,1024]{2,1,0:T(8,128)(2,1)}, u32[]{:S(2)}) %copy-start.2) | copy-done | bytes 1966104
  7.2 4.0 %front.1 = (bf16[80,1536]{1,0:T(8,128)(2,1)S(1)}, bf16[80,1664]{1,0:T(8,128)(2,1)S(1)}, bf16[5,192,256]{2,1,0:T(8,128)(2,1)S(1)}, bf16[5,192,256]{2,1,0:T(8,128)...) custom-call(s32[4]{0:T(128)S(1)} %pad_add_fusion.place_ref, ...), custom_call_target="tpu_custom_call" | custom-call | flops 1 | bytes 1 | tf_op jit(solution)/shard_map/front/pallas_call | solution.py:137
  11.9 2.9 %collective-permute-start = (bf16[5,192,256]{2,1,0:T(8,128)(2,1)S(1)}, bf16[5,192,256]{2,1,0:T(8,128)(2,1)S(1)}, u32[]{:S(2)}, u32[]{:S(2)}) collective-permute-start(bf16[5,192,256]{2,1,0:T(8,128)(2,1)S(1)} %get-tuple-element.51), channel_id=1, source_target_pairs={{0,8},{4,12},{8,0},{12,4},{16,24},{20,28},{24,16},{28,20},{1,9},{5... | collective-permute-start | bytes 1474568 | tf_op jit(solution)/shard_map/ppermute | solution.py:292
  16.9 2.6 %collective-permute-start.4 = (bf16[80,1664]{1,0:T(8,128)(2,1)S(1)}, bf16[80,1664]{1,0:T(8,128)(2,1)}, u32[]{:S(2)}, u32[]{:S(2)}) collective-permute-start(bf16[80,1664]{1,0:T(8,128)(2,1)S(1)} %get-tuple-element.62.refs_0_), channel_id=1, source_target_pairs={{0,2},{1,3},{2,0},{3,1},{4,6},{5,7},{6,4},{7,5},{8,10},{9,11},{10,... | collective-permute-start | bytes 798728 | tf_op jit(solution)/shard_map/ppermute | solution.py:295
  19.5 12.1 %collective-permute-done.4.refs_1_ = bf16[80,1664]{1,0:T(8,128)(2,1)} collective-permute-done((bf16[80,1664]{1,0:T(8,128)(2,1)S(1)}, bf16[80,1664]{1,0:T(8,128)(2,1)}, u32[]{:S(2)}, u32[]{:S(2)}) %collective-permute-start.4) | collective-permute-done | bytes 266272 | tf_op jit(solution)/shard_map/ppermute | solution.py:295
  34.8 6.3 %collective-permute-done.7.refs_2_ = bf16[80,1664]{1,0:T(8,128)(2,1)S(1)} collective-permute-done((bf16[80,1664]{1,0:T(8,128)(2,1)S(1)}, bf16[80,1664]{1,0:T(8,128)(2,1)S(1)}, u32[]{:S(2)}, u32[]{:S(2)}) %collective-permute-start.7) | collective-permute-done | bytes 266272 | tf_op jit(solution)/shard_map/ppermute | solution.py:295
  41.1 3.6 %collective-permute-done.8.refs_3_ = bf16[80,1664]{1,0:T(8,128)(2,1)S(1)} collective-permute-done((bf16[80,1664]{1,0:T(8,128)(2,1)}, bf16[80,1664]{1,0:T(8,128)(2,1)S(1)}, u32[]{:S(2)}, u32[]{:S(2)}) %collective-permute-start.8) | collective-permute-done | bytes 266272 | tf_op jit(solution)/shard_map/ppermute | solution.py:295
  53.1 2.7 %collective-permute-done.13.refs_4_ = bf16[80,1664]{1,0:T(8,128)(2,1)S(1)} collective-permute-done((bf16[80,1664]{1,0:T(8,128)(2,1)S(1)}, bf16[80,1664]{1,0:T(8,128)(2,1)S(1)}, u32[]{:S(2)}, u32[]{:S(2)}) %collective-permute-start.13) | collective-permute-done | bytes 266272 | tf_op jit(solution)/shard_map/ppermute | solution.py:292
  56.5 4.3 %collective-permute-done.14.refs_5_ = bf16[80,1664]{1,0:T(8,128)(2,1)} collective-permute-done((bf16[80,1664]{1,0:T(8,128)(2,1)}, bf16[80,1664]{1,0:T(8,128)(2,1)}, u32[]{:S(2)}, u32[]{:S(2)}) %collective-permute-start.14) | collective-permute-done | bytes 266272 | tf_op jit(solution)/shard_map/ppermute | solution.py:292
  66.7 7.8 %collective-permute-done.19.refs_15_ = bf16[5,192,256]{2,1,0:T(8,128)(2,1)S(1)} collective-permute-done((bf16[5,192,256]{2,1,0:T(8,128)(2,1)S(1)}, bf16[5,192,256]{2,1,0:T(8,128)(2,1)S(1)}, u32[]{:S(2)}, u32[]{:S(2)}) %collective-permute-start.19) | collective-permute-done | bytes 491552 | tf_op jit(solution)/shard_map/ppermute | solution.py:292
  74.6 3.2 %collective-permute-done.18.refs_7_ = bf16[80,1664]{1,0:T(8,128)(2,1)S(1)} collective-permute-done((bf16[80,1664]{1,0:T(8,128)(2,1)}, bf16[80,1664]{1,0:T(8,128)(2,1)S(1)}, u32[]{:S(2)}, u32[]{:S(2)}) %collective-permute-start.18) | collective-permute-done | bytes 266272 | tf_op jit(solution)/shard_map/ppermute | solution.py:292
  77.7 1.5 %collective-permute-start.23 = (bf16[5,384,128]{2,1,0:T(8,128)(2,1)S(1)}, bf16[5,384,128]{2,1,0:T(8,128)(2,1)S(1)}, u32[]{:S(2)}, u32[]{:S(2)}) collective-permute-start(bf16[5,384,128]{2,1,0:T(8,128)(2,1)S(1)} %maximum_select_fusion.near_ref), channel_id=1, source_target_pairs={{0,16},{4,20},{8,24},{12,28},{16,0},{20,4},{24,8},{28,12},{1,17},{... | collective-permute-start | bytes 1474568 | tf_op jit(solution)/shard_map/ppermute | solution.py:292
  81.9 9.4 %up.1.h_ref = bf16[640,1280]{1,0:T(8,128)(2,1)} custom-call(s32[4]{0:T(128)S(1)} %pad_add_fusion.place_ref, bf16[80,1664]{1,0:T(8,128)(2,1)S(1)} %get-tuple-element.62.refs_0_, bf16[80,1664]{1,0:T(8,128)(2,1)} %collective-permute-done.4.refs_1_, bf16[80,1664]{1,0:T(8,128)(2,1)S(1)} %collective-permute-done.7.refs_2_, bf16[80,1664]{1,0:T(8,128)(2,1)S(1)} %copy-done.16, ...), custom_call_target="tpu_custom_call" | custom-call | flops 1 | bytes 1 | tf_op jit(solution)/shard_map/up/pallas_call | solution.py:219
  94.9 1.8 %down.4 = bf16[320,768]{1,0:T(8,128)(2,1)} custom-call(bf16[640,1280]{1,0:T(8,128)(2,1)S(1)} %copy-done, bf16[5,384,128]{2,1,0:T(8,128)(2,1)S(1)} %maximum_select_fusion.near_ref, bf16[5,384,128]{2,1,0:T(8,128)(2,1)S(1)} %collective-permute-done.24.near_other_ref, bf16[5,384,128]{2,1,0:T(8,128)(2,1)S(1)} %collective-permute-done.26.far_ref, ...), custom_call_target="tpu_custom_call" | custom-call | flops 1 | bytes 1 | tf_op jit(solution)/shard_map/down/pallas_call | solution.py:259
  97.8 7.4 %collective-permute-done.32.far_ref = bf16[5,384,128]{2,1,0:T(8,128)(2,1)S(1)} collective-permute-done((bf16[5,384,128]{2,1,0:T(8,128)(2,1)S(1)}, bf16[5,384,128]{2,1,0:T(8,128)(2,1)S(1)}, u32[]{:S(2)}, u32[]{:S(2)}) %collective-permute-start.32) | collective-permute-done | bytes 491552 | tf_op jit(solution)/shard_map/ppermute | solution.py:292
  110.3 2.2 %down.6 = (bf16[320,384]{1,0:T(8,128)(2,1)S(1)}, bf16[320,384]{1,0:T(8,128)(2,1)S(1)}) custom-call(bf16[640,1280]{1,0:T(8,128)(2,1)S(1)} %copy-done.1, bf16[5,384,128]{2,1,0:T(8,128)(2,1)S(1)} %collective-permute-done.23.near_ref, bf16[5,384,128]{2,1,0:T(8,128)(2,1)} %collective-permute-done.31.near_other_ref, ...), custom_call_target="tpu_custom_call" | custom-call | flops 1 | bytes 1 | tf_op jit(solution)/shard_map/down/pallas_call | solution.py:259
  115.8 1.7 %collective-permute-start.29 = (bf16[160,768]{1,0:T(8,128)(2,1)S(1)}, bf16[160,768]{1,0:T(8,128)(2,1)S(1)}, u32[]{:S(2)}, u32[]{:S(2)}) collective-permute-start(bf16[160,768]{1,0:T(8,128)(2,1)S(1)} %slice.112), channel_id=1, source_target_pairs={{0,1},{1,0},{2,3},{3,2},{4,5},{5,4},{6,7},{7,6},{8,9},{9,8},{10,11... | collective-permute-start | bytes 737288 | tf_op jit(solution)/shard_map/ppermute | solution.py:295
  117.5 2.2 %down.7 = (f32[320,384]{1,0:T(8,128)S(1)}, f32[320,384]{1,0:T(8,128)S(1)}) custom-call(bf16[640,1280]{1,0:T(8,128)(2,1)S(1)} %copy-done.1, bf16[5,384,128]{2,1,0:T(8,128)(2,1)S(1)} %collective-permute-done.23.near_ref, bf16[5,384,128]{2,1,0:T(8,128)(2,1)} %collective-permute-done.31.near_other_ref, bf16[5,384,128]{2,1,0:T(8,128)(2,1)S(1)} %collective-permute-done.32.far_ref, ...), custom_call_target="tpu_custom_call" | custom-call | flops 1 | bytes 1 | tf_op jit(solution)/shard_map/down/pallas_call | solution.py:259
  119.7 5.5 %collective-permute-done.37 = bf16[320,384]{1,0:T(8,128)(2,1)S(1)} collective-permute-done((bf16[320,384]{1,0:T(8,128)(2,1)S(1)}, bf16[320,384]{1,0:T(8,128)(2,1)S(1)}, u32[]{:S(2)}, u32[]{:S(2)}) %collective-permute-start.37) | collective-permute-done | bytes 245792 | tf_op jit(solution)/shard_map/ppermute | solution.py:292
  125.3 1.7 %collective-permute-start.38 = (bf16[160,384]{1,0:T(8,128)(2,1)S(1)}, bf16[160,384]{1,0:T(8,128)(2,1)S(1)}, u32[]{:S(2)}, u32[]{:S(2)}) collective-permute-start(bf16[160,384]{1,0:T(8,128)(2,1)S(1)} %slice.113), channel_id=1, source_target_pairs={{0,1},{1,0},{2,3},{3,2},{4,5},{5,4},{6,7},{7,6},{8,9},{9,8},{10,11... | collective-permute-start | bytes 368648 | tf_op jit(solution)/shard_map/ppermute | solution.py:295
  127.7 3.4 %collective-permute-start.30 = (bf16[80,768]{1,0:T(8,128)(2,1)S(1)}, bf16[80,768]{1,0:T(8,128)(2,1)S(1)}, u32[]{:S(2)}, u32[]{:S(2)}) collective-permute-start(bf16[80,768]{1,0:T(8,128)(2,1)S(1)} %slice.115), channel_id=1, source_target_pairs={{0,2},{1,3},{2,0},{3,1},{4,6},{5,7},{6,4},{7,5},{8,10},{9,11},{10,... | collective-permute-start | bytes 368648 | tf_op jit(solution)/shard_map/ppermute | solution.py:295
  132.1 2.9 %collective-permute-start.39 = (bf16[80,384]{1,0:T(8,128)(2,1)S(1)}, bf16[80,384]{1,0:T(8,128)(2,1)S(1)}, u32[]{:S(2)}, u32[]{:S(2)}) collective-permute-start(bf16[80,384]{1,0:T(8,128)(2,1)S(1)} %slice.116), channel_id=1, source_target_pairs={{0,2},{1,3},{2,0},{3,1},{4,6},{5,7},{6,4},{7,5},{8,10},{9,11},{10,... | collective-permute-start | bytes 184328 | tf_op jit(solution)/shard_map/ppermute | solution.py:295
  135.1 2.6 %collective-permute-start.36 = (bf16[80,384]{1,0:T(8,128)(2,1)S(1)}, bf16[80,384]{1,0:T(8,128)(2,1)S(1)}, u32[]{:S(2)}, u32[]{:S(2)}) collective-permute-start(bf16[80,384]{1,0:T(8,128)(2,1)S(1)} %slice.117), channel_id=1, source_target_pairs={{0,2},{1,3},{2,0},{3,1},{4,6},{5,7},{6,4},{7,5},{8,10},{9,11},{10,... | collective-permute-start | bytes 184328 | tf_op jit(solution)/shard_map/ppermute | solution.py:295
  137.7 2.7 %collective-permute-done.39 = bf16[80,384]{1,0:T(8,128)(2,1)S(1)} collective-permute-done((bf16[80,384]{1,0:T(8,128)(2,1)S(1)}, bf16[80,384]{1,0:T(8,128)(2,1)S(1)}, u32[]{:S(2)}, u32[]{:S(2)}) %collective-permute-start.39) | collective-permute-done | bytes 61472 | tf_op jit(solution)/shard_map/ppermute | solution.py:295
  (157 shorter events, 45.4 us)
Async XLA Ops:
  11.9 19.7 %collective-permute-start = (bf16[5,192,256]{2,1,0:T(8,128)(2,1)S(1)}, bf16[5,192,256]{2,1,0:T(8,128)(2,1)S(1)}, u32[]{:S(2)}, u32[]{:S(2)}) collective-permute-start(bf16[5,192,256]{2,1,0:T(8,128)(2,1)S(1)} %get-tuple-element.51), channel_id=1, source_target_pairs={{0,8},{4,12},{8,0},{12,4},{16,24},{20,28},{24,16},{28,20},{1,9},{5... | collective-permute-start | bytes 1474568 | tf_op jit(solution)/shard_map/ppermute | solution.py:292
  14.9 16.8 %collective-permute-start.1 = (bf16[5,192,256]{2,1,0:T(8,128)(2,1)S(1)}, bf16[5,192,256]{2,1,0:T(8,128)(2,1)S(1)}, u32[]{:S(2)}, u32[]{:S(2)}) collective-permute-start(bf16[5,192,256]{2,1,0:T(8,128)(2,1)S(1)} %get-tuple-element.52.refs_16_), channel_id=1, source_target_pairs={{0,4},{4,0},{8,12},{12,8},{16,20},{20,16},{24,28},{28,24},{1,5},{5... | collective-permute-start | bytes 1474568 | tf_op jit(solution)/shard_map/ppermute | solution.py:292
  14.9 16.8 %collective-permute-start.2 = (bf16[5,192,256]{2,1,0:T(8,128)(2,1)S(1)}, bf16[5,192,256]{2,1,0:T(8,128)(2,1)S(1)}, u32[]{:S(2)}, u32[]{:S(2)}) collective-permute-start(bf16[5,192,256]{2,1,0:T(8,128)(2,1)S(1)} %get-tuple-element.53), channel_id=1, source_target_pairs={{0,4},{4,0},{8,12},{12,8},{16,20},{20,16},{24,28},{28,24},{1,5},{5... | collective-permute-start | bytes 1474568 | tf_op jit(solution)/shard_map/ppermute | solution.py:292
  15.4 16.3 %collective-permute-start.3 = (bf16[5,192,256]{2,1,0:T(8,128)(2,1)S(1)}, bf16[5,192,256]{2,1,0:T(8,128)(2,1)S(1)}, u32[]{:S(2)}, u32[]{:S(2)}) collective-permute-start(bf16[5,192,256]{2,1,0:T(8,128)(2,1)S(1)} %get-tuple-element.60.refs_8_), channel_id=1, source_target_pairs={{0,16},{4,20},{8,24},{12,28},{16,0},{20,4},{24,8},{28,12},{1,17},{... | collective-permute-start | bytes 1474568 | tf_op jit(solution)/shard_map/ppermute | solution.py:292
  16.9 14.7 %collective-permute-start.4 = (bf16[80,1664]{1,0:T(8,128)(2,1)S(1)}, bf16[80,1664]{1,0:T(8,128)(2,1)}, u32[]{:S(2)}, u32[]{:S(2)}) collective-permute-start(bf16[80,1664]{1,0:T(8,128)(2,1)S(1)} %get-tuple-element.62.refs_0_), channel_id=1, source_target_pairs={{0,2},{1,3},{2,0},{3,1},{4,6},{5,7},{6,4},{7,5},{8,10},{9,11},{10,... | collective-permute-start | bytes 798728 | tf_op jit(solution)/shard_map/ppermute | solution.py:295
  32.3 12.4 %collective-permute-start.8 = (bf16[80,1664]{1,0:T(8,128)(2,1)}, bf16[80,1664]{1,0:T(8,128)(2,1)S(1)}, u32[]{:S(2)}, u32[]{:S(2)}) collective-permute-start(bf16[80,1664]{1,0:T(8,128)(2,1)} %collective-permute-done.4.refs_1_), channel_id=1, source_target_pairs={{0,1},{1,0},{2,3},{3,2},{4,5},{5,4},{6,7},{7,6},{8,9},{9,8},{10,11... | collective-permute-start | bytes 798728 | tf_op jit(solution)/shard_map/ppermute | solution.py:295
  33.8 11.5 %collective-permute-start.5 = (bf16[5,192,256]{2,1,0:T(8,128)(2,1)S(1)}, bf16[5,192,256]{2,1,0:T(8,128)(2,1)S(1)}, u32[]{:S(2)}, u32[]{:S(2)}) collective-permute-start(bf16[5,192,256]{2,1,0:T(8,128)(2,1)S(1)} %collective-permute-done.2), channel_id=1, source_target_pairs={{0,8},{4,12},{8,0},{12,4},{16,24},{20,28},{24,16},{28,20},{1,9},{5... | collective-permute-start | bytes 1474568 | tf_op jit(solution)/shard_map/ppermute | solution.py:292
  34.3 11.4 %collective-permute-start.6 = (bf16[5,192,256]{2,1,0:T(8,128)(2,1)S(1)}, bf16[5,192,256]{2,1,0:T(8,128)(2,1)}, u32[]{:S(2)}, u32[]{:S(2)}) collective-permute-start(bf16[5,192,256]{2,1,0:T(8,128)(2,1)S(1)} %collective-permute-done.1.refs_9_), channel_id=1, source_target_pairs={{0,16},{4,20},{8,24},{12,28},{16,0},{20,4},{24,8},{28,12},{1,17},{... | collective-permute-start | bytes 1474568 | tf_op jit(solution)/shard_map/ppermute | solution.py:292
  47.9 12.9 %collective-permute-start.12 = (bf16[5,192,256]{2,1,0:T(8,128)(2,1)S(1)}, bf16[5,192,256]{2,1,0:T(8,128)(2,1)}, u32[]{:S(2)}, u32[]{:S(2)}) collective-permute-start(bf16[5,192,256]{2,1,0:T(8,128)(2,1)S(1)} %collective-permute-done.refs_10_), channel_id=1, source_target_pairs={{0,16},{4,20},{8,24},{12,28},{16,0},{20,4},{24,8},{28,12},{1,17},{... | collective-permute-start | bytes 1474568 | tf_op jit(solution)/shard_map/ppermute | solution.py:292
  48.5 12.4 %collective-permute-start.15 = (bf16[5,192,256]{2,1,0:T(8,128)(2,1)S(1)}, bf16[5,192,256]{2,1,0:T(8,128)(2,1)}, u32[]{:S(2)}, u32[]{:S(2)}) collective-permute-start(bf16[5,192,256]{2,1,0:T(8,128)(2,1)S(1)} %collective-permute-done.5.refs_11_), channel_id=1, source_target_pairs={{0,4},{4,0},{8,12},{12,8},{16,20},{20,16},{24,28},{28,24},{1,5},{5... | collective-permute-start | bytes 1474568 | tf_op jit(solution)/shard_map/ppermute | solution.py:292
  48.5 12.4 %collective-permute-start.16 = (bf16[5,192,256]{2,1,0:T(8,128)(2,1)}, bf16[5,192,256]{2,1,0:T(8,128)(2,1)}, u32[]{:S(2)}, u32[]{:S(2)}) collective-permute-start(bf16[5,192,256]{2,1,0:T(8,128)(2,1)} %collective-permute-done.6.refs_13_), channel_id=1, source_target_pairs={{0,4},{4,0},{8,12},{12,8},{16,20},{20,16},{24,28},{28,24},{1,5},{5... | collective-permute-start | bytes 1474568 | tf_op jit(solution)/shard_map/ppermute | solution.py:292
  49.0 11.9 %collective-permute-start.14 = (bf16[80,1664]{1,0:T(8,128)(2,1)}, bf16[80,1664]{1,0:T(8,128)(2,1)}, u32[]{:S(2)}, u32[]{:S(2)}) collective-permute-start(bf16[80,1664]{1,0:T(8,128)(2,1)} %collective-permute-done.4.refs_1_), channel_id=1, source_target_pairs={{0,8},{4,12},{8,0},{12,4},{16,24},{20,28},{24,16},{28,20},{1,9},{5... | collective-permute-start | bytes 798728 | tf_op jit(solution)/shard_map/ppermute | solution.py:292
  60.8 13.7 %collective-permute-start.19 = (bf16[5,192,256]{2,1,0:T(8,128)(2,1)S(1)}, bf16[5,192,256]{2,1,0:T(8,128)(2,1)S(1)}, u32[]{:S(2)}, u32[]{:S(2)}) collective-permute-start(bf16[5,192,256]{2,1,0:T(8,128)(2,1)S(1)} %collective-permute-done.5.refs_11_), channel_id=1, source_target_pairs={{0,16},{4,20},{8,24},{12,28},{16,0},{20,4},{24,8},{28,12},{1,17},{... | collective-permute-start | bytes 1474568 | tf_op jit(solution)/shard_map/ppermute | solution.py:292
  62.9 16.3 %collective-permute-start.24 = (bf16[5,384,128]{2,1,0:T(8,128)(2,1)S(1)}, bf16[5,384,128]{2,1,0:T(8,128)(2,1)S(1)}, u32[]{:S(2)}, u32[]{:S(2)}) collective-permute-start(bf16[5,384,128]{2,1,0:T(8,128)(2,1)S(1)} %maximum_select_fusion.near_ref), channel_id=1, source_target_pairs={{0,4},{4,0},{8,12},{12,8},{16,20},{20,16},{24,28},{28,24},{1,5},{5... | collective-permute-start | bytes 1474568 | tf_op jit(solution)/shard_map/ppermute | solution.py:292
  63.2 16.0 %collective-permute-start.21 = (bf16[5,192,256]{2,1,0:T(8,128)(2,1)}, bf16[5,192,256]{2,1,0:T(8,128)(2,1)S(1)}, u32[]{:S(2)}, u32[]{:S(2)}) collective-permute-start(bf16[5,192,256]{2,1,0:T(8,128)(2,1)} %collective-permute-done.12.refs_14_), channel_id=1, source_target_pairs={{0,4},{4,0},{8,12},{12,8},{16,20},{20,16},{24,28},{28,24},{1,5},{5... | collective-permute-start | bytes 1474568 | tf_op jit(solution)/shard_map/ppermute | solution.py:292
  64.3 13.4 %collective-permute-start.18 = (bf16[80,1664]{1,0:T(8,128)(2,1)}, bf16[80,1664]{1,0:T(8,128)(2,1)S(1)}, u32[]{:S(2)}, u32[]{:S(2)}) collective-permute-start(bf16[80,1664]{1,0:T(8,128)(2,1)} %copy-done.15), channel_id=1, source_target_pairs={{0,8},{4,12},{8,0},{12,4},{16,24},{20,28},{24,16},{28,20},{1,9},{5... | collective-permute-start | bytes 798728 | tf_op jit(solution)/shard_map/ppermute | solution.py:292
  77.7 13.6 %collective-permute-start.23 = (bf16[5,384,128]{2,1,0:T(8,128)(2,1)S(1)}, bf16[5,384,128]{2,1,0:T(8,128)(2,1)S(1)}, u32[]{:S(2)}, u32[]{:S(2)}) collective-permute-start(bf16[5,384,128]{2,1,0:T(8,128)(2,1)S(1)} %maximum_select_fusion.near_ref), channel_id=1, source_target_pairs={{0,16},{4,20},{8,24},{12,28},{16,0},{20,4},{24,8},{28,12},{1,17},{... | collective-permute-start | bytes 1474568 | tf_op jit(solution)/shard_map/ppermute | solution.py:292
  79.3 12.3 %collective-permute-start.26 = (bf16[5,384,128]{2,1,0:T(8,128)(2,1)S(1)}, bf16[5,384,128]{2,1,0:T(8,128)(2,1)S(1)}, u32[]{:S(2)}, u32[]{:S(2)}) collective-permute-start(bf16[5,384,128]{2,1,0:T(8,128)(2,1)S(1)} %maximum_select_fusion.1), channel_id=1, source_target_pairs={{0,8},{4,12},{8,0},{12,4},{16,24},{20,28},{24,16},{28,20},{1,9},{5... | collective-permute-start | bytes 1474568 | tf_op jit(solution)/shard_map/ppermute | solution.py:292
  91.6 13.6 %collective-permute-start.32 = (bf16[5,384,128]{2,1,0:T(8,128)(2,1)S(1)}, bf16[5,384,128]{2,1,0:T(8,128)(2,1)S(1)}, u32[]{:S(2)}, u32[]{:S(2)}) collective-permute-start(bf16[5,384,128]{2,1,0:T(8,128)(2,1)S(1)} %collective-permute-done.26.far_ref), channel_id=1, source_target_pairs={{0,16},{4,20},{8,24},{12,28},{16,0},{20,4},{24,8},{28,12},{1,17},{... | collective-permute-start | bytes 1474568 | tf_op jit(solution)/shard_map/ppermute | solution.py:292
  92.1 18.2 %collective-permute-start.31 = (bf16[5,384,128]{2,1,0:T(8,128)(2,1)S(1)}, bf16[5,384,128]{2,1,0:T(8,128)(2,1)}, u32[]{:S(2)}, u32[]{:S(2)}) collective-permute-start(bf16[5,384,128]{2,1,0:T(8,128)(2,1)S(1)} %collective-permute-done.23.near_ref), channel_id=1, source_target_pairs={{0,4},{4,0},{8,12},{12,8},{16,20},{20,16},{24,28},{28,24},{1,5},{5... | collective-permute-start | bytes 1474568 | tf_op jit(solution)/shard_map/ppermute | solution.py:292
  96.7 13.6 %collective-permute-start.28 = (bf16[320,768]{1,0:T(8,128)(2,1)}, bf16[320,768]{1,0:T(8,128)(2,1)}, u32[]{:S(2)}, u32[]{:S(2)}) collective-permute-start(bf16[320,768]{1,0:T(8,128)(2,1)} %down.4), channel_id=1, source_target_pairs={{0,8},{4,12},{8,0},{12,4},{16,24},{20,28},{24,16},{28,20},{1,9},{5... | collective-permute-start | bytes 1474568 | tf_op jit(solution)/shard_map/ppermute | solution.py:292
  112.5 14.5 %collective-permute-start.34 = (bf16[320,384]{1,0:T(8,128)(2,1)S(1)}, bf16[320,384]{1,0:T(8,128)(2,1)S(1)}, u32[]{:S(2)}, u32[]{:S(2)}) collective-permute-start(bf16[320,384]{1,0:T(8,128)(2,1)S(1)} %get-tuple-element.91), channel_id=1, source_target_pairs={{0,8},{4,12},{8,0},{12,4},{16,24},{20,28},{24,16},{28,20},{1,9},{5... | collective-permute-start | bytes 737288 | tf_op jit(solution)/shard_map/ppermute | solution.py:292
  113.7 11.6 %collective-permute-start.37 = (bf16[320,384]{1,0:T(8,128)(2,1)S(1)}, bf16[320,384]{1,0:T(8,128)(2,1)S(1)}, u32[]{:S(2)}, u32[]{:S(2)}) collective-permute-start(bf16[320,384]{1,0:T(8,128)(2,1)S(1)} %get-tuple-element.95), channel_id=1, source_target_pairs={{0,8},{4,12},{8,0},{12,4},{16,24},{20,28},{24,16},{28,20},{1,9},{5... | collective-permute-start | bytes 737288 | tf_op jit(solution)/shard_map/ppermute | solution.py:292
  115.8 11.7 %collective-permute-start.29 = (bf16[160,768]{1,0:T(8,128)(2,1)S(1)}, bf16[160,768]{1,0:T(8,128)(2,1)S(1)}, u32[]{:S(2)}, u32[]{:S(2)}) collective-permute-start(bf16[160,768]{1,0:T(8,128)(2,1)S(1)} %slice.112), channel_id=1, source_target_pairs={{0,1},{1,0},{2,3},{3,2},{4,5},{5,4},{6,7},{7,6},{8,9},{9,8},{10,11... | collective-permute-start | bytes 737288 | tf_op jit(solution)/shard_map/ppermute | solution.py:295
  (48 other events, 405.7 us)

commit v7 on v6

v7 whole, which is shorter than its diff:
```python
import functools

import jax
import jax.numpy as jnp
from jax import lax
from jax.experimental import pallas as pl
from jax.experimental.pallas import tpu as pltpu
from jax.sharding import PartitionSpec as P

EPS = 1e-06
LOGIT_SCALE = 0.5
LANES = 128
LOW = 64
QUAD = 4


def normalize(values, gain):
    return values * lax.rsqrt(jnp.mean(values * values, axis=-1, keepdims=True) + EPS) * gain


def after(values, *others):
    return lax.optimization_barrier((values, *others))[0]


def after_all(values, *others):
    return list(lax.optimization_barrier((*values, *others)))[: len(values)]


def swap_blocks(values, index, blocks):
    size = values.shape[1] // blocks
    bit = 1
    while bit < blocks:
        swapped = jnp.concatenate(
            [values[:, (m ^ bit) * size : ((m ^ bit) + 1) * size] for m in range(blocks)], axis=1
        )
        values = jnp.where((index & bit) != 0, swapped, values)
        bit *= 2
    return values


def swap_lanes(values, index, blocks):
    width = values.shape[1]
    size = width // blocks
    lane = lax.broadcasted_iota(jnp.int32, values.shape, 1)
    bit = 1
    while bit < blocks:
        step = bit * size
        upper = (lane // step) % 2 == 1
        swapped = jnp.where(
            upper, pltpu.roll(values, step, 1), pltpu.roll(values, width - step, 1)
        )
        values = jnp.where((index & bit) != 0, swapped, values)
        bit *= 2
    return values


def front_kernel(
    ranks,
    att_ref,
    res_ref,
    w_ref,
    gain_ref,
    routes_ref,
    logits_ref,
    placed_ref,
    stream_ref,
    sent_ref,
    keep_ref,
):
    step = pl.program_id(0)
    cols = w_ref.shape[1]
    width = att_ref.shape[1]
    mixed = res_ref[...].astype(jnp.float32) + jnp.dot(
        att_ref[...], w_ref[...], preferred_element_type=jnp.float32
    )
    stored = mixed.astype(jnp.bfloat16)
    stream_ref[...] = stored
    keep_ref[:, pl.ds(pl.multiple_of(step * cols, cols), cols)] = stored.astype(jnp.float32)

    @pl.when(step == pl.num_programs(0) - 1)
    def _():
        normed = normalize(keep_ref[...], gain_ref[...])
        sent_ref[:, :width] = swap_lanes(normed, lax.axis_index("dp") // 2, ranks // 2).astype(jnp.bfloat16)
        scores = jnp.exp(logits_ref[...].astype(jnp.float32) * LOGIT_SCALE)
        gates = scores / jnp.sum(scores, axis=1, keepdims=True)
        routes = routes_ref[...]
        spread = jnp.zeros((gates.shape[0], LANES), jnp.float32)
        for k in range(gates.shape[1]):
            hit = routes[:, k : k + 1] == placed_ref[...]
            spread = jnp.where(hit, gates[:, k : k + 1], spread)
        high = spread.astype(jnp.bfloat16).astype(jnp.float32)
        lane = lax.broadcasted_iota(jnp.int32, spread.shape, 1)
        sent_ref[:, width:] = jnp.where(lane < LOW, high, spread - high).astype(jnp.bfloat16)


def front_call(ranks, attended, residual, weight, gain, routes, logits, placement):
    tok, width = attended.shape
    steps = 4
    cols = width // steps
    padded = jnp.pad(placement, (0, LOW - placement.shape[0]), constant_values=-1)
    placed = jnp.concatenate([padded, padded])[None, :]
    whole = lambda shape: pl.BlockSpec(shape, lambda i: (0, 0))
    return pl.pallas_call(
        functools.partial(front_kernel, ranks),
        grid=(steps,),
        in_specs=[
            whole((tok, width)),
            pl.BlockSpec((tok, cols), lambda i: (0, i)),
            pl.BlockSpec((width, cols), lambda i: (0, i)),
            whole((1, width)),
            whole(routes.shape),
            whole(logits.shape),
            whole((1, LANES)),
        ],
        out_specs=[
            pl.BlockSpec((tok, cols), lambda i: (0, i)),
            whole((tok, width + LANES)),
        ],
        out_shape=[
            jax.ShapeDtypeStruct((tok, width), jnp.bfloat16),
            jax.ShapeDtypeStruct((tok, width + LANES), jnp.bfloat16),
        ],
        scratch_shapes=[pltpu.VMEM((tok, width), jnp.float32)],
        compiler_params=pltpu.CompilerParams(vmem_limit_bytes=12 * 1024 * 1024),
        cost_estimate=pl.CostEstimate(flops=1, bytes_accessed=1, transcendentals=0),
        name="front",
    )(attended, residual, weight, gain[None, :], routes, logits, placed)


def cut(weight, out_ref, rows, part, c, s):
    for b in range(out_ref.shape[2] // part):
        at = pl.multiple_of(b * QUAD * part + (2 * c + s) * part, part)
        out_ref[:, rows, b * part : (b + 1) * part] = weight[:, :, pl.ds(at, part)]


def give_kernel(part, w_ref, near_ref, away_ref):
    core, side = lax.axis_index("dp") % 2, (lax.axis_index("dp") // 2) % 2
    cut(w_ref, near_ref, slice(None), part, 1 - core, side)
    cut(w_ref, away_ref, slice(None), part, 1 - core, 1 - side)


def join_kernel(part, w_ref, near_in_ref, away_in_ref, near_ref, away_ref):
    core, side = lax.axis_index("dp") % 2, (lax.axis_index("dp") // 2) % 2
    depth = w_ref.shape[1]
    here = pl.ds(pl.multiple_of(core * depth, depth), depth)
    there = pl.ds(pl.multiple_of((1 - core) * depth, depth), depth)
    cut(w_ref, near_ref, here, part, core, side)
    cut(w_ref, away_ref, here, part, core, 1 - side)
    near_ref[:, there, :] = near_in_ref[...]
    away_ref[:, there, :] = away_in_ref[...]


def weight_call(kernel, name, depth, part, weight, *received):
    local, _, cols = weight.shape
    out = jax.ShapeDtypeStruct((local, depth, cols // QUAD), jnp.bfloat16)
    whole = lambda v: pl.BlockSpec(v.shape, lambda i: (0, 0, 0))
    return pl.pallas_call(
        functools.partial(kernel, part),
        grid=(1,),
        in_specs=[whole(v) for v in (weight, *received)],
        out_specs=[whole(out)] * 2,
        out_shape=[out] * 2,
        compiler_params=pltpu.CompilerParams(vmem_limit_bytes=16 * 1024 * 1024),
        cost_estimate=pl.CostEstimate(flops=1, bytes_accessed=1, transcendentals=0),
        name=name,
    )(weight, *received)


def up_kernel(rows, count, *refs):
    here, away = refs[:count], refs[count : 2 * count]
    pieces = refs[2 * count : 2 * count + 4 * rows]
    out_ref, x_ref = refs[2 * count + 4 * rows :]
    zone = lax.axis_index("expert")
    local, half, width = pieces[0].shape
    part = width // 2
    feats = x_ref.shape[1] - LANES
    middle = x_ref.shape[0] // 2

    at = 0
    for block, across in zip(here, away):
        some = slice(at, at + block.shape[0])
        x_ref[some, :] = block[...]
        some = slice(middle + at, middle + at + block.shape[0])
        for j in range(2 * rows):
            to, come = j * half, (j ^ 1) * half
            x_ref[some, to : to + half] = across[:, come : come + half]
        x_ref[some, feats:] = across[:, feats:]
        at += block.shape[0]

    lane = lax.broadcasted_iota(jnp.int32, (LANES, width), 0)
    for e in range(local):
        mine, other = (
            jnp.concatenate([p[e] for p in pieces[2 * i * rows : 2 * (i + 1) * rows]], axis=0)
            for i in range(2)
        )
        w = jnp.concatenate(
            [mine[:, :part], other[:, :part], mine[:, part:], other[:, part:]], axis=1
        )
        slot = zone * local + e
        pick = jnp.where((lane == slot) | (lane == slot + LOW), 0.5, 0.0).astype(jnp.bfloat16)
        acc = jnp.dot(x_ref[:, :feats], w, preferred_element_type=jnp.float32)
        gate = jnp.dot(x_ref[:, feats:], pick, preferred_element_type=jnp.float32)
        g, u = acc[:, :width], acc[:, width:]
        out_ref[:, e * width : (e + 1) * width] = (
            (g + g * jnp.tanh(0.5 * g)) * (u * gate)
        ).astype(jnp.bfloat16)


def up_call(here, away, mine, other):
    local, _, cols = mine[0].shape
    lanes = here[0].shape[1]
    tokens = 2 * sum(v.shape[0] for v in here)
    operands = [*here, *away, *mine, *other]
    return pl.pallas_call(
        functools.partial(up_kernel, len(mine) // 2, len(here)),
        in_specs=[pl.BlockSpec(memory_space=pltpu.VMEM)] * len(operands),
        out_specs=pl.BlockSpec(memory_space=pltpu.VMEM),
        scratch_shapes=[pltpu.VMEM((tokens, lanes), jnp.bfloat16)],
        out_shape=jax.ShapeDtypeStruct((tokens, local * cols), jnp.bfloat16),
        compiler_params=pltpu.CompilerParams(vmem_limit_bytes=28 * 1024 * 1024),
        cost_estimate=pl.CostEstimate(flops=1, bytes_accessed=1, transcendentals=0),
        name="up",
    )(*operands)


def product(hidden, mine, other):
    w = [part[e] for e in range(mine.shape[0]) for part in (mine, other)]
    return lax.dot_general(
        hidden,
        jnp.concatenate(w, axis=1),
        (((1,), (1,)), ((), ())),
        preferred_element_type=jnp.float32,
    )


def down_kernel(start, h_ref, near_ref, near_other_ref, far_ref, far_other_ref, *out_refs):
    rows = out_refs[0].shape[0]
    feats = near_ref.shape[1]
    hidden = h_ref[start : start + rows, :]
    for j, pair in enumerate(((near_ref, near_other_ref), (far_ref, far_other_ref))):
        partial = product(hidden, *pair)
        if len(out_refs) == 2:
            out_refs[j][...] = partial.astype(out_refs[j].dtype)
        else:
            out_refs[0][:, j * feats : (j + 1) * feats] = partial.astype(out_refs[0].dtype)


def down_call(hidden, near, far, send, parts):
    tokens = hidden.shape[0] // 2
    feats = 2 * near[0].shape[1] // parts
    kind = jnp.bfloat16 if send else jnp.float32
    out = [jax.ShapeDtypeStruct((tokens, feats), kind)] * parts
    return pl.pallas_call(
        functools.partial(down_kernel, tokens if send else 0),
        in_specs=[pl.BlockSpec(memory_space=pltpu.VMEM)] * 5,
        out_specs=[pl.BlockSpec(memory_space=pltpu.VMEM)] * parts,
        out_shape=out,
        compiler_params=pltpu.CompilerParams(vmem_limit_bytes=16 * 1024 * 1024),
        cost_estimate=pl.CostEstimate(flops=1, bytes_accessed=1, transcendentals=0),
        name="down",
    )(hidden, *near, *far)


def body(
    attended,
    residual,
    out_weight,
    norm_gain,
    final_gain,
    routes,
    gate_logits,
    placement,
    gate_up,
    down_weight,
):
    ranks = lax.axis_size("dp")
    zones = lax.axis_size("expert")
    rows = ranks // QUAD
    me = lax.axis_index("dp")
    hid = down_weight.shape[2]
    part = hid // QUAD

    def flip(values, bit):
        return lax.ppermute(values, "dp", [(i, i ^ bit) for i in range(ranks)])

    def hop(values, bit):
        return lax.ppermute(values, "expert", [(i, i ^ bit) for i in range(zones)])

    def widen(pieces):
        bit = 1
        while bit < rows:
            pieces = pieces + [flip(p, bit * QUAD) for p in pieces]
            bit *= 2
        return pieces

    zone_bits = []
    while 1 << len(zone_bits) < zones:
        zone_bits.append(1 << len(zone_bits))
    depth = gate_up.shape[1]
    give = weight_call(give_kernel, "give", depth, part, gate_up)
    got = [flip(v, 1) for v in give]
    gu_near, gu_away = weight_call(join_kernel, "join", 2 * depth, part, gate_up, *got)
    gu_far = flip(gu_away, 2)
    gu_nears = widen([gu_near])

    stored, sent = front_call(
        ranks,
        after(attended, give[0]),
        residual,
        out_weight,
        norm_gain,
        routes,
        gate_logits,
        placement,
    )
    stream_in = stored.astype(jnp.float32)
    near = sent
    for bit in reversed(zone_bits[1:]):
        near = jnp.concatenate([near, hop(near, bit)], axis=0)
    far = hop(near, 1)
    gu_near_other = flip(gu_near, 1)
    near_x = flip(after(near, gu_far, gu_near_other), 2)
    gu_fars = widen([after(gu_far, gu_nears[-1])])
    gu_nears_other = [gu_near_other] + [flip(v, 1) for v in gu_nears[1:]]
    gu_far_other = flip(gu_far, 1)
    far_x = flip(after(far, near_x, gu_far_other, *gu_nears_other[1:]), 2)
    gu_fars_other = [gu_far_other] + [flip(v, 1) for v in gu_fars[1:]]
    mine = [v for pair in zip(gu_nears, gu_fars) for v in pair]
    other = [v for pair in zip(gu_nears_other, gu_fars_other) for v in pair]

    down_weight = after(down_weight, sent)
    give = weight_call(give_kernel, "give", depth, part, down_weight)
    got = [flip(v, 1) for v in give]
    dn_near, dn_away = weight_call(join_kernel, "join", 2 * depth, part, down_weight, *got)
    dn_near_other = flip(dn_near, 1)
    dn_far = flip(after(dn_away, far_x, dn_near_other), 2)
    dn_nears = widen([after(dn_near, gu_fars[-1])])

    hidden = up_call([near, far], [near_x, far_x], mine, other)
    hidden = after(hidden, dn_nears[-1])
    dn_far = after(dn_far, hidden)
    dn_fars = widen([dn_far])
    nears = [(dn_near, dn_near_other)] + [(v, flip(after(v, hidden), 1)) for v in dn_nears[1:]]
    fars = [(dn_far, flip(dn_far, 1))]

    chunks, crossed = [], []
    for m in range(rows):
        parts = 2 if m == rows - 1 else 1
        if m > 0:
            fars.append((dn_fars[m], flip(after(dn_fars[m], sends[0]), 1)))
        sends = down_call(after(hidden, *crossed), nears[m], fars[m], True, parts)
        keeps = down_call(after(hidden, sends[0]), nears[m], fars[m], False, parts)
        crossed = []
        for i, keep in enumerate(keeps):
            crossed.append(flip(sends[parts - 1 - i], 2))
            total = crossed[-1]
            if parts == 1:
                size = total.shape[1] // 2
                total = jnp.concatenate([total[:, size:], total[:, :size]], axis=1)
            total = keep + total.astype(jnp.float32)
            for bit in zone_bits:
                size = total.shape[0] // 2
                moved = total[size:].astype(jnp.bfloat16)
                total = total[:size] + hop(moved, bit).astype(jnp.float32)
            chunks.append(total)
    branch = swap_blocks(jnp.concatenate(chunks, axis=1), me // 2, 2 * rows)
    total = stream_in + branch
    return (total.astype(jnp.bfloat16), normalize(total, final_gain).astype(jnp.bfloat16))


def solution(mesh):
    tokens = P(("dp", "expert"), None)
    weights = P("expert", "dp", None)
    return jax.shard_map(
        body,
        mesh=mesh,
        in_specs=(tokens, tokens, P(), P(), P(), tokens, tokens, P(), weights, weights),
        out_specs=(tokens, tokens),
        check_vma=False,
    )
```

time: 143 us -> 122 us (0.85)
  local copies, waits for them, and re-layouts: 18.7 us -> 9.76 us
  Pallas kernels: 22.1 us -> 17.1 us
  starting transfers between devices: 35.8 us -> 32.1 us
  other arithmetic: 4.21 us -> 1.44 us
    ppermute x9 -> x8, waiting for transfers between devices: 26.4 us -> 15.1 us  [hop(): return lax.ppermute(values, 'expert', [(i, i ^ bit) for i in range(zones)])]
    ppermute x31 -> x23, waiting for transfers between devices: 34.3 us -> 44.9 us  [flip(): return lax.ppermute(values, 'dp', [(i, i ^ bit) for i in range(ranks)])]
    unnamed x66 -> x39, local copies, waits for them, and re-layouts: 16.1 us -> 8.83 us
    pallas_call x3 -> x6, Pallas kernels: 14.9 us -> 11 us  [the longest x1 6.89 us: up_call(): pl.pallas_call(functools.partial(up_kernel, len(mine) // 2, len(here)), i...]
    select_n x2 -> x0, other arithmetic: 2.68 us -> none  [pair(): jnp.where(core == 0, jnp.concatenate([own, mate], axis=1), jnp.concatenat...]
    ppermute x31 -> x23, starting transfers between devices: 18.4 us -> 15.9 us  [flip(): return lax.ppermute(values, 'dp', [(i, i ^ bit) for i in range(ranks)])]
    ppermute x9 -> x8, starting transfers between devices: 17.4 us -> 16.3 us  [hop(): return lax.ppermute(values, 'expert', [(i, i ^ bit) for i in range(zones)])]
  transfers between devices with their start and end apart: 40 -> 31, of which waited for: 18 -> 19; matrix products, arithmetic and copies ran while one was open for 3% -> 1% of each run, Pallas kernels for 11% -> 13%
where the time goes in v7:
time: 122 us; the launch traced here: 121 us
  waiting for transfers between devices  60 us (49%)
  starting transfers between devices  32.1 us (26%)
  Pallas kernels  17.1 us (14%)
  local copies, waits for them, and re-layouts  9.76 us (8%)
  other arithmetic  1.44 us (1%)
    ppermute x23, waiting for transfers between devices, flip(): return lax.ppermute(values, 'dp', [(i, i ^ bit) for i in range(ranks)])  44.9 us
    ppermute x8, starting transfers between devices, hop(): return lax.ppermute(values, 'expert', [(i, i ^ bit) for i in range(zones)])  16.3 us
    ppermute x23, starting transfers between devices, flip(): return lax.ppermute(values, 'dp', [(i, i ^ bit) for i in range(ranks)])  15.9 us
    ppermute x8, waiting for transfers between devices, hop(): return lax.ppermute(values, 'expert', [(i, i ^ bit) for i in range(zones)])  15.1 us
    unnamed x39, local copies, waits for them, and re-layouts  8.83 us
    pallas_call x1, Pallas kernels, up_call(): pl.pallas_call(functools.partial(up_kernel, len(mine) // 2, len(here)), i...  6.89 us
    pallas_call x4, Pallas kernels, down_call(): pl.pallas_call(functools.partial(down_kernel, tokens if send else 0), in_...  6.1 us
  transfers between devices with their start and end apart: 31, of which 19 were waited for; matrix products, arithmetic and copies ran while one was open for 1% of the time, Pallas kernels for 13%

profile of v7, /device:TPU:0, one launch (start us, length us, event | category | flops | bytes accessed | tf_op | source)
XLA Modules:
  0.0 121.5 jit_solution(18068227665239834926)
XLA Ops:
  6.5 2.9 %collective-permute-start.8 = (bf16[5,384,256]{2,1,0:T(8,128)(2,1)S(1)}, bf16[5,384,256]{2,1,0:T(8,128)(2,1)S(1)}, u32[]{:S(2)}, u32[]{:S(2)}) collective-permute-start(bf16[5,384,256]{2,1,0:T(8,128)(2,1)S(1)} %get-tuple-element.36.refs_4_), channel_id=1, source_target_pairs={{0,16},{4,20},{8,24},{12,28},{16,0},{20,4},{24,8},{28,12},{1,17},{... | collective-permute-start | bytes 2949128 | tf_op jit(solution)/shard_map/ppermute | solution.py:284
  11.2 2.3 %copy-done.1 = bf16[1536,1536]{1,0:T(8,128)(2,1)S(1)} copy-done((bf16[1536,1536]{1,0:T(8,128)(2,1)S(1)}, bf16[1536,1536]{1,0:T(8,128)(2,1)}, u32[]{:S(2)}) %copy-start.1) | copy-done | bytes 4718616
  14.5 2.4 %front.1 = (bf16[80,1536]{1,0:T(8,128)(2,1)S(1)}, bf16[80,1664]{1,0:T(8,128)(2,1)S(1)}) custom-call(bf16[80,1536]{1,0:T(8,128)(2,1)S(1)} %copy-done.7, bf16[80,1536]{1,0:T(8,128)(2,1)S(1)} %copy-done.8, bf16[1536,1536]{1,0:T(8,128)(2,1)S(1)} %copy-done.1, f32[1,1536]{1,0:T(1,128)S(1)} %broadcast_in_dim.8.gain_ref, s32[80,8]{1,0:T(8,128)S(1)} %copy.12.routes_ref, ...), custom_call_target="tpu_custom_call" | custom-call | flops 1 | bytes 1 | tf_op jit(solution)/shard_map/front/pallas_call | solution.py:103
  16.9 2.6 %collective-permute-start = (bf16[80,1664]{1,0:T(8,128)(2,1)S(1)}, bf16[80,1664]{1,0:T(8,128)(2,1)S(1)}, u32[]{:S(2)}, u32[]{:S(2)}) collective-permute-start(bf16[80,1664]{1,0:T(8,128)(2,1)S(1)} %get-tuple-element.33), channel_id=1, source_target_pairs={{0,2},{1,3},{2,0},{3,1},{4,6},{5,7},{6,4},{7,5},{8,10},{9,11},{10,... | collective-permute-start | bytes 798728 | tf_op jit(solution)/shard_map/ppermute | solution.py:287
  19.5 11.9 %collective-permute-done.8.refs_6_ = bf16[5,384,256]{2,1,0:T(8,128)(2,1)S(1)} collective-permute-done((bf16[5,384,256]{2,1,0:T(8,128)(2,1)S(1)}, bf16[5,384,256]{2,1,0:T(8,128)(2,1)S(1)}, u32[]{:S(2)}, u32[]{:S(2)}) %collective-permute-start.8) | collective-permute-done | bytes 983072 | tf_op jit(solution)/shard_map/ppermute | solution.py:284
  31.4 1.7 %collective-permute-done.4.refs_5_ = bf16[5,384,256]{2,1,0:T(8,128)(2,1)S(1)} collective-permute-done((bf16[5,384,256]{2,1,0:T(8,128)(2,1)}, bf16[5,384,256]{2,1,0:T(8,128)(2,1)S(1)}, u32[]{:S(2)}, u32[]{:S(2)}) %collective-permute-start.4) | collective-permute-done | bytes 983072 | tf_op jit(solution)/shard_map/ppermute | solution.py:284
  33.8 1.6 %collective-permute-start.1 = (bf16[160,1664]{1,0:T(8,128)(2,1)S(1)}, bf16[160,1664]{1,0:T(8,128)(2,1)S(1)}, u32[]{:S(2)}, u32[]{:S(2)}) collective-permute-start(bf16[160,1664]{1,0:T(8,128)(2,1)S(1)} %constant_dynamic-update-slice_fusion.refs_0_), channel_id=1, source_target_pairs={{0,1},{1,0},{2,3},{3,2},{4,5},{5,4},{6,7},{7,6},{8,9},{9,8},{10,11... | collective-permute-start | bytes 1597448 | tf_op jit(solution)/shard_map/ppermute | solution.py:287
  37.1 10.8 %collective-permute-done.1.refs_1_ = bf16[160,1664]{1,0:T(8,128)(2,1)S(1)} collective-permute-done((bf16[160,1664]{1,0:T(8,128)(2,1)S(1)}, bf16[160,1664]{1,0:T(8,128)(2,1)S(1)}, u32[]{:S(2)}, u32[]{:S(2)}) %collective-permute-start.1) | collective-permute-done | bytes 532512 | tf_op jit(solution)/shard_map/ppermute | solution.py:287
  49.4 1.6 %collective-permute-start.10 = (bf16[160,1664]{1,0:T(8,128)(2,1)S(1)}, bf16[160,1664]{1,0:T(8,128)(2,1)S(1)}, u32[]{:S(2)}, u32[]{:S(2)}) collective-permute-start(bf16[160,1664]{1,0:T(8,128)(2,1)S(1)} %collective-permute-done.1.refs_1_), channel_id=1, source_target_pairs={{0,8},{4,12},{8,0},{12,4},{16,24},{20,28},{24,16},{28,20},{1,9},{5... | collective-permute-start | bytes 1597448 | tf_op jit(solution)/shard_map/ppermute | solution.py:284
  51.3 6.1 %collective-permute-done.11.refs_7_ = bf16[5,384,256]{2,1,0:T(8,128)(2,1)S(1)} collective-permute-done((bf16[5,384,256]{2,1,0:T(8,128)(2,1)S(1)}, bf16[5,384,256]{2,1,0:T(8,128)(2,1)S(1)}, u32[]{:S(2)}, u32[]{:S(2)}) %collective-permute-start.11) | collective-permute-done | bytes 983072 | tf_op jit(solution)/shard_map/ppermute | solution.py:284
  57.7 6.2 %collective-permute-done.10.refs_3_ = bf16[160,1664]{1,0:T(8,128)(2,1)S(1)} collective-permute-done((bf16[160,1664]{1,0:T(8,128)(2,1)S(1)}, bf16[160,1664]{1,0:T(8,128)(2,1)S(1)}, u32[]{:S(2)}, u32[]{:S(2)}) %collective-permute-start.10) | collective-permute-done | bytes 532512 | tf_op jit(solution)/shard_map/ppermute | solution.py:284
  67.8 6.9 %up.1.h_ref = bf16[640,1280]{1,0:T(8,128)(2,1)S(1)} custom-call(bf16[160,1664]{1,0:T(8,128)(2,1)S(1)} %constant_dynamic-update-slice_fusion.refs_0_, bf16[160,1664]{1,0:T(8,128)(2,1)S(1)} %collective-permute-done.1.refs_1_, bf16[160,1664]{1,0:T(8,128)(2,1)S(1)} %collective-permute-done.6.refs_2_, bf16[160,1664]{1,0:T(8,128)(2,1)S(1)} %collective-permute-done.10.refs_3_, ...), custom_call_target="tpu_custom_call" | custom-call | flops 1 | bytes 1 | tf_op jit(solution)/shard_map/up/pallas_call | solution.py:214
  74.7 2.0 %collective-permute-done.17.far_ref = bf16[5,384,128]{2,1,0:T(8,128)(2,1)S(1)} collective-permute-done((bf16[5,384,128]{2,1,0:T(8,128)(2,1)S(1)}, bf16[5,384,128]{2,1,0:T(8,128)(2,1)S(1)}, u32[]{:S(2)}, u32[]{:S(2)}) %collective-permute-start.17) | collective-permute-done | bytes 491552 | tf_op jit(solution)/shard_map/ppermute | solution.py:284
  79.5 1.6 %collective-permute-start.19 = (bf16[320,768]{1,0:T(8,128)(2,1)S(1)}, bf16[320,768]{1,0:T(8,128)(2,1)S(1)}, u32[]{:S(2)}, u32[]{:S(2)}) collective-permute-start(bf16[320,768]{1,0:T(8,128)(2,1)S(1)} %down.4), channel_id=1, source_target_pairs={{0,8},{4,12},{8,0},{12,4},{16,24},{20,28},{24,16},{28,20},{1,9},{5... | collective-permute-start | bytes 1474568 | tf_op jit(solution)/shard_map/ppermute | solution.py:284
  81.1 9.2 %collective-permute-done.23.far_ref = bf16[5,384,128]{2,1,0:T(8,128)(2,1)S(1)} collective-permute-done((bf16[5,384,128]{2,1,0:T(8,128)(2,1)S(1)}, bf16[5,384,128]{2,1,0:T(8,128)(2,1)S(1)}, u32[]{:S(2)}, u32[]{:S(2)}) %collective-permute-start.23) | collective-permute-done | bytes 491552 | tf_op jit(solution)/shard_map/ppermute | solution.py:284
  94.7 2.0 %down.6 = (bf16[320,384]{1,0:T(8,128)(2,1)S(1)}, bf16[320,384]{1,0:T(8,128)(2,1)S(1)}) custom-call(bf16[640,1280]{1,0:T(8,128)(2,1)S(1)} %up.1.h_ref, bf16[5,384,128]{2,1,0:T(8,128)(2,1)S(1)} %collective-permute-done.15.near_ref, bf16[5,384,128]{2,1,0:T(8,128)(2,1)S(1)} %collective-permute-done.22.near_other_ref, ...), custom_call_target="tpu_custom_call" | custom-call | flops 1 | bytes 1 | tf_op jit(solution)/shard_map/down/pallas_call | solution.py:253
  96.8 1.7 %collective-permute-start.25 = (bf16[320,384]{1,0:T(8,128)(2,1)S(1)}, bf16[320,384]{1,0:T(8,128)(2,1)S(1)}, u32[]{:S(2)}, u32[]{:S(2)}) collective-permute-start(bf16[320,384]{1,0:T(8,128)(2,1)S(1)} %get-tuple-element.53), channel_id=1, source_target_pairs={{0,8},{4,12},{8,0},{12,4},{16,24},{20,28},{24,16},{28,20},{1,9},{5... | collective-permute-start | bytes 737288 | tf_op jit(solution)/shard_map/ppermute | solution.py:284
  98.9 2.0 %down.7 = (f32[320,384]{1,0:T(8,128)S(1)}, f32[320,384]{1,0:T(8,128)S(1)}) custom-call(bf16[640,1280]{1,0:T(8,128)(2,1)S(1)} %up.1.h_ref, bf16[5,384,128]{2,1,0:T(8,128)(2,1)S(1)} %collective-permute-done.15.near_ref, bf16[5,384,128]{2,1,0:T(8,128)(2,1)S(1)} %collective-permute-done.22.near_other_ref, ...), custom_call_target="tpu_custom_call" | custom-call | flops 1 | bytes 1 | tf_op jit(solution)/shard_map/down/pallas_call | solution.py:253
  102.2 2.6 %collective-permute-start.21 = (bf16[80,768]{1,0:T(8,128)(2,1)S(1)}, bf16[80,768]{1,0:T(8,128)(2,1)S(1)}, u32[]{:S(2)}, u32[]{:S(2)}) collective-permute-start(bf16[80,768]{1,0:T(8,128)(2,1)S(1)} %slice.115), channel_id=1, source_target_pairs={{0,2},{1,3},{2,0},{3,1},{4,6},{5,7},{6,4},{7,5},{8,10},{9,11},{10,... | collective-permute-start | bytes 368648 | tf_op jit(solution)/shard_map/ppermute | solution.py:287
  105.8 2.1 %collective-permute-start.26 = (bf16[160,384]{1,0:T(8,128)(2,1)S(1)}, bf16[160,384]{1,0:T(8,128)(2,1)S(1)}, u32[]{:S(2)}, u32[]{:S(2)}) collective-permute-start(bf16[160,384]{1,0:T(8,128)(2,1)S(1)} %slice.114), channel_id=1, source_target_pairs={{0,1},{1,0},{2,3},{3,2},{4,5},{5,4},{6,7},{7,6},{8,9},{9,8},{10,11... | collective-permute-start | bytes 368648 | tf_op jit(solution)/shard_map/ppermute | solution.py:287
  109.4 1.8 %collective-permute-start.29 = (bf16[160,384]{1,0:T(8,128)(2,1)S(1)}, bf16[160,384]{1,0:T(8,128)(2,1)S(1)}, u32[]{:S(2)}, u32[]{:S(2)}) collective-permute-start(bf16[160,384]{1,0:T(8,128)(2,1)S(1)} %slice.113), channel_id=1, source_target_pairs={{0,1},{1,0},{2,3},{3,2},{4,5},{5,4},{6,7},{7,6},{8,9},{9,8},{10,11... | collective-permute-start | bytes 368648 | tf_op jit(solution)/shard_map/ppermute | solution.py:287
  111.4 3.2 %collective-permute-start.27 = (bf16[80,384]{1,0:T(8,128)(2,1)S(1)}, bf16[80,384]{1,0:T(8,128)(2,1)S(1)}, u32[]{:S(2)}, u32[]{:S(2)}) collective-permute-start(bf16[80,384]{1,0:T(8,128)(2,1)S(1)} %slice.117), channel_id=1, source_target_pairs={{0,2},{1,3},{2,0},{3,1},{4,6},{5,7},{6,4},{7,5},{8,10},{9,11},{10,... | collective-permute-start | bytes 184328 | tf_op jit(solution)/shard_map/ppermute | solution.py:287
  114.7 2.3 %collective-permute-start.30 = (bf16[80,384]{1,0:T(8,128)(2,1)S(1)}, bf16[80,384]{1,0:T(8,128)(2,1)S(1)}, u32[]{:S(2)}, u32[]{:S(2)}) collective-permute-start(bf16[80,384]{1,0:T(8,128)(2,1)S(1)} %slice.116), channel_id=1, source_target_pairs={{0,2},{1,3},{2,0},{3,1},{4,6},{5,7},{6,4},{7,5},{8,10},{9,11},{10,... | collective-permute-start | bytes 184328 | tf_op jit(solution)/shard_map/ppermute | solution.py:287
  117.3 2.6 %collective-permute-done.30 = bf16[80,384]{1,0:T(8,128)(2,1)S(1)} collective-permute-done((bf16[80,384]{1,0:T(8,128)(2,1)S(1)}, bf16[80,384]{1,0:T(8,128)(2,1)S(1)}, u32[]{:S(2)}, u32[]{:S(2)}) %collective-permute-start.30) | collective-permute-done | bytes 61472 | tf_op jit(solution)/shard_map/ppermute | solution.py:287
  (113 shorter events, 30.3 us)
Async XLA Ops:
  6.5 25.0 %collective-permute-start.8 = (bf16[5,384,256]{2,1,0:T(8,128)(2,1)S(1)}, bf16[5,384,256]{2,1,0:T(8,128)(2,1)S(1)}, u32[]{:S(2)}, u32[]{:S(2)}) collective-permute-start(bf16[5,384,256]{2,1,0:T(8,128)(2,1)S(1)} %get-tuple-element.36.refs_4_), channel_id=1, source_target_pairs={{0,16},{4,20},{8,24},{12,28},{16,0},{20,4},{24,8},{28,12},{1,17},{... | collective-permute-start | bytes 2949128 | tf_op jit(solution)/shard_map/ppermute | solution.py:284
  9.4 23.7 %collective-permute-start.4 = (bf16[5,384,256]{2,1,0:T(8,128)(2,1)}, bf16[5,384,256]{2,1,0:T(8,128)(2,1)S(1)}, u32[]{:S(2)}, u32[]{:S(2)}) collective-permute-start(bf16[5,384,256]{2,1,0:T(8,128)(2,1)} %get-tuple-element.35), channel_id=1, source_target_pairs={{0,8},{4,12},{8,0},{12,4},{16,24},{20,28},{24,16},{28,20},{1,9},{5... | collective-permute-start | bytes 2949128 | tf_op jit(solution)/shard_map/ppermute | solution.py:284
  10.9 24.6 %collective-permute-start.5 = (bf16[5,384,256]{2,1,0:T(8,128)(2,1)S(1)}, bf16[5,384,256]{2,1,0:T(8,128)(2,1)}, u32[]{:S(2)}, u32[]{:S(2)}) collective-permute-start(bf16[5,384,256]{2,1,0:T(8,128)(2,1)S(1)} %get-tuple-element.36.refs_4_), channel_id=1, source_target_pairs={{0,4},{4,0},{8,12},{12,8},{16,20},{20,16},{24,28},{28,24},{1,5},{5... | collective-permute-start | bytes 2949128 | tf_op jit(solution)/shard_map/ppermute | solution.py:284
  16.9 16.9 %collective-permute-start = (bf16[80,1664]{1,0:T(8,128)(2,1)S(1)}, bf16[80,1664]{1,0:T(8,128)(2,1)S(1)}, u32[]{:S(2)}, u32[]{:S(2)}) collective-permute-start(bf16[80,1664]{1,0:T(8,128)(2,1)S(1)} %get-tuple-element.33), channel_id=1, source_target_pairs={{0,2},{1,3},{2,0},{3,1},{4,6},{5,7},{6,4},{7,5},{8,10},{9,11},{10,... | collective-permute-start | bytes 798728 | tf_op jit(solution)/shard_map/ppermute | solution.py:287
  31.4 17.9 %collective-permute-start.9 = (bf16[5,384,256]{2,1,0:T(8,128)(2,1)S(1)}, bf16[5,384,256]{2,1,0:T(8,128)(2,1)S(1)}, u32[]{:S(2)}, u32[]{:S(2)}) collective-permute-start(bf16[5,384,256]{2,1,0:T(8,128)(2,1)S(1)} %collective-permute-done.8.refs_6_), channel_id=1, source_target_pairs={{0,4},{4,0},{8,12},{12,8},{16,20},{20,16},{24,28},{28,24},{1,5},{5... | collective-permute-start | bytes 2949128 | tf_op jit(solution)/shard_map/ppermute | solution.py:284
  33.1 16.3 %collective-permute-start.7 = (bf16[5,384,256]{2,1,0:T(8,128)(2,1)S(1)}, bf16[5,384,256]{2,1,0:T(8,128)(2,1)S(1)}, u32[]{:S(2)}, u32[]{:S(2)}) collective-permute-start(bf16[5,384,256]{2,1,0:T(8,128)(2,1)S(1)} %collective-permute-done.4.refs_5_), channel_id=1, source_target_pairs={{0,4},{4,0},{8,12},{12,8},{16,20},{20,16},{24,28},{28,24},{1,5},{5... | collective-permute-start | bytes 2949128 | tf_op jit(solution)/shard_map/ppermute | solution.py:284
  33.1 24.2 %collective-permute-start.11 = (bf16[5,384,256]{2,1,0:T(8,128)(2,1)S(1)}, bf16[5,384,256]{2,1,0:T(8,128)(2,1)S(1)}, u32[]{:S(2)}, u32[]{:S(2)}) collective-permute-start(bf16[5,384,256]{2,1,0:T(8,128)(2,1)S(1)} %collective-permute-done.4.refs_5_), channel_id=1, source_target_pairs={{0,16},{4,20},{8,24},{12,28},{16,0},{20,4},{24,8},{28,12},{1,17},{... | collective-permute-start | bytes 2949128 | tf_op jit(solution)/shard_map/ppermute | solution.py:284
  33.8 14.1 %collective-permute-start.1 = (bf16[160,1664]{1,0:T(8,128)(2,1)S(1)}, bf16[160,1664]{1,0:T(8,128)(2,1)S(1)}, u32[]{:S(2)}, u32[]{:S(2)}) collective-permute-start(bf16[160,1664]{1,0:T(8,128)(2,1)S(1)} %constant_dynamic-update-slice_fusion.refs_0_), channel_id=1, source_target_pairs={{0,1},{1,0},{2,3},{3,2},{4,5},{5,4},{6,7},{7,6},{8,9},{9,8},{10,11... | collective-permute-start | bytes 1597448 | tf_op jit(solution)/shard_map/ppermute | solution.py:287
  35.5 13.9 %collective-permute-start.6 = (bf16[160,1664]{1,0:T(8,128)(2,1)S(1)}, bf16[160,1664]{1,0:T(8,128)(2,1)S(1)}, u32[]{:S(2)}, u32[]{:S(2)}) collective-permute-start(bf16[160,1664]{1,0:T(8,128)(2,1)S(1)} %constant_dynamic-update-slice_fusion.refs_0_), channel_id=1, source_target_pairs={{0,8},{4,12},{8,0},{12,4},{16,24},{20,28},{24,16},{28,20},{1,9},{5... | collective-permute-start | bytes 1597448 | tf_op jit(solution)/shard_map/ppermute | solution.py:284
  49.4 14.5 %collective-permute-start.10 = (bf16[160,1664]{1,0:T(8,128)(2,1)S(1)}, bf16[160,1664]{1,0:T(8,128)(2,1)S(1)}, u32[]{:S(2)}, u32[]{:S(2)}) collective-permute-start(bf16[160,1664]{1,0:T(8,128)(2,1)S(1)} %collective-permute-done.1.refs_1_), channel_id=1, source_target_pairs={{0,8},{4,12},{8,0},{12,4},{16,24},{20,28},{24,16},{28,20},{1,9},{5... | collective-permute-start | bytes 1597448 | tf_op jit(solution)/shard_map/ppermute | solution.py:284
  51.1 6.6 %collective-permute-start.16 = (bf16[5,384,128]{2,1,0:T(8,128)(2,1)S(1)}, bf16[5,384,128]{2,1,0:T(8,128)(2,1)S(1)}, u32[]{:S(2)}, u32[]{:S(2)}) collective-permute-start(bf16[5,384,128]{2,1,0:T(8,128)(2,1)S(1)} %get-tuple-element.44.near_ref), channel_id=1, source_target_pairs={{0,4},{4,0},{8,12},{12,8},{16,20},{20,16},{24,28},{28,24},{1,5},{5... | collective-permute-start | bytes 1474568 | tf_op jit(solution)/shard_map/ppermute | solution.py:284
  57.4 8.0 %collective-permute-start.12 = (bf16[5,384,256]{2,1,0:T(8,128)(2,1)S(1)}, bf16[5,384,256]{2,1,0:T(8,128)(2,1)S(1)}, u32[]{:S(2)}, u32[]{:S(2)}) collective-permute-start(bf16[5,384,256]{2,1,0:T(8,128)(2,1)S(1)} %collective-permute-done.11.refs_7_), channel_id=1, source_target_pairs={{0,4},{4,0},{8,12},{12,8},{16,20},{20,16},{24,28},{28,24},{1,5},{5... | collective-permute-start | bytes 2949128 | tf_op jit(solution)/shard_map/ppermute | solution.py:284
  57.4 17.3 %collective-permute-start.15 = (bf16[5,384,128]{2,1,0:T(8,128)(2,1)S(1)}, bf16[5,384,128]{2,1,0:T(8,128)(2,1)S(1)}, u32[]{:S(2)}, u32[]{:S(2)}) collective-permute-start(bf16[5,384,128]{2,1,0:T(8,128)(2,1)S(1)} %get-tuple-element.44.near_ref), channel_id=1, source_target_pairs={{0,16},{4,20},{8,24},{12,28},{16,0},{20,4},{24,8},{28,12},{1,17},{... | collective-permute-start | bytes 1474568 | tf_op jit(solution)/shard_map/ppermute | solution.py:284
  63.9 12.8 %collective-permute-start.17 = (bf16[5,384,128]{2,1,0:T(8,128)(2,1)S(1)}, bf16[5,384,128]{2,1,0:T(8,128)(2,1)S(1)}, u32[]{:S(2)}, u32[]{:S(2)}) collective-permute-start(bf16[5,384,128]{2,1,0:T(8,128)(2,1)S(1)} %get-tuple-element.47), channel_id=1, source_target_pairs={{0,8},{4,12},{8,0},{12,4},{16,24},{20,28},{24,16},{28,20},{1,9},{5... | collective-permute-start | bytes 1474568 | tf_op jit(solution)/shard_map/ppermute | solution.py:284
  76.7 13.6 %collective-permute-start.23 = (bf16[5,384,128]{2,1,0:T(8,128)(2,1)S(1)}, bf16[5,384,128]{2,1,0:T(8,128)(2,1)S(1)}, u32[]{:S(2)}, u32[]{:S(2)}) collective-permute-start(bf16[5,384,128]{2,1,0:T(8,128)(2,1)S(1)} %collective-permute-done.17.far_ref), channel_id=1, source_target_pairs={{0,16},{4,20},{8,24},{12,28},{16,0},{20,4},{24,8},{28,12},{1,17},{... | collective-permute-start | bytes 1474568 | tf_op jit(solution)/shard_map/ppermute | solution.py:284
  79.5 13.3 %collective-permute-start.19 = (bf16[320,768]{1,0:T(8,128)(2,1)S(1)}, bf16[320,768]{1,0:T(8,128)(2,1)S(1)}, u32[]{:S(2)}, u32[]{:S(2)}) collective-permute-start(bf16[320,768]{1,0:T(8,128)(2,1)S(1)} %down.4), channel_id=1, source_target_pairs={{0,8},{4,12},{8,0},{12,4},{16,24},{20,28},{24,16},{28,20},{1,9},{5... | collective-permute-start | bytes 1474568 | tf_op jit(solution)/shard_map/ppermute | solution.py:284
  81.1 13.6 %collective-permute-start.22 = (bf16[5,384,128]{2,1,0:T(8,128)(2,1)S(1)}, bf16[5,384,128]{2,1,0:T(8,128)(2,1)S(1)}, u32[]{:S(2)}, u32[]{:S(2)}) collective-permute-start(bf16[5,384,128]{2,1,0:T(8,128)(2,1)S(1)} %collective-permute-done.15.near_ref), channel_id=1, source_target_pairs={{0,4},{4,0},{8,12},{12,8},{16,20},{20,16},{24,28},{28,24},{1,5},{5... | collective-permute-start | bytes 1474568 | tf_op jit(solution)/shard_map/ppermute | solution.py:284
  94.7 7.4 %collective-permute-start.20 = (bf16[160,768]{1,0:T(8,128)(2,1)}, bf16[160,768]{1,0:T(8,128)(2,1)S(1)}, u32[]{:S(2)}, u32[]{:S(2)}) collective-permute-start(bf16[160,768]{1,0:T(8,128)(2,1)} %slice.112), channel_id=1, source_target_pairs={{0,1},{1,0},{2,3},{3,2},{4,5},{5,4},{6,7},{7,6},{8,9},{9,8},{10,11... | collective-permute-start | bytes 737288 | tf_op jit(solution)/shard_map/ppermute | solution.py:287
  96.8 9.0 %collective-permute-start.25 = (bf16[320,384]{1,0:T(8,128)(2,1)S(1)}, bf16[320,384]{1,0:T(8,128)(2,1)S(1)}, u32[]{:S(2)}, u32[]{:S(2)}) collective-permute-start(bf16[320,384]{1,0:T(8,128)(2,1)S(1)} %get-tuple-element.53), channel_id=1, source_target_pairs={{0,8},{4,12},{8,0},{12,4},{16,24},{20,28},{24,16},{28,20},{1,9},{5... | collective-permute-start | bytes 737288 | tf_op jit(solution)/shard_map/ppermute | solution.py:284
  98.5 10.8 %collective-permute-start.28 = (bf16[320,384]{1,0:T(8,128)(2,1)S(1)}, bf16[320,384]{1,0:T(8,128)(2,1)S(1)}, u32[]{:S(2)}, u32[]{:S(2)}) collective-permute-start(bf16[320,384]{1,0:T(8,128)(2,1)S(1)} %get-tuple-element.57), channel_id=1, source_target_pairs={{0,8},{4,12},{8,0},{12,4},{16,24},{20,28},{24,16},{28,20},{1,9},{5... | collective-permute-start | bytes 737288 | tf_op jit(solution)/shard_map/ppermute | solution.py:284
  102.2 12.4 %collective-permute-start.21 = (bf16[80,768]{1,0:T(8,128)(2,1)S(1)}, bf16[80,768]{1,0:T(8,128)(2,1)S(1)}, u32[]{:S(2)}, u32[]{:S(2)}) collective-permute-start(bf16[80,768]{1,0:T(8,128)(2,1)S(1)} %slice.115), channel_id=1, source_target_pairs={{0,2},{1,3},{2,0},{3,1},{4,6},{5,7},{6,4},{7,5},{8,10},{9,11},{10,... | collective-permute-start | bytes 368648 | tf_op jit(solution)/shard_map/ppermute | solution.py:287
  105.8 5.5 %collective-permute-start.26 = (bf16[160,384]{1,0:T(8,128)(2,1)S(1)}, bf16[160,384]{1,0:T(8,128)(2,1)S(1)}, u32[]{:S(2)}, u32[]{:S(2)}) collective-permute-start(bf16[160,384]{1,0:T(8,128)(2,1)S(1)} %slice.114), channel_id=1, source_target_pairs={{0,1},{1,0},{2,3},{3,2},{4,5},{5,4},{6,7},{7,6},{8,9},{9,8},{10,11... | collective-permute-start | bytes 368648 | tf_op jit(solution)/shard_map/ppermute | solution.py:287
  109.4 5.3 %collective-permute-start.29 = (bf16[160,384]{1,0:T(8,128)(2,1)S(1)}, bf16[160,384]{1,0:T(8,128)(2,1)S(1)}, u32[]{:S(2)}, u32[]{:S(2)}) collective-permute-start(bf16[160,384]{1,0:T(8,128)(2,1)S(1)} %slice.113), channel_id=1, source_target_pairs={{0,1},{1,0},{2,3},{3,2},{4,5},{5,4},{6,7},{7,6},{8,9},{9,8},{10,11... | collective-permute-start | bytes 368648 | tf_op jit(solution)/shard_map/ppermute | solution.py:287
  111.4 5.9 %collective-permute-start.27 = (bf16[80,384]{1,0:T(8,128)(2,1)S(1)}, bf16[80,384]{1,0:T(8,128)(2,1)S(1)}, u32[]{:S(2)}, u32[]{:S(2)}) collective-permute-start(bf16[80,384]{1,0:T(8,128)(2,1)S(1)} %slice.117), channel_id=1, source_target_pairs={{0,2},{1,3},{2,0},{3,1},{4,6},{5,7},{6,4},{7,5},{8,10},{9,11},{10,... | collective-permute-start | bytes 184328 | tf_op jit(solution)/shard_map/ppermute | solution.py:287
  (25 other events, 182.2 us)

commit v8 on v7

--- a/solution.py
+++ b/solution.py
@@ -319,7 +319,7 @@
         near = jnp.concatenate([near, hop(near, bit)], axis=0)
     far = hop(near, 1)
     gu_near_other = flip(gu_near, 1)
-    near_x = flip(after(near, gu_far, gu_near_other), 2)
+    near_x = flip(after(near, gu_near_other), 2)
     gu_fars = widen([after(gu_far, gu_nears[-1])])
     gu_nears_other = [gu_near_other] + [flip(v, 1) for v in gu_nears[1:]]
     gu_far_other = flip(gu_far, 1)
@@ -332,15 +332,14 @@
     give = weight_call(give_kernel, "give", depth, part, down_weight)
     got = [flip(v, 1) for v in give]
     dn_near, dn_away = weight_call(join_kernel, "join", 2 * depth, part, down_weight, *got)
-    dn_near_other = flip(dn_near, 1)
-    dn_far = flip(after(dn_away, far_x, dn_near_other), 2)
+    dn_far = flip(after(dn_away, far_x), 2)
     dn_nears = widen([after(dn_near, gu_fars[-1])])
 
     hidden = up_call([near, far], [near_x, far_x], mine, other)
     hidden = after(hidden, dn_nears[-1])
     dn_far = after(dn_far, hidden)
     dn_fars = widen([dn_far])
-    nears = [(dn_near, dn_near_other)] + [(v, flip(after(v, hidden), 1)) for v in dn_nears[1:]]
+    nears = [(v, flip(after(v, hidden), 1)) for v in dn_nears]
     fars = [(dn_far, flip(dn_far, 1))]
 
     chunks, crossed = [], []

time: 122 us -> 120 us (0.984)
  waiting for transfers between devices: 60 us -> 58.1 us
    ppermute x23, waiting for transfers between devices: 44.9 us -> 42.6 us  [flip(): return lax.ppermute(values, 'dp', [(i, i ^ bit) for i in range(ranks)])]
  transfers between devices with their start and end apart: 31 -> 31, of which waited for: 19 -> 20; matrix products, arithmetic and copies ran while one was open for 1% -> 1% of each run, Pallas kernels for 13% -> 13%
where the time goes in v8:
time: 120 us; the launch traced here: 119 us
  waiting for transfers between devices  58.1 us (48%)
  starting transfers between devices  32 us (27%)
  Pallas kernels  17.1 us (14%)
  local copies, waits for them, and re-layouts  9.76 us (8%)
  other arithmetic  1.45 us (1%)
    ppermute x23, waiting for transfers between devices, flip(): return lax.ppermute(values, 'dp', [(i, i ^ bit) for i in range(ranks)])  42.6 us
    ppermute x23, starting transfers between devices, flip(): return lax.ppermute(values, 'dp', [(i, i ^ bit) for i in range(ranks)])  16.6 us
    ppermute x8, waiting for transfers between devices, hop(): return lax.ppermute(values, 'expert', [(i, i ^ bit) for i in range(zones)])  15.5 us
    ppermute x8, starting transfers between devices, hop(): return lax.ppermute(values, 'expert', [(i, i ^ bit) for i in range(zones)])  15.4 us
    unnamed x39, local copies, waits for them, and re-layouts  8.83 us
    pallas_call x1, Pallas kernels, up_call(): pl.pallas_call(functools.partial(up_kernel, len(mine) // 2, len(here)), i...  6.89 us
    pallas_call x4, Pallas kernels, down_call(): pl.pallas_call(functools.partial(down_kernel, tokens if send else 0), in_...  6.1 us
  transfers between devices with their start and end apart: 31, of which 20 were waited for; matrix products, arithmetic and copies ran while one was open for 1% of the time, Pallas kernels for 13%

profile of v8, /device:TPU:0, one launch (start us, length us, event | category | flops | bytes accessed | tf_op | source)
XLA Modules:
  0.0 119.5 jit_solution(14514497940468700867)
XLA Ops:
  0.6 1.5 %copy-done = bf16[5,192,1024]{2,1,0:T(8,128)(2,1)S(1)} copy-done((bf16[5,192,1024]{2,1,0:T(8,128)(2,1)S(1)}, bf16[5,192,1024]{2,1,0:T(8,128)(2,1)}, u32[]{:S(2)}) %copy-start) | copy-done | bytes 1966104
  6.5 2.9 %collective-permute-start.8 = (bf16[5,384,256]{2,1,0:T(8,128)(2,1)S(1)}, bf16[5,384,256]{2,1,0:T(8,128)(2,1)S(1)}, u32[]{:S(2)}, u32[]{:S(2)}) collective-permute-start(bf16[5,384,256]{2,1,0:T(8,128)(2,1)S(1)} %get-tuple-element.36.refs_4_), channel_id=1, source_target_pairs={{0,16},{4,20},{8,24},{12,28},{16,0},{20,4},{24,8},{28,12},{1,17},{... | collective-permute-start | bytes 2949128 | tf_op jit(solution)/shard_map/ppermute | solution.py:284
  11.2 2.3 %copy-done.1 = bf16[1536,1536]{1,0:T(8,128)(2,1)S(1)} copy-done((bf16[1536,1536]{1,0:T(8,128)(2,1)S(1)}, bf16[1536,1536]{1,0:T(8,128)(2,1)}, u32[]{:S(2)}) %copy-start.1) | copy-done | bytes 4718616
  14.5 2.4 %front.1 = (bf16[80,1536]{1,0:T(8,128)(2,1)S(1)}, bf16[80,1664]{1,0:T(8,128)(2,1)S(1)}) custom-call(bf16[80,1536]{1,0:T(8,128)(2,1)S(1)} %copy-done.7, bf16[80,1536]{1,0:T(8,128)(2,1)S(1)} %copy-done.8, bf16[1536,1536]{1,0:T(8,128)(2,1)S(1)} %copy-done.1, f32[1,1536]{1,0:T(1,128)S(1)} %broadcast_in_dim.8.gain_ref, s32[80,8]{1,0:T(8,128)S(1)} %copy.12.routes_ref, ...), custom_call_target="tpu_custom_call" | custom-call | flops 1 | bytes 1 | tf_op jit(solution)/shard_map/front/pallas_call | solution.py:103
  16.9 2.6 %collective-permute-start = (bf16[80,1664]{1,0:T(8,128)(2,1)S(1)}, bf16[80,1664]{1,0:T(8,128)(2,1)S(1)}, u32[]{:S(2)}, u32[]{:S(2)}) collective-permute-start(bf16[80,1664]{1,0:T(8,128)(2,1)S(1)} %get-tuple-element.34), channel_id=1, source_target_pairs={{0,2},{1,3},{2,0},{3,1},{4,6},{5,7},{6,4},{7,5},{8,10},{9,11},{10,... | collective-permute-start | bytes 798728 | tf_op jit(solution)/shard_map/ppermute | solution.py:287
  19.5 11.9 %collective-permute-done.8.refs_6_ = bf16[5,384,256]{2,1,0:T(8,128)(2,1)S(1)} collective-permute-done((bf16[5,384,256]{2,1,0:T(8,128)(2,1)S(1)}, bf16[5,384,256]{2,1,0:T(8,128)(2,1)S(1)}, u32[]{:S(2)}, u32[]{:S(2)}) %collective-permute-start.8) | collective-permute-done | bytes 983072 | tf_op jit(solution)/shard_map/ppermute | solution.py:284
  31.4 1.7 %collective-permute-done.6.refs_5_ = bf16[5,384,256]{2,1,0:T(8,128)(2,1)S(1)} collective-permute-done((bf16[5,384,256]{2,1,0:T(8,128)(2,1)}, bf16[5,384,256]{2,1,0:T(8,128)(2,1)S(1)}, u32[]{:S(2)}, u32[]{:S(2)}) %collective-permute-start.6) | collective-permute-done | bytes 983072 | tf_op jit(solution)/shard_map/ppermute | solution.py:284
  34.0 1.9 %collective-permute-start.1 = (bf16[160,1664]{1,0:T(8,128)(2,1)S(1)}, bf16[160,1664]{1,0:T(8,128)(2,1)S(1)}, u32[]{:S(2)}, u32[]{:S(2)}) collective-permute-start(bf16[160,1664]{1,0:T(8,128)(2,1)S(1)} %constant_dynamic-update-slice_fusion.refs_0_), channel_id=1, source_target_pairs={{0,1},{1,0},{2,3},{3,2},{4,5},{5,4},{6,7},{7,6},{8,9},{9,8},{10,11... | collective-permute-start | bytes 1597448 | tf_op jit(solution)/shard_map/ppermute | solution.py:287
  37.3 10.8 %collective-permute-done.1.refs_1_ = bf16[160,1664]{1,0:T(8,128)(2,1)S(1)} collective-permute-done((bf16[160,1664]{1,0:T(8,128)(2,1)S(1)}, bf16[160,1664]{1,0:T(8,128)(2,1)S(1)}, u32[]{:S(2)}, u32[]{:S(2)}) %collective-permute-start.1) | collective-permute-done | bytes 532512 | tf_op jit(solution)/shard_map/ppermute | solution.py:287
  51.1 4.7 %collective-permute-done.11.refs_7_ = bf16[5,384,256]{2,1,0:T(8,128)(2,1)S(1)} collective-permute-done((bf16[5,384,256]{2,1,0:T(8,128)(2,1)S(1)}, bf16[5,384,256]{2,1,0:T(8,128)(2,1)S(1)}, u32[]{:S(2)}, u32[]{:S(2)}) %collective-permute-start.11) | collective-permute-done | bytes 983072 | tf_op jit(solution)/shard_map/ppermute | solution.py:284
  56.5 2.2 %collective-permute-done.13.near_in_ref = bf16[5,192,128]{2,1,0:T(8,128)(2,1)S(1)} collective-permute-done((bf16[5,192,128]{2,1,0:T(8,128)(2,1)S(1)}, bf16[5,192,128]{2,1,0:T(8,128)(2,1)S(1)}, u32[]{:S(2)}, u32[]{:S(2)}) %collective-permute-start.13) | collective-permute-done | bytes 245792 | tf_op jit(solution)/shard_map/ppermute | solution.py:284
  59.8 2.6 %collective-permute-done.10.refs_3_ = bf16[160,1664]{1,0:T(8,128)(2,1)S(1)} collective-permute-done((bf16[160,1664]{1,0:T(8,128)(2,1)S(1)}, bf16[160,1664]{1,0:T(8,128)(2,1)S(1)}, u32[]{:S(2)}, u32[]{:S(2)}) %collective-permute-start.10) | collective-permute-done | bytes 532512 | tf_op jit(solution)/shard_map/ppermute | solution.py:284
  66.3 6.9 %up.1.h_ref = bf16[640,1280]{1,0:T(8,128)(2,1)S(1)} custom-call(bf16[160,1664]{1,0:T(8,128)(2,1)S(1)} %constant_dynamic-update-slice_fusion.refs_0_, bf16[160,1664]{1,0:T(8,128)(2,1)S(1)} %collective-permute-done.1.refs_1_, bf16[160,1664]{1,0:T(8,128)(2,1)S(1)} %collective-permute-done.5.refs_2_, bf16[160,1664]{1,0:T(8,128)(2,1)S(1)} %collective-permute-done.10.refs_3_, ...), custom_call_target="tpu_custom_call" | custom-call | flops 1 | bytes 1 | tf_op jit(solution)/shard_map/up/pallas_call | solution.py:214
  77.9 9.2 %collective-permute-done.23.far_ref = bf16[5,384,128]{2,1,0:T(8,128)(2,1)S(1)} collective-permute-done((bf16[5,384,128]{2,1,0:T(8,128)(2,1)S(1)}, bf16[5,384,128]{2,1,0:T(8,128)(2,1)S(1)}, u32[]{:S(2)}, u32[]{:S(2)}) %collective-permute-start.23) | collective-permute-done | bytes 491552 | tf_op jit(solution)/shard_map/ppermute | solution.py:284
  88.1 2.1 %collective-permute-done.19 = bf16[320,768]{1,0:T(8,128)(2,1)S(1)} collective-permute-done((bf16[320,768]{1,0:T(8,128)(2,1)S(1)}, bf16[320,768]{1,0:T(8,128)(2,1)S(1)}, u32[]{:S(2)}, u32[]{:S(2)}) %collective-permute-start.19) | collective-permute-done | bytes 491552 | tf_op jit(solution)/shard_map/ppermute | solution.py:284
  92.9 2.0 %down.6 = (bf16[320,384]{1,0:T(8,128)(2,1)S(1)}, bf16[320,384]{1,0:T(8,128)(2,1)S(1)}) custom-call(bf16[640,1280]{1,0:T(8,128)(2,1)S(1)} %up.1.h_ref, bf16[5,384,128]{2,1,0:T(8,128)(2,1)S(1)} %collective-permute-done.15.near_ref, bf16[5,384,128]{2,1,0:T(8,128)(2,1)S(1)} %collective-permute-done.22.near_other_ref, ...), custom_call_target="tpu_custom_call" | custom-call | flops 1 | bytes 1 | tf_op jit(solution)/shard_map/down/pallas_call | solution.py:253
  94.9 1.6 %collective-permute-start.25 = (bf16[320,384]{1,0:T(8,128)(2,1)S(1)}, bf16[320,384]{1,0:T(8,128)(2,1)S(1)}, u32[]{:S(2)}, u32[]{:S(2)}) collective-permute-start(bf16[320,384]{1,0:T(8,128)(2,1)S(1)} %get-tuple-element.55), channel_id=1, source_target_pairs={{0,8},{4,12},{8,0},{12,4},{16,24},{20,28},{24,16},{28,20},{1,9},{5... | collective-permute-start | bytes 737288 | tf_op jit(solution)/shard_map/ppermute | solution.py:284
  97.0 2.0 %down.7 = (f32[320,384]{1,0:T(8,128)S(1)}, f32[320,384]{1,0:T(8,128)S(1)}) custom-call(bf16[640,1280]{1,0:T(8,128)(2,1)S(1)} %up.1.h_ref, bf16[5,384,128]{2,1,0:T(8,128)(2,1)S(1)} %collective-permute-done.15.near_ref, bf16[5,384,128]{2,1,0:T(8,128)(2,1)S(1)} %collective-permute-done.22.near_other_ref, ...), custom_call_target="tpu_custom_call" | custom-call | flops 1 | bytes 1 | tf_op jit(solution)/shard_map/down/pallas_call | solution.py:253
  99.5 2.6 %collective-permute-start.21 = (bf16[80,768]{1,0:T(8,128)(2,1)S(1)}, bf16[80,768]{1,0:T(8,128)(2,1)S(1)}, u32[]{:S(2)}, u32[]{:S(2)}) collective-permute-start(bf16[80,768]{1,0:T(8,128)(2,1)S(1)} %slice.115), channel_id=1, source_target_pairs={{0,2},{1,3},{2,0},{3,1},{4,6},{5,7},{6,4},{7,5},{8,10},{9,11},{10,... | collective-permute-start | bytes 368648 | tf_op jit(solution)/shard_map/ppermute | solution.py:287
  102.1 1.7 %collective-permute-done.25 = bf16[320,384]{1,0:T(8,128)(2,1)S(1)} collective-permute-done((bf16[320,384]{1,0:T(8,128)(2,1)S(1)}, bf16[320,384]{1,0:T(8,128)(2,1)S(1)}, u32[]{:S(2)}, u32[]{:S(2)}) %collective-permute-start.25) | collective-permute-done | bytes 245792 | tf_op jit(solution)/shard_map/ppermute | solution.py:284
  105.2 1.9 %collective-permute-done.28 = bf16[320,384]{1,0:T(8,128)(2,1)S(1)} collective-permute-done((bf16[320,384]{1,0:T(8,128)(2,1)S(1)}, bf16[320,384]{1,0:T(8,128)(2,1)S(1)}, u32[]{:S(2)}, u32[]{:S(2)}) %collective-permute-start.28) | collective-permute-done | bytes 245792 | tf_op jit(solution)/shard_map/ppermute | solution.py:284
  110.0 2.7 %collective-permute-start.27 = (bf16[80,384]{1,0:T(8,128)(2,1)S(1)}, bf16[80,384]{1,0:T(8,128)(2,1)S(1)}, u32[]{:S(2)}, u32[]{:S(2)}) collective-permute-start(bf16[80,384]{1,0:T(8,128)(2,1)S(1)} %slice.117), channel_id=1, source_target_pairs={{0,2},{1,3},{2,0},{3,1},{4,6},{5,7},{6,4},{7,5},{8,10},{9,11},{10,... | collective-permute-start | bytes 184328 | tf_op jit(solution)/shard_map/ppermute | solution.py:287
  112.7 2.2 %collective-permute-start.30 = (bf16[80,384]{1,0:T(8,128)(2,1)S(1)}, bf16[80,384]{1,0:T(8,128)(2,1)S(1)}, u32[]{:S(2)}, u32[]{:S(2)}) collective-permute-start(bf16[80,384]{1,0:T(8,128)(2,1)S(1)} %slice.116), channel_id=1, source_target_pairs={{0,2},{1,3},{2,0},{3,1},{4,6},{5,7},{6,4},{7,5},{8,10},{9,11},{10,... | collective-permute-start | bytes 184328 | tf_op jit(solution)/shard_map/ppermute | solution.py:287
  114.9 2.0 %collective-permute-done.27 = bf16[80,384]{1,0:T(8,128)(2,1)S(1)} collective-permute-done((bf16[80,384]{1,0:T(8,128)(2,1)S(1)}, bf16[80,384]{1,0:T(8,128)(2,1)S(1)}, u32[]{:S(2)}, u32[]{:S(2)}) %collective-permute-start.27) | collective-permute-done | bytes 61472 | tf_op jit(solution)/shard_map/ppermute | solution.py:287
  (113 shorter events, 34.0 us)
Async XLA Ops:
  6.5 25.0 %collective-permute-start.8 = (bf16[5,384,256]{2,1,0:T(8,128)(2,1)S(1)}, bf16[5,384,256]{2,1,0:T(8,128)(2,1)S(1)}, u32[]{:S(2)}, u32[]{:S(2)}) collective-permute-start(bf16[5,384,256]{2,1,0:T(8,128)(2,1)S(1)} %get-tuple-element.36.refs_4_), channel_id=1, source_target_pairs={{0,16},{4,20},{8,24},{12,28},{16,0},{20,4},{24,8},{28,12},{1,17},{... | collective-permute-start | bytes 2949128 | tf_op jit(solution)/shard_map/ppermute | solution.py:284
  9.4 23.7 %collective-permute-start.6 = (bf16[5,384,256]{2,1,0:T(8,128)(2,1)}, bf16[5,384,256]{2,1,0:T(8,128)(2,1)S(1)}, u32[]{:S(2)}, u32[]{:S(2)}) collective-permute-start(bf16[5,384,256]{2,1,0:T(8,128)(2,1)} %get-tuple-element.38), channel_id=1, source_target_pairs={{0,8},{4,12},{8,0},{12,4},{16,24},{20,28},{24,16},{28,20},{1,9},{5... | collective-permute-start | bytes 2949128 | tf_op jit(solution)/shard_map/ppermute | solution.py:284
  10.9 25.0 %collective-permute-start.4 = (bf16[5,384,256]{2,1,0:T(8,128)(2,1)S(1)}, bf16[5,384,256]{2,1,0:T(8,128)(2,1)}, u32[]{:S(2)}, u32[]{:S(2)}) collective-permute-start(bf16[5,384,256]{2,1,0:T(8,128)(2,1)S(1)} %get-tuple-element.36.refs_4_), channel_id=1, source_target_pairs={{0,4},{4,0},{8,12},{12,8},{16,20},{20,16},{24,28},{28,24},{1,5},{5... | collective-permute-start | bytes 2949128 | tf_op jit(solution)/shard_map/ppermute | solution.py:284
  16.9 17.1 %collective-permute-start = (bf16[80,1664]{1,0:T(8,128)(2,1)S(1)}, bf16[80,1664]{1,0:T(8,128)(2,1)S(1)}, u32[]{:S(2)}, u32[]{:S(2)}) collective-permute-start(bf16[80,1664]{1,0:T(8,128)(2,1)S(1)} %get-tuple-element.34), channel_id=1, source_target_pairs={{0,2},{1,3},{2,0},{3,1},{4,6},{5,7},{6,4},{7,5},{8,10},{9,11},{10,... | collective-permute-start | bytes 798728 | tf_op jit(solution)/shard_map/ppermute | solution.py:287
  33.1 22.7 %collective-permute-start.11 = (bf16[5,384,256]{2,1,0:T(8,128)(2,1)S(1)}, bf16[5,384,256]{2,1,0:T(8,128)(2,1)S(1)}, u32[]{:S(2)}, u32[]{:S(2)}) collective-permute-start(bf16[5,384,256]{2,1,0:T(8,128)(2,1)S(1)} %collective-permute-done.6.refs_5_), channel_id=1, source_target_pairs={{0,16},{4,20},{8,24},{12,28},{16,0},{20,4},{24,8},{28,12},{1,17},{... | collective-permute-start | bytes 2949128 | tf_op jit(solution)/shard_map/ppermute | solution.py:284
  33.4 16.2 %collective-permute-start.9 = (bf16[5,384,256]{2,1,0:T(8,128)(2,1)S(1)}, bf16[5,384,256]{2,1,0:T(8,128)(2,1)S(1)}, u32[]{:S(2)}, u32[]{:S(2)}) collective-permute-start(bf16[5,384,256]{2,1,0:T(8,128)(2,1)S(1)} %collective-permute-done.8.refs_6_), channel_id=1, source_target_pairs={{0,4},{4,0},{8,12},{12,8},{16,20},{20,16},{24,28},{28,24},{1,5},{5... | collective-permute-start | bytes 2949128 | tf_op jit(solution)/shard_map/ppermute | solution.py:284
  33.4 16.2 %collective-permute-start.7 = (bf16[5,384,256]{2,1,0:T(8,128)(2,1)S(1)}, bf16[5,384,256]{2,1,0:T(8,128)(2,1)S(1)}, u32[]{:S(2)}, u32[]{:S(2)}) collective-permute-start(bf16[5,384,256]{2,1,0:T(8,128)(2,1)S(1)} %collective-permute-done.6.refs_5_), channel_id=1, source_target_pairs={{0,4},{4,0},{8,12},{12,8},{16,20},{20,16},{24,28},{28,24},{1,5},{5... | collective-permute-start | bytes 2949128 | tf_op jit(solution)/shard_map/ppermute | solution.py:284
  34.0 14.1 %collective-permute-start.1 = (bf16[160,1664]{1,0:T(8,128)(2,1)S(1)}, bf16[160,1664]{1,0:T(8,128)(2,1)S(1)}, u32[]{:S(2)}, u32[]{:S(2)}) collective-permute-start(bf16[160,1664]{1,0:T(8,128)(2,1)S(1)} %constant_dynamic-update-slice_fusion.refs_0_), channel_id=1, source_target_pairs={{0,1},{1,0},{2,3},{3,2},{4,5},{5,4},{6,7},{7,6},{8,9},{9,8},{10,11... | collective-permute-start | bytes 1597448 | tf_op jit(solution)/shard_map/ppermute | solution.py:287
  35.8 13.7 %collective-permute-start.5 = (bf16[160,1664]{1,0:T(8,128)(2,1)S(1)}, bf16[160,1664]{1,0:T(8,128)(2,1)S(1)}, u32[]{:S(2)}, u32[]{:S(2)}) collective-permute-start(bf16[160,1664]{1,0:T(8,128)(2,1)S(1)} %constant_dynamic-update-slice_fusion.refs_0_), channel_id=1, source_target_pairs={{0,8},{4,12},{8,0},{12,4},{16,24},{20,28},{24,16},{28,20},{1,9},{5... | collective-permute-start | bytes 1597448 | tf_op jit(solution)/shard_map/ppermute | solution.py:284
  49.6 12.8 %collective-permute-start.10 = (bf16[160,1664]{1,0:T(8,128)(2,1)S(1)}, bf16[160,1664]{1,0:T(8,128)(2,1)S(1)}, u32[]{:S(2)}, u32[]{:S(2)}) collective-permute-start(bf16[160,1664]{1,0:T(8,128)(2,1)S(1)} %collective-permute-done.1.refs_1_), channel_id=1, source_target_pairs={{0,8},{4,12},{8,0},{12,4},{16,24},{20,28},{24,16},{28,20},{1,9},{5... | collective-permute-start | bytes 1597448 | tf_op jit(solution)/shard_map/ppermute | solution.py:284
  55.8 8.1 %collective-permute-start.12 = (bf16[5,384,256]{2,1,0:T(8,128)(2,1)S(1)}, bf16[5,384,256]{2,1,0:T(8,128)(2,1)S(1)}, u32[]{:S(2)}, u32[]{:S(2)}) collective-permute-start(bf16[5,384,256]{2,1,0:T(8,128)(2,1)S(1)} %collective-permute-done.11.refs_7_), channel_id=1, source_target_pairs={{0,4},{4,0},{8,12},{12,8},{16,20},{20,16},{24,28},{28,24},{1,5},{5... | collective-permute-start | bytes 2949128 | tf_op jit(solution)/shard_map/ppermute | solution.py:284
  59.2 14.0 %collective-permute-start.15 = (bf16[5,384,128]{2,1,0:T(8,128)(2,1)S(1)}, bf16[5,384,128]{2,1,0:T(8,128)(2,1)S(1)}, u32[]{:S(2)}, u32[]{:S(2)}) collective-permute-start(bf16[5,384,128]{2,1,0:T(8,128)(2,1)S(1)} %get-tuple-element.47.near_ref), channel_id=1, source_target_pairs={{0,16},{4,20},{8,24},{12,28},{16,0},{20,4},{24,8},{28,12},{1,17},{... | collective-permute-start | bytes 1474568 | tf_op jit(solution)/shard_map/ppermute | solution.py:284
  62.4 11.0 %collective-permute-start.17 = (bf16[5,384,128]{2,1,0:T(8,128)(2,1)S(1)}, bf16[5,384,128]{2,1,0:T(8,128)(2,1)S(1)}, u32[]{:S(2)}, u32[]{:S(2)}) collective-permute-start(bf16[5,384,128]{2,1,0:T(8,128)(2,1)S(1)} %get-tuple-element.49), channel_id=1, source_target_pairs={{0,8},{4,12},{8,0},{12,4},{16,24},{20,28},{24,16},{28,20},{1,9},{5... | collective-permute-start | bytes 1474568 | tf_op jit(solution)/shard_map/ppermute | solution.py:284
  73.8 13.3 %collective-permute-start.23 = (bf16[5,384,128]{2,1,0:T(8,128)(2,1)S(1)}, bf16[5,384,128]{2,1,0:T(8,128)(2,1)S(1)}, u32[]{:S(2)}, u32[]{:S(2)}) collective-permute-start(bf16[5,384,128]{2,1,0:T(8,128)(2,1)S(1)} %collective-permute-done.17.far_ref), channel_id=1, source_target_pairs={{0,16},{4,20},{8,24},{12,28},{16,0},{20,4},{24,8},{28,12},{1,17},{... | collective-permute-start | bytes 1474568 | tf_op jit(solution)/shard_map/ppermute | solution.py:284
  76.9 13.3 %collective-permute-start.19 = (bf16[320,768]{1,0:T(8,128)(2,1)S(1)}, bf16[320,768]{1,0:T(8,128)(2,1)S(1)}, u32[]{:S(2)}, u32[]{:S(2)}) collective-permute-start(bf16[320,768]{1,0:T(8,128)(2,1)S(1)} %down.4), channel_id=1, source_target_pairs={{0,8},{4,12},{8,0},{12,4},{16,24},{20,28},{24,16},{28,20},{1,9},{5... | collective-permute-start | bytes 1474568 | tf_op jit(solution)/shard_map/ppermute | solution.py:284
  77.9 15.0 %collective-permute-start.22 = (bf16[5,384,128]{2,1,0:T(8,128)(2,1)S(1)}, bf16[5,384,128]{2,1,0:T(8,128)(2,1)S(1)}, u32[]{:S(2)}, u32[]{:S(2)}) collective-permute-start(bf16[5,384,128]{2,1,0:T(8,128)(2,1)S(1)} %collective-permute-done.15.near_ref), channel_id=1, source_target_pairs={{0,4},{4,0},{8,12},{12,8},{16,20},{20,16},{24,28},{28,24},{1,5},{5... | collective-permute-start | bytes 1474568 | tf_op jit(solution)/shard_map/ppermute | solution.py:284
  87.1 5.8 %collective-permute-start.24 = (bf16[5,384,128]{2,1,0:T(8,128)(2,1)S(1)}, bf16[5,384,128]{2,1,0:T(8,128)(2,1)}, u32[]{:S(2)}, u32[]{:S(2)}) collective-permute-start(bf16[5,384,128]{2,1,0:T(8,128)(2,1)S(1)} %collective-permute-done.23.far_ref), channel_id=1, source_target_pairs={{0,4},{4,0},{8,12},{12,8},{16,20},{20,16},{24,28},{28,24},{1,5},{5... | collective-permute-start | bytes 1474568 | tf_op jit(solution)/shard_map/ppermute | solution.py:284
  92.1 7.4 %collective-permute-start.20 = (bf16[160,768]{1,0:T(8,128)(2,1)}, bf16[160,768]{1,0:T(8,128)(2,1)S(1)}, u32[]{:S(2)}, u32[]{:S(2)}) collective-permute-start(bf16[160,768]{1,0:T(8,128)(2,1)} %slice.112), channel_id=1, source_target_pairs={{0,1},{1,0},{2,3},{3,2},{4,5},{5,4},{6,7},{7,6},{8,9},{9,8},{10,11... | collective-permute-start | bytes 737288 | tf_op jit(solution)/shard_map/ppermute | solution.py:287
  94.9 9.0 %collective-permute-start.25 = (bf16[320,384]{1,0:T(8,128)(2,1)S(1)}, bf16[320,384]{1,0:T(8,128)(2,1)S(1)}, u32[]{:S(2)}, u32[]{:S(2)}) collective-permute-start(bf16[320,384]{1,0:T(8,128)(2,1)S(1)} %get-tuple-element.55), channel_id=1, source_target_pairs={{0,8},{4,12},{8,0},{12,4},{16,24},{20,28},{24,16},{28,20},{1,9},{5... | collective-permute-start | bytes 737288 | tf_op jit(solution)/shard_map/ppermute | solution.py:284
  96.5 10.7 %collective-permute-start.28 = (bf16[320,384]{1,0:T(8,128)(2,1)S(1)}, bf16[320,384]{1,0:T(8,128)(2,1)S(1)}, u32[]{:S(2)}, u32[]{:S(2)}) collective-permute-start(bf16[320,384]{1,0:T(8,128)(2,1)S(1)} %get-tuple-element.59), channel_id=1, source_target_pairs={{0,8},{4,12},{8,0},{12,4},{16,24},{20,28},{24,16},{28,20},{1,9},{5... | collective-permute-start | bytes 737288 | tf_op jit(solution)/shard_map/ppermute | solution.py:284
  99.5 13.1 %collective-permute-start.21 = (bf16[80,768]{1,0:T(8,128)(2,1)S(1)}, bf16[80,768]{1,0:T(8,128)(2,1)S(1)}, u32[]{:S(2)}, u32[]{:S(2)}) collective-permute-start(bf16[80,768]{1,0:T(8,128)(2,1)S(1)} %slice.115), channel_id=1, source_target_pairs={{0,2},{1,3},{2,0},{3,1},{4,6},{5,7},{6,4},{7,5},{8,10},{9,11},{10,... | collective-permute-start | bytes 368648 | tf_op jit(solution)/shard_map/ppermute | solution.py:287
  104.0 6.0 %collective-permute-start.26 = (bf16[160,384]{1,0:T(8,128)(2,1)S(1)}, bf16[160,384]{1,0:T(8,128)(2,1)S(1)}, u32[]{:S(2)}, u32[]{:S(2)}) collective-permute-start(bf16[160,384]{1,0:T(8,128)(2,1)S(1)} %slice.114), channel_id=1, source_target_pairs={{0,1},{1,0},{2,3},{3,2},{4,5},{5,4},{6,7},{7,6},{8,9},{9,8},{10,11... | collective-permute-start | bytes 368648 | tf_op jit(solution)/shard_map/ppermute | solution.py:287
  107.2 5.4 %collective-permute-start.29 = (bf16[160,384]{1,0:T(8,128)(2,1)S(1)}, bf16[160,384]{1,0:T(8,128)(2,1)S(1)}, u32[]{:S(2)}, u32[]{:S(2)}) collective-permute-start(bf16[160,384]{1,0:T(8,128)(2,1)S(1)} %slice.113), channel_id=1, source_target_pairs={{0,1},{1,0},{2,3},{3,2},{4,5},{5,4},{6,7},{7,6},{8,9},{9,8},{10,11... | collective-permute-start | bytes 368648 | tf_op jit(solution)/shard_map/ppermute | solution.py:287
  110.0 7.0 %collective-permute-start.27 = (bf16[80,384]{1,0:T(8,128)(2,1)S(1)}, bf16[80,384]{1,0:T(8,128)(2,1)S(1)}, u32[]{:S(2)}, u32[]{:S(2)}) collective-permute-start(bf16[80,384]{1,0:T(8,128)(2,1)S(1)} %slice.117), channel_id=1, source_target_pairs={{0,2},{1,3},{2,0},{3,1},{4,6},{5,7},{6,4},{7,5},{8,10},{9,11},{10,... | collective-permute-start | bytes 184328 | tf_op jit(solution)/shard_map/ppermute | solution.py:287
  (25 other events, 219.8 us)

commit v9 on v8

--- a/solution.py
+++ b/solution.py
@@ -24,18 +24,6 @@
 
 def after_all(values, *others):
     return list(lax.optimization_barrier((*values, *others)))[: len(values)]
-
-
-def swap_blocks(values, index, blocks):
-    size = values.shape[1] // blocks
-    bit = 1
-    while bit < blocks:
-        swapped = jnp.concatenate(
-            [values[:, (m ^ bit) * size : ((m ^ bit) + 1) * size] for m in range(blocks)], axis=1
-        )
-        values = jnp.where((index & bit) != 0, swapped, values)
-        bit *= 2
-    return values
 
 
 def swap_lanes(values, index, blocks):
@@ -261,6 +249,34 @@
     )(hidden, *near, *far)
 
 
+def finish_kernel(blocks, stored_ref, gain_ref, *refs):
+    parts, (stream_ref, normed_ref, sum_ref) = refs[:-3], refs[-3:]
+    at = 0
+    for i in range(len(parts) // 2):
+        width = parts[2 * i].shape[1]
+        sum_ref[:, at : at + width] = parts[2 * i][...] + parts[2 * i + 1][...].astype(jnp.float32)
+        at += width
+    branch = swap_lanes(sum_ref[...], lax.axis_index("dp") // 2, blocks)
+    total = stored_ref[...].astype(jnp.float32) + branch
+    stream_ref[...] = total.astype(jnp.bfloat16)
+    normed_ref[...] = normalize(total, gain_ref[...]).astype(jnp.bfloat16)
+
+
+def finish_call(blocks, stored, gain, chunks):
+    vmem = pl.BlockSpec(memory_space=pltpu.VMEM)
+    operands = [v for chunk in chunks for v in chunk]
+    return pl.pallas_call(
+        functools.partial(finish_kernel, blocks),
+        in_specs=[vmem] * (2 + len(operands)),
+        out_specs=[vmem] * 2,
+        out_shape=[jax.ShapeDtypeStruct(stored.shape, jnp.bfloat16)] * 2,
+        scratch_shapes=[pltpu.VMEM(stored.shape, jnp.float32)],
+        compiler_params=pltpu.CompilerParams(vmem_limit_bytes=12 * 1024 * 1024),
+        cost_estimate=pl.CostEstimate(flops=1, bytes_accessed=1, transcendentals=0),
+        name="finish",
+    )(stored, gain[None, :], *operands)
+
+
 def body(
     attended,
     residual,
@@ -313,7 +329,6 @@
         gate_logits,
         placement,
     )
-    stream_in = stored.astype(jnp.float32)
     near = sent
     for bit in reversed(zone_bits[1:]):
         near = jnp.concatenate([near, hop(near, bit)], axis=0)
@@ -360,11 +375,14 @@
             for bit in zone_bits:
                 size = total.shape[0] // 2
                 moved = total[size:].astype(jnp.bfloat16)
-                total = total[:size] + hop(moved, bit).astype(jnp.float32)
-            chunks.append(total)
-    branch = swap_blocks(jnp.concatenate(chunks, axis=1), me // 2, 2 * rows)
-    total = stream_in + branch
-    return (total.astype(jnp.bfloat16), normalize(total, final_gain).astype(jnp.bfloat16))
+                if bit == zone_bits[-1] and m == rows - 1:
+                    moved = after(moved, chunks[0][1])
+                received = hop(moved, bit)
+                total = total[:size]
+                if bit != zone_bits[-1]:
+                    total = total + received.astype(jnp.float32)
+            chunks.append((total, received))
+    return tuple(finish_call(2 * rows, stored, final_gain, chunks))
 
 
 def solution(mesh):

time: 120 us -> 117 us (0.975)
  waiting for transfers between devices: 58.1 us -> 63.9 us
  local copies, waits for them, and re-layouts: 9.76 us -> 4.35 us
    unnamed x39 -> x23, local copies, waits for them, and re-layouts: 8.83 us -> 4.12 us
    ppermute x23, waiting for transfers between devices: 42.6 us -> 45.8 us  [flip(): return lax.ppermute(values, 'dp', [(i, i ^ bit) for i in range(ranks)])]
    ppermute x8, waiting for transfers between devices: 15.5 us -> 18.1 us  [hop(): return lax.ppermute(values, 'expert', [(i, i ^ bit) for i in range(zones)])]
    pallas_call x4, Pallas kernels: 6.1 us -> 4.04 us  [down_call(): pl.pallas_call(functools.partial(down_kernel, tokens if send else 0), in_...]
    ppermute x8, starting transfers between devices: 15.4 us -> 14.1 us  [hop(): return lax.ppermute(values, 'expert', [(i, i ^ bit) for i in range(zones)])]
  transfers between devices with their start and end apart: 31 -> 31, of which waited for: 20 -> 20; matrix products, arithmetic and copies ran while one was open for 1% -> 1% of each run, Pallas kernels for 13% -> 11%
where the time goes in v9:
time: 117 us
  waiting for transfers between devices  63.9 us (55%)
  starting transfers between devices  31.1 us (27%)
  Pallas kernels  16 us (14%)
  local copies, waits for them, and re-layouts  4.35 us (4%)
    ppermute x23, waiting for transfers between devices, flip(): return lax.ppermute(values, 'dp', [(i, i ^ bit) for i in range(ranks)])  45.8 us
    ppermute x8, waiting for transfers between devices, hop(): return lax.ppermute(values, 'expert', [(i, i ^ bit) for i in range(zones)])  18.1 us
    ppermute x23, starting transfers between devices, flip(): return lax.ppermute(values, 'dp', [(i, i ^ bit) for i in range(ranks)])  17 us
    ppermute x8, starting transfers between devices, hop(): return lax.ppermute(values, 'expert', [(i, i ^ bit) for i in range(zones)])  14.1 us
    pallas_call x1, Pallas kernels, up_call(): pl.pallas_call(functools.partial(up_kernel, len(mine) // 2, len(here)), i...  6.89 us
    unnamed x23, local copies, waits for them, and re-layouts  4.12 us
    pallas_call x4, Pallas kernels, down_call(): pl.pallas_call(functools.partial(down_kernel, tokens if send else 0), in_...  4.04 us
    pallas_call x1, Pallas kernels, front_call(): pl.pallas_call(functools.partial(front_kernel, ranks), grid=(steps,), in_...  2.38 us
  transfers between devices with their start and end apart: 31, of which 20 were waited for; matrix products, arithmetic and copies ran while one was open for 1% of the time, Pallas kernels for 11%

profile of v9, /device:TPU:0, one launch (start us, length us, event | category | flops | bytes accessed | tf_op | source)
XLA Modules:
  0.0 116.6 jit_solution(2684842661407995641)
XLA Ops:
  6.5 2.9 %collective-permute-start.8 = (bf16[5,384,256]{2,1,0:T(8,128)(2,1)S(1)}, bf16[5,384,256]{2,1,0:T(8,128)(2,1)S(1)}, u32[]{:S(2)}, u32[]{:S(2)}) collective-permute-start(bf16[5,384,256]{2,1,0:T(8,128)(2,1)S(1)} %get-tuple-element.38.refs_4_), channel_id=1, source_target_pairs={{0,16},{4,20},{8,24},{12,28},{16,0},{20,4},{24,8},{28,12},{1,17},{... | collective-permute-start | bytes 2949128 | tf_op jit(solution)/shard_map/ppermute | solution.py:300
  11.2 2.3 %copy-done.1 = bf16[1536,1536]{1,0:T(8,128)(2,1)S(1)} copy-done((bf16[1536,1536]{1,0:T(8,128)(2,1)S(1)}, bf16[1536,1536]{1,0:T(8,128)(2,1)}, u32[]{:S(2)}) %copy-start.1) | copy-done | bytes 4718616
  13.5 2.4 %front.1 = (bf16[80,1536]{1,0:T(8,128)(2,1)S(1)}, bf16[80,1664]{1,0:T(8,128)(2,1)S(1)}) custom-call(bf16[80,1536]{1,0:T(8,128)(2,1)S(1)} %copy-done.3, bf16[80,1536]{1,0:T(8,128)(2,1)S(1)} %copy-done.4, bf16[1536,1536]{1,0:T(8,128)(2,1)S(1)} %copy-done.1, f32[1,1536]{1,0:T(1,128)S(1)} %broadcast_in_dim.9.gain_ref, s32[80,8]{1,0:T(8,128)S(1)} %copy.12.routes_ref, ...), custom_call_target="tpu_custom_call" | custom-call | flops 1 | bytes 1 | tf_op jit(solution)/shard_map/front/pallas_call | solution.py:91
  15.9 2.7 %collective-permute-start = (bf16[80,1664]{1,0:T(8,128)(2,1)S(1)}, bf16[80,1664]{1,0:T(8,128)(2,1)S(1)}, u32[]{:S(2)}, u32[]{:S(2)}) collective-permute-start(bf16[80,1664]{1,0:T(8,128)(2,1)S(1)} %get-tuple-element.36), channel_id=1, source_target_pairs={{0,2},{1,3},{2,0},{3,1},{4,6},{5,7},{6,4},{7,5},{8,10},{9,11},{10,... | collective-permute-start | bytes 798728 | tf_op jit(solution)/shard_map/ppermute | solution.py:303
  18.6 12.9 %collective-permute-done.8.refs_6_ = bf16[5,384,256]{2,1,0:T(8,128)(2,1)S(1)} collective-permute-done((bf16[5,384,256]{2,1,0:T(8,128)(2,1)S(1)}, bf16[5,384,256]{2,1,0:T(8,128)(2,1)S(1)}, u32[]{:S(2)}, u32[]{:S(2)}) %collective-permute-start.8) | collective-permute-done | bytes 983072 | tf_op jit(solution)/shard_map/ppermute | solution.py:300
  31.4 1.7 %collective-permute-done.6.refs_5_ = bf16[5,384,256]{2,1,0:T(8,128)(2,1)S(1)} collective-permute-done((bf16[5,384,256]{2,1,0:T(8,128)(2,1)}, bf16[5,384,256]{2,1,0:T(8,128)(2,1)S(1)}, u32[]{:S(2)}, u32[]{:S(2)}) %collective-permute-start.6) | collective-permute-done | bytes 983072 | tf_op jit(solution)/shard_map/ppermute | solution.py:300
  34.0 1.9 %collective-permute-start.1 = (bf16[160,1664]{1,0:T(8,128)(2,1)S(1)}, bf16[160,1664]{1,0:T(8,128)(2,1)S(1)}, u32[]{:S(2)}, u32[]{:S(2)}) collective-permute-start(bf16[160,1664]{1,0:T(8,128)(2,1)S(1)} %constant_dynamic-update-slice_fusion.refs_0_), channel_id=1, source_target_pairs={{0,1},{1,0},{2,3},{3,2},{4,5},{5,4},{6,7},{7,6},{8,9},{9,8},{10,11... | collective-permute-start | bytes 1597448 | tf_op jit(solution)/shard_map/ppermute | solution.py:303
  37.3 10.8 %collective-permute-done.1.refs_1_ = bf16[160,1664]{1,0:T(8,128)(2,1)S(1)} collective-permute-done((bf16[160,1664]{1,0:T(8,128)(2,1)S(1)}, bf16[160,1664]{1,0:T(8,128)(2,1)S(1)}, u32[]{:S(2)}, u32[]{:S(2)}) %collective-permute-start.1) | collective-permute-done | bytes 532512 | tf_op jit(solution)/shard_map/ppermute | solution.py:303
  51.1 4.7 %collective-permute-done.11.refs_7_ = bf16[5,384,256]{2,1,0:T(8,128)(2,1)S(1)} collective-permute-done((bf16[5,384,256]{2,1,0:T(8,128)(2,1)S(1)}, bf16[5,384,256]{2,1,0:T(8,128)(2,1)S(1)}, u32[]{:S(2)}, u32[]{:S(2)}) %collective-permute-start.11) | collective-permute-done | bytes 983072 | tf_op jit(solution)/shard_map/ppermute | solution.py:300
  56.5 2.2 %collective-permute-done.13.near_in_ref = bf16[5,192,128]{2,1,0:T(8,128)(2,1)S(1)} collective-permute-done((bf16[5,192,128]{2,1,0:T(8,128)(2,1)S(1)}, bf16[5,192,128]{2,1,0:T(8,128)(2,1)S(1)}, u32[]{:S(2)}, u32[]{:S(2)}) %collective-permute-start.13) | collective-permute-done | bytes 245792 | tf_op jit(solution)/shard_map/ppermute | solution.py:300
  59.8 2.6 %collective-permute-done.10.refs_3_ = bf16[160,1664]{1,0:T(8,128)(2,1)S(1)} collective-permute-done((bf16[160,1664]{1,0:T(8,128)(2,1)S(1)}, bf16[160,1664]{1,0:T(8,128)(2,1)S(1)}, u32[]{:S(2)}, u32[]{:S(2)}) %collective-permute-start.10) | collective-permute-done | bytes 532512 | tf_op jit(solution)/shard_map/ppermute | solution.py:300
  63.9 6.9 %up.1.h_ref = bf16[640,1280]{1,0:T(8,128)(2,1)S(1)} custom-call(bf16[160,1664]{1,0:T(8,128)(2,1)S(1)} %constant_dynamic-update-slice_fusion.refs_0_, bf16[160,1664]{1,0:T(8,128)(2,1)S(1)} %collective-permute-done.1.refs_1_, bf16[160,1664]{1,0:T(8,128)(2,1)S(1)} %collective-permute-done.5.refs_2_, bf16[160,1664]{1,0:T(8,128)(2,1)S(1)} %collective-permute-done.10.refs_3_, ...), custom_call_target="tpu_custom_call" | custom-call | flops 1 | bytes 1 | tf_op jit(solution)/shard_map/up/pallas_call | solution.py:202
  70.8 1.7 %collective-permute-done.15.near_ref = bf16[5,384,128]{2,1,0:T(8,128)(2,1)S(1)} collective-permute-done((bf16[5,384,128]{2,1,0:T(8,128)(2,1)S(1)}, bf16[5,384,128]{2,1,0:T(8,128)(2,1)S(1)}, u32[]{:S(2)}, u32[]{:S(2)}) %collective-permute-start.15) | collective-permute-done | bytes 491552 | tf_op jit(solution)/shard_map/ppermute | solution.py:300
  76.3 1.6 %collective-permute-start.19 = (bf16[320,768]{1,0:T(8,128)(2,1)S(1)}, bf16[320,768]{1,0:T(8,128)(2,1)S(1)}, u32[]{:S(2)}, u32[]{:S(2)}) collective-permute-start(bf16[320,768]{1,0:T(8,128)(2,1)S(1)} %down.4), channel_id=1, source_target_pairs={{0,8},{4,12},{8,0},{12,4},{16,24},{20,28},{24,16},{28,20},{1,9},{5... | collective-permute-start | bytes 1474568 | tf_op jit(solution)/shard_map/ppermute | solution.py:300
  77.9 9.2 %collective-permute-done.23.far_ref = bf16[5,384,128]{2,1,0:T(8,128)(2,1)S(1)} collective-permute-done((bf16[5,384,128]{2,1,0:T(8,128)(2,1)S(1)}, bf16[5,384,128]{2,1,0:T(8,128)(2,1)S(1)}, u32[]{:S(2)}, u32[]{:S(2)}) %collective-permute-start.23) | collective-permute-done | bytes 491552 | tf_op jit(solution)/shard_map/ppermute | solution.py:300
  88.1 1.6 %collective-permute-done.19 = bf16[320,768]{1,0:T(8,128)(2,1)S(1)} collective-permute-done((bf16[320,768]{1,0:T(8,128)(2,1)S(1)}, bf16[320,768]{1,0:T(8,128)(2,1)S(1)}, u32[]{:S(2)}, u32[]{:S(2)}) %collective-permute-start.19) | collective-permute-done | bytes 491552 | tf_op jit(solution)/shard_map/ppermute | solution.py:300
  90.7 1.6 %collective-permute-start.28 = (bf16[320,384]{1,0:T(8,128)(2,1)S(1)}, bf16[320,384]{1,0:T(8,128)(2,1)S(1)}, u32[]{:S(2)}, u32[]{:S(2)}) collective-permute-start(bf16[320,384]{1,0:T(8,128)(2,1)S(1)} %get-tuple-element.57), channel_id=1, source_target_pairs={{0,8},{4,12},{8,0},{12,4},{16,24},{20,28},{24,16},{28,20},{1,9},{5... | collective-permute-start | bytes 737288 | tf_op jit(solution)/shard_map/ppermute | solution.py:300
  95.4 4.3 %collective-permute-done.28 = bf16[320,384]{1,0:T(8,128)(2,1)S(1)} collective-permute-done((bf16[320,384]{1,0:T(8,128)(2,1)S(1)}, bf16[320,384]{1,0:T(8,128)(2,1)S(1)}, u32[]{:S(2)}, u32[]{:S(2)}) %collective-permute-start.28) | collective-permute-done | bytes 245792 | tf_op jit(solution)/shard_map/ppermute | solution.py:300
  101.2 2.7 %collective-permute-start.21 = (bf16[80,768]{1,0:T(8,128)(2,1)S(1)}, bf16[80,768]{1,0:T(8,128)(2,1)S(1)}, u32[]{:S(2)}, u32[]{:S(2)}) collective-permute-start(bf16[80,768]{1,0:T(8,128)(2,1)S(1)} %slice.88), channel_id=1, source_target_pairs={{0,2},{1,3},{2,0},{3,1},{4,6},{5,7},{6,4},{7,5},{8,10},{9,11},{10,... | collective-permute-start | bytes 368648 | tf_op jit(solution)/shard_map/ppermute | solution.py:303
  105.0 3.6 %collective-permute-done.21.refs_1_ = bf16[80,768]{1,0:T(8,128)(2,1)S(1)} collective-permute-done((bf16[80,768]{1,0:T(8,128)(2,1)S(1)}, bf16[80,768]{1,0:T(8,128)(2,1)S(1)}, u32[]{:S(2)}, u32[]{:S(2)}) %collective-permute-start.21) | collective-permute-done | bytes 122912 | tf_op jit(solution)/shard_map/ppermute | solution.py:303
  108.6 1.8 %collective-permute-start.30 = (bf16[80,384]{1,0:T(8,128)(2,1)S(1)}, bf16[80,384]{1,0:T(8,128)(2,1)S(1)}, u32[]{:S(2)}, u32[]{:S(2)}) collective-permute-start(bf16[80,384]{1,0:T(8,128)(2,1)S(1)} %slice.89), channel_id=1, source_target_pairs={{0,2},{1,3},{2,0},{3,1},{4,6},{5,7},{6,4},{7,5},{8,10},{9,11},{10,... | collective-permute-start | bytes 184328 | tf_op jit(solution)/shard_map/ppermute | solution.py:303
  110.5 1.6 %collective-permute-start.27 = (bf16[80,384]{1,0:T(8,128)(2,1)S(1)}, bf16[80,384]{1,0:T(8,128)(2,1)S(1)}, u32[]{:S(2)}, u32[]{:S(2)}) collective-permute-start(bf16[80,384]{1,0:T(8,128)(2,1)S(1)} %slice.90), channel_id=1, source_target_pairs={{0,2},{1,3},{2,0},{3,1},{4,6},{5,7},{6,4},{7,5},{8,10},{9,11},{10,... | collective-permute-start | bytes 184328 | tf_op jit(solution)/shard_map/ppermute | solution.py:303
  112.1 1.6 %collective-permute-done.30.refs_5_ = bf16[80,384]{1,0:T(8,128)(2,1)S(1)} collective-permute-done((bf16[80,384]{1,0:T(8,128)(2,1)S(1)}, bf16[80,384]{1,0:T(8,128)(2,1)S(1)}, u32[]{:S(2)}, u32[]{:S(2)}) %collective-permute-start.30) | collective-permute-done | bytes 61472 | tf_op jit(solution)/shard_map/ppermute | solution.py:303
  113.7 2.0 %collective-permute-done.27.refs_3_ = bf16[80,384]{1,0:T(8,128)(2,1)S(1)} collective-permute-done((bf16[80,384]{1,0:T(8,128)(2,1)S(1)}, bf16[80,384]{1,0:T(8,128)(2,1)S(1)}, u32[]{:S(2)}, u32[]{:S(2)}) %collective-permute-start.27) | collective-permute-done | bytes 61472 | tf_op jit(solution)/shard_map/ppermute | solution.py:303
  (93 shorter events, 28.8 us)
Async XLA Ops:
  6.5 25.0 %collective-permute-start.8 = (bf16[5,384,256]{2,1,0:T(8,128)(2,1)S(1)}, bf16[5,384,256]{2,1,0:T(8,128)(2,1)S(1)}, u32[]{:S(2)}, u32[]{:S(2)}) collective-permute-start(bf16[5,384,256]{2,1,0:T(8,128)(2,1)S(1)} %get-tuple-element.38.refs_4_), channel_id=1, source_target_pairs={{0,16},{4,20},{8,24},{12,28},{16,0},{20,4},{24,8},{28,12},{1,17},{... | collective-permute-start | bytes 2949128 | tf_op jit(solution)/shard_map/ppermute | solution.py:300
  9.4 23.7 %collective-permute-start.6 = (bf16[5,384,256]{2,1,0:T(8,128)(2,1)}, bf16[5,384,256]{2,1,0:T(8,128)(2,1)S(1)}, u32[]{:S(2)}, u32[]{:S(2)}) collective-permute-start(bf16[5,384,256]{2,1,0:T(8,128)(2,1)} %get-tuple-element.40), channel_id=1, source_target_pairs={{0,8},{4,12},{8,0},{12,4},{16,24},{20,28},{24,16},{28,20},{1,9},{5... | collective-permute-start | bytes 2949128 | tf_op jit(solution)/shard_map/ppermute | solution.py:300
  10.9 25.0 %collective-permute-start.4 = (bf16[5,384,256]{2,1,0:T(8,128)(2,1)S(1)}, bf16[5,384,256]{2,1,0:T(8,128)(2,1)}, u32[]{:S(2)}, u32[]{:S(2)}) collective-permute-start(bf16[5,384,256]{2,1,0:T(8,128)(2,1)S(1)} %get-tuple-element.38.refs_4_), channel_id=1, source_target_pairs={{0,4},{4,0},{8,12},{12,8},{16,20},{20,16},{24,28},{28,24},{1,5},{5... | collective-permute-start | bytes 2949128 | tf_op jit(solution)/shard_map/ppermute | solution.py:300
  15.9 18.0 %collective-permute-start = (bf16[80,1664]{1,0:T(8,128)(2,1)S(1)}, bf16[80,1664]{1,0:T(8,128)(2,1)S(1)}, u32[]{:S(2)}, u32[]{:S(2)}) collective-permute-start(bf16[80,1664]{1,0:T(8,128)(2,1)S(1)} %get-tuple-element.36), channel_id=1, source_target_pairs={{0,2},{1,3},{2,0},{3,1},{4,6},{5,7},{6,4},{7,5},{8,10},{9,11},{10,... | collective-permute-start | bytes 798728 | tf_op jit(solution)/shard_map/ppermute | solution.py:303
  33.1 22.7 %collective-permute-start.11 = (bf16[5,384,256]{2,1,0:T(8,128)(2,1)S(1)}, bf16[5,384,256]{2,1,0:T(8,128)(2,1)S(1)}, u32[]{:S(2)}, u32[]{:S(2)}) collective-permute-start(bf16[5,384,256]{2,1,0:T(8,128)(2,1)S(1)} %collective-permute-done.6.refs_5_), channel_id=1, source_target_pairs={{0,16},{4,20},{8,24},{12,28},{16,0},{20,4},{24,8},{28,12},{1,17},{... | collective-permute-start | bytes 2949128 | tf_op jit(solution)/shard_map/ppermute | solution.py:300
  33.4 16.2 %collective-permute-start.9 = (bf16[5,384,256]{2,1,0:T(8,128)(2,1)S(1)}, bf16[5,384,256]{2,1,0:T(8,128)(2,1)S(1)}, u32[]{:S(2)}, u32[]{:S(2)}) collective-permute-start(bf16[5,384,256]{2,1,0:T(8,128)(2,1)S(1)} %collective-permute-done.8.refs_6_), channel_id=1, source_target_pairs={{0,4},{4,0},{8,12},{12,8},{16,20},{20,16},{24,28},{28,24},{1,5},{5... | collective-permute-start | bytes 2949128 | tf_op jit(solution)/shard_map/ppermute | solution.py:300
  33.4 16.2 %collective-permute-start.7 = (bf16[5,384,256]{2,1,0:T(8,128)(2,1)S(1)}, bf16[5,384,256]{2,1,0:T(8,128)(2,1)S(1)}, u32[]{:S(2)}, u32[]{:S(2)}) collective-permute-start(bf16[5,384,256]{2,1,0:T(8,128)(2,1)S(1)} %collective-permute-done.6.refs_5_), channel_id=1, source_target_pairs={{0,4},{4,0},{8,12},{12,8},{16,20},{20,16},{24,28},{28,24},{1,5},{5... | collective-permute-start | bytes 2949128 | tf_op jit(solution)/shard_map/ppermute | solution.py:300
  34.0 14.1 %collective-permute-start.1 = (bf16[160,1664]{1,0:T(8,128)(2,1)S(1)}, bf16[160,1664]{1,0:T(8,128)(2,1)S(1)}, u32[]{:S(2)}, u32[]{:S(2)}) collective-permute-start(bf16[160,1664]{1,0:T(8,128)(2,1)S(1)} %constant_dynamic-update-slice_fusion.refs_0_), channel_id=1, source_target_pairs={{0,1},{1,0},{2,3},{3,2},{4,5},{5,4},{6,7},{7,6},{8,9},{9,8},{10,11... | collective-permute-start | bytes 1597448 | tf_op jit(solution)/shard_map/ppermute | solution.py:303
  35.9 13.7 %collective-permute-start.5 = (bf16[160,1664]{1,0:T(8,128)(2,1)S(1)}, bf16[160,1664]{1,0:T(8,128)(2,1)S(1)}, u32[]{:S(2)}, u32[]{:S(2)}) collective-permute-start(bf16[160,1664]{1,0:T(8,128)(2,1)S(1)} %constant_dynamic-update-slice_fusion.refs_0_), channel_id=1, source_target_pairs={{0,8},{4,12},{8,0},{12,4},{16,24},{20,28},{24,16},{28,20},{1,9},{5... | collective-permute-start | bytes 1597448 | tf_op jit(solution)/shard_map/ppermute | solution.py:300
  49.6 12.8 %collective-permute-start.10 = (bf16[160,1664]{1,0:T(8,128)(2,1)S(1)}, bf16[160,1664]{1,0:T(8,128)(2,1)S(1)}, u32[]{:S(2)}, u32[]{:S(2)}) collective-permute-start(bf16[160,1664]{1,0:T(8,128)(2,1)S(1)} %collective-permute-done.1.refs_1_), channel_id=1, source_target_pairs={{0,8},{4,12},{8,0},{12,4},{16,24},{20,28},{24,16},{28,20},{1,9},{5... | collective-permute-start | bytes 1597448 | tf_op jit(solution)/shard_map/ppermute | solution.py:300
  55.8 8.1 %collective-permute-start.12 = (bf16[5,384,256]{2,1,0:T(8,128)(2,1)S(1)}, bf16[5,384,256]{2,1,0:T(8,128)(2,1)S(1)}, u32[]{:S(2)}, u32[]{:S(2)}) collective-permute-start(bf16[5,384,256]{2,1,0:T(8,128)(2,1)S(1)} %collective-permute-done.11.refs_7_), channel_id=1, source_target_pairs={{0,4},{4,0},{8,12},{12,8},{16,20},{20,16},{24,28},{28,24},{1,5},{5... | collective-permute-start | bytes 2949128 | tf_op jit(solution)/shard_map/ppermute | solution.py:300
  59.2 13.3 %collective-permute-start.15 = (bf16[5,384,128]{2,1,0:T(8,128)(2,1)S(1)}, bf16[5,384,128]{2,1,0:T(8,128)(2,1)S(1)}, u32[]{:S(2)}, u32[]{:S(2)}) collective-permute-start(bf16[5,384,128]{2,1,0:T(8,128)(2,1)S(1)} %get-tuple-element.49.near_ref), channel_id=1, source_target_pairs={{0,16},{4,20},{8,24},{12,28},{16,0},{20,4},{24,8},{28,12},{1,17},{... | collective-permute-start | bytes 1474568 | tf_op jit(solution)/shard_map/ppermute | solution.py:300
  62.4 11.0 %collective-permute-start.17 = (bf16[5,384,128]{2,1,0:T(8,128)(2,1)S(1)}, bf16[5,384,128]{2,1,0:T(8,128)(2,1)S(1)}, u32[]{:S(2)}, u32[]{:S(2)}) collective-permute-start(bf16[5,384,128]{2,1,0:T(8,128)(2,1)S(1)} %get-tuple-element.51), channel_id=1, source_target_pairs={{0,8},{4,12},{8,0},{12,4},{16,24},{20,28},{24,16},{28,20},{1,9},{5... | collective-permute-start | bytes 1474568 | tf_op jit(solution)/shard_map/ppermute | solution.py:300
  73.5 13.6 %collective-permute-start.23 = (bf16[5,384,128]{2,1,0:T(8,128)(2,1)S(1)}, bf16[5,384,128]{2,1,0:T(8,128)(2,1)S(1)}, u32[]{:S(2)}, u32[]{:S(2)}) collective-permute-start(bf16[5,384,128]{2,1,0:T(8,128)(2,1)S(1)} %collective-permute-done.17.far_ref), channel_id=1, source_target_pairs={{0,16},{4,20},{8,24},{12,28},{16,0},{20,4},{24,8},{28,12},{1,17},{... | collective-permute-start | bytes 1474568 | tf_op jit(solution)/shard_map/ppermute | solution.py:300
  75.0 14.7 %collective-permute-start.22 = (bf16[5,384,128]{2,1,0:T(8,128)(2,1)S(1)}, bf16[5,384,128]{2,1,0:T(8,128)(2,1)S(1)}, u32[]{:S(2)}, u32[]{:S(2)}) collective-permute-start(bf16[5,384,128]{2,1,0:T(8,128)(2,1)S(1)} %collective-permute-done.15.near_ref), channel_id=1, source_target_pairs={{0,4},{4,0},{8,12},{12,8},{16,20},{20,16},{24,28},{28,24},{1,5},{5... | collective-permute-start | bytes 1474568 | tf_op jit(solution)/shard_map/ppermute | solution.py:300
  76.3 13.4 %collective-permute-start.19 = (bf16[320,768]{1,0:T(8,128)(2,1)S(1)}, bf16[320,768]{1,0:T(8,128)(2,1)S(1)}, u32[]{:S(2)}, u32[]{:S(2)}) collective-permute-start(bf16[320,768]{1,0:T(8,128)(2,1)S(1)} %down.4), channel_id=1, source_target_pairs={{0,8},{4,12},{8,0},{12,4},{16,24},{20,28},{24,16},{28,20},{1,9},{5... | collective-permute-start | bytes 1474568 | tf_op jit(solution)/shard_map/ppermute | solution.py:300
  90.7 9.0 %collective-permute-start.28 = (bf16[320,384]{1,0:T(8,128)(2,1)S(1)}, bf16[320,384]{1,0:T(8,128)(2,1)S(1)}, u32[]{:S(2)}, u32[]{:S(2)}) collective-permute-start(bf16[320,384]{1,0:T(8,128)(2,1)S(1)} %get-tuple-element.57), channel_id=1, source_target_pairs={{0,8},{4,12},{8,0},{12,4},{16,24},{20,28},{24,16},{28,20},{1,9},{5... | collective-permute-start | bytes 737288 | tf_op jit(solution)/shard_map/ppermute | solution.py:300
  92.5 8.7 %collective-permute-start.20 = (bf16[160,768]{1,0:T(8,128)(2,1)S(1)}, bf16[160,768]{1,0:T(8,128)(2,1)S(1)}, u32[]{:S(2)}, u32[]{:S(2)}) collective-permute-start(bf16[160,768]{1,0:T(8,128)(2,1)S(1)} %slice.85), channel_id=1, source_target_pairs={{0,1},{1,0},{2,3},{3,2},{4,5},{5,4},{6,7},{7,6},{8,9},{9,8},{10,11... | collective-permute-start | bytes 737288 | tf_op jit(solution)/shard_map/ppermute | solution.py:303
  93.8 10.0 %collective-permute-start.25 = (bf16[320,384]{1,0:T(8,128)(2,1)S(1)}, bf16[320,384]{1,0:T(8,128)(2,1)S(1)}, u32[]{:S(2)}, u32[]{:S(2)}) collective-permute-start(bf16[320,384]{1,0:T(8,128)(2,1)S(1)} %get-tuple-element.60), channel_id=1, source_target_pairs={{0,8},{4,12},{8,0},{12,4},{16,24},{20,28},{24,16},{28,20},{1,9},{5... | collective-permute-start | bytes 737288 | tf_op jit(solution)/shard_map/ppermute | solution.py:300
  99.8 5.2 %collective-permute-start.29 = (bf16[160,384]{1,0:T(8,128)(2,1)S(1)}, bf16[160,384]{1,0:T(8,128)(2,1)S(1)}, u32[]{:S(2)}, u32[]{:S(2)}) collective-permute-start(bf16[160,384]{1,0:T(8,128)(2,1)S(1)} %slice.86), channel_id=1, source_target_pairs={{0,1},{1,0},{2,3},{3,2},{4,5},{5,4},{6,7},{7,6},{8,9},{9,8},{10,11... | collective-permute-start | bytes 368648 | tf_op jit(solution)/shard_map/ppermute | solution.py:303
  101.2 7.3 %collective-permute-start.21 = (bf16[80,768]{1,0:T(8,128)(2,1)S(1)}, bf16[80,768]{1,0:T(8,128)(2,1)S(1)}, u32[]{:S(2)}, u32[]{:S(2)}) collective-permute-start(bf16[80,768]{1,0:T(8,128)(2,1)S(1)} %slice.88), channel_id=1, source_target_pairs={{0,2},{1,3},{2,0},{3,1},{4,6},{5,7},{6,4},{7,5},{8,10},{9,11},{10,... | collective-permute-start | bytes 368648 | tf_op jit(solution)/shard_map/ppermute | solution.py:303
  103.9 6.5 %collective-permute-start.26 = (bf16[160,384]{1,0:T(8,128)(2,1)S(1)}, bf16[160,384]{1,0:T(8,128)(2,1)S(1)}, u32[]{:S(2)}, u32[]{:S(2)}) collective-permute-start(bf16[160,384]{1,0:T(8,128)(2,1)S(1)} %slice.87), channel_id=1, source_target_pairs={{0,1},{1,0},{2,3},{3,2},{4,5},{5,4},{6,7},{7,6},{8,9},{9,8},{10,11... | collective-permute-start | bytes 368648 | tf_op jit(solution)/shard_map/ppermute | solution.py:303
  108.6 5.1 %collective-permute-start.30 = (bf16[80,384]{1,0:T(8,128)(2,1)S(1)}, bf16[80,384]{1,0:T(8,128)(2,1)S(1)}, u32[]{:S(2)}, u32[]{:S(2)}) collective-permute-start(bf16[80,384]{1,0:T(8,128)(2,1)S(1)} %slice.89), channel_id=1, source_target_pairs={{0,2},{1,3},{2,0},{3,1},{4,6},{5,7},{6,4},{7,5},{8,10},{9,11},{10,... | collective-permute-start | bytes 184328 | tf_op jit(solution)/shard_map/ppermute | solution.py:303
  110.5 5.2 %collective-permute-start.27 = (bf16[80,384]{1,0:T(8,128)(2,1)S(1)}, bf16[80,384]{1,0:T(8,128)(2,1)S(1)}, u32[]{:S(2)}, u32[]{:S(2)}) collective-permute-start(bf16[80,384]{1,0:T(8,128)(2,1)S(1)} %slice.90), channel_id=1, source_target_pairs={{0,2},{1,3},{2,0},{3,1},{4,6},{5,7},{6,4},{7,5},{8,10},{9,11},{10,... | collective-permute-start | bytes 184328 | tf_op jit(solution)/shard_map/ppermute | solution.py:303
  (17 other events, 126.8 us)

commit v10 on v9

--- a/solution.py
+++ b/solution.py
@@ -338,7 +338,7 @@
     gu_fars = widen([after(gu_far, gu_nears[-1])])
     gu_nears_other = [gu_near_other] + [flip(v, 1) for v in gu_nears[1:]]
     gu_far_other = flip(gu_far, 1)
-    far_x = flip(after(far, near_x, gu_far_other, *gu_nears_other[1:]), 2)
+    far_x = flip(after(far, near_x), 2)
     gu_fars_other = [gu_far_other] + [flip(v, 1) for v in gu_fars[1:]]
     mine = [v for pair in zip(gu_nears, gu_fars) for v in pair]
     other = [v for pair in zip(gu_nears_other, gu_fars_other) for v in pair]
@@ -375,7 +375,7 @@
             for bit in zone_bits:
                 size = total.shape[0] // 2
                 moved = total[size:].astype(jnp.bfloat16)
-                if bit == zone_bits[-1] and m == rows - 1:
+                if bit == zone_bits[-1] and m == rows - 1 and i == 1:
                     moved = after(moved, chunks[0][1])
                 received = hop(moved, bit)
                 total = total[:size]

time: 117 us -> 117 us (level)
  transfers between devices with their start and end apart: 31 -> 31, of which waited for: 20 -> 18; matrix products, arithmetic and copies ran while one was open for 1% -> 1% of each run, Pallas kernels for 11% -> 11%
where the time goes in v10:
time: 117 us
  waiting for transfers between devices  63.8 us (55%)
  starting transfers between devices  31 us (26%)
  Pallas kernels  16 us (14%)
  local copies, waits for them, and re-layouts  4.35 us (4%)
    ppermute x23, waiting for transfers between devices, flip(): return lax.ppermute(values, 'dp', [(i, i ^ bit) for i in range(ranks)])  46.3 us
    ppermute x8, waiting for transfers between devices, hop(): return lax.ppermute(values, 'expert', [(i, i ^ bit) for i in range(zones)])  17.5 us
    ppermute x23, starting transfers between devices, flip(): return lax.ppermute(values, 'dp', [(i, i ^ bit) for i in range(ranks)])  16.9 us
    ppermute x8, starting transfers between devices, hop(): return lax.ppermute(values, 'expert', [(i, i ^ bit) for i in range(zones)])  14.2 us
    pallas_call x1, Pallas kernels, up_call(): pl.pallas_call(functools.partial(up_kernel, len(mine) // 2, len(here)), i...  6.89 us
    unnamed x23, local copies, waits for them, and re-layouts  4.12 us
    pallas_call x4, Pallas kernels, down_call(): pl.pallas_call(functools.partial(down_kernel, tokens if send else 0), in_...  4.04 us
    pallas_call x1, Pallas kernels, front_call(): pl.pallas_call(functools.partial(front_kernel, ranks), grid=(steps,), in_...  2.38 us
  transfers between devices with their start and end apart: 31, of which 18 were waited for; matrix products, arithmetic and copies ran while one was open for 1% of the time, Pallas kernels for 11%

profile of v10, /device:TPU:0, one launch (start us, length us, event | category | flops | bytes accessed | tf_op | source)
XLA Modules:
  0.0 116.5 jit_solution(5091180623403230571)
XLA Ops:
  0.6 1.5 %copy-done = bf16[5,192,1024]{2,1,0:T(8,128)(2,1)S(1)} copy-done((bf16[5,192,1024]{2,1,0:T(8,128)(2,1)S(1)}, bf16[5,192,1024]{2,1,0:T(8,128)(2,1)}, u32[]{:S(2)}) %copy-start) | copy-done | bytes 1966104
  6.5 2.9 %collective-permute-start.8 = (bf16[5,384,256]{2,1,0:T(8,128)(2,1)S(1)}, bf16[5,384,256]{2,1,0:T(8,128)(2,1)S(1)}, u32[]{:S(2)}, u32[]{:S(2)}) collective-permute-start(bf16[5,384,256]{2,1,0:T(8,128)(2,1)S(1)} %get-tuple-element.37.refs_4_), channel_id=1, source_target_pairs={{0,16},{4,20},{8,24},{12,28},{16,0},{20,4},{24,8},{28,12},{1,17},{... | collective-permute-start | bytes 2949128 | tf_op jit(solution)/shard_map/ppermute | solution.py:300
  11.2 2.3 %copy-done.1 = bf16[1536,1536]{1,0:T(8,128)(2,1)S(1)} copy-done((bf16[1536,1536]{1,0:T(8,128)(2,1)S(1)}, bf16[1536,1536]{1,0:T(8,128)(2,1)}, u32[]{:S(2)}) %copy-start.1) | copy-done | bytes 4718616
  13.5 2.4 %front.1 = (bf16[80,1536]{1,0:T(8,128)(2,1)S(1)}, bf16[80,1664]{1,0:T(8,128)(2,1)S(1)}) custom-call(bf16[80,1536]{1,0:T(8,128)(2,1)S(1)} %copy-done.3, bf16[80,1536]{1,0:T(8,128)(2,1)S(1)} %copy-done.4, bf16[1536,1536]{1,0:T(8,128)(2,1)S(1)} %copy-done.1, f32[1,1536]{1,0:T(1,128)S(1)} %broadcast_in_dim.9.gain_ref, s32[80,8]{1,0:T(8,128)S(1)} %copy.12.routes_ref, ...), custom_call_target="tpu_custom_call" | custom-call | flops 1 | bytes 1 | tf_op jit(solution)/shard_map/front/pallas_call | solution.py:91
  15.9 2.7 %collective-permute-start = (bf16[80,1664]{1,0:T(8,128)(2,1)S(1)}, bf16[80,1664]{1,0:T(8,128)(2,1)S(1)}, u32[]{:S(2)}, u32[]{:S(2)}) collective-permute-start(bf16[80,1664]{1,0:T(8,128)(2,1)S(1)} %get-tuple-element.35), channel_id=1, source_target_pairs={{0,2},{1,3},{2,0},{3,1},{4,6},{5,7},{6,4},{7,5},{8,10},{9,11},{10,... | collective-permute-start | bytes 798728 | tf_op jit(solution)/shard_map/ppermute | solution.py:303
  18.6 12.9 %collective-permute-done.8.refs_6_ = bf16[5,384,256]{2,1,0:T(8,128)(2,1)S(1)} collective-permute-done((bf16[5,384,256]{2,1,0:T(8,128)(2,1)S(1)}, bf16[5,384,256]{2,1,0:T(8,128)(2,1)S(1)}, u32[]{:S(2)}, u32[]{:S(2)}) %collective-permute-start.8) | collective-permute-done | bytes 983072 | tf_op jit(solution)/shard_map/ppermute | solution.py:300
  31.4 1.7 %collective-permute-done.7.refs_5_ = bf16[5,384,256]{2,1,0:T(8,128)(2,1)S(1)} collective-permute-done((bf16[5,384,256]{2,1,0:T(8,128)(2,1)}, bf16[5,384,256]{2,1,0:T(8,128)(2,1)S(1)}, u32[]{:S(2)}, u32[]{:S(2)}) %collective-permute-start.7) | collective-permute-done | bytes 983072 | tf_op jit(solution)/shard_map/ppermute | solution.py:300
  33.5 1.9 %collective-permute-start.1 = (bf16[160,1664]{1,0:T(8,128)(2,1)S(1)}, bf16[160,1664]{1,0:T(8,128)(2,1)S(1)}, u32[]{:S(2)}, u32[]{:S(2)}) collective-permute-start(bf16[160,1664]{1,0:T(8,128)(2,1)S(1)} %constant_dynamic-update-slice_fusion.refs_0_), channel_id=1, source_target_pairs={{0,1},{1,0},{2,3},{3,2},{4,5},{5,4},{6,7},{7,6},{8,9},{9,8},{10,11... | collective-permute-start | bytes 1597448 | tf_op jit(solution)/shard_map/ppermute | solution.py:303
  35.3 1.5 %collective-permute-start.5 = (bf16[160,1664]{1,0:T(8,128)(2,1)S(1)}, bf16[160,1664]{1,0:T(8,128)(2,1)S(1)}, u32[]{:S(2)}, u32[]{:S(2)}) collective-permute-start(bf16[160,1664]{1,0:T(8,128)(2,1)S(1)} %constant_dynamic-update-slice_fusion.refs_0_), channel_id=1, source_target_pairs={{0,8},{4,12},{8,0},{12,4},{16,24},{20,28},{24,16},{28,20},{1,9},{5... | collective-permute-start | bytes 1597448 | tf_op jit(solution)/shard_map/ppermute | solution.py:300
  36.8 9.7 %collective-permute-done.1.refs_1_ = bf16[160,1664]{1,0:T(8,128)(2,1)S(1)} collective-permute-done((bf16[160,1664]{1,0:T(8,128)(2,1)S(1)}, bf16[160,1664]{1,0:T(8,128)(2,1)S(1)}, u32[]{:S(2)}, u32[]{:S(2)}) %collective-permute-start.1) | collective-permute-done | bytes 532512 | tf_op jit(solution)/shard_map/ppermute | solution.py:303
  50.0 5.8 %collective-permute-done.9.refs_7_ = bf16[5,384,256]{2,1,0:T(8,128)(2,1)S(1)} collective-permute-done((bf16[5,384,256]{2,1,0:T(8,128)(2,1)S(1)}, bf16[5,384,256]{2,1,0:T(8,128)(2,1)S(1)}, u32[]{:S(2)}, u32[]{:S(2)}) %collective-permute-start.9) | collective-permute-done | bytes 983072 | tf_op jit(solution)/shard_map/ppermute | solution.py:300
  56.3 2.4 %collective-permute-done.14.away_in_ref = bf16[5,192,128]{2,1,0:T(8,128)(2,1)S(1)} collective-permute-done((bf16[5,192,128]{2,1,0:T(8,128)(2,1)S(1)}, bf16[5,192,128]{2,1,0:T(8,128)(2,1)S(1)}, u32[]{:S(2)}, u32[]{:S(2)}) %collective-permute-start.14) | collective-permute-done | bytes 245792 | tf_op jit(solution)/shard_map/ppermute | solution.py:300
  60.9 6.9 %up.1.h_ref = bf16[640,1280]{1,0:T(8,128)(2,1)S(1)} custom-call(bf16[160,1664]{1,0:T(8,128)(2,1)S(1)} %constant_dynamic-update-slice_fusion.refs_0_, bf16[160,1664]{1,0:T(8,128)(2,1)S(1)} %collective-permute-done.1.refs_1_, bf16[160,1664]{1,0:T(8,128)(2,1)S(1)} %collective-permute-done.5.refs_2_, bf16[160,1664]{1,0:T(8,128)(2,1)S(1)} %collective-permute-done.6.refs_3_, ...), custom_call_target="tpu_custom_call" | custom-call | flops 1 | bytes 1 | tf_op jit(solution)/shard_map/up/pallas_call | solution.py:202
  67.8 4.4 %collective-permute-done.15.near_ref = bf16[5,384,128]{2,1,0:T(8,128)(2,1)S(1)} collective-permute-done((bf16[5,384,128]{2,1,0:T(8,128)(2,1)S(1)}, bf16[5,384,128]{2,1,0:T(8,128)(2,1)S(1)}, u32[]{:S(2)}, u32[]{:S(2)}) %collective-permute-start.15) | collective-permute-done | bytes 491552 | tf_op jit(solution)/shard_map/ppermute | solution.py:300
  77.5 8.6 %collective-permute-done.23.far_ref = bf16[5,384,128]{2,1,0:T(8,128)(2,1)S(1)} collective-permute-done((bf16[5,384,128]{2,1,0:T(8,128)(2,1)S(1)}, bf16[5,384,128]{2,1,0:T(8,128)(2,1)S(1)}, u32[]{:S(2)}, u32[]{:S(2)}) %collective-permute-start.23) | collective-permute-done | bytes 491552 | tf_op jit(solution)/shard_map/ppermute | solution.py:300
  87.2 2.3 %collective-permute-done.19 = bf16[320,768]{1,0:T(8,128)(2,1)S(1)} collective-permute-done((bf16[320,768]{1,0:T(8,128)(2,1)S(1)}, bf16[320,768]{1,0:T(8,128)(2,1)S(1)}, u32[]{:S(2)}, u32[]{:S(2)}) %collective-permute-start.19) | collective-permute-done | bytes 491552 | tf_op jit(solution)/shard_map/ppermute | solution.py:300
  92.1 1.6 %collective-permute-start.20 = (bf16[160,768]{1,0:T(8,128)(2,1)S(1)}, bf16[160,768]{1,0:T(8,128)(2,1)S(1)}, u32[]{:S(2)}, u32[]{:S(2)}) collective-permute-start(bf16[160,768]{1,0:T(8,128)(2,1)S(1)} %slice.85), channel_id=1, source_target_pairs={{0,1},{1,0},{2,3},{3,2},{4,5},{5,4},{6,7},{7,6},{8,9},{9,8},{10,11... | collective-permute-start | bytes 737288 | tf_op jit(solution)/shard_map/ppermute | solution.py:303
  95.3 4.1 %collective-permute-done.28 = bf16[320,384]{1,0:T(8,128)(2,1)S(1)} collective-permute-done((bf16[320,384]{1,0:T(8,128)(2,1)S(1)}, bf16[320,384]{1,0:T(8,128)(2,1)S(1)}, u32[]{:S(2)}, u32[]{:S(2)}) %collective-permute-start.28) | collective-permute-done | bytes 245792 | tf_op jit(solution)/shard_map/ppermute | solution.py:300
  99.5 1.5 %collective-permute-start.29 = (bf16[160,384]{1,0:T(8,128)(2,1)S(1)}, bf16[160,384]{1,0:T(8,128)(2,1)S(1)}, u32[]{:S(2)}, u32[]{:S(2)}) collective-permute-start(bf16[160,384]{1,0:T(8,128)(2,1)S(1)} %slice.86), channel_id=1, source_target_pairs={{0,1},{1,0},{2,3},{3,2},{4,5},{5,4},{6,7},{7,6},{8,9},{9,8},{10,11... | collective-permute-start | bytes 368648 | tf_op jit(solution)/shard_map/ppermute | solution.py:303
  101.1 2.7 %collective-permute-start.21 = (bf16[80,768]{1,0:T(8,128)(2,1)S(1)}, bf16[80,768]{1,0:T(8,128)(2,1)S(1)}, u32[]{:S(2)}, u32[]{:S(2)}) collective-permute-start(bf16[80,768]{1,0:T(8,128)(2,1)S(1)} %slice.88), channel_id=1, source_target_pairs={{0,2},{1,3},{2,0},{3,1},{4,6},{5,7},{6,4},{7,5},{8,10},{9,11},{10,... | collective-permute-start | bytes 368648 | tf_op jit(solution)/shard_map/ppermute | solution.py:303
  104.8 3.7 %collective-permute-done.21.refs_1_ = bf16[80,768]{1,0:T(8,128)(2,1)S(1)} collective-permute-done((bf16[80,768]{1,0:T(8,128)(2,1)S(1)}, bf16[80,768]{1,0:T(8,128)(2,1)S(1)}, u32[]{:S(2)}, u32[]{:S(2)}) %collective-permute-start.21) | collective-permute-done | bytes 122912 | tf_op jit(solution)/shard_map/ppermute | solution.py:303
  108.5 1.8 %collective-permute-start.30 = (bf16[80,384]{1,0:T(8,128)(2,1)S(1)}, bf16[80,384]{1,0:T(8,128)(2,1)S(1)}, u32[]{:S(2)}, u32[]{:S(2)}) collective-permute-start(bf16[80,384]{1,0:T(8,128)(2,1)S(1)} %slice.89), channel_id=1, source_target_pairs={{0,2},{1,3},{2,0},{3,1},{4,6},{5,7},{6,4},{7,5},{8,10},{9,11},{10,... | collective-permute-start | bytes 184328 | tf_op jit(solution)/shard_map/ppermute | solution.py:303
  111.7 1.9 %collective-permute-done.30.refs_5_ = bf16[80,384]{1,0:T(8,128)(2,1)S(1)} collective-permute-done((bf16[80,384]{1,0:T(8,128)(2,1)S(1)}, bf16[80,384]{1,0:T(8,128)(2,1)S(1)}, u32[]{:S(2)}, u32[]{:S(2)}) %collective-permute-start.30) | collective-permute-done | bytes 61472 | tf_op jit(solution)/shard_map/ppermute | solution.py:303
  113.6 1.9 %collective-permute-done.27.refs_3_ = bf16[80,384]{1,0:T(8,128)(2,1)S(1)} collective-permute-done((bf16[80,384]{1,0:T(8,128)(2,1)S(1)}, bf16[80,384]{1,0:T(8,128)(2,1)S(1)}, u32[]{:S(2)}, u32[]{:S(2)}) %collective-permute-start.27) | collective-permute-done | bytes 61472 | tf_op jit(solution)/shard_map/ppermute | solution.py:303
  (93 shorter events, 26.6 us)
Async XLA Ops:
  6.5 25.0 %collective-permute-start.8 = (bf16[5,384,256]{2,1,0:T(8,128)(2,1)S(1)}, bf16[5,384,256]{2,1,0:T(8,128)(2,1)S(1)}, u32[]{:S(2)}, u32[]{:S(2)}) collective-permute-start(bf16[5,384,256]{2,1,0:T(8,128)(2,1)S(1)} %get-tuple-element.37.refs_4_), channel_id=1, source_target_pairs={{0,16},{4,20},{8,24},{12,28},{16,0},{20,4},{24,8},{28,12},{1,17},{... | collective-permute-start | bytes 2949128 | tf_op jit(solution)/shard_map/ppermute | solution.py:300
  9.4 23.7 %collective-permute-start.7 = (bf16[5,384,256]{2,1,0:T(8,128)(2,1)}, bf16[5,384,256]{2,1,0:T(8,128)(2,1)S(1)}, u32[]{:S(2)}, u32[]{:S(2)}) collective-permute-start(bf16[5,384,256]{2,1,0:T(8,128)(2,1)} %get-tuple-element.40), channel_id=1, source_target_pairs={{0,8},{4,12},{8,0},{12,4},{16,24},{20,28},{24,16},{28,20},{1,9},{5... | collective-permute-start | bytes 2949128 | tf_op jit(solution)/shard_map/ppermute | solution.py:300
  10.9 24.5 %collective-permute-start.4 = (bf16[5,384,256]{2,1,0:T(8,128)(2,1)S(1)}, bf16[5,384,256]{2,1,0:T(8,128)(2,1)}, u32[]{:S(2)}, u32[]{:S(2)}) collective-permute-start(bf16[5,384,256]{2,1,0:T(8,128)(2,1)S(1)} %get-tuple-element.37.refs_4_), channel_id=1, source_target_pairs={{0,4},{4,0},{8,12},{12,8},{16,20},{20,16},{24,28},{28,24},{1,5},{5... | collective-permute-start | bytes 2949128 | tf_op jit(solution)/shard_map/ppermute | solution.py:300
  15.9 17.5 %collective-permute-start = (bf16[80,1664]{1,0:T(8,128)(2,1)S(1)}, bf16[80,1664]{1,0:T(8,128)(2,1)S(1)}, u32[]{:S(2)}, u32[]{:S(2)}) collective-permute-start(bf16[80,1664]{1,0:T(8,128)(2,1)S(1)} %get-tuple-element.35), channel_id=1, source_target_pairs={{0,2},{1,3},{2,0},{3,1},{4,6},{5,7},{6,4},{7,5},{8,10},{9,11},{10,... | collective-permute-start | bytes 798728 | tf_op jit(solution)/shard_map/ppermute | solution.py:303
  33.1 22.7 %collective-permute-start.9 = (bf16[5,384,256]{2,1,0:T(8,128)(2,1)S(1)}, bf16[5,384,256]{2,1,0:T(8,128)(2,1)S(1)}, u32[]{:S(2)}, u32[]{:S(2)}) collective-permute-start(bf16[5,384,256]{2,1,0:T(8,128)(2,1)S(1)} %collective-permute-done.7.refs_5_), channel_id=1, source_target_pairs={{0,16},{4,20},{8,24},{12,28},{16,0},{20,4},{24,8},{28,12},{1,17},{... | collective-permute-start | bytes 2949128 | tf_op jit(solution)/shard_map/ppermute | solution.py:300
  33.5 13.1 %collective-permute-start.1 = (bf16[160,1664]{1,0:T(8,128)(2,1)S(1)}, bf16[160,1664]{1,0:T(8,128)(2,1)S(1)}, u32[]{:S(2)}, u32[]{:S(2)}) collective-permute-start(bf16[160,1664]{1,0:T(8,128)(2,1)S(1)} %constant_dynamic-update-slice_fusion.refs_0_), channel_id=1, source_target_pairs={{0,1},{1,0},{2,3},{3,2},{4,5},{5,4},{6,7},{7,6},{8,9},{9,8},{10,11... | collective-permute-start | bytes 1597448 | tf_op jit(solution)/shard_map/ppermute | solution.py:303
  35.3 12.4 %collective-permute-start.5 = (bf16[160,1664]{1,0:T(8,128)(2,1)S(1)}, bf16[160,1664]{1,0:T(8,128)(2,1)S(1)}, u32[]{:S(2)}, u32[]{:S(2)}) collective-permute-start(bf16[160,1664]{1,0:T(8,128)(2,1)S(1)} %constant_dynamic-update-slice_fusion.refs_0_), channel_id=1, source_target_pairs={{0,8},{4,12},{8,0},{12,4},{16,24},{20,28},{24,16},{28,20},{1,9},{5... | collective-permute-start | bytes 1597448 | tf_op jit(solution)/shard_map/ppermute | solution.py:300
  47.8 11.7 %collective-permute-start.6 = (bf16[160,1664]{1,0:T(8,128)(2,1)S(1)}, bf16[160,1664]{1,0:T(8,128)(2,1)S(1)}, u32[]{:S(2)}, u32[]{:S(2)}) collective-permute-start(bf16[160,1664]{1,0:T(8,128)(2,1)S(1)} %collective-permute-done.1.refs_1_), channel_id=1, source_target_pairs={{0,8},{4,12},{8,0},{12,4},{16,24},{20,28},{24,16},{28,20},{1,9},{5... | collective-permute-start | bytes 1597448 | tf_op jit(solution)/shard_map/ppermute | solution.py:300
  49.4 6.4 %collective-permute-start.13 = (bf16[5,192,128]{2,1,0:T(8,128)(2,1)S(1)}, bf16[5,192,128]{2,1,0:T(8,128)(2,1)S(1)}, u32[]{:S(2)}, u32[]{:S(2)}) collective-permute-start(bf16[5,192,128]{2,1,0:T(8,128)(2,1)S(1)} %get-tuple-element.43), channel_id=1, source_target_pairs={{0,4},{4,0},{8,12},{12,8},{16,20},{20,16},{24,28},{28,24},{1,5},{5... | collective-permute-start | bytes 737288 | tf_op jit(solution)/shard_map/ppermute | solution.py:300
  49.4 11.4 %collective-permute-start.11 = (bf16[5,384,256]{2,1,0:T(8,128)(2,1)S(1)}, bf16[5,384,256]{2,1,0:T(8,128)(2,1)S(1)}, u32[]{:S(2)}, u32[]{:S(2)}) collective-permute-start(bf16[5,384,256]{2,1,0:T(8,128)(2,1)S(1)} %collective-permute-done.8.refs_6_), channel_id=1, source_target_pairs={{0,4},{4,0},{8,12},{12,8},{16,20},{20,16},{24,28},{28,24},{1,5},{5... | collective-permute-start | bytes 2949128 | tf_op jit(solution)/shard_map/ppermute | solution.py:300
  49.9 10.9 %collective-permute-start.10 = (bf16[5,384,256]{2,1,0:T(8,128)(2,1)S(1)}, bf16[5,384,256]{2,1,0:T(8,128)(2,1)S(1)}, u32[]{:S(2)}, u32[]{:S(2)}) collective-permute-start(bf16[5,384,256]{2,1,0:T(8,128)(2,1)S(1)} %collective-permute-done.7.refs_5_), channel_id=1, source_target_pairs={{0,4},{4,0},{8,12},{12,8},{16,20},{20,16},{24,28},{28,24},{1,5},{5... | collective-permute-start | bytes 2949128 | tf_op jit(solution)/shard_map/ppermute | solution.py:300
  58.8 13.3 %collective-permute-start.15 = (bf16[5,384,128]{2,1,0:T(8,128)(2,1)S(1)}, bf16[5,384,128]{2,1,0:T(8,128)(2,1)S(1)}, u32[]{:S(2)}, u32[]{:S(2)}) collective-permute-start(bf16[5,384,128]{2,1,0:T(8,128)(2,1)S(1)} %get-tuple-element.48.near_ref), channel_id=1, source_target_pairs={{0,16},{4,20},{8,24},{12,28},{16,0},{20,4},{24,8},{28,12},{1,17},{... | collective-permute-start | bytes 1474568 | tf_op jit(solution)/shard_map/ppermute | solution.py:300
  59.5 13.0 %collective-permute-start.17 = (bf16[5,384,128]{2,1,0:T(8,128)(2,1)S(1)}, bf16[5,384,128]{2,1,0:T(8,128)(2,1)S(1)}, u32[]{:S(2)}, u32[]{:S(2)}) collective-permute-start(bf16[5,384,128]{2,1,0:T(8,128)(2,1)S(1)} %get-tuple-element.50), channel_id=1, source_target_pairs={{0,8},{4,12},{8,0},{12,4},{16,24},{20,28},{24,16},{28,20},{1,9},{5... | collective-permute-start | bytes 1474568 | tf_op jit(solution)/shard_map/ppermute | solution.py:300
  73.0 13.1 %collective-permute-start.23 = (bf16[5,384,128]{2,1,0:T(8,128)(2,1)S(1)}, bf16[5,384,128]{2,1,0:T(8,128)(2,1)S(1)}, u32[]{:S(2)}, u32[]{:S(2)}) collective-permute-start(bf16[5,384,128]{2,1,0:T(8,128)(2,1)S(1)} %collective-permute-done.17.far_ref), channel_id=1, source_target_pairs={{0,16},{4,20},{8,24},{12,28},{16,0},{20,4},{24,8},{28,12},{1,17},{... | collective-permute-start | bytes 1474568 | tf_op jit(solution)/shard_map/ppermute | solution.py:300
  74.4 15.0 %collective-permute-start.22 = (bf16[5,384,128]{2,1,0:T(8,128)(2,1)S(1)}, bf16[5,384,128]{2,1,0:T(8,128)(2,1)S(1)}, u32[]{:S(2)}, u32[]{:S(2)}) collective-permute-start(bf16[5,384,128]{2,1,0:T(8,128)(2,1)S(1)} %collective-permute-done.15.near_ref), channel_id=1, source_target_pairs={{0,4},{4,0},{8,12},{12,8},{16,20},{20,16},{24,28},{28,24},{1,5},{5... | collective-permute-start | bytes 1474568 | tf_op jit(solution)/shard_map/ppermute | solution.py:300
  76.1 13.3 %collective-permute-start.19 = (bf16[320,768]{1,0:T(8,128)(2,1)S(1)}, bf16[320,768]{1,0:T(8,128)(2,1)S(1)}, u32[]{:S(2)}, u32[]{:S(2)}) collective-permute-start(bf16[320,768]{1,0:T(8,128)(2,1)S(1)} %down.4), channel_id=1, source_target_pairs={{0,8},{4,12},{8,0},{12,4},{16,24},{20,28},{24,16},{28,20},{1,9},{5... | collective-permute-start | bytes 1474568 | tf_op jit(solution)/shard_map/ppermute | solution.py:300
  90.4 9.0 %collective-permute-start.28 = (bf16[320,384]{1,0:T(8,128)(2,1)S(1)}, bf16[320,384]{1,0:T(8,128)(2,1)S(1)}, u32[]{:S(2)}, u32[]{:S(2)}) collective-permute-start(bf16[320,384]{1,0:T(8,128)(2,1)S(1)} %get-tuple-element.56), channel_id=1, source_target_pairs={{0,8},{4,12},{8,0},{12,4},{16,24},{20,28},{24,16},{28,20},{1,9},{5... | collective-permute-start | bytes 737288 | tf_op jit(solution)/shard_map/ppermute | solution.py:300
  92.1 8.9 %collective-permute-start.20 = (bf16[160,768]{1,0:T(8,128)(2,1)S(1)}, bf16[160,768]{1,0:T(8,128)(2,1)S(1)}, u32[]{:S(2)}, u32[]{:S(2)}) collective-permute-start(bf16[160,768]{1,0:T(8,128)(2,1)S(1)} %slice.85), channel_id=1, source_target_pairs={{0,1},{1,0},{2,3},{3,2},{4,5},{5,4},{6,7},{7,6},{8,9},{9,8},{10,11... | collective-permute-start | bytes 737288 | tf_op jit(solution)/shard_map/ppermute | solution.py:303
  93.7 10.0 %collective-permute-start.25 = (bf16[320,384]{1,0:T(8,128)(2,1)S(1)}, bf16[320,384]{1,0:T(8,128)(2,1)S(1)}, u32[]{:S(2)}, u32[]{:S(2)}) collective-permute-start(bf16[320,384]{1,0:T(8,128)(2,1)S(1)} %get-tuple-element.59), channel_id=1, source_target_pairs={{0,8},{4,12},{8,0},{12,4},{16,24},{20,28},{24,16},{28,20},{1,9},{5... | collective-permute-start | bytes 737288 | tf_op jit(solution)/shard_map/ppermute | solution.py:300
  99.5 5.3 %collective-permute-start.29 = (bf16[160,384]{1,0:T(8,128)(2,1)S(1)}, bf16[160,384]{1,0:T(8,128)(2,1)S(1)}, u32[]{:S(2)}, u32[]{:S(2)}) collective-permute-start(bf16[160,384]{1,0:T(8,128)(2,1)S(1)} %slice.86), channel_id=1, source_target_pairs={{0,1},{1,0},{2,3},{3,2},{4,5},{5,4},{6,7},{7,6},{8,9},{9,8},{10,11... | collective-permute-start | bytes 368648 | tf_op jit(solution)/shard_map/ppermute | solution.py:303
  101.1 7.4 %collective-permute-start.21 = (bf16[80,768]{1,0:T(8,128)(2,1)S(1)}, bf16[80,768]{1,0:T(8,128)(2,1)S(1)}, u32[]{:S(2)}, u32[]{:S(2)}) collective-permute-start(bf16[80,768]{1,0:T(8,128)(2,1)S(1)} %slice.88), channel_id=1, source_target_pairs={{0,2},{1,3},{2,0},{3,1},{4,6},{5,7},{6,4},{7,5},{8,10},{9,11},{10,... | collective-permute-start | bytes 368648 | tf_op jit(solution)/shard_map/ppermute | solution.py:303
  103.8 6.5 %collective-permute-start.26 = (bf16[160,384]{1,0:T(8,128)(2,1)S(1)}, bf16[160,384]{1,0:T(8,128)(2,1)S(1)}, u32[]{:S(2)}, u32[]{:S(2)}) collective-permute-start(bf16[160,384]{1,0:T(8,128)(2,1)S(1)} %slice.87), channel_id=1, source_target_pairs={{0,1},{1,0},{2,3},{3,2},{4,5},{5,4},{6,7},{7,6},{8,9},{9,8},{10,11... | collective-permute-start | bytes 368648 | tf_op jit(solution)/shard_map/ppermute | solution.py:303
  108.5 5.1 %collective-permute-start.30 = (bf16[80,384]{1,0:T(8,128)(2,1)S(1)}, bf16[80,384]{1,0:T(8,128)(2,1)S(1)}, u32[]{:S(2)}, u32[]{:S(2)}) collective-permute-start(bf16[80,384]{1,0:T(8,128)(2,1)S(1)} %slice.89), channel_id=1, source_target_pairs={{0,2},{1,3},{2,0},{3,1},{4,6},{5,7},{6,4},{7,5},{8,10},{9,11},{10,... | collective-permute-start | bytes 184328 | tf_op jit(solution)/shard_map/ppermute | solution.py:303
  110.3 5.2 %collective-permute-start.27 = (bf16[80,384]{1,0:T(8,128)(2,1)S(1)}, bf16[80,384]{1,0:T(8,128)(2,1)S(1)}, u32[]{:S(2)}, u32[]{:S(2)}) collective-permute-start(bf16[80,384]{1,0:T(8,128)(2,1)S(1)} %slice.90), channel_id=1, source_target_pairs={{0,2},{1,3},{2,0},{3,1},{4,6},{5,7},{6,4},{7,5},{8,10},{9,11},{10,... | collective-permute-start | bytes 184328 | tf_op jit(solution)/shard_map/ppermute | solution.py:303
  (17 other events, 123.4 us)

commit v11 on v10

--- a/solution.py
+++ b/solution.py
@@ -351,10 +351,11 @@
     dn_nears = widen([after(dn_near, gu_fars[-1])])
 
     hidden = up_call([near, far], [near_x, far_x], mine, other)
+    near_first = flip(after(dn_near, hidden), 1)
     hidden = after(hidden, dn_nears[-1])
     dn_far = after(dn_far, hidden)
     dn_fars = widen([dn_far])
-    nears = [(v, flip(after(v, hidden), 1)) for v in dn_nears]
+    nears = [(dn_near, near_first)] + [(v, flip(after(v, hidden), 1)) for v in dn_nears[1:]]
     fars = [(dn_far, flip(dn_far, 1))]
 
     chunks, crossed = [], []

time: 117 us -> 117 us (level)
  no operation moved by 1% of the time
where the time goes in v11:
time: 117 us
  waiting for transfers between devices  63.8 us (55%)
  starting transfers between devices  31 us (26%)
  Pallas kernels  16 us (14%)
  local copies, waits for them, and re-layouts  4.35 us (4%)
    ppermute x23, waiting for transfers between devices, flip(): return lax.ppermute(values, 'dp', [(i, i ^ bit) for i in range(ranks)])  46.3 us
    ppermute x8, waiting for transfers between devices, hop(): return lax.ppermute(values, 'expert', [(i, i ^ bit) for i in range(zones)])  17.5 us
    ppermute x23, starting transfers between devices, flip(): return lax.ppermute(values, 'dp', [(i, i ^ bit) for i in range(ranks)])  16.9 us
    ppermute x8, starting transfers between devices, hop(): return lax.ppermute(values, 'expert', [(i, i ^ bit) for i in range(zones)])  14.2 us
    pallas_call x1, Pallas kernels, up_call(): pl.pallas_call(functools.partial(up_kernel, len(mine) // 2, len(here)), i...  6.89 us
    unnamed x23, local copies, waits for them, and re-layouts  4.12 us
    pallas_call x4, Pallas kernels, down_call(): pl.pallas_call(functools.partial(down_kernel, tokens if send else 0), in_...  4.04 us
    pallas_call x1, Pallas kernels, front_call(): pl.pallas_call(functools.partial(front_kernel, ranks), grid=(steps,), in_...  2.38 us
  transfers between devices with their start and end apart: 31, of which 18 were waited for; matrix products, arithmetic and copies ran while one was open for 1% of the time, Pallas kernels for 11%

profile of v11, /device:TPU:0, one launch (start us, length us, event | category | flops | bytes accessed | tf_op | source)
XLA Modules:
  0.0 116.5 jit_solution(5091180623403230571)
XLA Ops:
  0.6 1.5 %copy-done = bf16[5,192,1024]{2,1,0:T(8,128)(2,1)S(1)} copy-done((bf16[5,192,1024]{2,1,0:T(8,128)(2,1)S(1)}, bf16[5,192,1024]{2,1,0:T(8,128)(2,1)}, u32[]{:S(2)}) %copy-start) | copy-done | bytes 1966104
  6.5 2.9 %collective-permute-start.8 = (bf16[5,384,256]{2,1,0:T(8,128)(2,1)S(1)}, bf16[5,384,256]{2,1,0:T(8,128)(2,1)S(1)}, u32[]{:S(2)}, u32[]{:S(2)}) collective-permute-start(bf16[5,384,256]{2,1,0:T(8,128)(2,1)S(1)} %get-tuple-element.37.refs_4_), channel_id=1, source_target_pairs={{0,16},{4,20},{8,24},{12,28},{16,0},{20,4},{24,8},{28,12},{1,17},{... | collective-permute-start | bytes 2949128 | tf_op jit(solution)/shard_map/ppermute | solution.py:300
  11.2 2.3 %copy-done.1 = bf16[1536,1536]{1,0:T(8,128)(2,1)S(1)} copy-done((bf16[1536,1536]{1,0:T(8,128)(2,1)S(1)}, bf16[1536,1536]{1,0:T(8,128)(2,1)}, u32[]{:S(2)}) %copy-start.1) | copy-done | bytes 4718616
  13.5 2.4 %front.1 = (bf16[80,1536]{1,0:T(8,128)(2,1)S(1)}, bf16[80,1664]{1,0:T(8,128)(2,1)S(1)}) custom-call(bf16[80,1536]{1,0:T(8,128)(2,1)S(1)} %copy-done.3, bf16[80,1536]{1,0:T(8,128)(2,1)S(1)} %copy-done.4, bf16[1536,1536]{1,0:T(8,128)(2,1)S(1)} %copy-done.1, f32[1,1536]{1,0:T(1,128)S(1)} %broadcast_in_dim.9.gain_ref, s32[80,8]{1,0:T(8,128)S(1)} %copy.12.routes_ref, ...), custom_call_target="tpu_custom_call" | custom-call | flops 1 | bytes 1 | tf_op jit(solution)/shard_map/front/pallas_call | solution.py:91
  15.9 2.7 %collective-permute-start = (bf16[80,1664]{1,0:T(8,128)(2,1)S(1)}, bf16[80,1664]{1,0:T(8,128)(2,1)S(1)}, u32[]{:S(2)}, u32[]{:S(2)}) collective-permute-start(bf16[80,1664]{1,0:T(8,128)(2,1)S(1)} %get-tuple-element.35), channel_id=1, source_target_pairs={{0,2},{1,3},{2,0},{3,1},{4,6},{5,7},{6,4},{7,5},{8,10},{9,11},{10,... | collective-permute-start | bytes 798728 | tf_op jit(solution)/shard_map/ppermute | solution.py:303
  18.6 12.9 %collective-permute-done.8.refs_6_ = bf16[5,384,256]{2,1,0:T(8,128)(2,1)S(1)} collective-permute-done((bf16[5,384,256]{2,1,0:T(8,128)(2,1)S(1)}, bf16[5,384,256]{2,1,0:T(8,128)(2,1)S(1)}, u32[]{:S(2)}, u32[]{:S(2)}) %collective-permute-start.8) | collective-permute-done | bytes 983072 | tf_op jit(solution)/shard_map/ppermute | solution.py:300
  31.4 1.7 %collective-permute-done.7.refs_5_ = bf16[5,384,256]{2,1,0:T(8,128)(2,1)S(1)} collective-permute-done((bf16[5,384,256]{2,1,0:T(8,128)(2,1)}, bf16[5,384,256]{2,1,0:T(8,128)(2,1)S(1)}, u32[]{:S(2)}, u32[]{:S(2)}) %collective-permute-start.7) | collective-permute-done | bytes 983072 | tf_op jit(solution)/shard_map/ppermute | solution.py:300
  33.5 1.9 %collective-permute-start.1 = (bf16[160,1664]{1,0:T(8,128)(2,1)S(1)}, bf16[160,1664]{1,0:T(8,128)(2,1)S(1)}, u32[]{:S(2)}, u32[]{:S(2)}) collective-permute-start(bf16[160,1664]{1,0:T(8,128)(2,1)S(1)} %constant_dynamic-update-slice_fusion.refs_0_), channel_id=1, source_target_pairs={{0,1},{1,0},{2,3},{3,2},{4,5},{5,4},{6,7},{7,6},{8,9},{9,8},{10,11... | collective-permute-start | bytes 1597448 | tf_op jit(solution)/shard_map/ppermute | solution.py:303
  35.3 1.5 %collective-permute-start.5 = (bf16[160,1664]{1,0:T(8,128)(2,1)S(1)}, bf16[160,1664]{1,0:T(8,128)(2,1)S(1)}, u32[]{:S(2)}, u32[]{:S(2)}) collective-permute-start(bf16[160,1664]{1,0:T(8,128)(2,1)S(1)} %constant_dynamic-update-slice_fusion.refs_0_), channel_id=1, source_target_pairs={{0,8},{4,12},{8,0},{12,4},{16,24},{20,28},{24,16},{28,20},{1,9},{5... | collective-permute-start | bytes 1597448 | tf_op jit(solution)/shard_map/ppermute | solution.py:300
  36.8 9.7 %collective-permute-done.1.refs_1_ = bf16[160,1664]{1,0:T(8,128)(2,1)S(1)} collective-permute-done((bf16[160,1664]{1,0:T(8,128)(2,1)S(1)}, bf16[160,1664]{1,0:T(8,128)(2,1)S(1)}, u32[]{:S(2)}, u32[]{:S(2)}) %collective-permute-start.1) | collective-permute-done | bytes 532512 | tf_op jit(solution)/shard_map/ppermute | solution.py:303
  50.0 5.8 %collective-permute-done.9.refs_7_ = bf16[5,384,256]{2,1,0:T(8,128)(2,1)S(1)} collective-permute-done((bf16[5,384,256]{2,1,0:T(8,128)(2,1)S(1)}, bf16[5,384,256]{2,1,0:T(8,128)(2,1)S(1)}, u32[]{:S(2)}, u32[]{:S(2)}) %collective-permute-start.9) | collective-permute-done | bytes 983072 | tf_op jit(solution)/shard_map/ppermute | solution.py:300
  56.3 2.4 %collective-permute-done.14.away_in_ref = bf16[5,192,128]{2,1,0:T(8,128)(2,1)S(1)} collective-permute-done((bf16[5,192,128]{2,1,0:T(8,128)(2,1)S(1)}, bf16[5,192,128]{2,1,0:T(8,128)(2,1)S(1)}, u32[]{:S(2)}, u32[]{:S(2)}) %collective-permute-start.14) | collective-permute-done | bytes 245792 | tf_op jit(solution)/shard_map/ppermute | solution.py:300
  60.9 6.9 %up.1.h_ref = bf16[640,1280]{1,0:T(8,128)(2,1)S(1)} custom-call(bf16[160,1664]{1,0:T(8,128)(2,1)S(1)} %constant_dynamic-update-slice_fusion.refs_0_, bf16[160,1664]{1,0:T(8,128)(2,1)S(1)} %collective-permute-done.1.refs_1_, bf16[160,1664]{1,0:T(8,128)(2,1)S(1)} %collective-permute-done.5.refs_2_, bf16[160,1664]{1,0:T(8,128)(2,1)S(1)} %collective-permute-done.6.refs_3_, ...), custom_call_target="tpu_custom_call" | custom-call | flops 1 | bytes 1 | tf_op jit(solution)/shard_map/up/pallas_call | solution.py:202
  67.8 4.4 %collective-permute-done.15.near_ref = bf16[5,384,128]{2,1,0:T(8,128)(2,1)S(1)} collective-permute-done((bf16[5,384,128]{2,1,0:T(8,128)(2,1)S(1)}, bf16[5,384,128]{2,1,0:T(8,128)(2,1)S(1)}, u32[]{:S(2)}, u32[]{:S(2)}) %collective-permute-start.15) | collective-permute-done | bytes 491552 | tf_op jit(solution)/shard_map/ppermute | solution.py:300
  77.5 8.6 %collective-permute-done.23.far_ref = bf16[5,384,128]{2,1,0:T(8,128)(2,1)S(1)} collective-permute-done((bf16[5,384,128]{2,1,0:T(8,128)(2,1)S(1)}, bf16[5,384,128]{2,1,0:T(8,128)(2,1)S(1)}, u32[]{:S(2)}, u32[]{:S(2)}) %collective-permute-start.23) | collective-permute-done | bytes 491552 | tf_op jit(solution)/shard_map/ppermute | solution.py:300
  87.2 2.3 %collective-permute-done.19 = bf16[320,768]{1,0:T(8,128)(2,1)S(1)} collective-permute-done((bf16[320,768]{1,0:T(8,128)(2,1)S(1)}, bf16[320,768]{1,0:T(8,128)(2,1)S(1)}, u32[]{:S(2)}, u32[]{:S(2)}) %collective-permute-start.19) | collective-permute-done | bytes 491552 | tf_op jit(solution)/shard_map/ppermute | solution.py:300
  92.1 1.6 %collective-permute-start.20 = (bf16[160,768]{1,0:T(8,128)(2,1)S(1)}, bf16[160,768]{1,0:T(8,128)(2,1)S(1)}, u32[]{:S(2)}, u32[]{:S(2)}) collective-permute-start(bf16[160,768]{1,0:T(8,128)(2,1)S(1)} %slice.85), channel_id=1, source_target_pairs={{0,1},{1,0},{2,3},{3,2},{4,5},{5,4},{6,7},{7,6},{8,9},{9,8},{10,11... | collective-permute-start | bytes 737288 | tf_op jit(solution)/shard_map/ppermute | solution.py:303
  95.3 4.1 %collective-permute-done.28 = bf16[320,384]{1,0:T(8,128)(2,1)S(1)} collective-permute-done((bf16[320,384]{1,0:T(8,128)(2,1)S(1)}, bf16[320,384]{1,0:T(8,128)(2,1)S(1)}, u32[]{:S(2)}, u32[]{:S(2)}) %collective-permute-start.28) | collective-permute-done | bytes 245792 | tf_op jit(solution)/shard_map/ppermute | solution.py:300
  99.5 1.5 %collective-permute-start.29 = (bf16[160,384]{1,0:T(8,128)(2,1)S(1)}, bf16[160,384]{1,0:T(8,128)(2,1)S(1)}, u32[]{:S(2)}, u32[]{:S(2)}) collective-permute-start(bf16[160,384]{1,0:T(8,128)(2,1)S(1)} %slice.86), channel_id=1, source_target_pairs={{0,1},{1,0},{2,3},{3,2},{4,5},{5,4},{6,7},{7,6},{8,9},{9,8},{10,11... | collective-permute-start | bytes 368648 | tf_op jit(solution)/shard_map/ppermute | solution.py:303
  101.1 2.7 %collective-permute-start.21 = (bf16[80,768]{1,0:T(8,128)(2,1)S(1)}, bf16[80,768]{1,0:T(8,128)(2,1)S(1)}, u32[]{:S(2)}, u32[]{:S(2)}) collective-permute-start(bf16[80,768]{1,0:T(8,128)(2,1)S(1)} %slice.88), channel_id=1, source_target_pairs={{0,2},{1,3},{2,0},{3,1},{4,6},{5,7},{6,4},{7,5},{8,10},{9,11},{10,... | collective-permute-start | bytes 368648 | tf_op jit(solution)/shard_map/ppermute | solution.py:303
  104.8 3.7 %collective-permute-done.21.refs_1_ = bf16[80,768]{1,0:T(8,128)(2,1)S(1)} collective-permute-done((bf16[80,768]{1,0:T(8,128)(2,1)S(1)}, bf16[80,768]{1,0:T(8,128)(2,1)S(1)}, u32[]{:S(2)}, u32[]{:S(2)}) %collective-permute-start.21) | collective-permute-done | bytes 122912 | tf_op jit(solution)/shard_map/ppermute | solution.py:303
  108.5 1.8 %collective-permute-start.30 = (bf16[80,384]{1,0:T(8,128)(2,1)S(1)}, bf16[80,384]{1,0:T(8,128)(2,1)S(1)}, u32[]{:S(2)}, u32[]{:S(2)}) collective-permute-start(bf16[80,384]{1,0:T(8,128)(2,1)S(1)} %slice.89), channel_id=1, source_target_pairs={{0,2},{1,3},{2,0},{3,1},{4,6},{5,7},{6,4},{7,5},{8,10},{9,11},{10,... | collective-permute-start | bytes 184328 | tf_op jit(solution)/shard_map/ppermute | solution.py:303
  111.7 1.9 %collective-permute-done.30.refs_5_ = bf16[80,384]{1,0:T(8,128)(2,1)S(1)} collective-permute-done((bf16[80,384]{1,0:T(8,128)(2,1)S(1)}, bf16[80,384]{1,0:T(8,128)(2,1)S(1)}, u32[]{:S(2)}, u32[]{:S(2)}) %collective-permute-start.30) | collective-permute-done | bytes 61472 | tf_op jit(solution)/shard_map/ppermute | solution.py:303
  113.6 1.9 %collective-permute-done.27.refs_3_ = bf16[80,384]{1,0:T(8,128)(2,1)S(1)} collective-permute-done((bf16[80,384]{1,0:T(8,128)(2,1)S(1)}, bf16[80,384]{1,0:T(8,128)(2,1)S(1)}, u32[]{:S(2)}, u32[]{:S(2)}) %collective-permute-start.27) | collective-permute-done | bytes 61472 | tf_op jit(solution)/shard_map/ppermute | solution.py:303
  (93 shorter events, 26.6 us)
Async XLA Ops:
  6.5 25.0 %collective-permute-start.8 = (bf16[5,384,256]{2,1,0:T(8,128)(2,1)S(1)}, bf16[5,384,256]{2,1,0:T(8,128)(2,1)S(1)}, u32[]{:S(2)}, u32[]{:S(2)}) collective-permute-start(bf16[5,384,256]{2,1,0:T(8,128)(2,1)S(1)} %get-tuple-element.37.refs_4_), channel_id=1, source_target_pairs={{0,16},{4,20},{8,24},{12,28},{16,0},{20,4},{24,8},{28,12},{1,17},{... | collective-permute-start | bytes 2949128 | tf_op jit(solution)/shard_map/ppermute | solution.py:300
  9.4 23.7 %collective-permute-start.7 = (bf16[5,384,256]{2,1,0:T(8,128)(2,1)}, bf16[5,384,256]{2,1,0:T(8,128)(2,1)S(1)}, u32[]{:S(2)}, u32[]{:S(2)}) collective-permute-start(bf16[5,384,256]{2,1,0:T(8,128)(2,1)} %get-tuple-element.40), channel_id=1, source_target_pairs={{0,8},{4,12},{8,0},{12,4},{16,24},{20,28},{24,16},{28,20},{1,9},{5... | collective-permute-start | bytes 2949128 | tf_op jit(solution)/shard_map/ppermute | solution.py:300
  10.9 24.5 %collective-permute-start.4 = (bf16[5,384,256]{2,1,0:T(8,128)(2,1)S(1)}, bf16[5,384,256]{2,1,0:T(8,128)(2,1)}, u32[]{:S(2)}, u32[]{:S(2)}) collective-permute-start(bf16[5,384,256]{2,1,0:T(8,128)(2,1)S(1)} %get-tuple-element.37.refs_4_), channel_id=1, source_target_pairs={{0,4},{4,0},{8,12},{12,8},{16,20},{20,16},{24,28},{28,24},{1,5},{5... | collective-permute-start | bytes 2949128 | tf_op jit(solution)/shard_map/ppermute | solution.py:300
  15.9 17.5 %collective-permute-start = (bf16[80,1664]{1,0:T(8,128)(2,1)S(1)}, bf16[80,1664]{1,0:T(8,128)(2,1)S(1)}, u32[]{:S(2)}, u32[]{:S(2)}) collective-permute-start(bf16[80,1664]{1,0:T(8,128)(2,1)S(1)} %get-tuple-element.35), channel_id=1, source_target_pairs={{0,2},{1,3},{2,0},{3,1},{4,6},{5,7},{6,4},{7,5},{8,10},{9,11},{10,... | collective-permute-start | bytes 798728 | tf_op jit(solution)/shard_map/ppermute | solution.py:303
  33.1 22.7 %collective-permute-start.9 = (bf16[5,384,256]{2,1,0:T(8,128)(2,1)S(1)}, bf16[5,384,256]{2,1,0:T(8,128)(2,1)S(1)}, u32[]{:S(2)}, u32[]{:S(2)}) collective-permute-start(bf16[5,384,256]{2,1,0:T(8,128)(2,1)S(1)} %collective-permute-done.7.refs_5_), channel_id=1, source_target_pairs={{0,16},{4,20},{8,24},{12,28},{16,0},{20,4},{24,8},{28,12},{1,17},{... | collective-permute-start | bytes 2949128 | tf_op jit(solution)/shard_map/ppermute | solution.py:300
  33.5 13.1 %collective-permute-start.1 = (bf16[160,1664]{1,0:T(8,128)(2,1)S(1)}, bf16[160,1664]{1,0:T(8,128)(2,1)S(1)}, u32[]{:S(2)}, u32[]{:S(2)}) collective-permute-start(bf16[160,1664]{1,0:T(8,128)(2,1)S(1)} %constant_dynamic-update-slice_fusion.refs_0_), channel_id=1, source_target_pairs={{0,1},{1,0},{2,3},{3,2},{4,5},{5,4},{6,7},{7,6},{8,9},{9,8},{10,11... | collective-permute-start | bytes 1597448 | tf_op jit(solution)/shard_map/ppermute | solution.py:303
  35.3 12.4 %collective-permute-start.5 = (bf16[160,1664]{1,0:T(8,128)(2,1)S(1)}, bf16[160,1664]{1,0:T(8,128)(2,1)S(1)}, u32[]{:S(2)}, u32[]{:S(2)}) collective-permute-start(bf16[160,1664]{1,0:T(8,128)(2,1)S(1)} %constant_dynamic-update-slice_fusion.refs_0_), channel_id=1, source_target_pairs={{0,8},{4,12},{8,0},{12,4},{16,24},{20,28},{24,16},{28,20},{1,9},{5... | collective-permute-start | bytes 1597448 | tf_op jit(solution)/shard_map/ppermute | solution.py:300
  47.8 11.7 %collective-permute-start.6 = (bf16[160,1664]{1,0:T(8,128)(2,1)S(1)}, bf16[160,1664]{1,0:T(8,128)(2,1)S(1)}, u32[]{:S(2)}, u32[]{:S(2)}) collective-permute-start(bf16[160,1664]{1,0:T(8,128)(2,1)S(1)} %collective-permute-done.1.refs_1_), channel_id=1, source_target_pairs={{0,8},{4,12},{8,0},{12,4},{16,24},{20,28},{24,16},{28,20},{1,9},{5... | collective-permute-start | bytes 1597448 | tf_op jit(solution)/shard_map/ppermute | solution.py:300
  49.4 6.4 %collective-permute-start.13 = (bf16[5,192,128]{2,1,0:T(8,128)(2,1)S(1)}, bf16[5,192,128]{2,1,0:T(8,128)(2,1)S(1)}, u32[]{:S(2)}, u32[]{:S(2)}) collective-permute-start(bf16[5,192,128]{2,1,0:T(8,128)(2,1)S(1)} %get-tuple-element.43), channel_id=1, source_target_pairs={{0,4},{4,0},{8,12},{12,8},{16,20},{20,16},{24,28},{28,24},{1,5},{5... | collective-permute-start | bytes 737288 | tf_op jit(solution)/shard_map/ppermute | solution.py:300
  49.4 11.4 %collective-permute-start.11 = (bf16[5,384,256]{2,1,0:T(8,128)(2,1)S(1)}, bf16[5,384,256]{2,1,0:T(8,128)(2,1)S(1)}, u32[]{:S(2)}, u32[]{:S(2)}) collective-permute-start(bf16[5,384,256]{2,1,0:T(8,128)(2,1)S(1)} %collective-permute-done.8.refs_6_), channel_id=1, source_target_pairs={{0,4},{4,0},{8,12},{12,8},{16,20},{20,16},{24,28},{28,24},{1,5},{5... | collective-permute-start | bytes 2949128 | tf_op jit(solution)/shard_map/ppermute | solution.py:300
  49.9 10.9 %collective-permute-start.10 = (bf16[5,384,256]{2,1,0:T(8,128)(2,1)S(1)}, bf16[5,384,256]{2,1,0:T(8,128)(2,1)S(1)}, u32[]{:S(2)}, u32[]{:S(2)}) collective-permute-start(bf16[5,384,256]{2,1,0:T(8,128)(2,1)S(1)} %collective-permute-done.7.refs_5_), channel_id=1, source_target_pairs={{0,4},{4,0},{8,12},{12,8},{16,20},{20,16},{24,28},{28,24},{1,5},{5... | collective-permute-start | bytes 2949128 | tf_op jit(solution)/shard_map/ppermute | solution.py:300
  58.8 13.3 %collective-permute-start.15 = (bf16[5,384,128]{2,1,0:T(8,128)(2,1)S(1)}, bf16[5,384,128]{2,1,0:T(8,128)(2,1)S(1)}, u32[]{:S(2)}, u32[]{:S(2)}) collective-permute-start(bf16[5,384,128]{2,1,0:T(8,128)(2,1)S(1)} %get-tuple-element.48.near_ref), channel_id=1, source_target_pairs={{0,16},{4,20},{8,24},{12,28},{16,0},{20,4},{24,8},{28,12},{1,17},{... | collective-permute-start | bytes 1474568 | tf_op jit(solution)/shard_map/ppermute | solution.py:300
  59.5 13.0 %collective-permute-start.17 = (bf16[5,384,128]{2,1,0:T(8,128)(2,1)S(1)}, bf16[5,384,128]{2,1,0:T(8,128)(2,1)S(1)}, u32[]{:S(2)}, u32[]{:S(2)}) collective-permute-start(bf16[5,384,128]{2,1,0:T(8,128)(2,1)S(1)} %get-tuple-element.50), channel_id=1, source_target_pairs={{0,8},{4,12},{8,0},{12,4},{16,24},{20,28},{24,16},{28,20},{1,9},{5... | collective-permute-start | bytes 1474568 | tf_op jit(solution)/shard_map/ppermute | solution.py:300
  73.0 13.1 %collective-permute-start.23 = (bf16[5,384,128]{2,1,0:T(8,128)(2,1)S(1)}, bf16[5,384,128]{2,1,0:T(8,128)(2,1)S(1)}, u32[]{:S(2)}, u32[]{:S(2)}) collective-permute-start(bf16[5,384,128]{2,1,0:T(8,128)(2,1)S(1)} %collective-permute-done.17.far_ref), channel_id=1, source_target_pairs={{0,16},{4,20},{8,24},{12,28},{16,0},{20,4},{24,8},{28,12},{1,17},{... | collective-permute-start | bytes 1474568 | tf_op jit(solution)/shard_map/ppermute | solution.py:300
  74.4 15.0 %collective-permute-start.22 = (bf16[5,384,128]{2,1,0:T(8,128)(2,1)S(1)}, bf16[5,384,128]{2,1,0:T(8,128)(2,1)S(1)}, u32[]{:S(2)}, u32[]{:S(2)}) collective-permute-start(bf16[5,384,128]{2,1,0:T(8,128)(2,1)S(1)} %collective-permute-done.15.near_ref), channel_id=1, source_target_pairs={{0,4},{4,0},{8,12},{12,8},{16,20},{20,16},{24,28},{28,24},{1,5},{5... | collective-permute-start | bytes 1474568 | tf_op jit(solution)/shard_map/ppermute | solution.py:300
  76.1 13.3 %collective-permute-start.19 = (bf16[320,768]{1,0:T(8,128)(2,1)S(1)}, bf16[320,768]{1,0:T(8,128)(2,1)S(1)}, u32[]{:S(2)}, u32[]{:S(2)}) collective-permute-start(bf16[320,768]{1,0:T(8,128)(2,1)S(1)} %down.4), channel_id=1, source_target_pairs={{0,8},{4,12},{8,0},{12,4},{16,24},{20,28},{24,16},{28,20},{1,9},{5... | collective-permute-start | bytes 1474568 | tf_op jit(solution)/shard_map/ppermute | solution.py:300
  90.4 9.0 %collective-permute-start.28 = (bf16[320,384]{1,0:T(8,128)(2,1)S(1)}, bf16[320,384]{1,0:T(8,128)(2,1)S(1)}, u32[]{:S(2)}, u32[]{:S(2)}) collective-permute-start(bf16[320,384]{1,0:T(8,128)(2,1)S(1)} %get-tuple-element.56), channel_id=1, source_target_pairs={{0,8},{4,12},{8,0},{12,4},{16,24},{20,28},{24,16},{28,20},{1,9},{5... | collective-permute-start | bytes 737288 | tf_op jit(solution)/shard_map/ppermute | solution.py:300
  92.1 8.9 %collective-permute-start.20 = (bf16[160,768]{1,0:T(8,128)(2,1)S(1)}, bf16[160,768]{1,0:T(8,128)(2,1)S(1)}, u32[]{:S(2)}, u32[]{:S(2)}) collective-permute-start(bf16[160,768]{1,0:T(8,128)(2,1)S(1)} %slice.85), channel_id=1, source_target_pairs={{0,1},{1,0},{2,3},{3,2},{4,5},{5,4},{6,7},{7,6},{8,9},{9,8},{10,11... | collective-permute-start | bytes 737288 | tf_op jit(solution)/shard_map/ppermute | solution.py:303
  93.7 10.0 %collective-permute-start.25 = (bf16[320,384]{1,0:T(8,128)(2,1)S(1)}, bf16[320,384]{1,0:T(8,128)(2,1)S(1)}, u32[]{:S(2)}, u32[]{:S(2)}) collective-permute-start(bf16[320,384]{1,0:T(8,128)(2,1)S(1)} %get-tuple-element.59), channel_id=1, source_target_pairs={{0,8},{4,12},{8,0},{12,4},{16,24},{20,28},{24,16},{28,20},{1,9},{5... | collective-permute-start | bytes 737288 | tf_op jit(solution)/shard_map/ppermute | solution.py:300
  99.5 5.3 %collective-permute-start.29 = (bf16[160,384]{1,0:T(8,128)(2,1)S(1)}, bf16[160,384]{1,0:T(8,128)(2,1)S(1)}, u32[]{:S(2)}, u32[]{:S(2)}) collective-permute-start(bf16[160,384]{1,0:T(8,128)(2,1)S(1)} %slice.86), channel_id=1, source_target_pairs={{0,1},{1,0},{2,3},{3,2},{4,5},{5,4},{6,7},{7,6},{8,9},{9,8},{10,11... | collective-permute-start | bytes 368648 | tf_op jit(solution)/shard_map/ppermute | solution.py:303
  101.1 7.4 %collective-permute-start.21 = (bf16[80,768]{1,0:T(8,128)(2,1)S(1)}, bf16[80,768]{1,0:T(8,128)(2,1)S(1)}, u32[]{:S(2)}, u32[]{:S(2)}) collective-permute-start(bf16[80,768]{1,0:T(8,128)(2,1)S(1)} %slice.88), channel_id=1, source_target_pairs={{0,2},{1,3},{2,0},{3,1},{4,6},{5,7},{6,4},{7,5},{8,10},{9,11},{10,... | collective-permute-start | bytes 368648 | tf_op jit(solution)/shard_map/ppermute | solution.py:303
  103.8 6.5 %collective-permute-start.26 = (bf16[160,384]{1,0:T(8,128)(2,1)S(1)}, bf16[160,384]{1,0:T(8,128)(2,1)S(1)}, u32[]{:S(2)}, u32[]{:S(2)}) collective-permute-start(bf16[160,384]{1,0:T(8,128)(2,1)S(1)} %slice.87), channel_id=1, source_target_pairs={{0,1},{1,0},{2,3},{3,2},{4,5},{5,4},{6,7},{7,6},{8,9},{9,8},{10,11... | collective-permute-start | bytes 368648 | tf_op jit(solution)/shard_map/ppermute | solution.py:303
  108.5 5.1 %collective-permute-start.30 = (bf16[80,384]{1,0:T(8,128)(2,1)S(1)}, bf16[80,384]{1,0:T(8,128)(2,1)S(1)}, u32[]{:S(2)}, u32[]{:S(2)}) collective-permute-start(bf16[80,384]{1,0:T(8,128)(2,1)S(1)} %slice.89), channel_id=1, source_target_pairs={{0,2},{1,3},{2,0},{3,1},{4,6},{5,7},{6,4},{7,5},{8,10},{9,11},{10,... | collective-permute-start | bytes 184328 | tf_op jit(solution)/shard_map/ppermute | solution.py:303
  110.3 5.2 %collective-permute-start.27 = (bf16[80,384]{1,0:T(8,128)(2,1)S(1)}, bf16[80,384]{1,0:T(8,128)(2,1)S(1)}, u32[]{:S(2)}, u32[]{:S(2)}) collective-permute-start(bf16[80,384]{1,0:T(8,128)(2,1)S(1)} %slice.90), channel_id=1, source_target_pairs={{0,2},{1,3},{2,0},{3,1},{4,6},{5,7},{6,4},{7,5},{8,10},{9,11},{10,... | collective-permute-start | bytes 184328 | tf_op jit(solution)/shard_map/ppermute | solution.py:303
  (17 other events, 123.4 us)
